TPU v7x, 32 devices: a whole 2x2x4 slice. The times are simulated.
32 devices in a mesh: seq: 4 (over y, core), ctx: 8 (over z, x).
Axes of the slice: x: 2, y: 2, z: 4, core: 2. Of those that a mesh axis runs over, the one named last changes fastest.
Arguments:
- block_input: bfloat16 [4, 8, 128, 1600], P('seq', 'ctx'), may hold values from -6 to 6
- out_cot: bfloat16 [4, 8, 128, 1600], P('seq', 'ctx'), may hold values from -6 to 6
- pair_of: int32 [8], replicated, may hold values from 0 to 7, each once
- ln1_gain: float32 [1600], replicated, may hold values from 0.5 to 1.5
- ln1_bias: float32 [1600], replicated, may hold values from -2 to 2
- qkv_weight: bfloat16 [1600, 4800], P('seq', 'ctx'), may hold values from -0.15625 to 0.15625
- qv_bias: float32 [2, 1600], replicated, may hold values from -3 to 3
- out_weight: bfloat16 [1600, 1600], P('seq', 'ctx'), may hold values from -0.625 to 0.625
- out_bias: float32 [1600], replicated, may hold values from -3 to 3
- ln2_gain: float32 [1600], replicated, may hold values from 0.5 to 1.5
- ln2_bias: float32 [1600], replicated, may hold values from -2 to 2
- fc_weight: bfloat16 [1600, 6400], P('seq', 'ctx'), may hold values from -0.15625 to 0.15625
- fc_bias: float32 [6400], replicated, may hold values from -3 to 3
- proj_weight: bfloat16 [6400, 1600], P('ctx', 'seq'), may hold values from -0.078125 to 0.078125
- proj_bias: float32 [1600], replicated, may hold values from -3 to 3
Outputs:
- block_output: bfloat16 [4, 8, 128, 1600], P('seq', 'ctx')
- input_grad: bfloat16 [4, 8, 128, 1600], P('seq', 'ctx')
- ln1_gain_grad: float32 [1600], replicated
- ln1_bias_grad: float32 [1600], replicated
- qkv_weight_grad: float32 [1600, 4800], P('seq', 'ctx')
- qv_bias_grad: float32 [2, 1600], replicated
- out_weight_grad: float32 [1600, 1600], P('seq', 'ctx')
- out_bias_grad: float32 [1600], replicated
- ln2_gain_grad: float32 [1600], replicated
- ln2_bias_grad: float32 [1600], replicated
- fc_weight_grad: float32 [1600, 6400], P('seq', 'ctx')
- fc_bias_grad: float32 [6400], replicated
- proj_weight_grad: float32 [6400, 1600], P('ctx', 'seq')
- proj_bias_grad: float32 [1600], replicated
Inputs may be any that keep to these rules, and one draw needn't show every extreme that they name: `pair_of`: a permutation: each context rank gets a different pair of blocks p and 15 - p.
All inputs are finite; a program needn't handle non-finite values.
Results may differ from a plain program's by a relative error of at most 0.012.
Values may be sent and summed in bfloat16 or wider, within the bound.
No kernel may reach another device: no remote copies, remote signals or barrier semaphores. Data moves between devices by JAX's collectives and lax.ppermute only.
A program may use at most 576 MiB of HBM per device.

v0:
```python
import math

import jax
import jax.numpy as jnp
from jax import lax
from jax.sharding import PartitionSpec as P

HEAD = 64


EPSILON = 1e-05
NEGATIVE = -1e30
GELU_COEF = 0.7978845608028654


def layer_norm(values, gain, shift):
    center = values - jnp.mean(values, axis=-1, keepdims=True)
    spread = jnp.mean(center * center, axis=-1, keepdims=True)
    return center * lax.rsqrt(spread + EPSILON) * gain + shift


def gelu_tanh(values):
    return (
        0.5 * values * (1.0 + jnp.tanh(GELU_COEF * (values + 0.044715 * values * values * values)))
    )


def positions(pair_of, block):
    ranks = pair_of.shape[0]
    local_index = jnp.arange(2 * block, dtype=jnp.int32)
    first_half = local_index < block
    chosen = jnp.where(first_half[None, :], pair_of[:, None], 2 * ranks - 1 - pair_of[:, None])
    return (chosen * block + local_index[None, :] % block).reshape(-1)


def split_heads(values):
    return values.reshape(values.shape[0], values.shape[1], values.shape[2] // HEAD, HEAD)


def times_transposed(left, right):
    return lax.dot_general(
        left, right, (((1,), (1,)), ((), ())), preferred_element_type=jnp.float32
    )


def transposed_times(left, right):
    return lax.dot_general(
        left, right, (((0,), (0,)), ((), ())), preferred_element_type=jnp.float32
    )


def with_bias(left, shift, piece):
    return jnp.dot(left, piece, preferred_element_type=jnp.float32) + shift


def fold_back(grad_low, piece):
    return times_transposed(grad_low, piece)


def body(
    block_input,
    out_cot,
    pair_of,
    ln1_gain,
    ln1_bias,
    qkv_weight,
    qv_bias,
    out_weight,
    out_bias,
    ln2_gain,
    ln2_bias,
    fc_weight,
    fc_bias,
    proj_weight,
    proj_bias,
):
    seqs_here = block_input.shape[0]
    rows_here = block_input.shape[2]
    width = block_input.shape[3]
    heads = width // HEAD
    scale = 1.0 / math.sqrt(HEAD)
    token_count = seqs_here * rows_here
    inputs = block_input.reshape(token_count, width).astype(jnp.float32)
    cot_low = out_cot.reshape(token_count, width)
    cot_full = cot_low.astype(jnp.float32)
    key_pos = positions(pair_of, rows_here // 2)
    my_rank = lax.axis_index("ctx")
    query_pos = lax.dynamic_slice_in_dim(key_pos, my_rank * rows_here, rows_here)
    qkv_cols, out_cols, fc_cols, proj_rows = (
        lax.all_gather(qkv_weight, "seq", axis=0, tiled=True),
        lax.all_gather(out_weight, "seq", axis=0, tiled=True),
        lax.all_gather(fc_weight, "seq", axis=0, tiled=True),
        lax.all_gather(proj_weight, "seq", axis=1, tiled=True),
    )
    qkv_shift = jnp.concatenate([qv_bias[0], jnp.zeros_like(qv_bias[0]), qv_bias[1]])
    normed_one = layer_norm(inputs, ln1_gain, ln1_bias)
    normed_low = normed_one.astype(jnp.bfloat16)
    qkv_full = with_bias(normed_low, qkv_shift, lax.all_gather(qkv_cols, "ctx", axis=1, tiled=True))
    qkv_low = qkv_full.astype(jnp.bfloat16).reshape(seqs_here, rows_here, 3, width)
    query_low = qkv_low[:, :, 0]
    key_low = qkv_low[:, :, 1]
    value_low = qkv_low[:, :, 2]
    query_heads = split_heads(query_low)
    key_heads = split_heads(key_low)
    value_heads = split_heads(value_low)
    top = jnp.full((seqs_here, heads, rows_here), NEGATIVE, jnp.float32)
    key_piece = lax.all_gather(key_low, "ctx", axis=1, tiled=True)
    value_piece = lax.all_gather(value_low, "ctx", axis=1, tiled=True)
    piece_pos = key_pos
    allowed = piece_pos[None, :] <= query_pos[:, None]
    score = (
        jnp.einsum(
            "sqhd,skhd->shqk",
            query_heads,
            split_heads(key_piece),
            preferred_element_type=jnp.float32,
        )
        * scale
    )
    masked = jnp.where(allowed, score, NEGATIVE)
    new_top = jnp.maximum(top, jnp.max(masked, axis=-1))
    weight = jnp.where(allowed, jnp.exp(masked - new_top[..., None]), 0.0)
    total = jnp.sum(weight, axis=-1)
    accum = jnp.einsum(
        "shqk,skhd->shqd",
        weight,
        split_heads(value_piece).astype(jnp.float32),
        precision=lax.Precision.HIGHEST,
    )
    top, total, accum = (new_top, total, accum)
    log_total = top + jnp.log(total)
    attn_heads = accum / total[..., None]
    attn_full = jnp.transpose(attn_heads, (0, 2, 1, 3)).reshape(token_count, width)
    attn_low = attn_full.astype(jnp.bfloat16)
    branch_one = with_bias(attn_low, out_bias, lax.all_gather(out_cols, "ctx", axis=1, tiled=True))
    middle = inputs + branch_one
    normed_two = layer_norm(middle, ln2_gain, ln2_bias)
    normed_two_low = normed_two.astype(jnp.bfloat16)
    hidden_pre = with_bias(
        normed_two_low, fc_bias, lax.all_gather(fc_cols, "ctx", axis=1, tiled=True)
    )
    hidden_low = gelu_tanh(hidden_pre).astype(jnp.bfloat16)
    branch_two = jnp.dot(
        hidden_low,
        lax.all_gather(proj_rows, "ctx", axis=0, tiled=True),
        preferred_element_type=jnp.float32,
    )
    output_full = middle + branch_two + proj_bias
    block_output = output_full.astype(jnp.bfloat16).reshape(block_input.shape)
    hidden_grad = times_transposed(cot_low, lax.all_gather(proj_rows, "ctx", axis=0, tiled=True))
    _, gelu_back = jax.vjp(gelu_tanh, hidden_pre)
    hidden_pre_grad = gelu_back(hidden_grad)[0].astype(jnp.bfloat16)
    normed_two_grad = fold_back(hidden_pre_grad, lax.all_gather(fc_cols, "ctx", axis=1, tiled=True))
    _, norm_two_back = jax.vjp(layer_norm, middle, ln2_gain, ln2_bias)
    middle_part, gain_two_grad, shift_two_grad = norm_two_back(normed_two_grad)
    middle_grad = cot_full + middle_part
    branch_grad_low = middle_grad.astype(jnp.bfloat16)
    attn_grad = fold_back(branch_grad_low, lax.all_gather(out_cols, "ctx", axis=1, tiled=True))
    attn_grad_low = attn_grad.astype(jnp.bfloat16)
    row_delta = jnp.sum(
        (attn_grad_low.astype(jnp.float32) * attn_full).reshape(seqs_here, rows_here, heads, HEAD),
        axis=-1,
    )
    delta_heads = jnp.transpose(row_delta, (0, 2, 1))
    log_rows = jnp.transpose(log_total, (0, 2, 1))
    grad_rows = attn_grad_low.reshape(seqs_here, rows_here, width)
    grad_heads = split_heads(grad_rows)
    sent = (
        key_low.astype(jnp.float32),
        value_low.astype(jnp.float32),
        query_low.astype(jnp.float32),
        grad_rows.astype(jnp.float32),
        log_rows,
        row_delta,
    )
    key_piece = lax.all_gather(sent[0], "ctx", axis=1, tiled=True)
    value_piece = lax.all_gather(sent[1], "ctx", axis=1, tiled=True)
    query_piece = lax.all_gather(sent[2], "ctx", axis=1, tiled=True)
    grad_piece = lax.all_gather(sent[3], "ctx", axis=1, tiled=True)
    log_piece = lax.all_gather(sent[4], "ctx", axis=1, tiled=True)
    delta_piece = lax.all_gather(sent[5], "ctx", axis=1, tiled=True)
    piece_pos = key_pos
    piece_keys = split_heads(key_piece.astype(jnp.bfloat16))
    piece_values = split_heads(value_piece.astype(jnp.bfloat16))
    piece_queries = split_heads(query_piece.astype(jnp.bfloat16))
    piece_grads = split_heads(grad_piece.astype(jnp.bfloat16))
    allowed = piece_pos[None, :] <= query_pos[:, None]
    score = (
        jnp.einsum("sqhd,skhd->shqk", query_heads, piece_keys, preferred_element_type=jnp.float32)
        * scale
    )
    prob = jnp.where(allowed, jnp.exp(score - log_total[..., None]), 0.0)
    prob_grad = jnp.einsum(
        "sqhd,skhd->shqk", grad_heads, piece_values, preferred_element_type=jnp.float32
    )
    score_grad = (prob * (prob_grad - delta_heads[..., None])).astype(jnp.bfloat16)
    query_grad = (
        jnp.einsum("shqk,skhd->sqhd", score_grad, piece_keys, preferred_element_type=jnp.float32)
        * scale
    )
    allowed_back = query_pos[None, :] <= piece_pos[:, None]
    score_back = (
        jnp.einsum("sqhd,skhd->shqk", piece_queries, key_heads, preferred_element_type=jnp.float32)
        * scale
    )
    log_back = jnp.transpose(log_piece, (0, 2, 1))
    delta_back = jnp.transpose(delta_piece, (0, 2, 1))
    prob_back = jnp.where(allowed_back, jnp.exp(score_back - log_back[..., None]), 0.0)
    prob_back_grad = jnp.einsum(
        "sqhd,skhd->shqk", piece_grads, value_heads, preferred_element_type=jnp.float32
    )
    score_back_grad = (prob_back * (prob_back_grad - delta_back[..., None])).astype(jnp.bfloat16)
    key_grad = (
        jnp.einsum(
            "shqk,sqhd->skhd", score_back_grad, piece_queries, preferred_element_type=jnp.float32
        )
        * scale
    )
    value_grad = jnp.einsum(
        "shqk,sqhd->skhd",
        prob_back,
        piece_grads.astype(jnp.float32),
        precision=lax.Precision.HIGHEST,
    )
    query_grad, key_grad, value_grad = (query_grad, key_grad, value_grad)
    qkv_grad_low = jnp.concatenate(
        [
            query_grad.reshape(token_count, width),
            key_grad.reshape(token_count, width),
            value_grad.reshape(token_count, width),
        ],
        axis=1,
    ).astype(jnp.bfloat16)
    normed_one_grad = fold_back(qkv_grad_low, lax.all_gather(qkv_cols, "ctx", axis=1, tiled=True))
    _, norm_one_back = jax.vjp(layer_norm, inputs, ln1_gain, ln1_bias)
    input_part, gain_one_grad, shift_one_grad = norm_one_back(normed_one_grad)
    input_grad = (middle_grad + input_part).astype(jnp.bfloat16).reshape(block_input.shape)
    qkv_width = qkv_cols.shape[1]
    out_width = out_cols.shape[1]
    fc_width = fc_cols.shape[1]
    proj_height = proj_rows.shape[0]
    per_rows = qkv_width + out_width + fc_width + proj_height
    pairs = (
        (qkv_grad_low, normed_low, qkv_width),
        (branch_grad_low, attn_low, out_width),
        (hidden_pre_grad, normed_two_low, fc_width),
        (hidden_low, cot_low, proj_height),
    )
    ctx_count = lax.axis_size("ctx")
    quarter = width // lax.axis_size("seq")
    span = lax.axis_size(("seq", "ctx")) * per_rows // per_rows
    devices = jnp.arange(span, dtype=jnp.int32)

    def one_device(device):
        column = device % ctx_count
        part = device // ctx_count
        blocks = []
        for grad_low, data_low, size in pairs:
            picked = lax.dynamic_slice_in_dim(grad_low, column * size, size, 1)
            sliced = lax.dynamic_slice_in_dim(data_low, part * quarter, quarter, 1)
            blocks.append(transposed_times(picked, sliced))
        return jnp.concatenate(blocks, axis=0)

    shares = lax.psum_scatter(
        jax.vmap(one_device)(devices).reshape(span * per_rows, quarter),
        ("seq", "ctx"),
        scatter_dimension=0,
        tiled=True,
    )
    qkv_weight_grad = jnp.transpose(shares[:qkv_width])
    out_weight_grad = jnp.transpose(shares[qkv_width : qkv_width + out_width])
    fc_weight_grad = jnp.transpose(shares[qkv_width + out_width : qkv_width + out_width + fc_width])
    proj_weight_grad = shares[qkv_width + out_width + fc_width :]
    qkv_sums = jnp.sum(qkv_grad_low.astype(jnp.float32), axis=0)
    qv_terms = jnp.stack([qkv_sums[:width], qkv_sums[2 * width :]])
    vector_terms = (
        gain_one_grad,
        shift_one_grad,
        qv_terms,
        jnp.sum(branch_grad_low.astype(jnp.float32), axis=0),
        gain_two_grad,
        shift_two_grad,
        jnp.sum(hidden_pre_grad.astype(jnp.float32), axis=0),
        jnp.sum(cot_full, axis=0),
    )
    summed = lax.psum(
        (
            vector_terms[0],
            vector_terms[1],
            vector_terms[2],
            vector_terms[3],
            vector_terms[4],
            vector_terms[5],
            vector_terms[6],
            vector_terms[7],
        ),
        ("seq", "ctx"),
    )
    return (
        block_output,
        input_grad,
        summed[0],
        summed[1],
        qkv_weight_grad,
        summed[2],
        out_weight_grad,
        summed[3],
        summed[4],
        summed[5],
        fc_weight_grad,
        summed[6],
        proj_weight_grad,
        summed[7],
    )


def solution(mesh):
    placed = (
        P("seq", "ctx", None, None),
        P("seq", "ctx", None, None),
        P(),
        P(),
        P(),
        P("seq", "ctx"),
        P(),
        P("seq", "ctx"),
        P(),
        P(),
        P(),
        P("seq", "ctx"),
        P(),
        P("ctx", "seq"),
        P(),
    )
    return jax.shard_map(
        body,
        mesh=mesh,
        in_specs=placed,
        out_specs=(
            P("seq", "ctx", None, None),
            P("seq", "ctx", None, None),
            P(),
            P(),
            P("seq", "ctx"),
            P(),
            P("seq", "ctx"),
            P(),
            P(),
            P(),
            P("seq", "ctx"),
            P(),
            P("ctx", "seq"),
            P(),
        ),
        check_vma=False,
    )
```

profile of v0, /device:TPU:0, one launch (start us, length us, event | category | flops | bytes accessed | tf_op | source)
XLA Modules:
  0.0 3743.8 jit_solution(8320652169602725491)
XLA Ops:
  8.0 26.6 all-gather.21.cloned.1.call-done
  34.6 4.1 copy.86
  41.3 215.4 %all-gather.23.cloned.1.call-done = bf16[1600,4800]{0,1:T(8,128)(2,1)} async-done(((bf16[1600,600]{0,1:T(8,128)(2,1)}), bf16[1600,4800]{0,1:T(8,128)(2,1)}) %all-gather.23.cloned.1.call-update) | async-done | bytes 15360016 | tf_op jit(solution)/shard_map/all_gather | solution.py:98
  256.7 9.9 fusion.8
  268.3 13.6 all_gather.56
  284.6 3.2 all-gather.27.cloned.1.call-done
  287.8 5.1 copy.88
  293.0 23.2 all-gather.31.cloned.1.call-done
  316.2 5.1 copy.89
  322.1 2.5 broadcast.448.clone
  324.6 66.0 %while.9 = (s32[]{:T(128)}, bf16[128,1600]{0,1:T(8,128)(2,1)S(1)}, s32[32,2]{0,1:T(2,128)S(1)}, bf16[32,128,400]{2,1,0:T(8,128)(2,1)}, s32[]{:T(128)}) while((s32[]{:T(128)}, bf16[128,1600]{0,1:T(8,128)(2,1)S(1)}, s32[32,2]{0,1:T(2,128)S(1)}, bf16[32,128,400]{2,1,0:T(8,128)(2,1)}, s32[]{:T(128)}) %tuple.143), condition=%wide.while_cond.1, body=%wide.while_body.1.sunk | while | flops 2 | bytes 643177 | solution.py:260
  390.7 2.4 broadcast.448.clone.3
  393.1 94.6 %while.15 = (s32[]{:T(128)}, bf16[128,1600]{0,1:T(8,128)(2,1)}, s32[32,2]{0,1:T(2,128)S(1)}, bf16[32,128,400]{2,1,0:T(8,128)(2,1)}, s32[]{:T(128)}) while((s32[]{:T(128)}, bf16[128,1600]{0,1:T(8,128)(2,1)}, s32[32,2]{0,1:T(2,128)S(1)}, bf16[32,128,400]{2,1,0:T(8,128)(2,1)}, s32[]{:T(128)}) %tuple.198), condition=%wide.while_cond.7, body=%wide.while_body.7.sunk | while | flops 2 | bytes 643177 | solution.py:260
  488.0 9.1 fusion
  497.1 8.5 fusion.1
  505.6 14.6 fusion.30
  520.2 31.2 all_gather.65
  551.5 2.5 broadcast.448.clone.1
  554.0 65.8 %while.11 = (s32[]{:T(128)}, bf16[128,1600]{0,1:T(8,128)(2,1)S(1)}, s32[32,2]{0,1:T(2,128)S(1)}, bf16[32,128,400]{2,1,0:T(8,128)(2,1)}, s32[]{:T(128)}) while((s32[]{:T(128)}, bf16[128,1600]{0,1:T(8,128)(2,1)S(1)}, s32[32,2]{0,1:T(2,128)S(1)}, bf16[32,128,400]{2,1,0:T(8,128)(2,1)}, s32[]{:T(128)}) %tuple.199), condition=%wide.while_cond.3, body=%wide.while_body.3.sunk | while | flops 2 | bytes 643177 | solution.py:260
  619.8 4.1 fusion.59
  627.1 66.0 %while.13 = (s32[]{:T(128)}, bf16[128,1600]{0,1:T(8,128)(2,1)S(1)}, s32[32,2]{0,1:T(2,128)S(1)}, bf16[32,128,400]{2,1,0:T(8,128)(2,1)}, s32[]{:T(128)}) while((s32[]{:T(128)}, bf16[128,1600]{0,1:T(8,128)(2,1)S(1)}, s32[32,2]{0,1:T(2,128)S(1)}, bf16[32,128,400]{2,1,0:T(8,128)(2,1)}, s32[]{:T(128)}) %tuple.200), condition=%wide.while_cond.5, body=%wide.while_body.5.sunk | while | flops 2 | bytes 643177 | solution.py:260
  693.1 8.7 fusion.60
  701.8 9.3 exponential_select_fusion
  711.1 364.9 %all-gather.29.cloned.1.call-done = bf16[1600,6400]{0,1:T(8,128)(2,1)} async-done(((bf16[1600,800]{0,1:T(8,128)(2,1)}), bf16[1600,6400]{0,1:T(8,128)(2,1)}) %all-gather.29.cloned.1.call-update) | async-done | bytes 20480016 | tf_op jit(solution)/shard_map/all_gather | solution.py:140
  1076.0 11.7 multiply_convert_fusion.2
  1087.8 397.7 %all-gather.33.cloned.1.call-done = bf16[6400,1600]{1,0:T(8,128)(2,1)} async-done(((bf16[800,1600]{1,0:T(8,128)(2,1)}), bf16[6400,1600]{1,0:T(8,128)(2,1)}) %all-gather.33.cloned.1.call-update) | async-done | bytes 20480016 | tf_op jit(solution)/shard_map/all_gather | solution.py:145
  1485.5 13.0 convert_reduce_fusion
  1498.5 16.5 multiply_reduce_fusion
  1516.4 4.0 broadcast.469.clone
  1520.4 96.6 %while.12 = (s32[]{:T(128)}, bf16[128,6400]{1,0:T(8,128)(2,1)}, s32[32,2]{0,1:T(2,128)S(1)}, bf16[32,128,800]{2,1,0:T(8,128)(2,1)}, s32[]{:T(128)}) while((s32[]{:T(128)}, bf16[128,6400]{1,0:T(8,128)(2,1)}, s32[32,2]{0,1:T(2,128)S(1)}, bf16[32,128,800]{2,1,0:T(8,128)(2,1)}, s32[]{:T(128)}) %tuple.152), condition=%wide.while_cond.4, body=%wide.while_body.4.sunk | while | flops 2 | bytes 459365 | solution.py:259
  1521.0 2.4 bitcast_dynamic-update-slice_fusion.20
  1527.0 2.4 bitcast_dynamic-update-slice_fusion.20
  1533.1 2.4 bitcast_dynamic-update-slice_fusion.20
  1545.1 2.4 bitcast_dynamic-update-slice_fusion.20
  1560.2 2.4 bitcast_dynamic-update-slice_fusion.20
  1566.2 2.4 bitcast_dynamic-update-slice_fusion.20
  1569.3 2.4 bitcast_dynamic-update-slice_fusion.20
  1575.3 2.4 bitcast_dynamic-update-slice_fusion.20
  1584.3 2.5 bitcast_dynamic-update-slice_fusion.20
  1596.4 2.4 bitcast_dynamic-update-slice_fusion.20
  1602.4 2.4 bitcast_dynamic-update-slice_fusion.20
  1605.5 2.4 bitcast_dynamic-update-slice_fusion.20
  1611.5 2.4 bitcast_dynamic-update-slice_fusion.20
  1614.5 2.4 bitcast_dynamic-update-slice_fusion.20
  1618.8 5.6 bitcast_multiply_fusion
  1624.5 89.8 %while.10 = (s32[]{:T(128)}, bf16[128,1600]{0,1:T(8,128)(2,1)}, s32[32,2]{0,1:T(2,128)S(1)}, bf16[32,128,200]{2,1,0:T(8,128)(2,1)}, s32[]{:T(128)}) while((s32[]{:T(128)}, bf16[128,1600]{0,1:T(8,128)(2,1)}, s32[32,2]{0,1:T(2,128)S(1)}, bf16[32,128,200]{2,1,0:T(8,128)(2,1)}, s32[]{:T(128)}) %tuple.197), condition=%wide.while_cond.2, body=%wide.while_body.2.sunk | while | flops 2 | bytes 321641 | solution.py:259
  1714.4 4.0 broadcast.469.clone.1
  1718.3 66.1 %while.14 = (s32[]{:T(128)}, bf16[128,6400]{1,0:T(8,128)(2,1)S(1)}, s32[32,2]{0,1:T(2,128)S(1)}, bf16[32,128,800]{2,1,0:T(8,128)(2,1)}, s32[]{:T(128)}) while((s32[]{:T(128)}, bf16[128,6400]{1,0:T(8,128)(2,1)S(1)}, s32[32,2]{0,1:T(2,128)S(1)}, bf16[32,128,800]{2,1,0:T(8,128)(2,1)}, s32[]{:T(128)}) %tuple.201), condition=%wide.while_cond.6, body=%wide.while_body.6.sunk | while | flops 2 | bytes 434789 | solution.py:259
  1784.7 12.9 fusion.24
  1798.6 31.2 all-gather.4
  1829.9 9.6 fusion.62
  1839.5 19.2 fusion.64
  1858.7 20.3 fusion.63
  1879.0 11.6 convolution_convert_fusion.1
  1890.6 12.3 fusion.23
  1907.7 64.7 %while.8 = (s32[]{:T(128)}, bf16[128,4800]{1,0:T(8,128)(2,1)S(1)}, s32[32,2]{0,1:T(2,128)S(1)}, bf16[32,128,600]{2,1,0:T(8,128)(2,1)}, s32[]{:T(128)}) while((s32[]{:T(128)}, bf16[128,4800]{1,0:T(8,128)(2,1)S(1)}, s32[32,2]{0,1:T(2,128)S(1)}, bf16[32,128,600]{2,1,0:T(8,128)(2,1)}, s32[]{:T(128)}) %tuple.140), condition=%wide.while_cond, body=%wide.while_body.sunk | while | flops 2 | bytes 318053 | solution.py:259
  1972.4 15.7 fusion.61
  1988.1 148.3 %concatenate.32 = f32[32,2400,400]{1,2,0:T(8,128)} concatenate(f32[32,600,400]{1,2,0:T(8,128)} %fusion.61, f32[32,200,400]{1,2,0:T(8,128)} %fusion.62, f32[32,800,400]{1,2,0:T(8,128)} %fusion.63, f32[32,800,400]{1,2,0:T(8,128)} %fusion.64), dimensions={1} | concatenate | bytes 245760000 | tf_op jit(solution)/shard_map/vmap()/concatenate | solution.py:262
  2136.4 146.9 %copy.119 = f32[32,2400,400]{2,1,0:T(8,128)} copy(f32[32,2400,400]{1,2,0:T(8,128)} %concatenate.32) | data formatting | bytes 245760000
  2284.4 13.5 fusion.18
  2298.2 13.0 fusion.53
  2315.2 1280.1 %reduce-scatter.4.cloned.1.call-done = f32[2400,400]{1,0:T(8,128)} async-done(((f32[76800,400]{1,0:T(8,128)}), f32[2400,400]{1,0:T(8,128)}) %reduce-scatter.4.cloned.1.call-update) | async-done | bytes 3840016
  3603.6 2.6 copy.126
  3609.4 117.2 %all-reduce.7.cloned.1.call-done = (f32[1600]{0:T(1024)}, f32[1600]{0:T(1024)}, f32[2,1600]{1,0:T(2,128)}, f32[1600]{0:T(1024)}, f32[1600]{0:T(1024)}, /*index=5*/f32[1600]{0:T(1024)}, f32[6400]{0:T(1024)}, f32[1600]{0:T(1024)}) async-done(((f32[1600]{0:T(1024)}, f32[1600]{0:T(1024)}, f32[2,1600]{1,0:T(2,128)}, f32[1600]{0:T(1024)}, f32[1600]{0:T(1024)}, /*index=5*/f32[1600]{0:T(1024)}, f32[6400]{0:T(1024)}, ...) | async-done | bytes 76816 | tf_op jit(solution)/shard_map/psum | solution.py:286
  (1259 shorter events, 621.5 us)
Async XLA Ops:
  7.2 32.9 copy-start.23
  7.2 33.1 copy-start.4
  7.2 27.4 all-gather.21.cloned.1.call-start
  7.9 32.8 copy-start.20
  7.9 32.8 copy-start.26
  8.0 248.7 %all-gather.23.cloned.1.call-start = ((), (), s32[]{:S(2)}) async-start(), calls=%async_computation.2 | async-start | bytes 17971200 | tf_op jit(solution)/shard_map/all_gather | solution.py:98
  38.7 249.1 %all-gather.27.cloned.1.call-start = ((), (), s32[]{:S(2)}) async-start(), calls=%async_computation.4 | async-start | bytes 3584000 | tf_op jit(solution)/shard_map/all_gather | solution.py:92
  39.5 276.7 %all-gather.31.cloned.1.call-start = ((), (), s32[]{:S(2)}) async-start(), calls=%async_computation.6 | async-start | bytes 3584000 | tf_op jit(solution)/shard_map/all_gather | solution.py:93
  40.0 447.9 %all-gather.35.cloned.1.call-start = ((), (), s32[]{:S(2)}) async-start(), calls=%async_computation.8 | async-start | bytes 3686400 | tf_op jit(solution)/shard_map/all_gather | solution.py:107
  40.5 226.1 %copy-start.24 = (f32[128]{0:T(128)}, f32[128]{0:T(128)S(1)}, u32[]{:S(2)}) copy-start(f32[128]{0:T(128)S(1)} %broadcast_multiply_fusion.1) | copy-start | bytes 1540
  40.7 225.8 %copy-start.33 = (f32[128]{0:T(128)}, f32[128]{0:T(128)S(1)}, u32[]{:S(2)}) copy-start(f32[128]{0:T(128)S(1)} %fusion.36) | copy-start | bytes 1540
  40.7 225.8 %copy-start.29 = (f32[128]{0:T(128)}, f32[128]{0:T(128)S(1)}, u32[]{:S(2)}) copy-start(f32[128]{0:T(128)S(1)} %fusion.42) | copy-start | bytes 1540
  41.2 227.0 %copy-start.19 = (bf16[400,200]{1,0:T(8,128)(2,1)S(1)}, bf16[400,200]{1,0:T(8,128)(2,1)}, u32[]{:S(2)}) copy-start(bf16[400,200]{1,0:T(8,128)(2,1)} %param.22) | copy-start | bytes 480004
  267.7 238.0 %all-gather.37.cloned.1.call-start = ((), (), s32[]{:S(2)}) async-start(), calls=%async_computation.9 | async-start | bytes 3686400 | tf_op jit(solution)/shard_map/all_gather | solution.py:108
  268.2 351.6 %all-gather.25.cloned.1.call-start = ((), (), s32[]{:S(2)}) async-start(), calls=%async_computation.3 | async-start | bytes 5990400 | tf_op jit(solution)/shard_map/all_gather | solution.py:135
  283.1 410.0 %all-gather.43.cloned.1.call-start = ((), (), s32[]{:S(2)}) async-start(), calls=%async_computation.12 | async-start | bytes 3686400 | tf_op jit(solution)/shard_map/all_gather | solution.py:176
  283.8 418.0 %all-gather.39.cloned.1.call-start = ((), (), s32[]{:S(2)}) async-start(), calls=%async_computation.10 | async-start | bytes 3686400 | tf_op jit(solution)/shard_map/all_gather | solution.py:178
  284.6 791.4 %all-gather.29.cloned.1.call-start = ((), (), s32[]{:S(2)}) async-start(), calls=%async_computation.5 | async-start | bytes 23961600 | tf_op jit(solution)/shard_map/all_gather | solution.py:140
  293.0 28.6 copy-start.35
  293.0 1192.5 %all-gather.33.cloned.1.call-start = ((), (), s32[]{:S(2)}) async-start(), calls=%async_computation.7 | async-start | bytes 23961600 | tf_op jit(solution)/shard_map/all_gather | solution.py:145
  321.3 1463.3 %all-gather.45.cloned.1.call-start = ((), (), s32[]{:S(2)}) async-start(), calls=%async_computation.13 | async-start | bytes 3686400 | tf_op jit(solution)/shard_map/all_gather | solution.py:177
  390.7 97.3 %copy-start.9 = (bf16[1,128,1,1600]{1,3,2,0:T(8,128)(2,1)S(1)}, bf16[1,128,1,1600]{1,3,2,0:T(8,128)(2,1)}, u32[]{:S(2)}) copy-start(bf16[1,128,1,1600]{1,3,2,0:T(8,128)(2,1)} %get-tuple-element.245) | copy-start | bytes 1228804
  487.7 1391.3 %all-gather.41.cloned.1.call-start = ((), (), s32[]{:S(2)}) async-start(), calls=%async_computation.11 | async-start | bytes 3686400 | tf_op jit(solution)/shard_map/all_gather | solution.py:179
  520.2 31.2 copy-start.14
  551.5 68.3 %copy-start.37 = (f32[1600]{0:T(1024)S(1)}, f32[1600]{0:T(1024)}, u32[]{:S(2)}) copy-start(f32[1600]{0:T(1024)} %param.23) | copy-start | bytes 19204
  619.8 4.4 copy-start.22
  619.8 4.4 copy-start.27
  624.0 891.0 %copy-start = (f32[128,1600]{0,1:T(8,128)}, f32[128,1600]{0,1:T(8,128)S(1)}, u32[]{:S(2)}) copy-start(f32[128,1600]{0,1:T(8,128)S(1)} %get-tuple-element.257) | copy-start | bytes 2457604
  693.1 8.7 copy-start.16
  693.1 8.7 copy-start.13
  701.8 374.2 %copy-start.17 = (bf16[128,1600]{0,1:T(8,128)(2,1)S(1)}, bf16[128,1600]{0,1:T(8,128)(2,1)}, u32[]{:S(2)}) copy-start(bf16[128,1600]{0,1:T(8,128)(2,1)} %copy-done.16) | copy-start | bytes 1228804
  701.8 374.2 %copy-start.36 = (f32[6400]{0:T(1024)S(1)}, f32[6400]{0:T(1024)}, u32[]{:S(2)}) copy-start(f32[6400]{0:T(1024)} %param.27) | copy-start | bytes 76804
  711.1 774.4 %copy-start.11 = (bf16[128,1600]{0,1:T(8,128)(2,1)S(1)}, bf16[128,1600]{0,1:T(8,128)(2,1)}, u32[]{:S(2)}) copy-start(bf16[128,1600]{0,1:T(8,128)(2,1)} %get-tuple-element.650) | copy-start | bytes 1228804
  1516.4 100.6 %copy-start.7 = (f32[128,1600]{0,1:T(8,128)}, f32[128,1600]{0,1:T(8,128)S(1)}, u32[]{:S(2)}) copy-start(f32[128,1600]{0,1:T(8,128)S(1)} %get-tuple-element.242) | copy-start | bytes 2457604
  1516.4 100.6 %copy-start.31 = (f32[128]{0:T(128)}, f32[128]{0:T(128)S(1)}, u32[]{:S(2)}) copy-start(f32[128]{0:T(128)S(1)} %negate_multiply_fusion.1) | copy-start | bytes 1540
  1516.4 100.6 %copy-start.12 = (bf16[128,1600]{0,1:T(8,128)(2,1)S(1)}, bf16[128,1600]{0,1:T(8,128)(2,1)}, u32[]{:S(2)}) copy-start(bf16[128,1600]{0,1:T(8,128)(2,1)} %get-tuple-element.650) | copy-start | bytes 1228804
  1618.1 0.8 copy-start.15
  1714.4 70.3 %copy-start.18 = (bf16[128,1600]{0,1:T(8,128)(2,1)S(1)}, bf16[128,1600]{0,1:T(8,128)(2,1)}, u32[]{:S(2)}) copy-start(bf16[128,1600]{0,1:T(8,128)(2,1)} %get-tuple-element.262) | copy-start | bytes 1228804
  1784.4 13.2 copy-start.10
  1784.4 1810.8 %reduce-scatter.4.cloned.1.call-start = ((), (), s32[]{:S(2)}) async-start(), calls=%async_computation.14 | async-start | bytes 162201600
  1829.9 9.6 slice-start
  1829.9 9.6 slice-start.1
  1879.0 11.6 copy-start.6
  1972.4 15.7 copy-start.2
  2283.3 1.1 copy-start.1
  2283.3 1.1 copy-start.28
  2283.3 14.6 copy-start.3
  2283.3 14.8 copy-start.5
  2283.3 14.8 copy-start.21
  2283.3 14.8 copy-start.25
  2283.3 1443.3 %all-reduce.7.cloned.1.call-start = ((), (), s32[]{:S(2)}) async-start(), calls=%async_computation.15 | async-start | bytes 182272 | tf_op jit(solution)/shard_map/psum | solution.py:286
  2298.2 13.0 copy-start.34
  2298.2 13.0 copy-start.30
  2298.2 14.8 copy-start.8
  2298.2 14.8 copy-start.32
Sparse Core Ops, SparseCore 0:
  9.6 25.0 all-gather.20
  38.9 217.7 all-gather.22
  258.2 29.5 all-gather.26
  289.2 26.9 all-gather.30
  318.7 64.5 all-gather.34
  385.7 62.7 all-gather.36
  451.3 86.1 all-gather.24
  540.1 63.7 all-gather.42
  606.5 61.8 all-gather.38
  669.8 406.1 all-gather.28
  1077.6 407.8 all-gather.32
  1488.0 64.5 all-gather.44
  1784.6 65.4 all-gather.40
  2283.4 1311.8 reduce-scatter.3
  3603.8 122.8 all-reduce.6
where the time goes:
time: 3760 us; the launch traced here: 3740 us
  waiting for transfers between devices  2430 us (65%)
  local copies, waits for them, and re-layouts  969 us (26%)
  matrix products  230 us (6%)
  blocking collectives  76.1 us (2%)
    unnamed x16, waiting for transfers between devices  1280 us
    gather x1088, local copies, waits for them, and re-layouts  607 us
    all_gather x1, waiting for transfers between devices, body(): lax.all_gather(proj_rows, 'ctx', axis=0, tiled=True)  398 us
    all_gather x1, waiting for transfers between devices, body(): lax.all_gather(fc_cols, 'ctx', axis=1, tiled=True)  365 us
    all_gather x1, waiting for transfers between devices, body(): lax.all_gather(qkv_cols, 'ctx', axis=1, tiled=True)  215 us
    unnamed x99, local copies, waits for them, and re-layouts  185 us
    concatenate x1, local copies, waits for them, and re-layouts, one_device(): return jnp.concatenate(blocks, axis=0)  148 us
    psum x1, waiting for transfers between devices, body(): lax.psum((vector_terms[0], vector_terms[1], vector_terms[2], vector_terms...  117 us
  transfers between devices with their start and end apart: 15, of which 8 were waited for; matrix products, arithmetic and copies ran while one was open for 21% of the time, Pallas kernels for 0%

commit v1 on v0

v1 whole, which is shorter than its diff:
```python
import functools
import math

import jax
import jax.numpy as jnp
import numpy as np
from jax import lax
from jax.experimental import pallas as pl
from jax.experimental.pallas import tpu as pltpu
from jax.sharding import PartitionSpec as P

HEAD = 64
EPSILON = 1e-05
NEGATIVE = -1e30
GELU_COEF = 0.7978845608028654
LOW = jnp.bfloat16
FULL = jnp.float32


def norm_parts(values):
    center = values - jnp.mean(values, axis=-1, keepdims=True)
    rate = lax.rsqrt(jnp.mean(center * center, axis=-1, keepdims=True) + EPSILON)
    return center * rate, rate


def norm_back(grad, scaled, rate, gain):
    inner = grad * gain
    return rate * (
        inner
        - jnp.mean(inner, axis=-1, keepdims=True)
        - scaled * jnp.mean(inner * scaled, axis=-1, keepdims=True)
    )


def gelu_parts(values):
    square = values * values
    bent = jnp.tanh(GELU_COEF * values * (1.0 + 0.044715 * square))
    slope = 0.5 * (1.0 + bent) + 0.5 * values * (1.0 - bent * bent) * GELU_COEF * (
        1.0 + 3.0 * 0.044715 * square
    )
    return 0.5 * values * (1.0 + bent), slope


def dot(left, right):
    return jnp.dot(left, right, preferred_element_type=FULL)


def dot_t(left, right):
    return lax.dot_general(left, right, (((1,), (1,)), ((), ())), preferred_element_type=FULL)


def t_dot(left, right):
    return lax.dot_general(left, right, (((0,), (0,)), ((), ())), preferred_element_type=FULL)


def swap(values, axis, bit):
    count = lax.axis_size(axis)
    return lax.ppermute(values, axis, [(i, i ^ bit) for i in range(count)])


def ordered(flag, own, got):
    return jnp.where(flag == 0, own, got), jnp.where(flag == 0, got, own)


def joined(flag, own, got, axis):
    return jnp.concatenate(ordered(flag, own, got), axis)


def ring_order(count):
    return list(range(0, count, 2)) + list(range(count - 1, 0, -2))


def shift(values, offset):
    order = ring_order(lax.axis_size("ctx"))
    count = len(order)
    return lax.ppermute(
        values, "ctx", [(order[i], order[(i + offset) % count]) for i in range(count)]
    )


def ring_offsets(count):
    half = count // 2
    found = [0]
    for k in range(1, half):
        found += [-k, k]
    return found + [half]


def ring_gather(values):
    count = lax.axis_size("ctx")
    half = count // 2
    rows = values.shape[0] // 2
    ahead = [values[:rows], values[rows:]]
    behind = [values[:rows], values[rows:]]
    pieces = {0: values}
    for k in range(1, half):
        ahead = [shift(a, 1) for a in ahead]
        behind = [shift(b, -1) for b in behind]
        pieces[-k] = jnp.concatenate(ahead)
        pieces[k] = jnp.concatenate(behind)
    pieces[half] = jnp.concatenate([shift(ahead[0], 1), shift(behind[1], -1)])
    return [pieces[o] for o in ring_offsets(count)]


def ring_sum(pieces):
    count = lax.axis_size("ctx")
    half = count // 2
    held = dict(zip(ring_offsets(count), pieces, strict=True))
    rows = held[0].shape[0] // 2
    up = [held[half][:rows], None]
    down = [None, held[half][rows:]]
    for k in range(half - 1, -1, -1):
        for which in range(2):
            part = slice(which * rows, (which + 1) * rows)
            if up[which] is not None:
                got = shift(up[which].astype(LOW), 1).astype(FULL)
                up[which] = got if k == 0 else held[k][part] + got
            else:
                up[which] = held[k][part]
            if down[which] is not None:
                got = shift(down[which].astype(LOW), -1).astype(FULL)
                down[which] = got if k == 0 else held[-k][part] + got
            else:
                down[which] = held[-k][part]
    return held[0] + jnp.concatenate(up) + jnp.concatenate(down)


def square_gather(values):
    rows = values.shape[0] // 2
    one, two = values[:rows], values[rows:]
    one = jnp.concatenate([one, swap(one, "ctx", 1)])
    two = jnp.concatenate([two, swap(two, "ctx", 2)])
    near = jnp.concatenate([one, two])
    far = jnp.concatenate([swap(one, "ctx", 2), swap(two, "ctx", 1)])
    return jnp.concatenate([near, swap(near, "seq", 1), far, swap(far, "seq", 1)])


def square_sum(partial):
    rows = partial.shape[0] // 16
    near, near_other, far, far_other = jnp.split(partial, 4)
    far = far + swap(far_other.astype(LOW), "seq", 1).astype(FULL)
    near = near + swap(near_other.astype(LOW), "seq", 1).astype(FULL)
    one = near[: 2 * rows] + swap(far[: 2 * rows].astype(LOW), "ctx", 2).astype(FULL)
    two = near[2 * rows :] + swap(far[2 * rows :].astype(LOW), "ctx", 1).astype(FULL)
    one = one[:rows] + swap(one[rows:].astype(LOW), "ctx", 1).astype(FULL)
    two = two[:rows] + swap(two[rows:].astype(LOW), "ctx", 2).astype(FULL)
    return jnp.concatenate([one, two])


def sum_everywhere(values):
    for axis in ("seq", "ctx"):
        bit = 1
        while bit < lax.axis_size(axis):
            values = values + swap(values, axis, bit)
            bit *= 2
    return values


def head_plan(count, width):
    heads = width // HEAD
    group = -(-heads // count) * HEAD
    shard = 3 * width // count
    edges = []
    for to in range(count):
        for part in range(3):
            low = part * width + to * group
            high = min(part * width + (to + 1) * group, (part + 1) * width)
            for come in range(count):
                a, b = max(low, come * shard), min(high, (come + 1) * shard)
                if a < b:
                    edges.append((come, to, a - come * shard, part * group + a - low, b - a))
    edges.sort(key=lambda e: -e[4])
    rounds = []
    for edge in edges:
        for known in rounds:
            if all(edge[0] != e[0] and edge[1] != e[1] for e in known):
                known.append(edge)
                break
        else:
            rounds.append([edge])
    sent = np.full((count, len(rounds) * group), -1, np.int32)
    kept = np.full((count, 3 * group), -1, np.int32)
    pairs = []
    for number, known in enumerate(rounds):
        pairs.append([(e[0], e[1]) for e in known])
        for come, to, start, place, size in known:
            sent[come, number * group : number * group + size] = np.arange(start, start + size)
            kept[to, place : place + size] = number * group + np.arange(size)
    return group, pairs, sent, kept


def picker(places, size):
    return (lax.broadcasted_iota(jnp.int32, (size, places.shape[0]), 0) == places[None, :]).astype(LOW)


def to_heads(shard, group, pairs, pick_sent, pick_kept):
    sent = dot(shard, pick_sent).astype(LOW)
    got = [
        lax.ppermute(sent[:, i * group : (i + 1) * group], "ctx", pairs[i])
        for i in range(len(pairs))
    ]
    return dot(jnp.concatenate(got, axis=1), pick_kept).astype(LOW)


def from_heads(held, group, pairs, pick_sent, pick_kept):
    sent = dot_t(held, pick_kept).astype(LOW)
    got = [
        lax.ppermute(sent[:, i * group : (i + 1) * group], "ctx", [(b, a) for a, b in pairs[i]])
        for i in range(len(pairs))
    ]
    return dot_t(jnp.concatenate(got, axis=1), pick_sent)


def attend_kernel(heads, q_ref, k_ref, v_ref, row_ref, col_ref, full_ref, low_ref, lse_ref):
    allowed = col_ref[...] <= row_ref[...]
    for h in range(heads):
        part = slice(h * HEAD, (h + 1) * HEAD)
        query = q_ref[:, part] * (1.0 / math.sqrt(HEAD))
        score = jnp.where(allowed, dot_t(query.astype(LOW), k_ref[:, part]), NEGATIVE)
        top = jnp.max(score, axis=1, keepdims=True)
        weight = jnp.exp(score - top)
        total = jnp.sum(weight, axis=1, keepdims=True)
        result = dot(weight.astype(LOW), v_ref[:, part]) / total
        full_ref[:, part] = result
        low_ref[:, part] = result.astype(LOW)
        lse_ref[:, h : h + 1] = top + jnp.log(total)


def attend_back_kernel(
    heads, q_ref, k_ref, v_ref, row_ref, col_ref, full_ref, lse_ref, grad_ref, dq_ref, dk_ref, dv_ref
):
    @pl.when(pl.program_id(0) == 0)
    def _():
        dk_ref[...] = jnp.zeros_like(dk_ref)
        dv_ref[...] = jnp.zeros_like(dv_ref)

    allowed = col_ref[...] <= row_ref[...]
    scale = 1.0 / math.sqrt(HEAD)
    for h in range(heads):
        part = slice(h * HEAD, (h + 1) * HEAD)
        query = (q_ref[:, part] * scale).astype(LOW)
        grad = grad_ref[:, part]
        delta = jnp.sum(grad.astype(FULL) * full_ref[:, part], axis=1, keepdims=True)
        score = dot_t(query, k_ref[:, part])
        prob = jnp.where(allowed, jnp.exp(score - lse_ref[:, h : h + 1]), 0.0)
        prob_grad = dot_t(grad, v_ref[:, part])
        score_grad = (prob * (prob_grad - delta)).astype(LOW)
        dq_ref[:, part] = (dot(score_grad, k_ref[:, part]) * scale).astype(LOW)
        dk_ref[:, part] += t_dot(score_grad, query)
        dv_ref[:, part] += t_dot(prob.astype(LOW), grad)


def attend_sizes(qkv):
    tokens, group = qkv.shape[0], qkv.shape[1] // 3
    rows = min(256, tokens)
    return tokens, group, rows


def attend(qkv, pos):
    tokens, group, rows = attend_sizes(qkv)
    heads = group // HEAD
    q, k, v = qkv[:, :group], qkv[:, group : 2 * group], qkv[:, 2 * group :]
    some = pl.BlockSpec((rows, group), lambda i: (i, 0))
    whole = pl.BlockSpec((tokens, group), lambda i: (0, 0))
    return pl.pallas_call(
        functools.partial(attend_kernel, heads),
        grid=(tokens // rows,),
        in_specs=[
            some,
            whole,
            whole,
            pl.BlockSpec((rows, 1), lambda i: (i, 0)),
            pl.BlockSpec((1, tokens), lambda i: (0, 0)),
        ],
        out_specs=[some, some, pl.BlockSpec((rows, heads), lambda i: (i, 0))],
        out_shape=[
            jax.ShapeDtypeStruct((tokens, group), FULL),
            jax.ShapeDtypeStruct((tokens, group), LOW),
            jax.ShapeDtypeStruct((tokens, heads), FULL),
        ],
        compiler_params=pltpu.CompilerParams(vmem_limit_bytes=48 * 2**20),
        cost_estimate=pl.CostEstimate(
            flops=4 * tokens * tokens * group,
            bytes_accessed=12 * tokens * group,
            transcendentals=tokens * tokens * heads,
        ),
        name="attend",
    )(q, k, v, pos[:, None], pos[None, :])


def attend_back(qkv, pos, full, lse, grad):
    tokens, group, rows = attend_sizes(qkv)
    heads = group // HEAD
    q, k, v = qkv[:, :group], qkv[:, group : 2 * group], qkv[:, 2 * group :]
    some = pl.BlockSpec((rows, group), lambda i: (i, 0))
    whole = pl.BlockSpec((tokens, group), lambda i: (0, 0))
    return pl.pallas_call(
        functools.partial(attend_back_kernel, heads),
        grid=(tokens // rows,),
        in_specs=[
            some,
            whole,
            whole,
            pl.BlockSpec((rows, 1), lambda i: (i, 0)),
            pl.BlockSpec((1, tokens), lambda i: (0, 0)),
            some,
            pl.BlockSpec((rows, heads), lambda i: (i, 0)),
            some,
        ],
        out_specs=[some, whole, whole],
        out_shape=[
            jax.ShapeDtypeStruct((tokens, group), LOW),
            jax.ShapeDtypeStruct((tokens, group), FULL),
            jax.ShapeDtypeStruct((tokens, group), FULL),
        ],
        compiler_params=pltpu.CompilerParams(vmem_limit_bytes=48 * 2**20),
        cost_estimate=pl.CostEstimate(
            flops=10 * tokens * tokens * group,
            bytes_accessed=24 * tokens * group,
            transcendentals=tokens * tokens * heads,
        ),
        name="attend_back",
    )(q, k, v, pos[:, None], pos[None, :], full, lse, grad)


def high_bits():
    bits, bit = [], 4
    while bit < lax.axis_size("ctx"):
        bits.append(bit)
        bit *= 2
    return bits


def unit_rows(shard, core, row):
    parts = shard.reshape(2, shard.shape[0] // 2, shard.shape[1])
    mine, other = ordered(core, parts[0], parts[1])
    held = joined(core, mine, swap(other, "seq", 1), 1)[None]
    for bit in high_bits():
        held = jnp.concatenate([held, swap(held, "ctx", bit)])
    held = joined(row, held, swap(held, "seq", 2), 2)
    return held.reshape(-1, held.shape[2])


def unit_rows_sum(grad, core, row):
    count = 2 ** len(high_bits())
    half = grad.shape[1] // 2
    keep, send = ordered(row, grad[:, :half], grad[:, half:])
    held = keep + swap(send.astype(LOW), "seq", 2).astype(FULL)
    held = held.reshape(count, -1, half)
    for bit in reversed(high_bits()):
        some = held.shape[0] // 2
        held = held[:some] + swap(held[some:].astype(LOW), "ctx", bit).astype(FULL)
    held = held[0]
    keep, send = ordered(core, held[:, : half // 2], held[:, half // 2 :])
    return joined(core, keep, swap(send, "seq", 1), 0)


def whole_out_weight(shard, core, row, ctx):
    held = jnp.transpose(shard)[None]
    bits = lax.axis_size("ctx").bit_length() - 1
    held = held.reshape((1,) * bits + held.shape[1:])
    for place in range(bits):
        bit = bits - 1 - place
        flag = (ctx >> bit) & 1
        held = joined(flag, held, swap(held, "ctx", 1 << bit), place)
    held = held.reshape(-1, held.shape[-1])
    both = jnp.stack(ordered(row, held, swap(held, "seq", 2)))
    peer = swap(both, "seq", 1)
    return jnp.concatenate([joined(core, both[i], peer[i], 1) for i in range(2)], axis=1)


def out_weight_sum(attn_low, branch_low, core, row, ctx):
    part = attn_low.shape[1] // 4
    blocks = [attn_low[:, i * part : (i + 1) * part] for i in range(4)]
    mine, other = ordered(
        core, jnp.concatenate([blocks[0], blocks[2]], 1), jnp.concatenate([blocks[1], blocks[3]], 1)
    )
    got = swap(t_dot(branch_low, other).astype(LOW), "seq", 1)
    held = t_dot(branch_low, mine) + got.astype(FULL)
    count = lax.axis_size("ctx")
    held = held.reshape(count, -1, held.shape[1])
    bit = 1
    while bit < count:
        flag = lax.bitwise_and(ctx, bit)
        held = held.reshape(held.shape[0] // 2, 2, *held.shape[1:])
        keep, send = ordered(flag, held[:, 0], held[:, 1])
        held = keep + swap(send.astype(LOW), "ctx", bit).astype(FULL)
        bit *= 2
    held = held[0]
    keep, send = ordered(row, held[:, :part], held[:, part:])
    return jnp.transpose(keep + swap(send.astype(LOW), "seq", 2).astype(FULL))


def body(
    block_input,
    out_cot,
    pair_of,
    ln1_gain,
    ln1_bias,
    qkv_weight,
    qv_bias,
    out_weight,
    out_bias,
    ln2_gain,
    ln2_bias,
    fc_weight,
    fc_bias,
    proj_weight,
    proj_bias,
):
    rows, width = block_input.shape[2], block_input.shape[3]
    block = rows // 2
    count = lax.axis_size("ctx")
    seq, ctx = lax.axis_index("seq"), lax.axis_index("ctx")
    core, row = seq % 2, seq // 2
    order = ring_order(count)
    place = np.argsort(np.array(order)).astype(np.int32)
    mine = jnp.asarray(place)[ctx]
    offsets = ring_offsets(count)
    inputs = block_input.reshape(rows, width).astype(FULL)
    cot_low = out_cot.reshape(rows, width)
    cot_full = cot_low.astype(FULL)

    members = jnp.asarray(np.array(order, np.int32))[(mine + np.array(offsets, np.int32)) % count]
    pairs = pair_of[members]
    inner = jnp.arange(block, dtype=jnp.int32)
    pos = jnp.stack(
        [pairs[:, None] * block + inner, (2 * count - 1 - pairs)[:, None] * block + inner], axis=1
    ).reshape(-1)

    scaled_one, rate_one = norm_parts(inputs)
    normed_one = (scaled_one * ln1_gain + ln1_bias).astype(LOW)
    group, rounds, sent, kept = head_plan(count, width)
    pick_sent = picker(jnp.asarray(sent)[ctx], qkv_weight.shape[1])
    pick_kept = picker(jnp.asarray(kept)[ctx], sent.shape[1])
    qkv_part = to_heads(qkv_weight, group, rounds, pick_sent, pick_kept)
    qkv_pair = ordered(row, qkv_part, swap(qkv_part, "seq", 2))
    qkv_pair = jnp.stack(qkv_pair)
    qkv_peer = swap(qkv_pair, "seq", 1)
    first, second = ordered(core, qkv_pair, qkv_peer)
    qkv_cols = jnp.stack([first, second], axis=1).reshape(width, 3 * group)
    bias_rows = jnp.pad(qv_bias, ((0, 0), (0, count * group - width)))
    bias_mine = lax.dynamic_slice_in_dim(bias_rows, ctx * group, group, 1)
    qkv_shift = jnp.concatenate([bias_mine[0], jnp.zeros((group,), FULL), bias_mine[1]])

    gathered = ring_gather(normed_one)
    qkv = jnp.concatenate([(dot(x, qkv_cols) + qkv_shift).astype(LOW) for x in gathered])
    attn_full, attn_part, lse = attend(qkv, pos)

    def chunk(values, at):
        return values[at * rows : (at + 1) * rows]

    at_offset = {o % count: i for i, o in enumerate(offsets)}
    back = [
        chunk(attn_part, at_offset[0]) if o == 0 else shift(chunk(attn_part, at_offset[(-o) % count]), -o)
        for o in range(count)
    ]
    back = jnp.stack(back)
    where_is = (jnp.asarray(place) - mine) % count
    attn_low = jnp.concatenate(
        [lax.dynamic_index_in_dim(back, where_is[d], keepdims=False) for d in range(count)], axis=1
    )[:, :width]
    out_rows = whole_out_weight(out_weight, core, row, ctx)
    middle = inputs + dot_t(attn_low, out_rows) + out_bias

    scaled_two, rate_two = norm_parts(middle)
    normed_two = (scaled_two * ln2_gain + ln2_bias).astype(LOW)
    fc_rows = unit_rows(jnp.transpose(fc_weight), core, row)
    proj_rows = unit_rows(proj_weight, core, row)
    high = 2 ** len(high_bits())
    units = jnp.concatenate(
        [
            lax.dynamic_index_in_dim(
                fc_bias.reshape(2 * count, -1), 2 * (ctx ^ (4 * j)) + core, keepdims=False
            )
            for j in range(high)
        ]
    )
    cots = square_gather(cot_low)
    hidden_grad = dot_t(cots, proj_rows)
    tokens = square_gather(normed_two)
    hidden_pre = dot_t(tokens, fc_rows) + units
    value, slope = gelu_parts(hidden_pre)
    hidden = value.astype(LOW)
    hidden_pre_grad = (hidden_grad * slope).astype(LOW)
    normed_two_grad = square_sum(dot(hidden_pre_grad, fc_rows))
    branch_two = square_sum(dot(hidden, proj_rows))
    block_output = (middle + branch_two + proj_bias).astype(LOW).reshape(block_input.shape)
    proj_weight_grad = unit_rows_sum(t_dot(hidden, cots), core, row)
    fc_weight_grad = jnp.transpose(unit_rows_sum(t_dot(hidden_pre_grad, tokens), core, row))
    units_grad = jnp.sum(hidden_pre_grad.astype(FULL), axis=0).reshape(high, -1)

    middle_grad = cot_full + norm_back(normed_two_grad, scaled_two, rate_two, ln2_gain)
    branch_low = middle_grad.astype(LOW)
    attn_grad = jnp.pad(dot(branch_low, out_rows).astype(LOW), ((0, 0), (0, count * group - width)))
    attn_grad = jnp.stack([attn_grad[:, d * group : (d + 1) * group] for d in range(count)])
    whose = jnp.asarray(np.array(order, np.int32))[(mine + np.arange(count, dtype=np.int32)) % count]
    came = {}
    for o in range(count):
        piece = lax.dynamic_index_in_dim(attn_grad, whose[o], keepdims=False)
        came[(-o) % count] = piece if o == 0 else shift(piece, o)
    grad_part = jnp.concatenate([came[o % count] for o in offsets])
    out_weight_grad = out_weight_sum(attn_low, branch_low, core, row, ctx)

    query_grad, key_grad, value_grad = attend_back(qkv, pos, attn_full, lse, grad_part)
    qkv_grad = jnp.concatenate([query_grad, key_grad.astype(LOW), value_grad.astype(LOW)], axis=1)
    normed_one_grad = ring_sum([dot_t(chunk(qkv_grad, i), qkv_cols) for i in range(count)])
    middle_part = norm_back(normed_one_grad, scaled_one, rate_one, ln1_gain)
    input_grad = (middle_grad + middle_part).astype(LOW).reshape(block_input.shape)

    whole = t_dot(jnp.concatenate(gathered), qkv_grad).reshape(2, 2, -1, 3 * group)
    keep, send = ordered(core, whole[:, 0], whole[:, 1])
    whole = keep + swap(send.astype(LOW), "seq", 1).astype(FULL)
    keep, send = ordered(row, whole[0], whole[1])
    whole = keep + swap(send.astype(LOW), "seq", 2).astype(FULL)
    qkv_weight_grad = from_heads(whole.astype(LOW), group, rounds, pick_sent, pick_kept)

    qkv_sums = jnp.sum(qkv_grad.astype(FULL), axis=0)
    qv_sums = jnp.stack([qkv_sums[:group], qkv_sums[2 * group :]])
    qv_sums = lax.dynamic_update_slice(
        jnp.zeros((2, count * group), FULL), qv_sums, (0, ctx * group)
    )[:, :width]
    unit_sums = jnp.zeros((2 * count, units_grad.shape[1]), FULL)
    for j in range(high):
        unit_sums = lax.dynamic_update_slice(
            unit_sums, units_grad[j : j + 1], (2 * (ctx ^ (4 * j)) + core, 0)
        )
    early = jnp.concatenate(
        [
            jnp.sum(branch_low.astype(FULL), axis=0),
            jnp.sum(normed_two_grad * scaled_two, axis=0),
            jnp.sum(normed_two_grad, axis=0),
            unit_sums.reshape(-1),
            jnp.sum(cot_full, axis=0),
        ]
    )
    early = sum_everywhere(early)
    late = jnp.concatenate(
        [
            jnp.sum(normed_one_grad * scaled_one, axis=0),
            jnp.sum(normed_one_grad, axis=0),
            qv_sums.reshape(-1),
        ]
    )
    late = sum_everywhere(late)
    ends = np.cumsum([0, width, width, width, fc_bias.shape[0], width])
    out_bias_grad, ln2_gain_grad, ln2_bias_grad, fc_bias_grad, proj_bias_grad = [
        early[ends[i] : ends[i + 1]] for i in range(5)
    ]
    return (
        block_output,
        input_grad,
        late[:width],
        late[width : 2 * width],
        qkv_weight_grad,
        late[2 * width :].reshape(2, width),
        out_weight_grad,
        out_bias_grad,
        ln2_gain_grad,
        ln2_bias_grad,
        fc_weight_grad,
        fc_bias_grad,
        proj_weight_grad,
        proj_bias_grad,
    )


def solution(mesh):
    rows = P("seq", "ctx", None, None)
    cols = P("seq", "ctx")
    flip = P("ctx", "seq")
    one = P()
    return jax.shard_map(
        body,
        mesh=mesh,
        in_specs=(rows, rows, one, one, one, cols, one, cols, one, one, one, cols, one, flip, one),
        out_specs=(rows, rows, one, one, cols, one, cols, one, one, one, cols, one, flip, one),
        check_vma=False,
    )
```

time: 3760 us -> 782 us (0.21)
  waiting for transfers between devices: 2430 us -> 235 us
  local copies, waits for them, and re-layouts: 969 us -> 96.7 us
  starting transfers between devices: 0.95 us -> 213 us
  matrix products: 230 us -> 78.5 us
  blocking collectives: 76.1 us -> 0 us
  other arithmetic: 17.5 us -> 86.6 us
    unnamed x16 -> x0, waiting for transfers between devices: 1280 us -> none
    all_gather x13 -> x0, waiting for transfers between devices: 1030 us -> none  [the longest x1 398 us: body(): lax.all_gather(proj_rows, 'ctx', axis=0, tiled=True)]
    gather x1088 -> x3, local copies, waits for them, and re-layouts: 607 us -> 1.93 us  [the longest x2 1.29 us: body(): jnp.asarray(np.array(order, np.int32))]
    ppermute x0 -> x114, waiting for transfers between devices: none -> 235 us  [the longest x60 126 us: swap(): return lax.ppermute(values, axis, [(i, i ^ bit) for i in range(count)])]
    ppermute x0 -> x114, starting transfers between devices: none -> 213 us  [the longest x42 108 us: shift(): lax.ppermute(values, 'ctx', [(order[i], order[(i + offset) % count]) for...]
    unnamed x99 -> x305, local copies, waits for them, and re-layouts: 185 us -> 25.7 us
    dot_general x19 -> x31, matrix products: 230 us -> 78.5 us  [the longest x13 27.4 us: dot_t(): lax.dot_general(left, right, (((1,), (1,)), ((), ())), preferred_element_...]
    concatenate x7 -> x10, local copies, waits for them, and re-layouts: 151 us -> 25 us  [the longest x2 13.8 us: square_gather(): jnp.concatenate([near, swap(near, 'seq', 1), far, swap(far, 'seq', 1)])]
  transfers between devices with their start and end apart: 15 -> 114, of which waited for: 8 -> 45; matrix products, arithmetic and copies ran while one was open for 21% -> 26% of each run, Pallas kernels for 0% -> 4%
where the time goes in v1:
time: 782 us; the launch traced here: 770 us
  waiting for transfers between devices  235 us (30%)
  starting transfers between devices  213 us (27%)
  local copies, waits for them, and re-layouts  96.7 us (12%)
  other arithmetic  86.6 us (11%)
  matrix products  78.5 us (10%)
  between operations  32 us (4%)
  Pallas kernels  28 us (4%)
    ppermute x60, waiting for transfers between devices, swap(): return lax.ppermute(values, axis, [(i, i ^ bit) for i in range(count)])  126 us
    ppermute x42, starting transfers between devices, shift(): lax.ppermute(values, 'ctx', [(order[i], order[(i + offset) % count]) for...  108 us
    ppermute x42, waiting for transfers between devices, shift(): lax.ppermute(values, 'ctx', [(order[i], order[(i + offset) % count]) for...  98.3 us
    ppermute x60, starting transfers between devices, swap(): return lax.ppermute(values, axis, [(i, i ^ bit) for i in range(count)])  72.8 us
    dot_general x13, matrix products, dot_t(): lax.dot_general(left, right, (((1,), (1,)), ((), ())), preferred_element_...  27.4 us
    dot_general x13, matrix products, dot(): return jnp.dot(left, right, preferred_element_type=FULL)  26.6 us
    unnamed x305, local copies, waits for them, and re-layouts  25.7 us
    dot_general x5, matrix products, t_dot(): lax.dot_general(left, right, (((0,), (0,)), ((), ())), preferred_element_...  24.4 us
  transfers between devices with their start and end apart: 114, of which 45 were waited for; matrix products, arithmetic and copies ran while one was open for 26% of the time, Pallas kernels for 4%

profile of v1, /device:TPU:0, one launch (start us, length us, event | category | flops | bytes accessed | tf_op | source)
XLA Modules:
  0.0 770.2 jit_solution(10945680106677540548)
XLA Ops:
  0.7 4.1 collective-permute-start.29
  14.0 3.5 collective-permute-start.1
  43.6 8.8 %collective-permute-start.2 = (bf16[400,256]{1,0:T(8,128)(2,1)S(1)}, bf16[400,256]{1,0:T(8,128)(2,1)S(1)}, u32[]{:S(2)}, u32[]{:S(2)}) collective-permute-start(bf16[400,256]{1,0:T(8,128)(2,1)S(1)} %copy-done.95), channel_id=1, source_target_pairs={{7,5},{4,3},{2,0},{1,4},{5,1},{0,2},{15,13},{12,11},{10,8},{9,12},... | collective-permute-start | bytes 614408 | tf_op jit(solution)/shard_map/ppermute | solution.py:199
  58.0 4.6 collective-permute-done.52
  65.3 8.1 %collective-permute-done.3 = bf16[400,256]{1,0:T(8,128)(2,1)S(1)} collective-permute-done((bf16[400,256]{1,0:T(8,128)(2,1)S(1)}, bf16[400,256]{1,0:T(8,128)(2,1)S(1)}, u32[]{:S(2)}, u32[]{:S(2)}) %collective-permute-start.3) | collective-permute-done | bytes 204832 | tf_op jit(solution)/shard_map/ppermute | solution.py:199
  80.4 5.4 collective-permute-done.30
  87.8 4.3 collective-permute-done.6
  101.7 19.4 %collective-permute-done.41 = bf16[1,400,800]{2,1,0:T(8,128)(2,1)S(1)} collective-permute-done((bf16[1,400,800]{2,1,0:T(8,128)(2,1)S(1)}, bf16[1,400,800]{2,1,0:T(8,128)(2,1)S(1)}, u32[]{:S(2)}, u32[]{:S(2)}) %collective-permute-start.41) | collective-permute-done | bytes 640032 | tf_op jit(solution)/shard_map/ppermute | solution.py:58
  129.4 6.9 collective-permute-start.12
  146.6 3.2 collective-permute-start.44
  149.8 5.6 collective-permute-done.13
  155.4 13.4 %collective-permute-start.16 = (bf16[64,1600]{0,1:T(8,128)(2,1)S(1)}, bf16[64,1600]{0,1:T(8,128)(2,1)S(1)}, u32[]{:S(2)}, u32[]{:S(2)}) collective-permute-start(bf16[64,1600]{0,1:T(8,128)(2,1)S(1)} %collective-permute-done.12), channel_id=1, source_target_pairs={{0,2},{2,4},{4,6},{6,7},{7,5},{5,3},{3,1},{1,0},{8,10},{10,12},{12... | collective-permute-start | bytes 614408 | tf_op jit(solution)/shard_map/ppermute | solution.py:76
  173.4 4.7 collective-permute-done.16
  178.0 7.1 collective-permute-start.19
  187.6 4.2 collective-permute-done.18
  191.7 10.3 %collective-permute-start.20 = (bf16[64,1600]{0,1:T(8,128)(2,1)S(1)}, bf16[64,1600]{0,1:T(8,128)(2,1)S(1)}, u32[]{:S(2)}, u32[]{:S(2)}) collective-permute-start(bf16[64,1600]{0,1:T(8,128)(2,1)S(1)} %collective-permute-done.16), channel_id=1, source_target_pairs={{0,2},{2,4},{4,6},{6,7},{7,5},{5,3},{3,1},{1,0},{8,10},{10,12},{12... | collective-permute-start | bytes 614408 | tf_op jit(solution)/shard_map/ppermute | solution.py:76
  203.3 4.2 collective-permute-done.20
  207.6 3.3 collective-permute-done.21
  211.8 10.0 %attend.1 = (f32[1024,256]{1,0:T(8,128)S(1)}, bf16[1024,256]{1,0:T(8,128)(2,1)S(1)}, f32[1024,4]{1,0:T(8,128)S(1)}) custom-call(bf16[1024,256]{1,0:T(8,128)(2,1)S(1)} %get-tuple-element.118.q_ref, bf16[1024,256]{1,0:T(8,128)(2,1)S(1)} %get-tuple-element.117.k_ref, bf16[1024,256]{1,0:T(8,128)(2,1)S(1)} %get-tuple-element.116.v_ref, ...), custom_call_target="tpu_custom_call" | custom-call | flops 1073741824 | bytes 3145728 | tf_op jit(solution)/shard_map/attend/pallas_call | solution.py:265
  223.2 4.2 collective-permute-done.22
  227.6 5.7 collective-permute-done.23
  233.4 6.0 collective-permute-done.24
  241.8 4.7 collective-permute-done.25
  249.4 3.7 collective-permute-done.26
  253.2 5.1 collective-permute-done.27
  258.4 4.1 collective-permute-done.28
  289.2 8.4 %concatenate.202 = bf16[1024,1600]{0,1:T(8,128)(2,1)} concatenate(bf16[128,1600]{0,1:T(8,128)(2,1)} %copy-done.31, bf16[64,1600]{0,1:T(8,128)(2,1)} %collective-permute-done.8, bf16[64,1600]{0,1:T(8,128)(2,1)} %collective-permute-done.9, bf16[64,1600]{0,1:T(8,128)(2,1)} %collective-permute-done.10, bf16[64,1600]{0,1:T(8,128)(2,1)} %collective-permute-done.11, ...), dimensions={0} | concatenate | bytes 6553600 | tf_op jit(solution)/shard_map/concatenate | solution.py:511
  300.3 6.9 concatenate.193
  310.7 5.3 collective-permute-done.34
  333.2 6.9 concatenate.180
  340.1 6.0 fusion.197
  346.2 5.9 fusion.169
  352.0 4.3 convert_reduce_fusion
  356.3 7.2 fusion.194
  363.5 5.0 fusion.196
  368.5 6.2 fusion.193
  377.5 3.4 select_convert_fusion.1
  384.8 3.4 select_convert_fusion
  394.8 7.6 collective-permute-done.48
  407.3 3.8 collective-permute-done.60
  418.0 27.5 %collective-permute-done.111 = bf16[800,800]{1,0:T(8,128)(2,1)S(1)} collective-permute-done((bf16[800,800]{1,0:T(8,128)(2,1)S(1)}, bf16[800,800]{1,0:T(8,128)(2,1)S(1)}, u32[]{:S(2)}, u32[]{:S(2)}) %collective-permute-start.111) | collective-permute-done | bytes 1280032 | tf_op jit(solution)/shard_map/ppermute | solution.py:58
  466.7 3.5 convolution_convert_fusion
  484.7 30.6 %collective-permute-start.67 = (bf16[128,256]{1,0:T(8,128)(2,1)}, bf16[128,256]{1,0:T(8,128)(2,1)S(1)}, u32[]{:S(2)}, u32[]{:S(2)}) collective-permute-start(bf16[128,256]{1,0:T(8,128)(2,1)} %bitcast.370), channel_id=1, source_target_pairs={{0,3},{2,1},{4,0},{6,2},{7,4},{5,6},{3,7},{1,5},{8,11},{10,9},{12,... | collective-permute-start | bytes 196616 | tf_op jit(solution)/shard_map/ppermute | solution.py:76
  517.8 3.1 collective-permute-start.69
  528.1 18.0 %attend_back.1 = (bf16[1024,256]{1,0:T(8,128)(2,1)S(1)}, f32[1024,256]{1,0:T(8,128)S(1)}, f32[1024,256]{1,0:T(8,128)S(1)}) custom-call(bf16[1024,256]{1,0:T(8,128)(2,1)S(1)} %get-tuple-element.118.q_ref, bf16[1024,256]{1,0:T(8,128)(2,1)S(1)} %get-tuple-element.117.k_ref, bf16[1024,256]{1,0:T(8,128)(2,1)S(1)} %get-tuple-element.116.v_ref, ...), custom_call_target="tpu_custom_call" | custom-call | flops 2684354560 | bytes 6291456 | tf_op jit(solution)/shard_map/attend_back/pallas_call | solution.py:297
  556.0 4.7 fusion.195
  563.9 3.3 collective-permute-done.105
  580.9 5.3 collective-permute-done.71
  588.3 10.2 %collective-permute-done.82 = bf16[64,1600]{0,1:T(8,128)(2,1)S(1)} collective-permute-done((bf16[64,1600]{0,1:T(8,128)(2,1)S(1)}, bf16[64,1600]{0,1:T(8,128)(2,1)S(1)}, u32[]{:S(2)}, u32[]{:S(2)}) %collective-permute-start.82) | collective-permute-done | bytes 204832 | tf_op jit(solution)/shard_map/ppermute | solution.py:76
  604.8 6.0 collective-permute-done.79
  610.8 8.7 %collective-permute-done.83 = bf16[64,1600]{0,1:T(8,128)(2,1)S(1)} collective-permute-done((bf16[64,1600]{0,1:T(8,128)(2,1)S(1)}, bf16[64,1600]{0,1:T(8,128)(2,1)S(1)}, u32[]{:S(2)}, u32[]{:S(2)}) %collective-permute-start.83) | collective-permute-done | bytes 204832 | tf_op jit(solution)/shard_map/ppermute | solution.py:76
  627.8 4.4 collective-permute-done.84
  643.5 3.8 collective-permute-done.87
  656.0 3.2 fusion.9
  662.8 5.4 convert_add_fusion
  668.2 6.8 copy.76
  675.1 4.2 fusion.16
  688.6 3.4 collective-permute-start.92
  692.0 16.5 %collective-permute-done.99 = bf16[4,200,800]{2,1,0:T(8,128)(2,1)} collective-permute-done((bf16[4,200,800]{2,1,0:T(8,128)(2,1)}, bf16[4,200,800]{2,1,0:T(8,128)(2,1)}, u32[]{:S(2)}, u32[]{:S(2)}) %collective-permute-start.99) | collective-permute-done | bytes 1280032 | tf_op jit(solution)/shard_map/ppermute | solution.py:58
  711.3 4.8 collective-permute-start.100
  720.4 3.2 collective-permute-start.93
  733.6 5.4 collective-permute-start.95
  741.4 15.8 %collective-permute-start.101 = (bf16[1,200,800]{2,1,0:T(8,128)(2,1)S(1)}, bf16[1,200,800]{2,1,0:T(8,128)(2,1)S(1)}, u32[]{:S(2)}, u32[]{:S(2)}) collective-permute-start(bf16[1,200,800]{2,1,0:T(8,128)(2,1)S(1)} %fusion.117), channel_id=1, source_target_pairs={{0,4},{1,5},{2,6},{3,7},{4,0},{5,1},{6,2},{7,3},{8,12},{9,13},{10,... | collective-permute-start | bytes 960008 | tf_op jit(solution)/shard_map/ppermute | solution.py:58
  757.3 5.3 collective-permute-done.101
  (694 shorter events, 290.1 us)
Async XLA Ops:
  0.7 40.2 %collective-permute-start.29 = (bf16[1,1,1,200,400]{3,4,2,1,0:T(8,128)(2,1)}, bf16[1,1,1,200,400]{3,4,2,1,0:T(8,128)(2,1)}, u32[]{:S(2)}, u32[]{:S(2)}) collective-permute-start(bf16[1,1,1,200,400]{3,4,2,1,0:T(8,128)(2,1)} %bitcast.365), channel_id=1, source_target_pairs={{0,4},{1,5},{2,6},{3,7},{4,0},{5,1},{6,2},{7,3},{8,12},{9,13},{10,... | collective-permute-start | bytes 480008 | tf_op jit(solution)/shard_map/ppermute | solution.py:58
  7.0 70.4 %collective-permute-start.40 = (bf16[400,400]{1,0:T(8,128)(2,1)}, bf16[400,400]{1,0:T(8,128)(2,1)}, u32[]{:S(2)}, u32[]{:S(2)}) collective-permute-start(bf16[400,400]{1,0:T(8,128)(2,1)} %broadcast_select_fusion.22), channel_id=1, source_target_pairs={{0,8},{8,0},{16,24},{24,16},{1,9},{9,1},{17,25},{25,17},{2,10},{10... | collective-permute-start | bytes 960008 | tf_op jit(solution)/shard_map/ppermute | solution.py:58
  8.5 86.6 %collective-permute-start.43 = (bf16[400,400]{1,0:T(8,128)(2,1)}, bf16[400,400]{1,0:T(8,128)(2,1)}, u32[]{:S(2)}, u32[]{:S(2)}) collective-permute-start(bf16[400,400]{1,0:T(8,128)(2,1)} %broadcast_select_fusion.18), channel_id=1, source_target_pairs={{0,8},{8,0},{16,24},{24,16},{1,9},{9,1},{17,25},{25,17},{2,10},{10... | collective-permute-start | bytes 960008 | tf_op jit(solution)/shard_map/ppermute | solution.py:58
  9.2 48.1 %collective-permute-start.53 = (bf16[64,1600]{0,1:T(8,128)(2,1)S(1)}, bf16[64,1600]{0,1:T(8,128)(2,1)S(1)}, u32[]{:S(2)}, u32[]{:S(2)}) collective-permute-start(bf16[64,1600]{0,1:T(8,128)(2,1)S(1)} %get-tuple-element.172), channel_id=1, source_target_pairs={{0,2},{1,3},{2,0},{3,1},{4,6},{5,7},{6,4},{7,5},{8,10},{9,11},{10,... | collective-permute-start | bytes 614408 | tf_op jit(solution)/shard_map/ppermute | solution.py:58
  14.0 38.5 %collective-permute-start.1 = (bf16[400,256]{1,0:T(8,128)(2,1)}, bf16[400,256]{1,0:T(8,128)(2,1)}, u32[]{:S(2)}, u32[]{:S(2)}) collective-permute-start(bf16[400,256]{1,0:T(8,128)(2,1)} %get-tuple-element.135), channel_id=1, source_target_pairs={{5,0},{0,1},{3,2},{7,4},{6,3},{4,5},{2,6},{13,8},{8,9},{11,10},{15... | collective-permute-start | bytes 614408 | tf_op jit(solution)/shard_map/ppermute | solution.py:199
  56.6 18.8 %collective-permute-start.5 = (bf16[400,256]{1,0:T(8,128)(2,1)S(1)}, bf16[400,256]{1,0:T(8,128)(2,1)S(1)}, u32[]{:S(2)}, u32[]{:S(2)}) collective-permute-start(bf16[400,256]{1,0:T(8,128)(2,1)S(1)} %copy-done.92), channel_id=1, source_target_pairs={{7,3},{15,11},{23,19},{31,27}} | collective-permute-start | bytes 614408 | tf_op jit(solution)/shard_map/ppermute | solution.py:199
  57.3 17.7 %collective-permute-start.4 = (bf16[400,256]{1,0:T(8,128)(2,1)S(1)}, bf16[400,256]{1,0:T(8,128)(2,1)S(1)}, u32[]{:S(2)}, u32[]{:S(2)}) collective-permute-start(bf16[400,256]{1,0:T(8,128)(2,1)S(1)} %copy-done.93), channel_id=1, source_target_pairs={{3,3},{11,11},{19,19},{27,27}} | collective-permute-start | bytes 614408 | tf_op jit(solution)/shard_map/ppermute | solution.py:199
  75.0 22.9 %collective-permute-start.56 = (bf16[128,1600]{0,1:T(8,128)(2,1)S(1)}, bf16[128,1600]{0,1:T(8,128)(2,1)S(1)}, u32[]{:S(2)}, u32[]{:S(2)}) collective-permute-start(bf16[128,1600]{0,1:T(8,128)(2,1)S(1)} %pad_maximum_fusion.23), channel_id=1, source_target_pairs={{0,1},{1,0},{2,3},{3,2},{4,5},{5,4},{6,7},{7,6},{8,9},{9,8},{10,11... | collective-permute-start | bytes 1228808 | tf_op jit(solution)/shard_map/ppermute | solution.py:58
  75.4 25.3 %collective-permute-start.55 = (bf16[128,1600]{0,1:T(8,128)(2,1)S(1)}, bf16[128,1600]{0,1:T(8,128)(2,1)S(1)}, u32[]{:S(2)}, u32[]{:S(2)}) collective-permute-start(bf16[128,1600]{0,1:T(8,128)(2,1)S(1)} %pad_maximum_fusion.22), channel_id=1, source_target_pairs={{0,2},{1,3},{2,0},{3,1},{4,6},{5,7},{6,4},{7,5},{8,10},{9,11},{10,... | collective-permute-start | bytes 1228808 | tf_op jit(solution)/shard_map/ppermute | solution.py:58
  77.4 14.7 %collective-permute-start.6 = (bf16[400,768]{1,0:T(8,128)(2,1)S(1)}, bf16[400,768]{1,0:T(8,128)(2,1)S(1)}, u32[]{:S(2)}, u32[]{:S(2)}) collective-permute-start(bf16[400,768]{1,0:T(8,128)(2,1)S(1)} %fusion.24), channel_id=1, source_target_pairs={{0,16},{8,24},{16,0},{24,8},{1,17},{9,25},{17,1},{25,9},{2,18},{10... | collective-permute-start | bytes 1843208 | tf_op jit(solution)/shard_map/ppermute | solution.py:58
  85.8 35.3 %collective-permute-start.41 = (bf16[1,400,800]{2,1,0:T(8,128)(2,1)S(1)}, bf16[1,400,800]{2,1,0:T(8,128)(2,1)S(1)}, u32[]{:S(2)}, u32[]{:S(2)}) collective-permute-start(bf16[1,400,800]{2,1,0:T(8,128)(2,1)S(1)} %maximum_bitcast_fusion.1), channel_id=1, source_target_pairs={{0,4},{1,5},{2,6},{3,7},{4,0},{5,1},{6,2},{7,3},{8,12},{9,13},{10,... | collective-permute-start | bytes 1920008 | tf_op jit(solution)/shard_map/ppermute | solution.py:58
  92.1 30.3 %collective-permute-start.31 = (bf16[2,2,1,200,400]{3,4,2,1,0:T(8,128)(2,1)S(1)}, bf16[2,2,1,200,400]{3,4,2,1,0:T(8,128)(2,1)S(1)}, u32[]{:S(2)}, u32[]{:S(2)}) collective-permute-start(bf16[2,2,1,200,400]{3,4,2,1,0:T(8,128)(2,1)S(1)} %pad_maximum_fusion.13), channel_id=1, source_target_pairs={{0,1},{1,0},{2,3},{3,2},{4,5},{5,4},{6,7},{7,6},{8,9},{9,8},{10,11... | collective-permute-start | bytes 1920008 | tf_op jit(solution)/shard_map/ppermute | solution.py:58
  95.1 41.3 %collective-permute-start.7 = (bf16[2,400,768]{2,1,0:T(8,128)(2,1)}, bf16[2,400,768]{2,1,0:T(8,128)(2,1)}, u32[]{:S(2)}, u32[]{:S(2)}) collective-permute-start(bf16[2,400,768]{2,1,0:T(8,128)(2,1)} %pad_maximum_fusion.10), channel_id=1, source_target_pairs={{0,8},{8,0},{16,24},{24,16},{1,9},{9,1},{17,25},{25,17},{2,10},{10... | collective-permute-start | bytes 3686408 | tf_op jit(solution)/shard_map/ppermute | solution.py:58
  97.9 31.5 %collective-permute-start.10 = (bf16[64,1600]{0,1:T(8,128)(2,1)}, bf16[64,1600]{0,1:T(8,128)(2,1)}, u32[]{:S(2)}, u32[]{:S(2)}) collective-permute-start(bf16[64,1600]{0,1:T(8,128)(2,1)} %get-tuple-element.176), channel_id=1, source_target_pairs={{0,1},{2,0},{4,2},{6,4},{7,6},{5,7},{3,5},{1,3},{8,9},{10,8},{12,1... | collective-permute-start | bytes 614408 | tf_op jit(solution)/shard_map/ppermute | solution.py:76
  100.7 28.6 %collective-permute-start.8 = (bf16[64,1600]{0,1:T(8,128)(2,1)}, bf16[64,1600]{0,1:T(8,128)(2,1)}, u32[]{:S(2)}, u32[]{:S(2)}) collective-permute-start(bf16[64,1600]{0,1:T(8,128)(2,1)} %get-tuple-element.176), channel_id=1, source_target_pairs={{0,2},{2,4},{4,6},{6,7},{7,5},{5,3},{3,1},{1,0},{8,10},{10,12},{12... | collective-permute-start | bytes 614408 | tf_op jit(solution)/shard_map/ppermute | solution.py:76
  129.3 171.0 %collective-permute-start.54 = (bf16[256,1600]{0,1:T(8,128)(2,1)}, bf16[256,1600]{0,1:T(8,128)(2,1)}, u32[]{:S(2)}, u32[]{:S(2)}) collective-permute-start(bf16[256,1600]{0,1:T(8,128)(2,1)} %pad_maximum_fusion.16), channel_id=1, source_target_pairs={{0,8},{8,0},{16,24},{24,16},{1,9},{9,1},{17,25},{25,17},{2,10},{10... | collective-permute-start | bytes 2457608 | tf_op jit(solution)/shard_map/ppermute | solution.py:58
  129.3 40.2 %collective-permute-start.14 = (bf16[64,1600]{0,1:T(8,128)(2,1)}, bf16[64,1600]{0,1:T(8,128)(2,1)S(1)}, u32[]{:S(2)}, u32[]{:S(2)}) collective-permute-start(bf16[64,1600]{0,1:T(8,128)(2,1)} %collective-permute-done.10), channel_id=1, source_target_pairs={{0,1},{2,0},{4,2},{6,4},{7,6},{5,7},{3,5},{1,3},{8,9},{10,8},{12,1... | collective-permute-start | bytes 614408 | tf_op jit(solution)/shard_map/ppermute | solution.py:76
  129.4 17.2 %collective-permute-start.12 = (bf16[64,1600]{0,1:T(8,128)(2,1)}, bf16[64,1600]{0,1:T(8,128)(2,1)S(1)}, u32[]{:S(2)}, u32[]{:S(2)}) collective-permute-start(bf16[64,1600]{0,1:T(8,128)(2,1)} %collective-permute-done.8), channel_id=1, source_target_pairs={{0,2},{2,4},{4,6},{6,7},{7,5},{5,3},{3,1},{1,0},{8,10},{10,12},{12... | collective-permute-start | bytes 614408 | tf_op jit(solution)/shard_map/ppermute | solution.py:76
  136.4 36.2 %collective-permute-start.15 = (bf16[64,1600]{0,1:T(8,128)(2,1)}, bf16[64,1600]{0,1:T(8,128)(2,1)S(1)}, u32[]{:S(2)}, u32[]{:S(2)}) collective-permute-start(bf16[64,1600]{0,1:T(8,128)(2,1)} %collective-permute-done.11), channel_id=1, source_target_pairs={{0,1},{2,0},{4,2},{6,4},{7,6},{5,7},{3,5},{1,3},{8,9},{10,8},{12,1... | collective-permute-start | bytes 614408 | tf_op jit(solution)/shard_map/ppermute | solution.py:76
  136.4 19.0 %collective-permute-start.13 = (bf16[64,1600]{0,1:T(8,128)(2,1)}, bf16[64,1600]{0,1:T(8,128)(2,1)S(1)}, u32[]{:S(2)}, u32[]{:S(2)}) collective-permute-start(bf16[64,1600]{0,1:T(8,128)(2,1)} %collective-permute-done.9), channel_id=1, source_target_pairs={{0,2},{2,4},{4,6},{6,7},{7,5},{5,3},{3,1},{1,0},{8,10},{10,12},{12... | collective-permute-start | bytes 614408 | tf_op jit(solution)/shard_map/ppermute | solution.py:76
  146.6 151.1 %collective-permute-start.44 = (bf16[1,400,800]{2,1,0:T(8,128)(2,1)}, bf16[1,400,800]{2,1,0:T(8,128)(2,1)}, u32[]{:S(2)}, u32[]{:S(2)}) collective-permute-start(bf16[1,400,800]{2,1,0:T(8,128)(2,1)} %maximum_bitcast_fusion.2), channel_id=1, source_target_pairs={{0,4},{1,5},{2,6},{3,7},{4,0},{5,1},{6,2},{7,3},{8,12},{9,13},{10,... | collective-permute-start | bytes 1920008 | tf_op jit(solution)/shard_map/ppermute | solution.py:58
  155.4 22.7 %collective-permute-start.16 = (bf16[64,1600]{0,1:T(8,128)(2,1)S(1)}, bf16[64,1600]{0,1:T(8,128)(2,1)S(1)}, u32[]{:S(2)}, u32[]{:S(2)}) collective-permute-start(bf16[64,1600]{0,1:T(8,128)(2,1)S(1)} %collective-permute-done.12), channel_id=1, source_target_pairs={{0,2},{2,4},{4,6},{6,7},{7,5},{5,3},{3,1},{1,0},{8,10},{10,12},{12... | collective-permute-start | bytes 614408 | tf_op jit(solution)/shard_map/ppermute | solution.py:76
  169.6 15.6 %collective-permute-start.17 = (bf16[64,1600]{0,1:T(8,128)(2,1)S(1)}, bf16[64,1600]{0,1:T(8,128)(2,1)S(1)}, u32[]{:S(2)}, u32[]{:S(2)}) collective-permute-start(bf16[64,1600]{0,1:T(8,128)(2,1)S(1)} %collective-permute-done.13), channel_id=1, source_target_pairs={{0,2},{2,4},{4,6},{6,7},{7,5},{5,3},{3,1},{1,0},{8,10},{10,12},{12... | collective-permute-start | bytes 614408 | tf_op jit(solution)/shard_map/ppermute | solution.py:76
  172.5 19.2 %collective-permute-start.18 = (bf16[64,1600]{0,1:T(8,128)(2,1)S(1)}, bf16[64,1600]{0,1:T(8,128)(2,1)S(1)}, u32[]{:S(2)}, u32[]{:S(2)}) collective-permute-start(bf16[64,1600]{0,1:T(8,128)(2,1)S(1)} %collective-permute-done.14), channel_id=1, source_target_pairs={{0,1},{2,0},{4,2},{6,4},{7,6},{5,7},{3,5},{1,3},{8,9},{10,8},{12,1... | collective-permute-start | bytes 614408 | tf_op jit(solution)/shard_map/ppermute | solution.py:76
  178.0 24.0 %collective-permute-start.19 = (bf16[64,1600]{0,1:T(8,128)(2,1)S(1)}, bf16[64,1600]{0,1:T(8,128)(2,1)S(1)}, u32[]{:S(2)}, u32[]{:S(2)}) collective-permute-start(bf16[64,1600]{0,1:T(8,128)(2,1)S(1)} %collective-permute-done.15), channel_id=1, source_target_pairs={{0,1},{2,0},{4,2},{6,4},{7,6},{5,7},{3,5},{1,3},{8,9},{10,8},{12,1... | collective-permute-start | bytes 614408 | tf_op jit(solution)/shard_map/ppermute | solution.py:76
  185.2 36.7 %collective-permute-start.32 = (bf16[1600,400]{0,1:T(8,128)(2,1)S(1)}, bf16[1600,400]{0,1:T(8,128)(2,1)S(1)}, u32[]{:S(2)}, u32[]{:S(2)}) collective-permute-start(bf16[1600,400]{0,1:T(8,128)(2,1)S(1)} %copy-done.39), channel_id=1, source_target_pairs={{0,16},{8,24},{16,0},{24,8},{1,17},{9,25},{17,1},{25,9},{2,18},{10... | collective-permute-start | bytes 3840008 | tf_op jit(solution)/shard_map/ppermute | solution.py:58
  191.7 15.8 %collective-permute-start.20 = (bf16[64,1600]{0,1:T(8,128)(2,1)S(1)}, bf16[64,1600]{0,1:T(8,128)(2,1)S(1)}, u32[]{:S(2)}, u32[]{:S(2)}) collective-permute-start(bf16[64,1600]{0,1:T(8,128)(2,1)S(1)} %collective-permute-done.16), channel_id=1, source_target_pairs={{0,2},{2,4},{4,6},{6,7},{7,5},{5,3},{3,1},{1,0},{8,10},{10,12},{12... | collective-permute-start | bytes 614408 | tf_op jit(solution)/shard_map/ppermute | solution.py:76
  207.6 92.8 %collective-permute-start.57 = (bf16[256,1600]{0,1:T(8,128)(2,1)}, bf16[256,1600]{0,1:T(8,128)(2,1)}, u32[]{:S(2)}, u32[]{:S(2)}) collective-permute-start(bf16[256,1600]{0,1:T(8,128)(2,1)} %pad_maximum_fusion.17), channel_id=1, source_target_pairs={{0,8},{8,0},{16,24},{24,16},{1,9},{9,1},{17,25},{25,17},{2,10},{10... | collective-permute-start | bytes 2457608 | tf_op jit(solution)/shard_map/ppermute | solution.py:58
  223.1 45.8 %collective-permute-start.33 = (bf16[2,1600,400]{1,2,0:T(8,128)(2,1)S(1)}, bf16[2,1600,400]{1,2,0:T(8,128)(2,1)S(1)}, u32[]{:S(2)}, u32[]{:S(2)}) collective-permute-start(bf16[2,1600,400]{1,2,0:T(8,128)(2,1)S(1)} %pad_maximum_fusion.1), channel_id=1, source_target_pairs={{0,8},{8,0},{16,24},{24,16},{1,9},{9,1},{17,25},{25,17},{2,10},{10... | collective-permute-start | bytes 7680008 | tf_op jit(solution)/shard_map/ppermute | solution.py:58
  262.5 56.8 %collective-permute-start.42 = (bf16[2,400,800]{2,1,0:T(8,128)(2,1)}, bf16[2,400,800]{2,1,0:T(8,128)(2,1)}, u32[]{:S(2)}, u32[]{:S(2)}) collective-permute-start(bf16[2,400,800]{2,1,0:T(8,128)(2,1)} %pad_maximum_fusion.8), channel_id=1, source_target_pairs={{0,16},{8,24},{16,0},{24,8},{1,17},{9,25},{17,1},{25,9},{2,18},{10... | collective-permute-start | bytes 3840008 | tf_op jit(solution)/shard_map/ppermute | solution.py:58
  274.1 34.7 %collective-permute-start.35 = (bf16[64,1600]{0,1:T(8,128)(2,1)}, bf16[64,1600]{0,1:T(8,128)(2,1)}, u32[]{:S(2)}, u32[]{:S(2)}) collective-permute-start(bf16[64,1600]{0,1:T(8,128)(2,1)} %get-tuple-element.174), channel_id=1, source_target_pairs={{0,2},{1,3},{2,0},{3,1},{4,6},{5,7},{6,4},{7,5},{8,10},{9,11},{10,... | collective-permute-start | bytes 614408 | tf_op jit(solution)/shard_map/ppermute | solution.py:58
  300.3 28.4 %collective-permute-start.45 = (bf16[2,400,800]{2,1,0:T(8,128)(2,1)}, bf16[2,400,800]{2,1,0:T(8,128)(2,1)}, u32[]{:S(2)}, u32[]{:S(2)}) collective-permute-start(bf16[2,400,800]{2,1,0:T(8,128)(2,1)} %pad_maximum_fusion.9), channel_id=1, source_target_pairs={{0,16},{8,24},{16,0},{24,8},{1,17},{9,25},{17,1},{25,9},{2,18},{10... | collective-permute-start | bytes 3840008 | tf_op jit(solution)/shard_map/ppermute | solution.py:58
  380.9 34.3 %collective-permute-start.108 = (bf16[800,800]{1,0:T(8,128)(2,1)S(1)}, bf16[800,800]{1,0:T(8,128)(2,1)S(1)}, u32[]{:S(2)}, u32[]{:S(2)}) collective-permute-start(bf16[800,800]{1,0:T(8,128)(2,1)S(1)} %select_convert_fusion.1), channel_id=1, source_target_pairs={{0,16},{8,24},{16,0},{24,8},{1,17},{9,25},{17,1},{25,9},{2,18},{10... | collective-permute-start | bytes 3840008 | tf_op jit(solution)/shard_map/ppermute | solution.py:58
  388.3 57.3 %collective-permute-start.111 = (bf16[800,800]{1,0:T(8,128)(2,1)S(1)}, bf16[800,800]{1,0:T(8,128)(2,1)S(1)}, u32[]{:S(2)}, u32[]{:S(2)}) collective-permute-start(bf16[800,800]{1,0:T(8,128)(2,1)S(1)} %select_convert_fusion), channel_id=1, source_target_pairs={{0,16},{8,24},{16,0},{24,8},{1,17},{9,25},{17,1},{25,9},{2,18},{10... | collective-permute-start | bytes 3840008 | tf_op jit(solution)/shard_map/ppermute | solution.py:58
  393.7 17.5 %collective-permute-start.60 = (bf16[128,1600]{0,1:T(8,128)(2,1)S(1)}, bf16[128,1600]{0,1:T(8,128)(2,1)S(1)}, u32[]{:S(2)}, u32[]{:S(2)}) collective-permute-start(bf16[128,1600]{0,1:T(8,128)(2,1)S(1)} %get-tuple-element.147), channel_id=1, source_target_pairs={{0,2},{1,3},{2,0},{3,1},{4,6},{5,7},{6,4},{7,5},{8,10},{9,11},{10,... | collective-permute-start | bytes 1228808 | tf_op jit(solution)/shard_map/ppermute | solution.py:58
  405.3 57.5 %collective-permute-start.51 = (bf16[64,1600]{0,1:T(8,128)(2,1)}, bf16[64,1600]{0,1:T(8,128)(2,1)}, u32[]{:S(2)}, u32[]{:S(2)}) collective-permute-start(bf16[64,1600]{0,1:T(8,128)(2,1)} %slice.949), channel_id=1, source_target_pairs={{0,2},{1,3},{2,0},{3,1},{4,6},{5,7},{6,4},{7,5},{8,10},{9,11},{10,... | collective-permute-start | bytes 614408 | tf_op jit(solution)/shard_map/ppermute | solution.py:58
  411.2 59.0 %collective-permute-start.49 = (bf16[64,1600]{0,1:T(8,128)(2,1)}, bf16[64,1600]{0,1:T(8,128)(2,1)}, u32[]{:S(2)}, u32[]{:S(2)}) collective-permute-start(bf16[64,1600]{0,1:T(8,128)(2,1)} %slice.950), channel_id=1, source_target_pairs={{0,1},{1,0},{2,3},{3,2},{4,5},{5,4},{6,7},{7,6},{8,9},{9,8},{10,11... | collective-permute-start | bytes 614408 | tf_op jit(solution)/shard_map/ppermute | solution.py:58
  412.7 37.7 %collective-permute-start.63 = (bf16[64,1600]{0,1:T(8,128)(2,1)S(1)}, bf16[64,1600]{0,1:T(8,128)(2,1)S(1)}, u32[]{:S(2)}, u32[]{:S(2)}) collective-permute-start(bf16[64,1600]{0,1:T(8,128)(2,1)S(1)} %slice.947), channel_id=1, source_target_pairs={{0,2},{1,3},{2,0},{3,1},{4,6},{5,7},{6,4},{7,5},{8,10},{9,11},{10,... | collective-permute-start | bytes 614408 | tf_op jit(solution)/shard_map/ppermute | solution.py:58
  415.2 35.9 %collective-permute-start.61 = (bf16[64,1600]{0,1:T(8,128)(2,1)S(1)}, bf16[64,1600]{0,1:T(8,128)(2,1)S(1)}, u32[]{:S(2)}, u32[]{:S(2)}) collective-permute-start(bf16[64,1600]{0,1:T(8,128)(2,1)S(1)} %slice.948), channel_id=1, source_target_pairs={{0,1},{1,0},{2,3},{3,2},{4,5},{5,4},{6,7},{7,6},{8,9},{9,8},{10,11... | collective-permute-start | bytes 614408 | tf_op jit(solution)/shard_map/ppermute | solution.py:58
  445.5 157.8 %collective-permute-start.109 = (bf16[1,400,800]{2,1,0:T(8,128)(2,1)}, bf16[1,400,800]{2,1,0:T(8,128)(2,1)}, u32[]{:S(2)}, u32[]{:S(2)}) collective-permute-start(bf16[1,400,800]{2,1,0:T(8,128)(2,1)} %fusion.77), channel_id=1, source_target_pairs={{0,4},{1,5},{2,6},{3,7},{4,0},{5,1},{6,2},{7,3},{8,12},{9,13},{10,... | collective-permute-start | bytes 1920008 | tf_op jit(solution)/shard_map/ppermute | solution.py:58
  450.4 187.2 %collective-permute-start.112 = (bf16[1,400,800]{2,1,0:T(8,128)(2,1)}, bf16[1,400,800]{2,1,0:T(8,128)(2,1)}, u32[]{:S(2)}, u32[]{:S(2)}) collective-permute-start(bf16[1,400,800]{2,1,0:T(8,128)(2,1)} %fusion.78), channel_id=1, source_target_pairs={{0,4},{1,5},{2,6},{3,7},{4,0},{5,1},{6,2},{7,3},{8,12},{9,13},{10,... | collective-permute-start | bytes 1920008 | tf_op jit(solution)/shard_map/ppermute | solution.py:58
  457.1 23.6 %collective-permute-start.103 = (f32[12800]{0:T(1024)}, f32[12800]{0:T(1024)}, u32[]{:S(2)}, u32[]{:S(2)}) collective-permute-start(f32[12800]{0:T(1024)} %concatenate.210), channel_id=1, source_target_pairs={{0,8},{8,0},{16,24},{24,16},{1,9},{9,1},{17,25},{25,17},{2,10},{10... | collective-permute-start | bytes 153608 | tf_op jit(solution)/shard_map/ppermute | solution.py:58
  462.8 21.9 %collective-permute-start.64 = (bf16[128,256]{1,0:T(8,128)(2,1)}, bf16[128,256]{1,0:T(8,128)(2,1)}, u32[]{:S(2)}, u32[]{:S(2)}) collective-permute-start(bf16[128,256]{1,0:T(8,128)(2,1)} %bitcast.369), channel_id=1, source_target_pairs={{0,2},{2,4},{4,6},{6,7},{7,5},{5,3},{3,1},{1,0},{8,10},{10,12},{12... | collective-permute-start | bytes 196616 | tf_op jit(solution)/shard_map/ppermute | solution.py:76
  470.2 46.0 %collective-permute-start.65 = (bf16[128,256]{1,0:T(8,128)(2,1)}, bf16[128,256]{1,0:T(8,128)(2,1)}, u32[]{:S(2)}, u32[]{:S(2)}) collective-permute-start(bf16[128,256]{1,0:T(8,128)(2,1)} %bitcast.65), channel_id=1, source_target_pairs={{0,1},{2,0},{4,2},{6,4},{7,6},{5,7},{3,5},{1,3},{8,9},{10,8},{12,1... | collective-permute-start | bytes 196616 | tf_op jit(solution)/shard_map/ppermute | solution.py:76
  480.7 37.1 %collective-permute-start.66 = (bf16[128,256]{1,0:T(8,128)(2,1)}, bf16[128,256]{1,0:T(8,128)(2,1)S(1)}, u32[]{:S(2)}, u32[]{:S(2)}) collective-permute-start(bf16[128,256]{1,0:T(8,128)(2,1)} %bitcast.371), channel_id=1, source_target_pairs={{0,4},{2,6},{4,7},{6,5},{7,3},{5,1},{3,0},{1,2},{8,12},{10,14},{12... | collective-permute-start | bytes 196616 | tf_op jit(solution)/shard_map/ppermute | solution.py:76
  484.7 36.2 %collective-permute-start.67 = (bf16[128,256]{1,0:T(8,128)(2,1)}, bf16[128,256]{1,0:T(8,128)(2,1)S(1)}, u32[]{:S(2)}, u32[]{:S(2)}) collective-permute-start(bf16[128,256]{1,0:T(8,128)(2,1)} %bitcast.370), channel_id=1, source_target_pairs={{0,3},{2,1},{4,0},{6,2},{7,4},{5,6},{3,7},{1,5},{8,11},{10,9},{12,... | collective-permute-start | bytes 196616 | tf_op jit(solution)/shard_map/ppermute | solution.py:76
  523.6 38.5 %collective-permute-start.104 = (f32[12800]{0:T(1024)}, f32[12800]{0:T(1024)}, u32[]{:S(2)}, u32[]{:S(2)}) collective-permute-start(f32[12800]{0:T(1024)} %add.536), channel_id=1, source_target_pairs={{0,16},{8,24},{16,0},{24,8},{1,17},{9,25},{17,1},{25,9},{2,18},{10... | collective-permute-start | bytes 153608 | tf_op jit(solution)/shard_map/ppermute | solution.py:58
  554.7 25.2 %collective-permute-start.81 = (bf16[64,1600]{0,1:T(8,128)(2,1)S(1)}, bf16[64,1600]{0,1:T(8,128)(2,1)S(1)}, u32[]{:S(2)}, u32[]{:S(2)}) collective-permute-start(bf16[64,1600]{0,1:T(8,128)(2,1)S(1)} %get-tuple-element.170), channel_id=1, source_target_pairs={{0,1},{2,0},{4,2},{6,4},{7,6},{5,7},{3,5},{1,3},{8,9},{10,8},{12,1... | collective-permute-start | bytes 614408 | tf_op jit(solution)/shard_map/ppermute | solution.py:76
  579.9 21.1 %collective-permute-start.75 = (bf16[64,1600]{0,1:T(8,128)(2,1)S(1)}, bf16[64,1600]{0,1:T(8,128)(2,1)S(1)}, u32[]{:S(2)}, u32[]{:S(2)}) collective-permute-start(bf16[64,1600]{0,1:T(8,128)(2,1)S(1)} %slice.946), channel_id=1, source_target_pairs={{0,2},{2,4},{4,6},{6,7},{7,5},{5,3},{3,1},{1,0},{8,10},{10,12},{12... | collective-permute-start | bytes 614408 | tf_op jit(solution)/shard_map/ppermute | solution.py:76
  601.0 18.5 %collective-permute-start.83 = (bf16[64,1600]{0,1:T(8,128)(2,1)S(1)}, bf16[64,1600]{0,1:T(8,128)(2,1)S(1)}, u32[]{:S(2)}, u32[]{:S(2)}) collective-permute-start(bf16[64,1600]{0,1:T(8,128)(2,1)S(1)} %get-tuple-element.142), channel_id=1, source_target_pairs={{0,1},{2,0},{4,2},{6,4},{7,6},{5,7},{3,5},{1,3},{8,9},{10,8},{12,1... | collective-permute-start | bytes 614408 | tf_op jit(solution)/shard_map/ppermute | solution.py:76
  601.8 21.0 %collective-permute-start.73 = (bf16[64,1600]{0,1:T(8,128)(2,1)S(1)}, bf16[64,1600]{0,1:T(8,128)(2,1)S(1)}, u32[]{:S(2)}, u32[]{:S(2)}) collective-permute-start(bf16[64,1600]{0,1:T(8,128)(2,1)S(1)} %get-tuple-element.145), channel_id=1, source_target_pairs={{0,2},{2,4},{4,6},{6,7},{7,5},{5,3},{3,1},{1,0},{8,10},{10,12},{12... | collective-permute-start | bytes 614408 | tf_op jit(solution)/shard_map/ppermute | solution.py:76
  603.4 19.4 %collective-permute-start.76 = (bf16[64,1600]{0,1:T(8,128)(2,1)S(1)}, bf16[64,1600]{0,1:T(8,128)(2,1)S(1)}, u32[]{:S(2)}, u32[]{:S(2)}) collective-permute-start(bf16[64,1600]{0,1:T(8,128)(2,1)S(1)} %get-tuple-element.146), channel_id=1, source_target_pairs={{0,2},{2,4},{4,6},{6,7},{7,5},{5,3},{3,1},{1,0},{8,10},{10,12},{12... | collective-permute-start | bytes 614408 | tf_op jit(solution)/shard_map/ppermute | solution.py:76
  627.8 35.1 %collective-permute-start.98 = (bf16[1600,800]{0,1:T(8,128)(2,1)}, bf16[1600,800]{0,1:T(8,128)(2,1)}, u32[]{:S(2)}, u32[]{:S(2)}) collective-permute-start(bf16[1600,800]{0,1:T(8,128)(2,1)} %convolution_convert_fusion), channel_id=1, source_target_pairs={{0,8},{8,0},{16,24},{24,16},{1,9},{9,1},{17,25},{25,17},{2,10},{10... | collective-permute-start | bytes 7680008 | tf_op jit(solution)/shard_map/ppermute | solution.py:58
  632.1 23.9 %collective-permute-start.90 = (bf16[2,400,768]{2,1,0:T(8,128)(2,1)}, bf16[2,400,768]{2,1,0:T(8,128)(2,1)}, u32[]{:S(2)}, u32[]{:S(2)}) collective-permute-start(bf16[2,400,768]{2,1,0:T(8,128)(2,1)} %fusion.25), channel_id=1, source_target_pairs={{0,8},{8,0},{16,24},{24,16},{1,9},{9,1},{17,25},{25,17},{2,10},{10... | collective-permute-start | bytes 3686408 | tf_op jit(solution)/shard_map/ppermute | solution.py:58
  632.2 48.7 %collective-permute-start.110 = (f32[400,400]{1,0:T(8,128)}, f32[400,400]{1,0:T(8,128)}, u32[]{:S(2)}, u32[]{:S(2)}) collective-permute-start(f32[400,400]{1,0:T(8,128)} %slice_select_fusion.2), channel_id=1, source_target_pairs={{0,8},{8,0},{16,24},{24,16},{1,9},{9,1},{17,25},{25,17},{2,10},{10... | collective-permute-start | bytes 1920008 | tf_op jit(solution)/shard_map/ppermute | solution.py:58
  641.9 40.4 %collective-permute-start.113 = (f32[400,400]{1,0:T(8,128)}, f32[400,400]{1,0:T(8,128)}, u32[]{:S(2)}, u32[]{:S(2)}) collective-permute-start(f32[400,400]{1,0:T(8,128)} %slice_select_fusion), channel_id=1, source_target_pairs={{0,8},{8,0},{16,24},{24,16},{1,9},{9,1},{17,25},{25,17},{2,10},{10... | collective-permute-start | bytes 1920008 | tf_op jit(solution)/shard_map/ppermute | solution.py:58
  661.6 23.5 %collective-permute-start.91 = (bf16[400,768]{1,0:T(8,128)(2,1)}, bf16[400,768]{1,0:T(8,128)(2,1)}, u32[]{:S(2)}, u32[]{:S(2)}) collective-permute-start(bf16[400,768]{1,0:T(8,128)(2,1)} %fusion.80), channel_id=1, source_target_pairs={{0,16},{8,24},{16,0},{24,8},{1,17},{9,25},{17,1},{25,9},{2,18},{10... | collective-permute-start | bytes 1843208 | tf_op jit(solution)/shard_map/ppermute | solution.py:58
  679.2 29.3 %collective-permute-start.99 = (bf16[4,200,800]{2,1,0:T(8,128)(2,1)}, bf16[4,200,800]{2,1,0:T(8,128)(2,1)}, u32[]{:S(2)}, u32[]{:S(2)}) collective-permute-start(bf16[4,200,800]{2,1,0:T(8,128)(2,1)} %fusion.16), channel_id=1, source_target_pairs={{0,1},{1,0},{2,3},{3,2},{4,5},{5,4},{6,7},{7,6},{8,9},{9,8},{10,11... | collective-permute-start | bytes 3840008 | tf_op jit(solution)/shard_map/ppermute | solution.py:58
  688.6 42.1 %collective-permute-start.92 = (bf16[400,256]{1,0:T(8,128)(2,1)}, bf16[400,256]{1,0:T(8,128)(2,1)}, u32[]{:S(2)}, u32[]{:S(2)}) collective-permute-start(bf16[400,256]{1,0:T(8,128)(2,1)} %get-tuple-element.124), channel_id=1, source_target_pairs={{0,0},{1,3},{2,6},{3,1},{4,4},{5,2},{6,5},{8,8},{9,11},{10,14},{11... | collective-permute-start | bytes 614408 | tf_op jit(solution)/shard_map/ppermute | solution.py:208
  711.3 28.8 %collective-permute-start.100 = (bf16[2,200,800]{2,1,0:T(8,128)(2,1)}, bf16[2,200,800]{2,1,0:T(8,128)(2,1)}, u32[]{:S(2)}, u32[]{:S(2)}) collective-permute-start(bf16[2,200,800]{2,1,0:T(8,128)(2,1)} %fusion.76), channel_id=1, source_target_pairs={{0,2},{1,3},{2,0},{3,1},{4,6},{5,7},{6,4},{7,5},{8,10},{9,11},{10,... | collective-permute-start | bytes 1920008 | tf_op jit(solution)/shard_map/ppermute | solution.py:58
  729.4 27.9 %collective-permute-start.97 = (bf16[400,256]{1,0:T(8,128)(2,1)}, bf16[400,256]{1,0:T(8,128)(2,1)S(1)}, u32[]{:S(2)}, u32[]{:S(2)}) collective-permute-start(bf16[400,256]{1,0:T(8,128)(2,1)} %get-tuple-element.119), channel_id=1, source_target_pairs={{3,7},{11,15},{19,23},{27,31}} | collective-permute-start | bytes 614408 | tf_op jit(solution)/shard_map/ppermute | solution.py:208
  730.0 27.2 %collective-permute-start.96 = (bf16[400,256]{1,0:T(8,128)(2,1)}, bf16[400,256]{1,0:T(8,128)(2,1)S(1)}, u32[]{:S(2)}, u32[]{:S(2)}) collective-permute-start(bf16[400,256]{1,0:T(8,128)(2,1)} %get-tuple-element.120), channel_id=1, source_target_pairs={{3,3},{11,11},{19,19},{27,27}} | collective-permute-start | bytes 614408 | tf_op jit(solution)/shard_map/ppermute | solution.py:208
  733.6 23.6 %collective-permute-start.95 = (bf16[400,256]{1,0:T(8,128)(2,1)}, bf16[400,256]{1,0:T(8,128)(2,1)S(1)}, u32[]{:S(2)}, u32[]{:S(2)}) collective-permute-start(bf16[400,256]{1,0:T(8,128)(2,1)} %get-tuple-element.121), channel_id=1, source_target_pairs={{2,1},{5,5},{1,6},{4,2},{6,7},{0,3},{10,9},{13,13},{9,14},{12,10},... | collective-permute-start | bytes 614408 | tf_op jit(solution)/shard_map/ppermute | solution.py:208
  741.4 21.2 %collective-permute-start.101 = (bf16[1,200,800]{2,1,0:T(8,128)(2,1)S(1)}, bf16[1,200,800]{2,1,0:T(8,128)(2,1)S(1)}, u32[]{:S(2)}, u32[]{:S(2)}) collective-permute-start(bf16[1,200,800]{2,1,0:T(8,128)(2,1)S(1)} %fusion.117), channel_id=1, source_target_pairs={{0,4},{1,5},{2,6},{3,7},{4,0},{5,1},{6,2},{7,3},{8,12},{9,13},{10,... | collective-permute-start | bytes 960008 | tf_op jit(solution)/shard_map/ppermute | solution.py:58
  (181 other events, 2137.2 us)

commit v2 on v0

v2 whole, which is shorter than its diff:
```python
import functools
import math
import random

import jax
import jax.numpy as jnp
import numpy as np
from jax import lax
from jax.experimental import pallas as pl
from jax.experimental.pallas import tpu as pltpu
from jax.sharding import PartitionSpec as P

HEAD = 64
EPSILON = 1e-05
NEGATIVE = -1e30
GELU_COEF = 0.7978845608028654
LOW = jnp.bfloat16
FULL = jnp.float32
VMEM_BYTES = 56 * 2**20


def norm_parts(values):
    center = values - jnp.mean(values, axis=-1, keepdims=True)
    rate = lax.rsqrt(jnp.mean(center * center, axis=-1, keepdims=True) + EPSILON)
    return center * rate, rate


def norm_back(grad, scaled, rate, gain):
    inner = grad * gain
    return rate * (
        inner
        - jnp.mean(inner, axis=-1, keepdims=True)
        - scaled * jnp.mean(inner * scaled, axis=-1, keepdims=True)
    )


def gelu_parts(values):
    square = values * values
    bent = jnp.tanh(GELU_COEF * values * (1.0 + 0.044715 * square))
    slope = 0.5 * (1.0 + bent) + 0.5 * values * (1.0 - bent * bent) * GELU_COEF * (
        1.0 + 3.0 * 0.044715 * square
    )
    return 0.5 * values * (1.0 + bent), slope


def dot(left, right):
    return jnp.dot(left, right, preferred_element_type=FULL)


def dot_t(left, right):
    return lax.dot_general(left, right, (((1,), (1,)), ((), ())), preferred_element_type=FULL)


def t_dot(left, right):
    return lax.dot_general(left, right, (((0,), (0,)), ((), ())), preferred_element_type=FULL)


def swap(values, axis, bit):
    count = lax.axis_size(axis)
    return lax.ppermute(values, axis, [(i, i ^ bit) for i in range(count)])


def pick(values, places, count):
    return jnp.stack([lax.dynamic_index_in_dim(values, places[i], keepdims=False) for i in range(count)])


def ordered(flag, own, got):
    return jnp.where(flag == 0, own, got), jnp.where(flag == 0, got, own)


def joined(flag, own, got, axis):
    return jnp.concatenate(ordered(flag, own, got), axis)


def after(value, *first):
    return lax.optimization_barrier((value, *first))[0]


def ring_order(count):
    return list(range(0, count, 2)) + list(range(count - 1, 0, -2))


def shift(values, offset):
    order = ring_order(lax.axis_size("ctx"))
    count = len(order)
    return lax.ppermute(
        values, "ctx", [(order[i], order[(i + offset) % count]) for i in range(count)]
    )


def ring_gather(values, riders=()):
    count = lax.axis_size("ctx")
    half, rows = count // 2, values.shape[0] // 2
    ahead = behind = values
    riders = list(riders)
    pieces = [values] + [None] * (count - 1)
    for k in range(1, half + 1):
        rode = riders.pop(0)(lambda x, *more: after(x, ahead, behind, *more)) if riders else ()
        if k == half:
            pieces[half] = (shift(ahead[:rows], 1), shift(behind[rows:], -1))
            break
        ahead, behind = shift(ahead, 1), shift(behind, -1)
        pieces[count - k], pieces[k] = ahead, behind
        if rode:
            ahead, behind, *_ = lax.optimization_barrier((ahead, behind, *rode))
    return pieces[:half] + list(pieces[half]) + pieces[half + 1 :]


def ring_sum(held, far, riders=()):
    count = lax.axis_size("ctx")
    half, rows = count // 2, far.shape[0] // 2
    riders = list(riders)
    up, down = far[:rows], far[rows:]
    for k in range(half - 1, -1, -1):
        rode = riders.pop(0)(lambda x, *more: after(x, up, down, *more)) if riders else ()
        low_up, low_down = up.astype(LOW), down.astype(LOW)
        up, down = shift(low_up, 1).astype(FULL), shift(low_down, -1).astype(FULL)
        if k == half - 1:
            near, back = held[k], held[count - k]
            up = jnp.concatenate([near[:rows] + up, near[rows:]])
            down = jnp.concatenate([back[:rows], back[rows:] + down])
        elif k:
            up, down = held[k] + up, held[count - k] + down
        if rode:
            up, down, *_ = lax.optimization_barrier((up, down, *rode))
    return held[0] + up + down


def sum_over(values, axis):
    bit = 1
    while bit < lax.axis_size(axis):
        values = values + swap(values, axis, bit)
        bit *= 2
    return values


def seq_parts(shard):
    other = swap(shard, "seq", 2)
    pair = jnp.stack([shard, other])
    return pair, swap(pair, "seq", 1)


def seq_columns(tokens, core):
    part = tokens.shape[1] // 4
    blocks = [tokens[:, i * part : (i + 1) * part] for i in range(4)]
    return ordered(
        core, jnp.concatenate([blocks[0], blocks[2]], 1), jnp.concatenate([blocks[1], blocks[3]], 1)
    )


def seq_halves(held, got, row):
    half = held.shape[-2] // 2
    held = held + got.astype(FULL)
    keep, send = ordered(row, held[..., :half, :], held[..., half:, :])
    return keep, send.astype(LOW)


def head_plan(count, width):
    heads = width // HEAD
    group = -(-heads // count) * HEAD
    shard = 3 * width // count
    small = min(group, 128)
    edges = []
    for to in range(count):
        for part in range(3):
            low = part * width + to * group
            high = min(part * width + (to + 1) * group, (part + 1) * width)
            for come in range(count):
                a, b = max(low, come * shard), min(high, (come + 1) * shard)
                if a < b:
                    edges.append((come, to, a - come * shard, part * group + a - low, b - a))
    draw = random.Random(0)
    best, least = None, None
    for _ in range(300):
        draw.shuffle(edges)
        rounds = []
        for edge in sorted(edges, key=lambda e: e[4] <= small):
            for known in rounds:
                if all(edge[0] != e[0] and edge[1] != e[1] for e in known):
                    known.append(edge)
                    break
            else:
                rounds.append([edge])
        cost = sum(200 + (small if all(e[4] <= small for e in r) else group) for r in rounds)
        if least is None or cost < least:
            best, least = [list(r) for r in rounds], cost
    pairs, starts, sizes, total = [], [], [], 0
    for known in best:
        pairs.append([(e[0], e[1]) for e in known])
        starts.append(total)
        sizes.append(small if all(e[4] <= small for e in known) else group)
        total += sizes[-1]
    sent = np.full((count, total), -1, np.int32)
    kept = np.full((count, 3 * group), -1, np.int32)
    for known, begin in zip(best, starts, strict=True):
        for come, to, start, place, size in known:
            sent[come, begin : begin + size] = np.arange(start, start + size)
            kept[to, place : place + size] = begin + np.arange(size)
    moves = list(zip(pairs, starts, sizes, strict=True))
    return group, moves, sent, kept


def picker(places, size):
    return (lax.broadcasted_iota(jnp.int32, (size, places.shape[0]), 0) == places[None, :]).astype(LOW)


def move(values, pairs):
    return values if all(a == b for a, b in pairs) else lax.ppermute(values, "ctx", pairs)


def take_rounds(sent, moves):
    return [move(sent[:, start : start + size], pairs) for pairs, start, size in moves]


def from_heads(sent, moves, pick_sent):
    got = [
        move(sent[:, start : start + size], [(b, a) for a, b in pairs]) for pairs, start, size in moves
    ]
    return dot_t(jnp.concatenate(got, axis=1), pick_sent)


COST_US = {
    "attend": 15,
    "out": 8,
    "hidden_grad": 9,
    "hidden": 20,
    "branch": 8,
    "out_back": 12,
    "unit_other": 8,
    "unit_mine": 10,
    "qkv_other": 5,
    "qkv_mine": 6,
    "attend_back": 20,
    "project_back": 6,
}


def call(kernel, outs, args, scalars, name, flops, scratch=()):
    spec = [pl.BlockSpec(memory_space=pltpu.SMEM)] * len(scalars)
    spec += [pl.BlockSpec(memory_space=pltpu.VMEM)] * len(args)
    moved = sum(math.prod(a.shape) * a.dtype.itemsize for a in args)
    moved += sum(math.prod(o[0]) * jnp.dtype(o[1]).itemsize for o in outs)
    return pl.pallas_call(
        kernel,
        in_specs=spec,
        out_specs=[pl.BlockSpec(memory_space=pltpu.VMEM)] * len(outs),
        out_shape=[jax.ShapeDtypeStruct(s, d) for s, d in outs],
        scratch_shapes=list(scratch),
        compiler_params=pltpu.CompilerParams(vmem_limit_bytes=VMEM_BYTES),
        cost_estimate=pl.CostEstimate(flops=1000, bytes_accessed=int(COST_US[name] * 3e6), transcendentals=0),
        name=name,
    )(*scalars, *args)


def put_tokens(member_ref, pieces, put, rows, count):
    half, middle = count // 2, rows // 2
    at = 0
    for k in range(count):
        member = member_ref[k]
        if k == half:
            put(member, 0, pieces[at][...])
            put(member, 1, pieces[at + 1][...])
            at += 2
        else:
            put(member, 0, pieces[at][:middle, :])
            put(member, 1, pieces[at][middle:, :])
            at += 1


def put_shards(place_ref, pair_ref, peer_ref, out_ref):
    seq = place_ref[0]
    height = out_ref.shape[0] // 4
    for k in range(4):
        source = pair_ref if k % 2 == 0 else peer_ref
        start = pl.multiple_of((seq ^ k) * height, 16)
        out_ref[pl.ds(start, height), :] = source[k // 2]


def causal(step, start, keys):
    query = lax.broadcasted_iota(jnp.int32, (step, keys), 0) + start
    return lax.broadcasted_iota(jnp.int32, (step, keys), 1) <= query


def each_step(tokens, run):
    if tokens <= 1024:
        step = min(256, tokens)
        for start in range(0, tokens, step):
            run(start, slice(start, start + step), step, start + step)
    else:
        step = 128

        @pl.loop(0, tokens // step)
        def _(i):
            start = pl.multiple_of(i * step, step)
            run(start, pl.ds(start, step), step, tokens)


def attend_kernel(
    n_pieces, heads, member_ref, place_ref, pair_of_ref, who_ref, pair_ref, peer_ref, shift_ref, *rest
):
    pieces = rest[:n_pieces]
    x_ref, w_ref, qkv_ref, full_ref, low_ref, lse_ref = rest[n_pieces:]
    count, rows, group = low_ref.shape
    tokens, block = count * rows, rows // 2
    put_shards(place_ref, pair_ref, peer_ref, w_ref)

    def put(member, half, values):
        pair = pair_of_ref[member]
        at = (2 * count - 1 - pair if half else pair) * block
        x_ref[pl.ds(pl.multiple_of(at, block), block), :] = values

    put_tokens(member_ref, pieces, put, rows, count)

    def project(start, part, step, keys):
        qkv_ref[part, :] = (dot(x_ref[part, :], w_ref[...]) + shift_ref[...]).astype(LOW)

    def some(start, part, step, keys):
        allowed = causal(step, start, keys)
        for h in range(heads):
            a, b = h * HEAD, (h + 1) * HEAD
            query = (qkv_ref[part, a:b] * (1.0 / math.sqrt(HEAD))).astype(LOW)
            score = jnp.where(allowed, dot_t(query, qkv_ref[:keys, group + a : group + b]), NEGATIVE)
            top = jnp.max(score, axis=1, keepdims=True)
            weight = jnp.exp(score - top)
            total = jnp.sum(weight, axis=1, keepdims=True)
            result = dot(weight.astype(LOW), qkv_ref[:keys, 2 * group + a : 2 * group + b]) / total
            full_ref[part, a:b] = result
            lse_ref[part, h : h + 1] = top + jnp.log(total)

    each_step(tokens, project)
    each_step(tokens, some)
    for j in range(2 * count):
        half = j // count * block
        low_ref[who_ref[j], half : half + block, :] = full_ref[j * block : (j + 1) * block, :].astype(LOW)


def attend_back_kernel(
    heads,
    who_ref,
    far_ref,
    qkv_ref,
    w_ref,
    full_ref,
    lse_ref,
    come_ref,
    out_ref,
    sum_ref,
    low_ref,
    dk_ref,
    dv_ref,
    grad_ref,
):
    count, rows, group = come_ref.shape
    tokens, block = count * rows, rows // 2
    scale = 1.0 / math.sqrt(HEAD)
    dk_ref[...] = jnp.zeros_like(dk_ref)
    dv_ref[...] = jnp.zeros_like(dv_ref)
    for j in range(2 * count):
        half = j // count * block
        grad_ref[j * block : (j + 1) * block, :] = come_ref[who_ref[j], half : half + block, :]

    def some(start, part, step, keys):
        allowed = causal(step, start, keys)
        for h in range(heads):
            a, b = h * HEAD, (h + 1) * HEAD
            query = (qkv_ref[part, a:b] * scale).astype(LOW)
            key = qkv_ref[:keys, group + a : group + b]
            value = qkv_ref[:keys, 2 * group + a : 2 * group + b]
            grad = grad_ref[part, a:b]
            delta = jnp.sum(grad.astype(FULL) * full_ref[part, a:b], axis=1, keepdims=True)
            score = dot_t(query, key)
            prob = jnp.where(allowed, jnp.exp(score - lse_ref[part, h : h + 1]), 0.0)
            score_grad = (prob * (dot_t(grad, value) - delta)).astype(LOW)
            out_ref[part, a:b] = (dot(score_grad, key) * scale).astype(LOW)
            dk_ref[:keys, a:b] += t_dot(score_grad, query)
            dv_ref[:keys, a:b] += t_dot(prob.astype(LOW), grad)

    each_step(tokens, some)
    out_ref[:, group : 2 * group] = dk_ref[...].astype(LOW)
    out_ref[:, 2 * group :] = dv_ref[...].astype(LOW)
    sum_ref[...] = jnp.sum(out_ref[...].astype(FULL), axis=0, keepdims=True)
    for half in range(2):
        start = pl.multiple_of(far_ref[half] * block, block)
        low_ref[half * block : (half + 1) * block, :] = dot_t(out_ref[pl.ds(start, block), :], w_ref[...]).astype(LOW)


def project_back_kernel(far_ref, grad_ref, w_ref, x_ref, norm_ref, gain_ref):
    count, rows, width = norm_ref.shape
    tokens, block = count * rows, rows // 2
    gain_ref[...] = jnp.zeros_like(gain_ref)
    step = min(256, tokens)
    for start in range(0, tokens, step):
        part = slice(start, start + step)
        total = dot_t(grad_ref[part, :], w_ref[...])
        gain_ref[0:1, :] += jnp.sum(total * x_ref[part, :].astype(FULL), axis=0, keepdims=True)
        gain_ref[1:2, :] += jnp.sum(total, axis=0, keepdims=True)
        for j in range(start // block, (start + step) // block):
            half, at = j // count * block, j * block - start
            norm_ref[far_ref[j], half : half + block, :] = total[at : at + block, :]


def put_ring(offset, count, full_ref, low_ref, start, values):
    end = start + values.shape[0]

    @pl.when(offset == count // 2)
    def _():
        low_ref[start:end, :] = values.astype(LOW)

    @pl.when(offset != count // 2)
    def _():
        full_ref[offset, start:end, :] = values


def out_kernel(back_ref, input_ref, bias_ref, gain_ref, shift_ref, w_ref, mid_ref, low_ref, scaled_ref, rate_ref, attn_ref, wide_ref):
    count, rows, group = back_ref.shape
    width = mid_ref.shape[1]
    for d in range(count):
        wide_ref[:, d * group : (d + 1) * group] = back_ref[d]
    attn_ref[...] = wide_ref[:, :width]
    quarter, size = w_ref.shape[3], w_ref.shape[2]
    mid_ref[...] = input_ref[...].astype(FULL) + bias_ref[...]
    parts = [attn_ref[:, s * quarter : (s + 1) * quarter] for s in range(4)]
    for d in range(count):
        total = dot_t(parts[0], w_ref[0, d])
        for s in range(1, 4):
            total = total + dot_t(parts[s], w_ref[s, d])
        mid_ref[:, d * size : (d + 1) * size] += total
    scaled, rate = norm_parts(mid_ref[...])
    scaled_ref[...] = scaled
    rate_ref[...] = rate
    low_ref[...] = (scaled * gain_ref[...] + shift_ref[...]).astype(LOW)


def out_back_kernel(
    core_ref,
    sum_ref,
    cot_ref,
    scaled_ref,
    rate_ref,
    gain_ref,
    w_ref,
    attn_ref,
    mid_ref,
    low_ref,
    grad_ref,
    line_ref,
    mine_ref,
    other_ref,
    wide_ref,
    part_ref,
):
    count, rows, group = grad_ref.shape
    width = mid_ref.shape[1]
    cot = cot_ref[...].astype(FULL)
    total, scaled = sum_ref[...], scaled_ref[...]
    mid_ref[...] = cot + norm_back(total, scaled, rate_ref[...], gain_ref[...])
    low_ref[...] = mid_ref[...].astype(LOW)
    line_ref[0:1, :] = jnp.sum(low_ref[...].astype(FULL), axis=0, keepdims=True)
    line_ref[1:2, :] = jnp.sum(total * scaled, axis=0, keepdims=True)
    line_ref[2:3, :] = jnp.sum(total, axis=0, keepdims=True)
    line_ref[3:4, :] = jnp.sum(cot, axis=0, keepdims=True)
    quarter, size = w_ref.shape[3], w_ref.shape[2]
    wide_ref[:, width:] = jnp.zeros((rows, count * group - width), LOW)
    parts = [low_ref[:, d * size : (d + 1) * size] for d in range(count)]
    for s in range(4):
        part_ref[s] = attn_ref[:, s * quarter : (s + 1) * quarter]
        total = dot(parts[0], w_ref[s, 0])
        for d in range(1, count):
            total = total + dot(parts[d], w_ref[s, d])
        wide_ref[:, s * quarter : (s + 1) * quarter] = total.astype(LOW)
    core = core_ref[0]
    for d in range(count):
        grad_ref[d] = wide_ref[:, d * group : (d + 1) * group]
        for y in range(2):
            lanes = slice(y * quarter, (y + 1) * quarter)
            mine_ref[d, :, lanes] = t_dot(parts[d], part_ref[2 * y + core])
            other_ref[d, :, lanes] = t_dot(parts[d], part_ref[2 * y + 1 - core]).astype(LOW)


def seq_dots(core, left_ref, right, put):
    part = left_ref.shape[1] // 4
    for some in range(2):

        @pl.when(core == some)
        def _(some=some):
            for y in range(2):
                at = (2 * y + some) * part
                put(y, t_dot(left_ref[:, at : at + part], right))


def other_kernel(core_ref, *rest):
    *pairs, out_ref = rest

    for m in range(len(pairs) // 2):

        def put(y, total, m=m):
            out_ref[m, y] = total.astype(LOW)

        seq_dots(1 - core_ref[0], pairs[2 * m], pairs[2 * m + 1][...], put)


def mine_kernel(core_ref, row_ref, got_ref, *rest):
    *pairs, keep_ref, send_ref = rest

    for m in range(len(pairs) // 2):

        def put(y, total, m=m):
            total = total + got_ref[m, y].astype(FULL)

            @pl.when(row_ref[0] == y)
            def _():
                keep_ref[m] = total

            @pl.when(row_ref[0] != y)
            def _():
                send_ref[m] = total.astype(LOW)

        seq_dots(core_ref[0], pairs[2 * m], pairs[2 * m + 1][...], put)


def hidden_grad_kernel(place_ref, cot_ref, pair_ref, peer_ref, w_ref, grad_ref):
    put_shards(place_ref, pair_ref, peer_ref, w_ref)
    step = min(512, cot_ref.shape[0])
    for start in range(0, cot_ref.shape[0], step):
        grad_ref[start : start + step, :] = dot(cot_ref[start : start + step, :], w_ref[...])


def hidden_kernel(
    n_pieces, member_ref, offset_ref, place_ref, pair_ref, peer_ref, bias_ref, grad_ref, *rest
):
    pieces = rest[:n_pieces]
    x_ref, value_ref, slope_ref, sum_ref, far_ref, unit_ref, w_ref = rest[n_pieces:]
    count, rows, _ = sum_ref.shape
    middle = rows // 2
    put_shards(place_ref, pair_ref, peer_ref, w_ref)

    def put(member, half, values):
        at = pl.multiple_of(member * rows + half * middle, middle)
        x_ref[pl.ds(at, middle), :] = values

    put_tokens(member_ref, pieces, put, rows, count)
    unit_ref[...] = jnp.zeros_like(unit_ref)
    step = min(512, count * rows)
    for start in range(0, count * rows, step):
        part = slice(start, start + step)
        value, slope = gelu_parts(dot(x_ref[part, :], w_ref[...]) + bias_ref[...])
        value_ref[part, :] = value.astype(LOW)
        low = (grad_ref[part, :] * slope).astype(LOW)
        slope_ref[part, :] = low
        unit_ref[...] += jnp.sum(low.astype(FULL), axis=0, keepdims=True)
        total = dot_t(low, w_ref[...])
        for m in range(start // rows, (start + step) // rows):
            at = m * rows - start
            put_ring(offset_ref[m], count, sum_ref, far_ref, 0, total[at : at + rows, :])


def branch_kernel(value_ref, w_ref, out_ref):
    step = min(512, value_ref.shape[0])
    for start in range(0, value_ref.shape[0], step):
        part = slice(start, start + step)
        out_ref[part, :] = dot_t(value_ref[part, :], w_ref[...]).astype(LOW)


def body(
    block_input,
    out_cot,
    pair_of,
    ln1_gain,
    ln1_bias,
    qkv_weight,
    qv_bias,
    out_weight,
    out_bias,
    ln2_gain,
    ln2_bias,
    fc_weight,
    fc_bias,
    proj_weight,
    proj_bias,
):
    rows, width = block_input.shape[2], block_input.shape[3]
    count = lax.axis_size("ctx")
    tokens = count * rows
    fused = count <= 8
    seq, ctx = lax.axis_index("seq"), lax.axis_index("ctx")
    core, row = seq % 2, seq // 2
    order = np.array(ring_order(count), np.int32)
    rank = np.argsort(order)
    member = jnp.asarray(np.stack([np.roll(order, -i) for i in rank]).astype(np.int32))[ctx]
    offset = jnp.asarray(((rank[None, :] - rank[:, None]) % count).astype(np.int32))[ctx]
    place, core_at, row_at = seq[None], core[None], row[None]
    ranks = jnp.arange(count, dtype=jnp.int32)
    who = jnp.sum(jnp.where(pair_of[None, :] == ranks[:, None], ranks[None, :], 0), axis=1)
    who = jnp.concatenate([who, who[::-1]]).astype(jnp.int32)
    far_of = offset[who]
    input_low = block_input.reshape(rows, width)
    inputs = input_low.astype(FULL)
    cot_low = out_cot.reshape(rows, width)

    group, moves, sent, kept = head_plan(count, width)
    heads = group // HEAD
    pick_sent = picker(jnp.asarray(sent)[ctx], qkv_weight.shape[1])
    pick_kept = picker(jnp.asarray(kept)[ctx], sent.shape[1])
    scaled_one, rate_one = norm_parts(inputs)
    normed_one = (scaled_one * ln1_gain + ln1_bias).astype(LOW)
    units = fc_weight.shape[1]
    held = {}

    with jax.named_scope("to_heads"):
        sent_heads = dot(qkv_weight, pick_sent).astype(LOW)
    first = len(moves) // 2

    def ride_first(hold):
        with jax.named_scope("to_heads"):
            held["first"] = take_rounds(sent_heads, moves[:first])
        return held["first"]

    def ride_second(hold):
        with jax.named_scope("to_heads"):
            held["second"] = take_rounds(hold(sent_heads), moves[first:])
        return held["second"]

    def ride_row_parts(hold):
        held["out"] = lax.all_gather(jnp.transpose(hold(out_weight)), ("seq", "ctx"), axis=0)
        with jax.named_scope("qkv_parts"):
            pieces = jnp.concatenate(held["first"] + held["second"], axis=1)
            own = dot(hold(pieces), pick_kept).astype(LOW)
            held["pair"] = jnp.stack([own, swap(own, "seq", 2)])
        return ()

    with jax.named_scope("gather_one"):
        gathered = ring_gather(normed_one, [ride_first, ride_second, ride_row_parts])
    with jax.named_scope("qkv_parts"):
        qkv_pair = held["pair"]
        qkv_peer = swap(qkv_pair, "seq", 1)
    out_t = held["out"].reshape(4, count, out_weight.shape[1], out_weight.shape[0])
    bias_rows = jnp.pad(qv_bias, ((0, 0), (0, count * group - width)))
    bias_mine = lax.dynamic_slice_in_dim(bias_rows, ctx * group, group, 1)
    qkv_shift = jnp.concatenate([bias_mine[:1], jnp.zeros((1, group), FULL), bias_mine[1:]], axis=1)
    with jax.named_scope("unit_parts"):
        proj_own = after(jnp.transpose(proj_weight), qkv_peer)
        proj_pair = jnp.stack([proj_own, swap(proj_own, "seq", 2)])

    one_tokens, qkv_cols, qkv, attn_full, attn_part, lse = call(
        functools.partial(attend_kernel, len(gathered), heads),
        [
            ((tokens, width), LOW),
            ((width, 3 * group), LOW),
            ((tokens, 3 * group), LOW),
            ((tokens, group), FULL),
            ((count, rows, group), LOW),
            ((tokens, heads), FULL),
        ],
        [qkv_pair, qkv_peer, qkv_shift, *gathered],
        [member, place, pair_of, who],
        "attend",
        2 * tokens * width * 3 * group + 16 * tokens * tokens * group,
    )
    attn_part, proj_pair = lax.optimization_barrier((attn_part, proj_pair))
    with jax.named_scope("unit_parts"):
        fc_own = after(fc_weight, attn_part)
        fc_pair = jnp.stack([fc_own, swap(fc_own, "seq", 2)])
    cots = lax.all_gather(after(cot_low, qkv_peer), "ctx", axis=0, tiled=True)

    back = lax.all_to_all(attn_part, "ctx", 0, 0, tiled=True)
    back, proj_pair, fc_pair = lax.optimization_barrier((back, proj_pair, fc_pair))
    with jax.named_scope("unit_parts"):
        proj_peer = swap(proj_pair, "seq", 1)
        fc_peer = swap(fc_pair, "seq", 1)
    middle, normed_two, scaled_two, rate_two, attn_low = call(
        out_kernel,
        [
            ((rows, width), FULL),
            ((rows, width), LOW),
            ((rows, width), FULL),
            ((rows, 1), FULL),
            ((rows, width), LOW),
        ],
        [back, input_low, out_bias[None], ln2_gain[None], ln2_bias[None], out_t],
        [],
        "out",
        2 * rows * width * width,
        [pltpu.VMEM((rows, count * group), LOW)],
    )

    proj_cols, hidden_grad = call(
        hidden_grad_kernel,
        [((width, units), LOW), ((tokens, units), FULL)],
        [cots, proj_pair, proj_peer],
        [place],
        "hidden_grad",
        2 * tokens * width * units,
    )
    with jax.named_scope("gather_two"):
        two_gathered = ring_gather(normed_two)
    bias_units = lax.dynamic_slice_in_dim(fc_bias, ctx * units, units)[None]
    if fused:
        two_tokens, hidden, hidden_pre_grad, two_parts, two_far, units_grad = call(
            functools.partial(hidden_kernel, len(two_gathered)),
            [
                ((tokens, width), LOW),
                ((tokens, units), LOW),
                ((tokens, units), LOW),
                ((count, rows, width), FULL),
                ((rows, width), LOW),
                ((1, units), FULL),
            ],
            [fc_pair, fc_peer, bias_units, hidden_grad, *two_gathered],
            [member, offset, place],
            "hidden",
            4 * tokens * width * units,
            [pltpu.VMEM((width, units), LOW)],
        )
    else:
        far = count // 2
        pieces = two_gathered[:far] + [jnp.concatenate(two_gathered[far : far + 2])] + two_gathered[far + 2 :]
        two_tokens = pick(jnp.stack(pieces), offset, count).reshape(tokens, width)
        shards = jnp.stack([fc_pair[0], fc_peer[0], fc_pair[1], fc_peer[1]])
        fc_cols = pick(shards, seq ^ jnp.arange(4), 4).reshape(width, units)
        value, slope = gelu_parts(dot(two_tokens, fc_cols) + bias_units)
        hidden = value.astype(LOW)
        hidden_pre_grad = (hidden_grad * slope).astype(LOW)
        two_parts = pick(dot_t(hidden_pre_grad, fc_cols).reshape(count, rows, width), member, count)
        two_far = two_parts[far].astype(LOW)
        units_grad = jnp.sum(hidden_pre_grad.astype(FULL), axis=0)
    def ride_branch(hold):
        (held["branch"],) = call(
            branch_kernel, [((tokens, width), LOW)], [hidden, proj_cols], [], "branch", 2 * tokens * width * units
        )
        return (held["branch"],)

    def ride_other(hold):
        with jax.named_scope("unit_sum"):
            (other,) = call(
                other_kernel,
                [((2, 2, width // 4, units), LOW)],
                [two_tokens, hidden_pre_grad, cots, hidden],
                [hold(core_at)],
                "unit_other",
                0,
            )
            held["peer"] = swap(other, "seq", 1)
        return (other,)

    with jax.named_scope("sum_two"):
        normed_two_grad = ring_sum(two_parts, two_far, [ride_branch, ride_other])
    branch_two = lax.psum_scatter(held["branch"], "ctx", scatter_dimension=0, tiled=True)
    block_output = (middle + branch_two.astype(FULL) + proj_bias).astype(LOW).reshape(block_input.shape)

    size, quarter = out_t.shape[2], out_t.shape[3]
    middle_grad, branch_low, attn_grad, lines, whole_out, other = call(
        out_back_kernel,
        [
            ((rows, width), FULL),
            ((rows, width), LOW),
            ((count, rows, group), LOW),
            ((4, width), FULL),
            ((count, size, 2 * quarter), FULL),
            ((count, size, 2 * quarter), LOW),
        ],
        [normed_two_grad, cot_low, scaled_two, rate_two, ln2_gain[None], out_t, attn_low],
        [core_at],
        "out_back",
        2 * rows * width * width,
        [pltpu.VMEM((rows, count * group), LOW), pltpu.VMEM((4, rows, quarter), LOW)],
    )
    grad_part = lax.all_to_all(attn_grad, "ctx", 0, 0, tiled=True)
    with jax.named_scope("unit_sum"):
        keep_units, send_units = call(
            mine_kernel,
            [((2, width // 4, units), FULL), ((2, width // 4, units), LOW)],
            [held["peer"], two_tokens, hidden_pre_grad, cots, hidden],
            [after(core_at, branch_low), row_at],
            "unit_mine",
            0,
        )
    with jax.named_scope("out_sum"):
        got_core_out = swap(other, "seq", 1)
        grad_part, got_core_out, block_output, send_units = lax.optimization_barrier(
            (grad_part, got_core_out, block_output, send_units)
        )
        with jax.named_scope("unit_sum"):
            got_units = swap(send_units, "seq", 2)
        half_sum = (whole_out + got_core_out.astype(FULL)).astype(LOW)
        out_sum = lax.psum_scatter(half_sum, "ctx", scatter_dimension=0)

    far_pair = pair_of[member[count // 2]]
    qkv_grad, cols_sum, one_far = call(
        functools.partial(attend_back_kernel, heads),
        [((tokens, 3 * group), LOW), ((1, 3 * group), FULL), ((rows, width), LOW)],
        [qkv, qkv_cols, attn_full, lse, grad_part],
        [who, jnp.stack([far_pair, 2 * count - 1 - far_pair])],
        "attend_back",
        0,
        [pltpu.VMEM((tokens, group), FULL)] * 2 + [pltpu.VMEM((tokens, group), LOW)],
    )
    if fused:
        one_parts, one_lines = call(
            project_back_kernel,
            [((count, rows, width), FULL), ((2, width), FULL)],
            [qkv_grad, qkv_cols, one_tokens],
            [far_of],
            "project_back",
            0,
        )
    else:
        parts = dot_t(qkv_grad, qkv_cols)
        one_lines = jnp.stack([jnp.sum(parts * one_tokens.astype(FULL), axis=0), jnp.sum(parts, axis=0)])
        parts = parts.reshape(2 * count, rows // 2, width)
        pairs = pair_of[member]
        one_parts = jnp.concatenate([pick(parts, pairs, count), pick(parts, 2 * count - 1 - pairs, count)], axis=1)

    shift_one = one_lines[1]
    gain_one = (one_lines[0] - ln1_bias * shift_one) / ln1_gain
    qv_sums = jnp.concatenate([cols_sum[:, :group], cols_sum[:, 2 * group :]])
    qv_sums = lax.dynamic_update_slice(
        jnp.zeros((2, count * group), FULL), qv_sums, (0, ctx * group)
    )[:, :width]
    unit_sums = lax.dynamic_update_slice(
        jnp.zeros((count * units,), FULL), units_grad.reshape(-1), (ctx * units,)
    )
    flat = [gain_one, shift_one, qv_sums.reshape(-1), lines.reshape(-1), unit_sums]
    flat = jnp.concatenate(flat)

    def ride_core(hold):
        with jax.named_scope("qkv_sum"):
            (other,) = call(
                other_kernel,
                [((1, 2, width // 4, 3 * group), LOW)],
                [one_tokens, qkv_grad],
                [hold(core_at)],
                "qkv_other",
                0,
            )
            held["core"] = swap(other, "seq", 1)
        return (held["core"],)

    def ride_row(hold):
        with jax.named_scope("qkv_sum"):
            held["qkv"], send = call(
                mine_kernel,
                [((1, width // 4, 3 * group), FULL), ((1, width // 4, 3 * group), LOW)],
                [held["core"], one_tokens, qkv_grad],
                [hold(core_at), row_at],
                "qkv_mine",
                0,
            )
            held["row"] = swap(send, "seq", 2)
        with jax.named_scope("sum_vectors"):
            held["flat"] = sum_over(hold(flat), "seq")
        return (send, held["flat"])

    def ride_heads(hold):
        with jax.named_scope("from_heads"):
            whole = (held["qkv"] + hold(held["row"]).astype(FULL))[0]
            sent = dot_t(whole.astype(LOW), pick_kept).astype(LOW)
            held["sent"] = sent
        with jax.named_scope("sum_vectors"):
            held["flat"] = sum_over(hold(held["flat"]), "ctx")
            got = hold(got_units).astype(FULL)
            held["fc"] = keep_units[0] + got[0]
            held["proj"] = jnp.transpose(keep_units[1] + got[1])
        return (out_sum, held["fc"], held["proj"])

    with jax.named_scope("sum_one"):
        normed_one_grad = ring_sum(one_parts, one_far, [lambda hold: (), ride_core, ride_row, ride_heads])
    with jax.named_scope("out_sum"):
        keep, send = ordered(row, out_sum[:, :quarter], out_sum[:, quarter:])
        out_weight_grad = jnp.transpose(keep.astype(FULL) + swap(send, "seq", 2).astype(FULL))
    middle_part = norm_back(normed_one_grad, scaled_one, rate_one, ln1_gain)
    input_grad = (middle_grad + middle_part).astype(LOW).reshape(block_input.shape)
    with jax.named_scope("from_heads"):
        qkv_weight_grad = from_heads(held["sent"], moves, pick_sent)

    fc_weight_grad, proj_weight_grad = held["fc"], held["proj"]
    flat = held["flat"]
    vectors = flat[: 8 * width].reshape(8, width)
    return (
        block_output,
        input_grad,
        vectors[0],
        vectors[1],
        qkv_weight_grad,
        vectors[2:4],
        out_weight_grad,
        vectors[4],
        vectors[5],
        vectors[6],
        fc_weight_grad,
        flat[8 * width :],
        proj_weight_grad,
        vectors[7],
    )


def solution(mesh):
    rows = P("seq", "ctx", None, None)
    cols = P("seq", "ctx")
    flip = P("ctx", "seq")
    one = P()
    return jax.shard_map(
        body,
        mesh=mesh,
        in_specs=(rows, rows, one, one, one, cols, one, cols, one, one, one, cols, one, flip, one),
        out_specs=(rows, rows, one, one, cols, one, cols, one, one, one, cols, one, flip, one),
        check_vma=False,
    )
```

time: 3760 us -> 532 us (0.14)
  waiting for transfers between devices: 2430 us -> 190 us
  local copies, waits for them, and re-layouts: 969 us -> 27.8 us
  matrix products: 230 us -> 5.66 us
  Pallas kernels: 0 us -> 139 us
  starting transfers between devices: 0.95 us -> 114 us
  blocking collectives: 76.1 us -> 0 us
    unnamed x16 -> x5, waiting for transfers between devices: 1280 us -> 0.09 us
    all_gather x13 -> x2, waiting for transfers between devices: 1030 us -> 0.02 us  [the longest x1 0.02 us: ride_row_parts(): lax.all_gather(jnp.transpose(hold(out_weight)), ('seq', 'ctx'), axis=0)]
    gather x1088 -> x1, local copies, waits for them, and re-layouts: 607 us -> 1.17 us  [body(): far_of = offset[who]]
    dot_general x19 -> x4, matrix products: 230 us -> 5.66 us  [the longest x2 3.84 us: dot_t(): lax.dot_general(left, right, (((1,), (1,)), ((), ())), preferred_element_...]
    ppermute x0 -> x57, waiting for transfers between devices: none -> 190 us  [the longest x32 128 us: shift(): lax.ppermute(values, 'ctx', [(order[i], order[(i + offset) % count]) for...]
    unnamed x99 -> x111, local copies, waits for them, and re-layouts: 185 us -> 8.82 us
    concatenate x7 -> x4, local copies, waits for them, and re-layouts: 151 us -> 0.17 us  [the longest x1 0.08 us: body(): flat = jnp.concatenate(flat)]
    pallas_call x0 -> x12, Pallas kernels: none -> 139 us  [call(): pl.pallas_call(kernel, in_specs=spec, out_specs=[pl.BlockSpec(memory_spac...]
  transfers between devices with their start and end apart: 15 -> 63, of which waited for: 8 -> 28; matrix products, arithmetic and copies ran while one was open for 21% -> 10% of each run, Pallas kernels for 0% -> 17%
where the time goes in v2:
time: 532 us; the launch traced here: 526 us
  waiting for transfers between devices  190 us (36%)
  Pallas kernels  139 us (26%)
  starting transfers between devices  114 us (21%)
  other arithmetic  31.7 us (6%)
  local copies, waits for them, and re-layouts  27.8 us (5%)
  between operations  17.8 us (3%)
  matrix products  5.66 us (1%)
    pallas_call x12, Pallas kernels, call(): pl.pallas_call(kernel, in_specs=spec, out_specs=[pl.BlockSpec(memory_spac...  139 us
    ppermute x32, waiting for transfers between devices, shift(): lax.ppermute(values, 'ctx', [(order[i], order[(i + offset) % count]) for...  128 us
    ppermute x32, starting transfers between devices, shift(): lax.ppermute(values, 'ctx', [(order[i], order[(i + offset) % count]) for...  56.2 us
    ppermute x17, waiting for transfers between devices, swap(): return lax.ppermute(values, axis, [(i, i ^ bit) for i in range(count)])  42.3 us
    ppermute x8, starting transfers between devices, move(): lax.ppermute(values, 'ctx', pairs)  34.8 us
    ppermute x8, waiting for transfers between devices, move(): lax.ppermute(values, 'ctx', pairs)  19.1 us
    ppermute x17, starting transfers between devices, swap(): return lax.ppermute(values, axis, [(i, i ^ bit) for i in range(count)])  13.9 us
  transfers between devices with their start and end apart: 63, of which 28 were waited for; matrix products, arithmetic and copies ran while one was open for 10% of the time, Pallas kernels for 17%

profile of v2, /device:TPU:0, one launch (start us, length us, event | category | flops | bytes accessed | tf_op | source)
XLA Modules:
  0.0 525.9 jit_solution(11059145003319321164)
XLA Ops:
  10.0 3.1 collective-permute-start.2
  16.1 7.0 %collective-permute-start.1 = (bf16[400,256]{1,0:T(8,128)(2,1)S(1)}, bf16[400,256]{1,0:T(8,128)(2,1)S(1)}, u32[]{:S(2)}, u32[]{:S(2)}) collective-permute-start(bf16[400,256]{1,0:T(8,128)(2,1)S(1)} %get-tuple-element.234), channel_id=1, source_target_pairs={{6,3},{1,2},{5,5},{7,4},{2,0},{0,1},{14,11},{9,10},{13,13},{15,12}... | collective-permute-start | bytes 614408 | tf_op jit(solution)/shard_map/gather_one/to_heads/ppermute | solution.py:208
  23.2 6.4 %collective-permute-done = bf16[400,256]{1,0:T(8,128)(2,1)S(1)} collective-permute-done((bf16[400,256]{1,0:T(8,128)(2,1)S(1)}, bf16[400,256]{1,0:T(8,128)(2,1)S(1)}, u32[]{:S(2)}, u32[]{:S(2)}) %collective-permute-start) | collective-permute-done | bytes 204832 | tf_op jit(solution)/shard_map/gather_one/to_heads/ppermute | solution.py:208
  29.6 6.7 %collective-permute-start.6 = (bf16[128,1600]{1,0:T(8,128)(2,1)S(1)}, bf16[128,1600]{1,0:T(8,128)(2,1)}, u32[]{:S(2)}, u32[]{:S(2)}) collective-permute-start(bf16[128,1600]{1,0:T(8,128)(2,1)S(1)} %collective-permute-done.2.rest_8_), channel_id=1, source_target_pairs={{0,2},{2,4},{4,6},{6,7},{7,5},{5,3},{3,1},{1,0},{8,10},{10,12},{12... | collective-permute-start | bytes 1228808 | tf_op jit(solution)/shard_map/gather_one/ppermute | solution.py:86
  37.0 7.2 %collective-permute-start.5 = (bf16[400,128]{1,0:T(8,128)(2,1)S(1)}, bf16[400,128]{1,0:T(8,128)(2,1)S(1)}, u32[]{:S(2)}, u32[]{:S(2)}) collective-permute-start(bf16[400,128]{1,0:T(8,128)(2,1)S(1)} %slice.241), channel_id=1, source_target_pairs={{2,4},{4,5},{3,0},{5,6},{0,2},{7,3},{6,1},{10,12},{12,13},{11,8},{... | collective-permute-start | bytes 307208 | tf_op jit(solution)/shard_map/gather_one/to_heads/ppermute | solution.py:208
  44.2 8.0 %collective-permute-done.5 = bf16[400,128]{1,0:T(8,128)(2,1)S(1)} collective-permute-done((bf16[400,128]{1,0:T(8,128)(2,1)S(1)}, bf16[400,128]{1,0:T(8,128)(2,1)S(1)}, u32[]{:S(2)}, u32[]{:S(2)}) %collective-permute-start.5) | collective-permute-done | bytes 102432 | tf_op jit(solution)/shard_map/gather_one/to_heads/ppermute | solution.py:208
  56.6 12.5 %collective-permute-done.8 = bf16[400,768]{1,0:T(8,128)(2,1)S(1)} collective-permute-done((bf16[400,768]{1,0:T(8,128)(2,1)S(1)}, bf16[400,768]{1,0:T(8,128)(2,1)S(1)}, u32[]{:S(2)}, u32[]{:S(2)}) %collective-permute-start.8) | collective-permute-done | bytes 614432 | tf_op jit(solution)/shard_map/gather_one/qkv_parts/ppermute | solution.py:60
  70.4 1.8 collective-permute-done.9.peer_ref
  73.8 2.1 collective-permute-start.11
  75.8 3.5 collective-permute-start.10
  80.9 14.3 %collective-permute-done.11.rest_6_ = bf16[128,1600]{1,0:T(8,128)(2,1)S(1)} collective-permute-done((bf16[128,1600]{1,0:T(8,128)(2,1)}, bf16[128,1600]{1,0:T(8,128)(2,1)S(1)}, u32[]{:S(2)}, u32[]{:S(2)}) %collective-permute-start.11) | collective-permute-done | bytes 409632 | tf_op jit(solution)/shard_map/gather_one/ppermute | solution.py:86
  95.3 5.0 collective-permute-start.13
  101.6 2.3 collective-permute-done.12.rest_4_
  104.6 15.9 %attend.1 = (bf16[1024,1600]{1,0:T(8,128)(2,1)}, bf16[1600,768]{1,0:T(8,128)(2,1)}, bf16[1024,768]{1,0:T(8,128)(2,1)}, f32[1024,256]{1,0:T(8,128)}, bf16[8,128,256]{2,1,0:T(8,128)(2,1)}, /*index=5*/f32[1024,4]{1,0:T(8,128)}) custom-call(s32[8]{0:T(128)} %get-tuple-element.249.member_ref, s32[1]{0:T(128)} %bitcast.3.place_ref, s32[8]{0:T(128)} %pair_of_ref.1, ...), custom_call_target="tpu_custom_call" | custom-call | flops 1000 | bytes 45000000 | tf_op jit(solution)/shard_map/attend/pallas_call | solution.py:243
  122.0 4.5 all-to-all-start
  129.4 12.2 %collective-permute-done.15 = bf16[400,800]{1,0:T(8,128)(2,1)S(1)} collective-permute-done((bf16[400,800]{1,0:T(8,128)(2,1)S(1)}, bf16[400,800]{1,0:T(8,128)(2,1)S(1)}, u32[]{:S(2)}, u32[]{:S(2)}) %collective-permute-start.15) | collective-permute-done | bytes 640032 | tf_op jit(solution)/shard_map/unit_parts/ppermute | solution.py:60
  142.9 7.9 %out.1 = (f32[128,1600]{1,0:T(8,128)}, bf16[128,1600]{1,0:T(8,128)(2,1)}, f32[128,1600]{1,0:T(8,128)}, f32[128,1]{1,0:T(8,128)}, bf16[128,1600]{1,0:T(8,128)(2,1)}) custom-call(bf16[8,128,256]{2,1,0:T(8,128)(2,1)} %all-to-all-done.back_ref, bf16[128,1600]{1,0:T(8,128)(2,1)} %bitcast.100, f32[1,1600]{1,0:T(1,128)} %broadcast_in_dim.61.bias_ref, ...), custom_call_target="tpu_custom_call" | custom-call | flops 1000 | bytes 24000000 | tf_op jit(solution)/shard_map/out/pallas_call | solution.py:243
  150.9 2.5 collective-permute-start.21
  153.8 13.6 %collective-permute-done.21.rest_8_ = bf16[128,1600]{1,0:T(8,128)(2,1)S(1)} collective-permute-done((bf16[128,1600]{1,0:T(8,128)(2,1)}, bf16[128,1600]{1,0:T(8,128)(2,1)S(1)}, u32[]{:S(2)}, u32[]{:S(2)}) %collective-permute-start.21) | collective-permute-done | bytes 409632 | tf_op jit(solution)/shard_map/gather_two/ppermute | solution.py:86
  167.5 2.4 collective-permute-start.22
  171.1 13.3 %collective-permute-done.22.rest_7_ = bf16[128,1600]{1,0:T(8,128)(2,1)S(1)} collective-permute-done((bf16[128,1600]{1,0:T(8,128)(2,1)S(1)}, bf16[128,1600]{1,0:T(8,128)(2,1)S(1)}, u32[]{:S(2)}, u32[]{:S(2)}) %collective-permute-start.22) | collective-permute-done | bytes 409632 | tf_op jit(solution)/shard_map/gather_two/ppermute | solution.py:86
  184.3 3.8 collective-permute-start.23
  188.2 3.4 collective-permute-done.19.rest_2_
  191.6 15.8 %collective-permute-done.23.rest_6_ = bf16[128,1600]{1,0:T(8,128)(2,1)S(1)} collective-permute-done((bf16[128,1600]{1,0:T(8,128)(2,1)S(1)}, bf16[128,1600]{1,0:T(8,128)(2,1)S(1)}, u32[]{:S(2)}, u32[]{:S(2)}) %collective-permute-start.23) | collective-permute-done | bytes 409632 | tf_op jit(solution)/shard_map/gather_two/ppermute | solution.py:86
  208.2 6.2 %collective-permute-start.24 = (bf16[64,1600]{1,0:T(8,128)(2,1)}, bf16[64,1600]{1,0:T(8,128)(2,1)}, u32[]{:S(2)}, u32[]{:S(2)}) collective-permute-start(bf16[64,1600]{1,0:T(8,128)(2,1)} %slice.311), channel_id=1, source_target_pairs={{0,2},{2,4},{4,6},{6,7},{7,5},{5,3},{3,1},{1,0},{8,10},{10,12},{12... | collective-permute-start | bytes 614408 | tf_op jit(solution)/shard_map/gather_two/ppermute | solution.py:86
  214.4 3.6 collective-permute-done.20.rest_3_
  219.5 2.6 collective-permute-start.25
  224.6 8.8 %hidden_grad.1 = (bf16[1600,800]{1,0:T(8,128)(2,1)}, f32[1024,800]{1,0:T(8,128)}) custom-call(s32[1]{0:T(128)} %bitcast.3.place_ref, bf16[1024,1600]{1,0:T(8,128)(2,1)} %all-gather.4.cloned.1.call-done.cot_ref.rest_2_, bf16[2,400,800]{2,1,0:T(8,128)(2,1)} %copy-done.6, bf16[2,400,800]{2,1,0:T(8,128)(2,1)} %collective-permute-done.17.peer_ref), custom_call_target="tpu_custom_call" | custom-call | flops 1000 | bytes 27000000 | tf_op jit(solution)/shard_map/hidden_grad/pallas_call | solution.py:243
  233.5 20.1 %hidden.1 = (bf16[1024,1600]{1,0:T(8,128)(2,1)}, bf16[1024,800]{1,0:T(8,128)(2,1)}, bf16[1024,800]{1,0:T(8,128)(2,1)}, f32[8,128,1600]{2,1,0:T(8,128)}, bf16[128,1600]{1,0:T(8,128)(2,1)}, /*index=5*/f32[1,800]{1,0:T(1,128)}) custom-call(s32[8]{0:T(128)} %get-tuple-element.249.member_ref, s32[8]{0:T(128)} %fusion.37.offset_ref, s32[1]{0:T(128)} %bitcast.3.place_ref, ...), custom_call_target="tpu_custom_call" | custom-call | flops 1000 | bytes 60000000 | tf_op jit(solution)/shard_map/hidden/pallas_call | solution.py:243
  253.5 8.0 %branch.1 = bf16[1024,1600]{1,0:T(8,128)(2,1)} custom-call(bf16[1024,800]{1,0:T(8,128)(2,1)} %get-tuple-element.103.value_ref.rest_3_, bf16[1600,800]{1,0:T(8,128)(2,1)} %get-tuple-element.104.w_ref), custom_call_target="tpu_custom_call" | custom-call | flops 1000 | bytes 24000000 | tf_op jit(solution)/shard_map/sum_two/branch/pallas_call | solution.py:243
  262.6 2.1 collective-permute-start.27
  265.9 2.6 collective-permute-done.27
  268.5 2.3 collective-permute-done.26
  273.1 1.9 collective-permute-start.28
  275.0 11.2 %unit_other.1 = bf16[2,2,400,800]{3,2,1,0:T(8,128)(2,1)} custom-call(s32[1]{0:T(128)} %bitcast.core_ref, bf16[1024,1600]{1,0:T(8,128)(2,1)} %get-tuple-element.108.rest_0_, bf16[1024,800]{1,0:T(8,128)(2,1)} %get-tuple-element.109.rest_1_, bf16[1024,1600]{1,0:T(8,128)(2,1)} %all-gather.4.cloned.1.call-done.cot_ref.rest_2_, ...), custom_call_target="tpu_custom_call" | custom-call | flops 1000 | bytes 24000000 | tf_op jit(solution)/shard_map/sum_two/unit_sum/unit_other/pallas_call | solution.py:243
  286.2 8.4 %collective-permute-done.29 = bf16[128,1600]{1,0:T(8,128)(2,1)S(1)} collective-permute-done((bf16[128,1600]{1,0:T(8,128)(2,1)}, bf16[128,1600]{1,0:T(8,128)(2,1)S(1)}, u32[]{:S(2)}, u32[]{:S(2)}) %collective-permute-start.29) | collective-permute-done | bytes 409632 | tf_op jit(solution)/shard_map/sum_two/ppermute | solution.py:86
  298.1 15.8 %collective-permute-done.30 = bf16[128,1600]{1,0:T(8,128)(2,1)S(1)} collective-permute-done((bf16[128,1600]{1,0:T(8,128)(2,1)S(1)}, bf16[128,1600]{1,0:T(8,128)(2,1)S(1)}, u32[]{:S(2)}, u32[]{:S(2)}) %collective-permute-start.30) | collective-permute-done | bytes 409632 | tf_op jit(solution)/shard_map/sum_two/ppermute | solution.py:86
  313.9 2.5 collective-permute-done.32
  316.6 2.4 collective-permute-start.31
  319.0 11.0 %collective-permute-done.33 = bf16[128,1600]{1,0:T(8,128)(2,1)S(1)} collective-permute-done((bf16[128,1600]{1,0:T(8,128)(2,1)S(1)}, bf16[128,1600]{1,0:T(8,128)(2,1)S(1)}, u32[]{:S(2)}, u32[]{:S(2)}) %collective-permute-start.33) | collective-permute-done | bytes 409632 | tf_op jit(solution)/shard_map/sum_two/ppermute | solution.py:86
  330.0 2.7 collective-permute-done.31
  333.7 10.8 %out_back.1 = (f32[128,1600]{1,0:T(8,128)}, bf16[128,1600]{1,0:T(8,128)(2,1)}, bf16[8,128,256]{2,1,0:T(8,128)(2,1)}, f32[4,1600]{1,0:T(4,128)}, f32[8,200,800]{2,1,0:T(8,128)}, /*index=5*/bf16[8,200,800]{2,1,0:T(8,128)(2,1)}) custom-call(s32[1]{0:T(128)} %bitcast.core_ref, f32[128,1600]{1,0:T(8,128)} %fusion.31.sum_ref, bf16[128,1600]{1,0:T(8,128)(2,1)} %bitcast.104, ...), custom_call_target="tpu_custom_call" | custom-call | flops 1000 | bytes 36000000 | tf_op jit(solution)/shard_map/out_back/pallas_call | solution.py:243
  344.5 4.8 all-to-all-start.1
  355.7 13.1 %unit_mine.1 = (f32[2,400,800]{2,1,0:T(8,128)}, bf16[2,400,800]{2,1,0:T(8,128)(2,1)}) custom-call(s32[1]{0:T(128)} %bitcast.core_ref, s32[1]{0:T(128)} %bitcast.27.row_ref, bf16[2,2,400,800]{3,2,1,0:T(8,128)(2,1)} %collective-permute-done.35.got_ref, bf16[1024,1600]{1,0:T(8,128)(2,1)} %get-tuple-element.108.rest_0_, ...), custom_call_target="tpu_custom_call" | custom-call | flops 1000 | bytes 30000000 | tf_op jit(solution)/shard_map/unit_sum/unit_mine/pallas_call | solution.py:243
  370.1 20.4 %attend_back.1 = (bf16[1024,768]{1,0:T(8,128)(2,1)}, f32[1,768]{1,0:T(1,128)}, bf16[128,1600]{1,0:T(8,128)(2,1)}) custom-call(s32[16]{0:T(128)} %pad_add_fusion.who_ref, s32[2]{0:T(128)} %pad_add_fusion.1.far_ref, bf16[1024,768]{1,0:T(8,128)(2,1)} %get-tuple-element.121.qkv_ref, bf16[1600,768]{1,0:T(8,128)(2,1)} %get-tuple-element.122.w_ref, ...), custom_call_target="tpu_custom_call" | custom-call | flops 1000 | bytes 60000000 | tf_op jit(solution)/shard_map/attend_back/pallas_call | solution.py:243
  392.3 2.0 collective-permute-start.38
  394.3 4.9 add_convert_fusion
  399.2 9.4 %project_back.1 = (f32[8,128,1600]{2,1,0:T(8,128)}, f32[2,1600]{1,0:T(2,128)}) custom-call(s32[16]{0:T(128)} %gather_fusion, bf16[1024,768]{1,0:T(8,128)(2,1)} %get-tuple-element.126.grad_ref.rest_1_, bf16[1600,768]{1,0:T(8,128)(2,1)} %get-tuple-element.122.w_ref, bf16[1024,1600]{1,0:T(8,128)(2,1)} %get-tuple-element.127.x_ref.rest_0_), custom_call_target="tpu_custom_call" | custom-call | flops 1000 | bytes 18000000 | tf_op jit(solution)/shard_map/project_back/pallas_call | solution.py:243
  409.9 6.0 %qkv_other.1 = bf16[1,2,400,768]{3,2,1,0:T(8,128)(2,1)} custom-call(s32[1]{0:T(128)} %bitcast.core_ref, bf16[1024,1600]{1,0:T(8,128)(2,1)} %get-tuple-element.127.x_ref.rest_0_, bf16[1024,768]{1,0:T(8,128)(2,1)} %get-tuple-element.126.grad_ref.rest_1_), custom_call_target="tpu_custom_call" | custom-call | flops 1000 | bytes 15000000 | tf_op jit(solution)/shard_map/sum_one/qkv_sum/qkv_other/pallas_call | solution.py:243
  422.3 16.3 %collective-permute-done.39 = bf16[128,1600]{1,0:T(8,128)(2,1)} collective-permute-done((bf16[128,1600]{1,0:T(8,128)(2,1)}, bf16[128,1600]{1,0:T(8,128)(2,1)}, u32[]{:S(2)}, u32[]{:S(2)}) %collective-permute-start.39) | collective-permute-done | bytes 409632 | tf_op jit(solution)/shard_map/sum_one/ppermute | solution.py:86
  438.6 2.7 bitcast_add_fusion.1
  446.0 7.3 %qkv_mine.1 = (f32[1,400,768]{2,1,0:T(8,128)}, bf16[1,400,768]{2,1,0:T(8,128)(2,1)}) custom-call(s32[1]{0:T(128)} %bitcast.core_ref, s32[1]{0:T(128)} %bitcast.27.row_ref, bf16[1,2,400,768]{3,2,1,0:T(8,128)(2,1)} %copy-done.11, bf16[1024,1600]{1,0:T(8,128)(2,1)} %get-tuple-element.127.x_ref.rest_0_, bf16[1024,768]{1,0:T(8,128)(2,1)} %get-tuple-element.126.grad_ref.rest_1_), custom_call_target="tpu_custom_call" | custom-call | flops 1000 | bytes 18000000 | tf_op jit(solution)/shard_map/sum_one/qkv_sum/qkv_mine/pallas_call | solution.py:243
  454.4 2.7 collective-permute-done.44
  457.5 2.7 bitcast_add_fusion
  466.8 1.9 fusion.6
  468.6 8.2 %collective-permute-done.49 = f32[19200]{0:T(1024)S(1)} collective-permute-done((f32[19200]{0:T(1024)S(1)}, f32[19200]{0:T(1024)S(1)}, u32[]{:S(2)}, u32[]{:S(2)}) %collective-permute-start.49) | collective-permute-done | bytes 76832 | tf_op jit(solution)/shard_map/sum_one/sum_vectors/ppermute | solution.py:60
  479.5 2.0 fusion.8
  481.6 2.3 collective-permute-start.52
  484.0 2.2 collective-permute-start.53
  488.9 2.6 collective-permute-done.52
  491.5 13.3 %collective-permute-start.55 = (bf16[400,128]{1,0:T(8,128)(2,1)S(1)}, bf16[400,128]{1,0:T(8,128)(2,1)S(1)}, u32[]{:S(2)}, u32[]{:S(2)}) collective-permute-start(bf16[400,128]{1,0:T(8,128)(2,1)S(1)} %slice.321), channel_id=1, source_target_pairs={{4,2},{5,4},{0,3},{6,5},{2,0},{3,7},{1,6},{12,10},{13,12},{8,11},{... | collective-permute-start | bytes 307208 | tf_op jit(solution)/shard_map/from_heads/ppermute | solution.py:208
  505.0 2.1 collective-permute-done.55
  507.2 1.8 fusion.2
  515.2 2.7 collective-permute-done.56
  (283 shorter events, 78.6 us)
Async XLA Ops:
  7.2 135.7 %all-gather.6.cloned.1.call-start = ((), (), s32[]{:S(2)}) async-start(), calls=%async_computation.6 | async-start | bytes 6758400 | tf_op jit(solution)/shard_map/gather_one/all_gather | solution.py:624
  10.0 43.0 %copy-start.10 = (bf16[128,1600]{1,0:T(8,128)(2,1)}, bf16[128,1600]{1,0:T(8,128)(2,1)S(1)}, u32[]{:S(2)}) copy-start(bf16[128,1600]{1,0:T(8,128)(2,1)S(1)} %fusion.20.rest_0_) | copy-start | bytes 1228804
  10.0 19.5 %collective-permute-start.2 = (bf16[128,1600]{1,0:T(8,128)(2,1)S(1)}, bf16[128,1600]{1,0:T(8,128)(2,1)S(1)}, u32[]{:S(2)}, u32[]{:S(2)}) collective-permute-start(bf16[128,1600]{1,0:T(8,128)(2,1)S(1)} %fusion.20.rest_0_), channel_id=1, source_target_pairs={{0,2},{2,4},{4,6},{6,7},{7,5},{5,3},{3,1},{1,0},{8,10},{10,12},{12... | collective-permute-start | bytes 1228808 | tf_op jit(solution)/shard_map/gather_one/ppermute | solution.py:86
  13.1 16.4 %collective-permute-start.3 = (bf16[128,1600]{1,0:T(8,128)(2,1)S(1)}, bf16[128,1600]{1,0:T(8,128)(2,1)S(1)}, u32[]{:S(2)}, u32[]{:S(2)}) collective-permute-start(bf16[128,1600]{1,0:T(8,128)(2,1)S(1)} %fusion.20.rest_0_), channel_id=1, source_target_pairs={{0,1},{2,0},{4,2},{6,4},{7,6},{5,7},{3,5},{1,3},{8,9},{10,8},{12,1... | collective-permute-start | bytes 1228808 | tf_op jit(solution)/shard_map/gather_one/ppermute | solution.py:86
  14.8 14.7 %collective-permute-start = (bf16[400,256]{1,0:T(8,128)(2,1)S(1)}, bf16[400,256]{1,0:T(8,128)(2,1)S(1)}, u32[]{:S(2)}, u32[]{:S(2)}) collective-permute-start(bf16[400,256]{1,0:T(8,128)(2,1)S(1)} %get-tuple-element.235), channel_id=1, source_target_pairs={{2,5},{4,3},{1,4},{5,0},{3,1},{6,2},{7,6},{10,13},{12,11},{9,12},{... | collective-permute-start | bytes 614408 | tf_op jit(solution)/shard_map/gather_one/to_heads/ppermute | solution.py:208
  16.1 13.4 %collective-permute-start.1 = (bf16[400,256]{1,0:T(8,128)(2,1)S(1)}, bf16[400,256]{1,0:T(8,128)(2,1)S(1)}, u32[]{:S(2)}, u32[]{:S(2)}) collective-permute-start(bf16[400,256]{1,0:T(8,128)(2,1)S(1)} %get-tuple-element.234), channel_id=1, source_target_pairs={{6,3},{1,2},{5,5},{7,4},{2,0},{0,1},{14,11},{9,10},{13,13},{15,12}... | collective-permute-start | bytes 614408 | tf_op jit(solution)/shard_map/gather_one/to_heads/ppermute | solution.py:208
  29.6 22.6 %collective-permute-start.6 = (bf16[128,1600]{1,0:T(8,128)(2,1)S(1)}, bf16[128,1600]{1,0:T(8,128)(2,1)}, u32[]{:S(2)}, u32[]{:S(2)}) collective-permute-start(bf16[128,1600]{1,0:T(8,128)(2,1)S(1)} %collective-permute-done.2.rest_8_), channel_id=1, source_target_pairs={{0,2},{2,4},{4,6},{6,7},{7,5},{5,3},{3,1},{1,0},{8,10},{10,12},{12... | collective-permute-start | bytes 1228808 | tf_op jit(solution)/shard_map/gather_one/ppermute | solution.py:86
  36.2 15.9 %collective-permute-start.7 = (bf16[128,1600]{1,0:T(8,128)(2,1)S(1)}, bf16[128,1600]{1,0:T(8,128)(2,1)S(1)}, u32[]{:S(2)}, u32[]{:S(2)}) collective-permute-start(bf16[128,1600]{1,0:T(8,128)(2,1)S(1)} %collective-permute-done.3.rest_1_), channel_id=1, source_target_pairs={{0,1},{2,0},{4,2},{6,4},{7,6},{5,7},{3,5},{1,3},{8,9},{10,8},{12,1... | collective-permute-start | bytes 1228808 | tf_op jit(solution)/shard_map/gather_one/ppermute | solution.py:86
  36.3 15.9 %collective-permute-start.4 = (bf16[400,256]{1,0:T(8,128)(2,1)S(1)}, bf16[400,256]{1,0:T(8,128)(2,1)S(1)}, u32[]{:S(2)}, u32[]{:S(2)}) collective-permute-start(bf16[400,256]{1,0:T(8,128)(2,1)S(1)} %slice.240), channel_id=1, source_target_pairs={{5,1},{0,0},{1,3},{3,2},{4,4},{7,5},{2,6},{13,9},{8,8},{9,11},{11,... | collective-permute-start | bytes 614408 | tf_op jit(solution)/shard_map/gather_one/to_heads/ppermute | solution.py:208
  37.0 15.2 %collective-permute-start.5 = (bf16[400,128]{1,0:T(8,128)(2,1)S(1)}, bf16[400,128]{1,0:T(8,128)(2,1)S(1)}, u32[]{:S(2)}, u32[]{:S(2)}) collective-permute-start(bf16[400,128]{1,0:T(8,128)(2,1)S(1)} %slice.241), channel_id=1, source_target_pairs={{2,4},{4,5},{3,0},{5,6},{0,2},{7,3},{6,1},{10,12},{12,13},{11,8},{... | collective-permute-start | bytes 307208 | tf_op jit(solution)/shard_map/gather_one/to_heads/ppermute | solution.py:208
  53.0 171.6 %all-gather.4.cloned.1.call-start = ((), (), s32[]{:S(2)}) async-start(), calls=%async_computation.4 | async-start | bytes 3833856 | tf_op jit(solution)/shard_map/all_gather | solution.py:663
  55.0 14.0 %collective-permute-start.8 = (bf16[400,768]{1,0:T(8,128)(2,1)S(1)}, bf16[400,768]{1,0:T(8,128)(2,1)S(1)}, u32[]{:S(2)}, u32[]{:S(2)}) collective-permute-start(bf16[400,768]{1,0:T(8,128)(2,1)S(1)} %fusion.10), channel_id=1, source_target_pairs={{0,16},{8,24},{16,0},{24,8},{1,17},{9,25},{17,1},{25,9},{2,18},{10... | collective-permute-start | bytes 1843208 | tf_op jit(solution)/shard_map/gather_one/qkv_parts/ppermute | solution.py:60
  69.2 3.0 collective-permute-start.9
  72.2 48.4 %collective-permute-start.14 = (bf16[400,800]{1,0:T(8,128)(2,1)}, bf16[400,800]{1,0:T(8,128)(2,1)}, u32[]{:S(2)}, u32[]{:S(2)}) collective-permute-start(bf16[400,800]{1,0:T(8,128)(2,1)} %bitcast.108), channel_id=1, source_target_pairs={{0,16},{8,24},{16,0},{24,8},{1,17},{9,25},{17,1},{25,9},{2,18},{10... | collective-permute-start | bytes 1920008 | tf_op jit(solution)/shard_map/unit_parts/ppermute | solution.py:60
  73.8 21.4 %collective-permute-start.11 = (bf16[128,1600]{1,0:T(8,128)(2,1)}, bf16[128,1600]{1,0:T(8,128)(2,1)S(1)}, u32[]{:S(2)}, u32[]{:S(2)}) collective-permute-start(bf16[128,1600]{1,0:T(8,128)(2,1)} %collective-permute-done.6.rest_7_), channel_id=1, source_target_pairs={{0,2},{2,4},{4,6},{6,7},{7,5},{5,3},{3,1},{1,0},{8,10},{10,12},{12... | collective-permute-start | bytes 1228808 | tf_op jit(solution)/shard_map/gather_one/ppermute | solution.py:86
  75.8 19.5 %collective-permute-start.10 = (bf16[128,1600]{1,0:T(8,128)(2,1)}, bf16[128,1600]{1,0:T(8,128)(2,1)S(1)}, u32[]{:S(2)}, u32[]{:S(2)}) collective-permute-start(bf16[128,1600]{1,0:T(8,128)(2,1)} %copy-done.23), channel_id=1, source_target_pairs={{0,1},{2,0},{4,2},{6,4},{7,6},{5,7},{3,5},{1,3},{8,9},{10,8},{12,1... | collective-permute-start | bytes 1228808 | tf_op jit(solution)/shard_map/gather_one/ppermute | solution.py:86
  95.2 8.6 %collective-permute-start.12 = (bf16[64,1600]{1,0:T(8,128)(2,1)S(1)}, bf16[64,1600]{1,0:T(8,128)(2,1)S(1)}, u32[]{:S(2)}, u32[]{:S(2)}) collective-permute-start(bf16[64,1600]{1,0:T(8,128)(2,1)S(1)} %slice.309), channel_id=1, source_target_pairs={{0,2},{2,4},{4,6},{6,7},{7,5},{5,3},{3,1},{1,0},{8,10},{10,12},{12... | collective-permute-start | bytes 614408 | tf_op jit(solution)/shard_map/gather_one/ppermute | solution.py:86
  95.3 8.5 %collective-permute-start.13 = (bf16[64,1600]{1,0:T(8,128)(2,1)S(1)}, bf16[64,1600]{1,0:T(8,128)(2,1)S(1)}, u32[]{:S(2)}, u32[]{:S(2)}) collective-permute-start(bf16[64,1600]{1,0:T(8,128)(2,1)S(1)} %slice.310), channel_id=1, source_target_pairs={{0,1},{2,0},{4,2},{6,4},{7,6},{5,7},{3,5},{1,3},{8,9},{10,8},{12,1... | collective-permute-start | bytes 614408 | tf_op jit(solution)/shard_map/gather_one/ppermute | solution.py:86
  122.0 20.8 %all-to-all-start = ((bf16[8,128,256]{2,1,0:T(8,128)(2,1)}), bf16[8,128,256]{2,1,0:T(8,128)(2,1)}, u32[]{:S(2)}, u32[]{:S(2)}) async-start(bf16[8,128,256]{2,1,0:T(8,128)(2,1)} %get-tuple-element.91), calls=%async_computation | async-start | bytes 1048576 | tf_op jit(solution)/shard_map/all_to_all | solution.py:665
  126.5 242.2 %reduce-scatter.5.cloned.1.call-start = ((), (), s32[]{:S(2)}) async-start(), calls=%async_computation.5 | async-start | bytes 3833856 | tf_op jit(solution)/shard_map/reduce_scatter | solution.py:747
  126.6 15.0 %collective-permute-start.15 = (bf16[400,800]{1,0:T(8,128)(2,1)S(1)}, bf16[400,800]{1,0:T(8,128)(2,1)S(1)}, u32[]{:S(2)}, u32[]{:S(2)}) collective-permute-start(bf16[400,800]{1,0:T(8,128)(2,1)S(1)} %copy-done.19), channel_id=1, source_target_pairs={{0,16},{8,24},{16,0},{24,8},{1,17},{9,25},{17,1},{25,9},{2,18},{10... | collective-permute-start | bytes 1920008 | tf_op jit(solution)/shard_map/unit_parts/ppermute | solution.py:60
  150.9 16.6 %collective-permute-start.21 = (bf16[128,1600]{1,0:T(8,128)(2,1)}, bf16[128,1600]{1,0:T(8,128)(2,1)S(1)}, u32[]{:S(2)}, u32[]{:S(2)}) collective-permute-start(bf16[128,1600]{1,0:T(8,128)(2,1)} %get-tuple-element.100.rest_0_), channel_id=1, source_target_pairs={{0,2},{2,4},{4,6},{6,7},{7,5},{5,3},{3,1},{1,0},{8,10},{10,12},{12... | collective-permute-start | bytes 1228808 | tf_op jit(solution)/shard_map/gather_two/ppermute | solution.py:86
  153.3 16.5 %collective-permute-start.18 = (bf16[128,1600]{1,0:T(8,128)(2,1)}, bf16[128,1600]{1,0:T(8,128)(2,1)S(1)}, u32[]{:S(2)}, u32[]{:S(2)}) collective-permute-start(bf16[128,1600]{1,0:T(8,128)(2,1)} %get-tuple-element.100.rest_0_), channel_id=1, source_target_pairs={{0,1},{2,0},{4,2},{6,4},{7,6},{5,7},{3,5},{1,3},{8,9},{10,8},{12,1... | collective-permute-start | bytes 1228808 | tf_op jit(solution)/shard_map/gather_two/ppermute | solution.py:86
  153.3 71.3 %collective-permute-start.17 = (bf16[2,400,800]{2,1,0:T(8,128)(2,1)S(1)}, bf16[2,400,800]{2,1,0:T(8,128)(2,1)}, u32[]{:S(2)}, u32[]{:S(2)}) collective-permute-start(bf16[2,400,800]{2,1,0:T(8,128)(2,1)S(1)} %pad_maximum_fusion.pair_ref), channel_id=1, source_target_pairs={{0,8},{8,0},{16,24},{24,16},{1,9},{9,1},{17,25},{25,17},{2,10},{10... | collective-permute-start | bytes 3840008 | tf_op jit(solution)/shard_map/unit_parts/ppermute | solution.py:60
  153.3 80.1 %collective-permute-start.16 = (bf16[2,400,800]{2,1,0:T(8,128)(2,1)S(1)}, bf16[2,400,800]{2,1,0:T(8,128)(2,1)}, u32[]{:S(2)}, u32[]{:S(2)}) collective-permute-start(bf16[2,400,800]{2,1,0:T(8,128)(2,1)S(1)} %pad_maximum_fusion.1.pair_ref), channel_id=1, source_target_pairs={{0,8},{8,0},{16,24},{24,16},{1,9},{9,1},{17,25},{25,17},{2,10},{10... | collective-permute-start | bytes 3840008 | tf_op jit(solution)/shard_map/unit_parts/ppermute | solution.py:60
  167.5 16.9 %collective-permute-start.22 = (bf16[128,1600]{1,0:T(8,128)(2,1)S(1)}, bf16[128,1600]{1,0:T(8,128)(2,1)S(1)}, u32[]{:S(2)}, u32[]{:S(2)}) collective-permute-start(bf16[128,1600]{1,0:T(8,128)(2,1)S(1)} %collective-permute-done.21.rest_8_), channel_id=1, source_target_pairs={{0,2},{2,4},{4,6},{6,7},{7,5},{5,3},{3,1},{1,0},{8,10},{10,12},{12... | collective-permute-start | bytes 1228808 | tf_op jit(solution)/shard_map/gather_two/ppermute | solution.py:86
  169.8 21.8 %collective-permute-start.19 = (bf16[128,1600]{1,0:T(8,128)(2,1)S(1)}, bf16[128,1600]{1,0:T(8,128)(2,1)S(1)}, u32[]{:S(2)}, u32[]{:S(2)}) collective-permute-start(bf16[128,1600]{1,0:T(8,128)(2,1)S(1)} %collective-permute-done.18.rest_1_), channel_id=1, source_target_pairs={{0,1},{2,0},{4,2},{6,4},{7,6},{5,7},{3,5},{1,3},{8,9},{10,8},{12,1... | collective-permute-start | bytes 1228808 | tf_op jit(solution)/shard_map/gather_two/ppermute | solution.py:86
  184.3 23.1 %collective-permute-start.23 = (bf16[128,1600]{1,0:T(8,128)(2,1)S(1)}, bf16[128,1600]{1,0:T(8,128)(2,1)S(1)}, u32[]{:S(2)}, u32[]{:S(2)}) collective-permute-start(bf16[128,1600]{1,0:T(8,128)(2,1)S(1)} %collective-permute-done.22.rest_7_), channel_id=1, source_target_pairs={{0,2},{2,4},{4,6},{6,7},{7,5},{5,3},{3,1},{1,0},{8,10},{10,12},{12... | collective-permute-start | bytes 1228808 | tf_op jit(solution)/shard_map/gather_two/ppermute | solution.py:86
  191.6 26.4 %collective-permute-start.20 = (bf16[128,1600]{1,0:T(8,128)(2,1)S(1)}, bf16[128,1600]{1,0:T(8,128)(2,1)S(1)}, u32[]{:S(2)}, u32[]{:S(2)}) collective-permute-start(bf16[128,1600]{1,0:T(8,128)(2,1)S(1)} %collective-permute-done.19.rest_2_), channel_id=1, source_target_pairs={{0,1},{2,0},{4,2},{6,4},{7,6},{5,7},{3,5},{1,3},{8,9},{10,8},{12,1... | collective-permute-start | bytes 1228808 | tf_op jit(solution)/shard_map/gather_two/ppermute | solution.py:86
  208.2 25.3 %collective-permute-start.24 = (bf16[64,1600]{1,0:T(8,128)(2,1)}, bf16[64,1600]{1,0:T(8,128)(2,1)}, u32[]{:S(2)}, u32[]{:S(2)}) collective-permute-start(bf16[64,1600]{1,0:T(8,128)(2,1)} %slice.311), channel_id=1, source_target_pairs={{0,2},{2,4},{4,6},{6,7},{7,5},{5,3},{3,1},{1,0},{8,10},{10,12},{12... | collective-permute-start | bytes 614408 | tf_op jit(solution)/shard_map/gather_two/ppermute | solution.py:86
  219.5 14.0 %collective-permute-start.25 = (bf16[64,1600]{1,0:T(8,128)(2,1)}, bf16[64,1600]{1,0:T(8,128)(2,1)}, u32[]{:S(2)}, u32[]{:S(2)}) collective-permute-start(bf16[64,1600]{1,0:T(8,128)(2,1)} %slice.312), channel_id=1, source_target_pairs={{0,1},{2,0},{4,2},{6,4},{7,6},{5,7},{3,5},{1,3},{8,9},{10,8},{12,1... | collective-permute-start | bytes 614408 | tf_op jit(solution)/shard_map/gather_two/ppermute | solution.py:86
  262.6 5.9 %collective-permute-start.27 = (bf16[64,1600]{1,0:T(8,128)(2,1)S(1)}, bf16[64,1600]{1,0:T(8,128)(2,1)S(1)}, u32[]{:S(2)}, u32[]{:S(2)}) collective-permute-start(bf16[64,1600]{1,0:T(8,128)(2,1)S(1)} %get-tuple-element.238), channel_id=1, source_target_pairs={{0,1},{2,0},{4,2},{6,4},{7,6},{5,7},{3,5},{1,3},{8,9},{10,8},{12,1... | collective-permute-start | bytes 614408 | tf_op jit(solution)/shard_map/sum_two/ppermute | solution.py:86
  264.7 6.1 %collective-permute-start.26 = (bf16[64,1600]{1,0:T(8,128)(2,1)S(1)}, bf16[64,1600]{1,0:T(8,128)(2,1)S(1)}, u32[]{:S(2)}, u32[]{:S(2)}) collective-permute-start(bf16[64,1600]{1,0:T(8,128)(2,1)S(1)} %get-tuple-element.239), channel_id=1, source_target_pairs={{0,2},{2,4},{4,6},{6,7},{7,5},{5,3},{3,1},{1,0},{8,10},{10,12},{12... | collective-permute-start | bytes 614408 | tf_op jit(solution)/shard_map/sum_two/ppermute | solution.py:86
  273.0 21.6 %collective-permute-start.29 = (bf16[128,1600]{1,0:T(8,128)(2,1)}, bf16[128,1600]{1,0:T(8,128)(2,1)S(1)}, u32[]{:S(2)}, u32[]{:S(2)}) collective-permute-start(bf16[128,1600]{1,0:T(8,128)(2,1)} %get-tuple-element.106), channel_id=1, source_target_pairs={{0,1},{2,0},{4,2},{6,4},{7,6},{5,7},{3,5},{1,3},{8,9},{10,8},{12,1... | collective-permute-start | bytes 1228808 | tf_op jit(solution)/shard_map/sum_two/ppermute | solution.py:86
  273.1 21.5 %collective-permute-start.28 = (bf16[128,1600]{1,0:T(8,128)(2,1)}, bf16[128,1600]{1,0:T(8,128)(2,1)}, u32[]{:S(2)}, u32[]{:S(2)}) collective-permute-start(bf16[128,1600]{1,0:T(8,128)(2,1)} %get-tuple-element.105), channel_id=1, source_target_pairs={{0,2},{2,4},{4,6},{6,7},{7,5},{5,3},{3,1},{1,0},{8,10},{10,12},{12... | collective-permute-start | bytes 1228808 | tf_op jit(solution)/shard_map/sum_two/ppermute | solution.py:86
  295.8 18.1 %collective-permute-start.30 = (bf16[128,1600]{1,0:T(8,128)(2,1)S(1)}, bf16[128,1600]{1,0:T(8,128)(2,1)S(1)}, u32[]{:S(2)}, u32[]{:S(2)}) collective-permute-start(bf16[128,1600]{1,0:T(8,128)(2,1)S(1)} %get-tuple-element.110), channel_id=1, source_target_pairs={{0,2},{2,4},{4,6},{6,7},{7,5},{5,3},{3,1},{1,0},{8,10},{10,12},{12... | collective-permute-start | bytes 1228808 | tf_op jit(solution)/shard_map/sum_two/ppermute | solution.py:86
  296.7 19.7 %collective-permute-start.32 = (bf16[128,1600]{1,0:T(8,128)(2,1)S(1)}, bf16[128,1600]{1,0:T(8,128)(2,1)S(1)}, u32[]{:S(2)}, u32[]{:S(2)}) collective-permute-start(bf16[128,1600]{1,0:T(8,128)(2,1)S(1)} %get-tuple-element.111), channel_id=1, source_target_pairs={{0,1},{2,0},{4,2},{6,4},{7,6},{5,7},{3,5},{1,3},{8,9},{10,8},{12,1... | collective-permute-start | bytes 1228808 | tf_op jit(solution)/shard_map/sum_two/ppermute | solution.py:86
  316.5 13.5 %collective-permute-start.33 = (bf16[128,1600]{1,0:T(8,128)(2,1)S(1)}, bf16[128,1600]{1,0:T(8,128)(2,1)S(1)}, u32[]{:S(2)}, u32[]{:S(2)}) collective-permute-start(bf16[128,1600]{1,0:T(8,128)(2,1)S(1)} %get-tuple-element.222), channel_id=1, source_target_pairs={{0,1},{2,0},{4,2},{6,4},{7,6},{5,7},{3,5},{1,3},{8,9},{10,8},{12,1... | collective-permute-start | bytes 1228808 | tf_op jit(solution)/shard_map/sum_two/ppermute | solution.py:86
  316.6 16.1 %collective-permute-start.31 = (bf16[128,1600]{1,0:T(8,128)(2,1)S(1)}, bf16[128,1600]{1,0:T(8,128)(2,1)S(1)}, u32[]{:S(2)}, u32[]{:S(2)}) collective-permute-start(bf16[128,1600]{1,0:T(8,128)(2,1)S(1)} %get-tuple-element.221), channel_id=1, source_target_pairs={{0,2},{2,4},{4,6},{6,7},{7,5},{5,3},{3,1},{1,0},{8,10},{10,12},{12... | collective-permute-start | bytes 1228808 | tf_op jit(solution)/shard_map/sum_two/ppermute | solution.py:86
  319.0 36.7 %collective-permute-start.35 = (bf16[2,2,400,800]{3,2,1,0:T(8,128)(2,1)}, bf16[2,2,400,800]{3,2,1,0:T(8,128)(2,1)}, u32[]{:S(2)}, u32[]{:S(2)}) collective-permute-start(bf16[2,2,400,800]{3,2,1,0:T(8,128)(2,1)} %unit_other.1), channel_id=1, source_target_pairs={{0,8},{8,0},{16,24},{24,16},{1,9},{9,1},{17,25},{25,17},{2,10},{10... | collective-permute-start | bytes 7680008 | tf_op jit(solution)/shard_map/sum_two/unit_sum/ppermute | solution.py:60
  344.5 25.6 %collective-permute-start.34 = (bf16[8,200,800]{2,1,0:T(8,128)(2,1)}, bf16[8,200,800]{2,1,0:T(8,128)(2,1)S(1)}, u32[]{:S(2)}, u32[]{:S(2)}) collective-permute-start(bf16[8,200,800]{2,1,0:T(8,128)(2,1)} %get-tuple-element.116), channel_id=1, source_target_pairs={{0,8},{8,0},{16,24},{24,16},{1,9},{9,1},{17,25},{25,17},{2,10},{10... | collective-permute-start | bytes 7680008 | tf_op jit(solution)/shard_map/out_sum/ppermute | solution.py:60
  344.5 25.6 %all-to-all-start.1 = ((bf16[8,128,256]{2,1,0:T(8,128)(2,1)}), bf16[8,128,256]{2,1,0:T(8,128)(2,1)}, u32[]{:S(2)}, u32[]{:S(2)}) async-start(bf16[8,128,256]{2,1,0:T(8,128)(2,1)} %get-tuple-element.115), calls=%async_computation.1 | async-start | bytes 1048576 | tf_op jit(solution)/shard_map/all_to_all | solution.py:767
  349.3 160.9 %reduce-scatter.7.cloned.1.call-start = ((), (), s32[]{:S(2)}) async-start(), calls=%async_computation.7 | async-start | bytes 3225600
  392.3 23.9 %collective-permute-start.38 = (bf16[64,1600]{1,0:T(8,128)(2,1)}, bf16[64,1600]{1,0:T(8,128)(2,1)}, u32[]{:S(2)}, u32[]{:S(2)}) collective-permute-start(bf16[64,1600]{1,0:T(8,128)(2,1)} %get-tuple-element.236), channel_id=1, source_target_pairs={{0,1},{2,0},{4,2},{6,4},{7,6},{5,7},{3,5},{1,3},{8,9},{10,8},{12,1... | collective-permute-start | bytes 614408 | tf_op jit(solution)/shard_map/sum_one/ppermute | solution.py:86
  394.3 21.9 %collective-permute-start.36 = (bf16[64,1600]{1,0:T(8,128)(2,1)}, bf16[64,1600]{1,0:T(8,128)(2,1)}, u32[]{:S(2)}, u32[]{:S(2)}) collective-permute-start(bf16[64,1600]{1,0:T(8,128)(2,1)} %get-tuple-element.237), channel_id=1, source_target_pairs={{0,2},{2,4},{4,6},{6,7},{7,5},{5,3},{3,1},{1,0},{8,10},{10,12},{12... | collective-permute-start | bytes 614408 | tf_op jit(solution)/shard_map/sum_one/ppermute | solution.py:86
  415.9 25.4 %collective-permute-start.40 = (bf16[1,2,400,768]{3,2,1,0:T(8,128)(2,1)}, bf16[1,2,400,768]{3,2,1,0:T(8,128)(2,1)S(1)}, u32[]{:S(2)}, u32[]{:S(2)}) collective-permute-start(bf16[1,2,400,768]{3,2,1,0:T(8,128)(2,1)} %qkv_other.1), channel_id=1, source_target_pairs={{0,8},{8,0},{16,24},{24,16},{1,9},{9,1},{17,25},{25,17},{2,10},{10... | collective-permute-start | bytes 3686408 | tf_op jit(solution)/shard_map/sum_one/qkv_sum/ppermute | solution.py:60
  418.3 20.3 %collective-permute-start.39 = (bf16[128,1600]{1,0:T(8,128)(2,1)}, bf16[128,1600]{1,0:T(8,128)(2,1)}, u32[]{:S(2)}, u32[]{:S(2)}) collective-permute-start(bf16[128,1600]{1,0:T(8,128)(2,1)} %fusion.40), channel_id=1, source_target_pairs={{0,1},{2,0},{4,2},{6,4},{7,6},{5,7},{3,5},{1,3},{8,9},{10,8},{12,1... | collective-permute-start | bytes 1228808 | tf_op jit(solution)/shard_map/sum_one/ppermute | solution.py:86
  420.9 17.7 %collective-permute-start.37 = (bf16[128,1600]{1,0:T(8,128)(2,1)}, bf16[128,1600]{1,0:T(8,128)(2,1)}, u32[]{:S(2)}, u32[]{:S(2)}) collective-permute-start(bf16[128,1600]{1,0:T(8,128)(2,1)} %fusion.41), channel_id=1, source_target_pairs={{0,2},{2,4},{4,6},{6,7},{7,5},{5,3},{3,1},{1,0},{8,10},{10,12},{12... | collective-permute-start | bytes 1228808 | tf_op jit(solution)/shard_map/sum_one/ppermute | solution.py:86
  421.6 43.4 %collective-permute-start.47 = (bf16[2,400,800]{2,1,0:T(8,128)(2,1)}, bf16[2,400,800]{2,1,0:T(8,128)(2,1)S(1)}, u32[]{:S(2)}, u32[]{:S(2)}) collective-permute-start(bf16[2,400,800]{2,1,0:T(8,128)(2,1)} %get-tuple-element.145), channel_id=1, source_target_pairs={{0,16},{8,24},{16,0},{24,8},{1,17},{9,25},{17,1},{25,9},{2,18},{10... | collective-permute-start | bytes 3840008 | tf_op jit(solution)/shard_map/out_sum/unit_sum/ppermute | solution.py:60
  441.3 16.2 %collective-permute-start.42 = (bf16[128,1600]{1,0:T(8,128)(2,1)}, bf16[128,1600]{1,0:T(8,128)(2,1)}, u32[]{:S(2)}, u32[]{:S(2)}) collective-permute-start(bf16[128,1600]{1,0:T(8,128)(2,1)} %get-tuple-element.132), channel_id=1, source_target_pairs={{0,1},{2,0},{4,2},{6,4},{7,6},{5,7},{3,5},{1,3},{8,9},{10,8},{12,1... | collective-permute-start | bytes 1228808 | tf_op jit(solution)/shard_map/sum_one/ppermute | solution.py:86
  442.9 14.6 %collective-permute-start.41 = (bf16[128,1600]{1,0:T(8,128)(2,1)}, bf16[128,1600]{1,0:T(8,128)(2,1)}, u32[]{:S(2)}, u32[]{:S(2)}) collective-permute-start(bf16[128,1600]{1,0:T(8,128)(2,1)} %get-tuple-element.131), channel_id=1, source_target_pairs={{0,2},{2,4},{4,6},{6,7},{7,5},{5,3},{3,1},{1,0},{8,10},{10,12},{12... | collective-permute-start | bytes 1228808 | tf_op jit(solution)/shard_map/sum_one/ppermute | solution.py:86
  443.7 1.3 collective-permute-start.43
  445.0 12.1 %collective-permute-start.44 = (f32[19200]{0:T(1024)S(1)}, f32[19200]{0:T(1024)S(1)}, u32[]{:S(2)}, u32[]{:S(2)}) collective-permute-start(f32[19200]{0:T(1024)S(1)} %add.182), channel_id=1, source_target_pairs={{0,16},{8,24},{16,0},{24,8},{1,17},{9,25},{17,1},{25,9},{2,18},{10... | collective-permute-start | bytes 230408 | tf_op jit(solution)/shard_map/sum_one/sum_vectors/ppermute | solution.py:60
  453.2 25.5 %collective-permute-start.51 = (bf16[1,400,768]{2,1,0:T(8,128)(2,1)}, bf16[1,400,768]{2,1,0:T(8,128)(2,1)S(1)}, u32[]{:S(2)}, u32[]{:S(2)}) collective-permute-start(bf16[1,400,768]{2,1,0:T(8,128)(2,1)} %get-tuple-element.134), channel_id=1, source_target_pairs={{0,16},{8,24},{16,0},{24,8},{1,17},{9,25},{17,1},{25,9},{2,18},{10... | collective-permute-start | bytes 1843208 | tf_op jit(solution)/shard_map/sum_one/qkv_sum/ppermute | solution.py:60
  460.2 5.9 %collective-permute-start.48 = (f32[19200]{0:T(1024)S(1)}, f32[19200]{0:T(1024)S(1)}, u32[]{:S(2)}, u32[]{:S(2)}) collective-permute-start(f32[19200]{0:T(1024)S(1)} %add.183), channel_id=1, source_target_pairs={{0,1},{1,0},{2,3},{3,2},{4,5},{5,4},{6,7},{7,6},{8,9},{9,8},{10,11... | collective-permute-start | bytes 230408 | tf_op jit(solution)/shard_map/sum_one/sum_vectors/ppermute | solution.py:60
  463.0 46.1 %collective-permute-start.45 = (bf16[128,1600]{1,0:T(8,128)(2,1)}, bf16[128,1600]{1,0:T(8,128)(2,1)}, u32[]{:S(2)}, u32[]{:S(2)}) collective-permute-start(bf16[128,1600]{1,0:T(8,128)(2,1)} %get-tuple-element.140), channel_id=1, source_target_pairs={{0,2},{2,4},{4,6},{6,7},{7,5},{5,3},{3,1},{1,0},{8,10},{10,12},{12... | collective-permute-start | bytes 1228808 | tf_op jit(solution)/shard_map/sum_one/ppermute | solution.py:86
  464.3 45.8 %collective-permute-start.46 = (bf16[128,1600]{1,0:T(8,128)(2,1)}, bf16[128,1600]{1,0:T(8,128)(2,1)S(1)}, u32[]{:S(2)}, u32[]{:S(2)}) collective-permute-start(bf16[128,1600]{1,0:T(8,128)(2,1)} %get-tuple-element.141), channel_id=1, source_target_pairs={{0,1},{2,0},{4,2},{6,4},{7,6},{5,7},{3,5},{1,3},{8,9},{10,8},{12,1... | collective-permute-start | bytes 1228808 | tf_op jit(solution)/shard_map/sum_one/ppermute | solution.py:86
  466.1 10.7 %collective-permute-start.49 = (f32[19200]{0:T(1024)S(1)}, f32[19200]{0:T(1024)S(1)}, u32[]{:S(2)}, u32[]{:S(2)}) collective-permute-start(f32[19200]{0:T(1024)S(1)} %add.192), channel_id=1, source_target_pairs={{0,2},{1,3},{2,0},{3,1},{4,6},{5,7},{6,4},{7,5},{8,10},{9,11},{10,... | collective-permute-start | bytes 230408 | tf_op jit(solution)/shard_map/sum_one/sum_vectors/ppermute | solution.py:60
  476.9 9.3 %collective-permute-start.50 = (f32[19200]{0:T(1024)S(1)}, f32[19200]{0:T(1024)S(1)}, u32[]{:S(2)}, u32[]{:S(2)}) collective-permute-start(f32[19200]{0:T(1024)S(1)} %add.193), channel_id=1, source_target_pairs={{0,4},{1,5},{2,6},{3,7},{4,0},{5,1},{6,2},{7,3},{8,12},{9,13},{10,... | collective-permute-start | bytes 230408 | tf_op jit(solution)/shard_map/sum_one/sum_vectors/ppermute | solution.py:60
  481.6 9.9 %collective-permute-start.52 = (bf16[400,256]{1,0:T(8,128)(2,1)S(1)}, bf16[400,256]{1,0:T(8,128)(2,1)S(1)}, u32[]{:S(2)}, u32[]{:S(2)}) collective-permute-start(bf16[400,256]{1,0:T(8,128)(2,1)S(1)} %get-tuple-element.233), channel_id=1, source_target_pairs={{5,2},{3,4},{4,1},{0,5},{1,3},{2,6},{6,7},{13,10},{11,12},{12,9},{... | collective-permute-start | bytes 614408 | tf_op jit(solution)/shard_map/from_heads/ppermute | solution.py:208
  484.0 20.9 %collective-permute-start.53 = (bf16[400,256]{1,0:T(8,128)(2,1)S(1)}, bf16[400,256]{1,0:T(8,128)(2,1)S(1)}, u32[]{:S(2)}, u32[]{:S(2)}) collective-permute-start(bf16[400,256]{1,0:T(8,128)(2,1)S(1)} %get-tuple-element.232), channel_id=1, source_target_pairs={{3,6},{2,1},{5,5},{4,7},{0,2},{1,0},{11,14},{10,9},{13,13},{12,15}... | collective-permute-start | bytes 614408 | tf_op jit(solution)/shard_map/from_heads/ppermute | solution.py:208
  486.2 18.7 %collective-permute-start.54 = (bf16[400,256]{1,0:T(8,128)(2,1)S(1)}, bf16[400,256]{1,0:T(8,128)(2,1)S(1)}, u32[]{:S(2)}, u32[]{:S(2)}) collective-permute-start(bf16[400,256]{1,0:T(8,128)(2,1)S(1)} %get-tuple-element.231), channel_id=1, source_target_pairs={{1,5},{0,0},{3,1},{2,3},{4,4},{5,7},{6,2},{9,13},{8,8},{11,9},{10,... | collective-permute-start | bytes 614408 | tf_op jit(solution)/shard_map/from_heads/ppermute | solution.py:208
  491.5 15.6 %collective-permute-start.55 = (bf16[400,128]{1,0:T(8,128)(2,1)S(1)}, bf16[400,128]{1,0:T(8,128)(2,1)S(1)}, u32[]{:S(2)}, u32[]{:S(2)}) collective-permute-start(bf16[400,128]{1,0:T(8,128)(2,1)S(1)} %slice.321), channel_id=1, source_target_pairs={{4,2},{5,4},{0,3},{6,5},{2,0},{3,7},{1,6},{12,10},{13,12},{8,11},{... | collective-permute-start | bytes 307208 | tf_op jit(solution)/shard_map/from_heads/ppermute | solution.py:208
  512.0 5.8 %collective-permute-start.56 = (bf16[200,400]{1,0:T(8,128)(2,1)S(1)}, bf16[200,400]{1,0:T(8,128)(2,1)S(1)}, u32[]{:S(2)}, u32[]{:S(2)}) collective-permute-start(bf16[200,400]{1,0:T(8,128)(2,1)S(1)} %broadcast_select_fusion), channel_id=1, source_target_pairs={{0,16},{8,24},{16,0},{24,8},{1,17},{9,25},{17,1},{25,9},{2,18},{10... | collective-permute-start | bytes 480008 | tf_op jit(solution)/shard_map/out_sum/ppermute | solution.py:60
  (48 other events, 636.4 us)
Sparse Core Ops, SparseCore 0:
  53.2 78.3 all-gather.5
  133.7 87.8 all-gather.3
  261.7 100.8 reduce-scatter.4
  399.4 105.9 reduce-scatter.6

commit v3 on v2

--- a/solution.py
+++ b/solution.py
@@ -74,6 +74,10 @@
 
 def after(value, *first):
     return lax.optimization_barrier((value, *first))[0]
+
+
+def after_all(first, value, *more):
+    return after(value, *first, *more)
 
 
 def ring_order(count):
@@ -111,26 +115,31 @@
     half, rows = count // 2, far.shape[0] // 2
     riders = list(riders)
     up, down = far[:rows], far[rows:]
+    state = (up, down)
     for k in range(half - 1, -1, -1):
-        rode = riders.pop(0)(lambda x, *more: after(x, up, down, *more)) if riders else ()
+        rode = riders.pop(0)(functools.partial(after_all, state)) if riders else ()
         low_up, low_down = up.astype(LOW), down.astype(LOW)
         up, down = shift(low_up, 1).astype(FULL), shift(low_down, -1).astype(FULL)
         if k == half - 1:
             near, back = held[k], held[count - k]
-            up = jnp.concatenate([near[:rows] + up, near[rows:]])
-            down = jnp.concatenate([back[:rows], back[rows:] + down])
+            zero = jnp.zeros_like(up)
+            up = near.astype(FULL) + jnp.concatenate([up, zero])
+            down = back.astype(FULL) + jnp.concatenate([zero, down])
         elif k:
-            up, down = held[k] + up, held[count - k] + down
+            up, down = held[k].astype(FULL) + up, held[count - k].astype(FULL) + down
+        state = (up, down)
         if rode:
             up, down, *_ = lax.optimization_barrier((up, down, *rode))
-    return held[0] + up + down
-
-
-def sum_over(values, axis):
+    return held[0].astype(FULL) + up + down
+
+
+def sum_over(values, axis, *gate):
     bit = 1
     while bit < lax.axis_size(axis):
         values = values + swap(values, axis, bit)
         bit *= 2
+        if gate and 2 * bit == lax.axis_size(axis):
+            values = after(values, *gate)
     return values
 
 
@@ -212,26 +221,20 @@
     return [move(sent[:, start : start + size], pairs) for pairs, start, size in moves]
 
 
-def from_heads(sent, moves, pick_sent):
-    got = [
-        move(sent[:, start : start + size], [(b, a) for a, b in pairs]) for pairs, start, size in moves
-    ]
-    return dot_t(jnp.concatenate(got, axis=1), pick_sent)
-
-
 COST_US = {
-    "attend": 15,
-    "out": 8,
+    "attend": 60,
+    "out": 30,
     "hidden_grad": 9,
-    "hidden": 20,
+    "hidden": 80,
     "branch": 8,
-    "out_back": 12,
+    "out_back": 45,
     "unit_other": 8,
     "unit_mine": 10,
     "qkv_other": 5,
     "qkv_mine": 6,
-    "attend_back": 20,
+    "attend_back": 80,
     "project_back": 6,
+    "input_grad": 100,
 }
 
 
@@ -396,7 +399,12 @@
         gain_ref[1:2, :] += jnp.sum(total, axis=0, keepdims=True)
         for j in range(start // block, (start + step) // block):
             half, at = j // count * block, j * block - start
-            norm_ref[far_ref[j], half : half + block, :] = total[at : at + block, :]
+            norm_ref[far_ref[j], half : half + block, :] = total[at : at + block, :].astype(LOW)
+
+
+def input_grad_kernel(sum_ref, mid_ref, scaled_ref, rate_ref, gain_ref, out_ref):
+    part = norm_back(sum_ref[...], scaled_ref[...], rate_ref[...], gain_ref[...])
+    out_ref[...] = (mid_ref[...] + part).astype(LOW)
 
 
 def put_ring(offset, count, full_ref, low_ref, start, values):
@@ -408,7 +416,7 @@
 
     @pl.when(offset != count // 2)
     def _():
-        full_ref[offset, start:end, :] = values
+        full_ref[offset, start:end, :] = values.astype(LOW)
 
 
 def out_kernel(back_ref, input_ref, bias_ref, gain_ref, shift_ref, w_ref, mid_ref, low_ref, scaled_ref, rate_ref, attn_ref, wide_ref):
@@ -618,21 +626,25 @@
     def ride_second(hold):
         with jax.named_scope("to_heads"):
             held["second"] = take_rounds(hold(sent_heads), moves[first:])
+        held["out"] = lax.all_gather(jnp.transpose(hold(out_weight)), ("seq", "ctx"), axis=0)
         return held["second"]
 
     def ride_row_parts(hold):
-        held["out"] = lax.all_gather(jnp.transpose(hold(out_weight)), ("seq", "ctx"), axis=0)
         with jax.named_scope("qkv_parts"):
             pieces = jnp.concatenate(held["first"] + held["second"], axis=1)
             own = dot(hold(pieces), pick_kept).astype(LOW)
-            held["pair"] = jnp.stack([own, swap(own, "seq", 2)])
+            held["own"], held["row"] = own, swap(own, "seq", 2)
         return ()
 
+    def ride_core_parts(hold):
+        with jax.named_scope("qkv_parts"):
+            held["pair"] = jnp.stack([held["own"], hold(held["row"])])
+            held["peer"] = swap(held["pair"], "seq", 1)
+        return ()
+
     with jax.named_scope("gather_one"):
-        gathered = ring_gather(normed_one, [ride_first, ride_second, ride_row_parts])
-    with jax.named_scope("qkv_parts"):
-        qkv_pair = held["pair"]
-        qkv_peer = swap(qkv_pair, "seq", 1)
+        gathered = ring_gather(normed_one, [ride_first, ride_second, ride_row_parts, ride_core_parts])
+    qkv_pair, qkv_peer = held["pair"], held["peer"]
     out_t = held["out"].reshape(4, count, out_weight.shape[1], out_weight.shape[0])
     bias_rows = jnp.pad(qv_bias, ((0, 0), (0, count * group - width)))
     bias_mine = lax.dynamic_slice_in_dim(bias_rows, ctx * group, group, 1)
@@ -701,7 +713,7 @@
                 ((tokens, width), LOW),
                 ((tokens, units), LOW),
                 ((tokens, units), LOW),
-                ((count, rows, width), FULL),
+                ((count, rows, width), LOW),
                 ((rows, width), LOW),
                 ((1, units), FULL),
             ],
@@ -725,7 +737,7 @@
         units_grad = jnp.sum(hidden_pre_grad.astype(FULL), axis=0)
     def ride_branch(hold):
         (held["branch"],) = call(
-            branch_kernel, [((tokens, width), LOW)], [hidden, proj_cols], [], "branch", 2 * tokens * width * units
+            branch_kernel, [((tokens, width), LOW)], [hold(hidden), proj_cols], [], "branch", 2 * tokens * width * units
         )
         return (held["branch"],)
 
@@ -743,7 +755,7 @@
         return (other,)
 
     with jax.named_scope("sum_two"):
-        normed_two_grad = ring_sum(two_parts, two_far, [ride_branch, ride_other])
+        normed_two_grad = ring_sum(two_parts, two_far, [lambda hold: (), ride_branch, ride_other])
     branch_two = lax.psum_scatter(held["branch"], "ctx", scatter_dimension=0, tiled=True)
     block_output = (middle + branch_two.astype(FULL) + proj_bias).astype(LOW).reshape(block_input.shape)
 
@@ -765,23 +777,22 @@
         [pltpu.VMEM((rows, count * group), LOW), pltpu.VMEM((4, rows, quarter), LOW)],
     )
     grad_part = lax.all_to_all(attn_grad, "ctx", 0, 0, tiled=True)
-    with jax.named_scope("unit_sum"):
-        keep_units, send_units = call(
-            mine_kernel,
-            [((2, width // 4, units), FULL), ((2, width // 4, units), LOW)],
-            [held["peer"], two_tokens, hidden_pre_grad, cots, hidden],
-            [after(core_at, branch_low), row_at],
-            "unit_mine",
-            0,
-        )
     with jax.named_scope("out_sum"):
         got_core_out = swap(other, "seq", 1)
-        grad_part, got_core_out, block_output, send_units = lax.optimization_barrier(
-            (grad_part, got_core_out, block_output, send_units)
-        )
+        half_sum = (whole_out + got_core_out.astype(FULL)).astype(LOW)
+        with jax.named_scope("unit_sum"):
+            keep_units, send_units = call(
+                mine_kernel,
+                [((2, width // 4, units), FULL), ((2, width // 4, units), LOW)],
+                [held["peer"], two_tokens, hidden_pre_grad, cots, hidden],
+                [after(core_at, half_sum), row_at],
+                "unit_mine",
+                0,
+            )
+        grad_part, send_units = lax.optimization_barrier((grad_part, send_units))
         with jax.named_scope("unit_sum"):
             got_units = swap(send_units, "seq", 2)
-        half_sum = (whole_out + got_core_out.astype(FULL)).astype(LOW)
+        grad_part, half_sum = lax.optimization_barrier((grad_part, half_sum))
         out_sum = lax.psum_scatter(half_sum, "ctx", scatter_dimension=0)
 
     far_pair = pair_of[member[count // 2]]
@@ -797,9 +808,9 @@
     if fused:
         one_parts, one_lines = call(
             project_back_kernel,
-            [((count, rows, width), FULL), ((2, width), FULL)],
+            [((count, rows, width), LOW), ((2, width), FULL)],
             [qkv_grad, qkv_cols, one_tokens],
-            [far_of],
+            [after(far_of, got_units)],
             "project_back",
             0,
         )
@@ -828,7 +839,7 @@
                 other_kernel,
                 [((1, 2, width // 4, 3 * group), LOW)],
                 [one_tokens, qkv_grad],
-                [hold(core_at)],
+                [core_at],
                 "qkv_other",
                 0,
             )
@@ -848,30 +859,43 @@
             held["row"] = swap(send, "seq", 2)
         with jax.named_scope("sum_vectors"):
             held["flat"] = sum_over(hold(flat), "seq")
-        return (send, held["flat"])
+        return (send, block_output)
+
+    def ride_out(hold):
+        with jax.named_scope("out_sum"):
+            keep, send = ordered(row, out_sum[:, :quarter], out_sum[:, quarter:])
+            held["out_sum"] = keep.astype(FULL) + swap(send, "seq", 2).astype(FULL)
+        return (held["out_sum"],)
 
     def ride_heads(hold):
         with jax.named_scope("from_heads"):
             whole = (held["qkv"] + hold(held["row"]).astype(FULL))[0]
-            sent = dot_t(whole.astype(LOW), pick_kept).astype(LOW)
-            held["sent"] = sent
+            sent_back = dot_t(whole.astype(LOW), pick_kept).astype(LOW)
+            held["sent"] = take_rounds(sent_back, backward)
         with jax.named_scope("sum_vectors"):
             held["flat"] = sum_over(hold(held["flat"]), "ctx")
+        with jax.named_scope("unit_sum"):
             got = hold(got_units).astype(FULL)
             held["fc"] = keep_units[0] + got[0]
             held["proj"] = jnp.transpose(keep_units[1] + got[1])
-        return (out_sum, held["fc"], held["proj"])
-
+        return ()
+
+    backward = [([(b, a) for a, b in pairs], start, size) for pairs, start, size in moves]
     with jax.named_scope("sum_one"):
-        normed_one_grad = ring_sum(one_parts, one_far, [lambda hold: (), ride_core, ride_row, ride_heads])
+        normed_one_grad = ring_sum(one_parts, one_far, [ride_core, ride_row, ride_out, ride_heads])
     with jax.named_scope("out_sum"):
-        keep, send = ordered(row, out_sum[:, :quarter], out_sum[:, quarter:])
-        out_weight_grad = jnp.transpose(keep.astype(FULL) + swap(send, "seq", 2).astype(FULL))
-    middle_part = norm_back(normed_one_grad, scaled_one, rate_one, ln1_gain)
-    input_grad = (middle_grad + middle_part).astype(LOW).reshape(block_input.shape)
+        out_weight_grad = jnp.transpose(held["out_sum"])
+    (input_grad,) = call(
+        input_grad_kernel,
+        [((rows, width), LOW)],
+        [normed_one_grad, middle_grad, scaled_one, rate_one, ln1_gain[None]],
+        [],
+        "input_grad",
+        0,
+    )
+    input_grad = input_grad.reshape(block_input.shape)
     with jax.named_scope("from_heads"):
-        qkv_weight_grad = from_heads(held["sent"], moves, pick_sent)
-
+        qkv_weight_grad = dot_t(jnp.concatenate(held["sent"], axis=1), pick_sent)
     fc_weight_grad, proj_weight_grad = held["fc"], held["proj"]
     flat = held["flat"]
     vectors = flat[: 8 * width].reshape(8, width)

time: 532 us -> 520 us (0.977)
  starting transfers between devices: 114 us -> 104 us
  waiting for transfers between devices: 190 us -> 184 us
    ppermute x8, starting transfers between devices: 34.8 us -> 21.7 us  [move(): lax.ppermute(values, 'ctx', pairs)]
    ppermute x32, waiting for transfers between devices: 128 us -> 116 us  [shift(): lax.ppermute(values, 'ctx', [(order[i], order[(i + offset) % count]) for...]
    ppermute x32, starting transfers between devices: 56.2 us -> 62.6 us  [shift(): lax.ppermute(values, 'ctx', [(order[i], order[(i + offset) % count]) for...]
    add x6 -> x8, other arithmetic: 10.2 us -> 15 us  [the longest x4 7.38 us: ring_sum(): up, down = (held[k].astype(FULL) + up, held[count - k].astype(FULL) + down)]
    pallas_call x12 -> x13, Pallas kernels: 139 us -> 138 us  [call(): pl.pallas_call(kernel, in_specs=spec, out_specs=[pl.BlockSpec(memory_spac...]
  transfers between devices with their start and end apart: 63 -> 63, of which waited for: 28 -> 29; matrix products, arithmetic and copies ran while one was open for 10% -> 11% of each run, Pallas kernels for 17% -> 23%
where the time goes in v3:
time: 520 us; the launch traced here: 514 us
  waiting for transfers between devices  184 us (35%)
  Pallas kernels  138 us (27%)
  starting transfers between devices  104 us (20%)
  other arithmetic  34.2 us (7%)
  local copies, waits for them, and re-layouts  28.6 us (6%)
  between operations  17.8 us (3%)
  matrix products  6.8 us (1%)
    pallas_call x13, Pallas kernels, call(): pl.pallas_call(kernel, in_specs=spec, out_specs=[pl.BlockSpec(memory_spac...  138 us
    ppermute x32, waiting for transfers between devices, shift(): lax.ppermute(values, 'ctx', [(order[i], order[(i + offset) % count]) for...  116 us
    ppermute x32, starting transfers between devices, shift(): lax.ppermute(values, 'ctx', [(order[i], order[(i + offset) % count]) for...  62.6 us
    ppermute x17, waiting for transfers between devices, swap(): return lax.ppermute(values, axis, [(i, i ^ bit) for i in range(count)])  44.8 us
    ppermute x8, starting transfers between devices, move(): lax.ppermute(values, 'ctx', pairs)  21.7 us
    ppermute x8, waiting for transfers between devices, move(): lax.ppermute(values, 'ctx', pairs)  20.4 us
    ppermute x17, starting transfers between devices, swap(): return lax.ppermute(values, axis, [(i, i ^ bit) for i in range(count)])  10.8 us
  transfers between devices with their start and end apart: 63, of which 29 were waited for; matrix products, arithmetic and copies ran while one was open for 11% of the time, Pallas kernels for 23%

profile of v3, /device:TPU:0, one launch (start us, length us, event | category | flops | bytes accessed | tf_op | source)
XLA Modules:
  0.0 514.1 jit_solution(9463467121893965391)
XLA Ops:
  11.0 3.0 collective-permute-start.2
  17.0 7.0 %collective-permute-start.1 = (bf16[400,256]{1,0:T(8,128)(2,1)S(1)}, bf16[400,256]{1,0:T(8,128)(2,1)S(1)}, u32[]{:S(2)}, u32[]{:S(2)}) collective-permute-start(bf16[400,256]{1,0:T(8,128)(2,1)S(1)} %get-tuple-element.233), channel_id=1, source_target_pairs={{6,3},{1,2},{5,5},{7,4},{2,0},{0,1},{14,11},{9,10},{13,13},{15,12}... | collective-permute-start | bytes 614408 | tf_op jit(solution)/shard_map/gather_one/to_heads/ppermute | solution.py:217
  24.1 6.4 %collective-permute-done = bf16[400,256]{1,0:T(8,128)(2,1)S(1)} collective-permute-done((bf16[400,256]{1,0:T(8,128)(2,1)S(1)}, bf16[400,256]{1,0:T(8,128)(2,1)S(1)}, u32[]{:S(2)}, u32[]{:S(2)}) %collective-permute-start) | collective-permute-done | bytes 204832 | tf_op jit(solution)/shard_map/gather_one/to_heads/ppermute | solution.py:217
  33.1 7.8 %collective-permute-start.6 = (bf16[128,1600]{1,0:T(8,128)(2,1)S(1)}, bf16[128,1600]{1,0:T(8,128)(2,1)S(1)}, u32[]{:S(2)}, u32[]{:S(2)}) collective-permute-start(bf16[128,1600]{1,0:T(8,128)(2,1)S(1)} %collective-permute-done.2.rest_8_), channel_id=1, source_target_pairs={{0,2},{2,4},{4,6},{6,7},{7,5},{5,3},{3,1},{1,0},{8,10},{10,12},{12... | collective-permute-start | bytes 1228808 | tf_op jit(solution)/shard_map/gather_one/ppermute | solution.py:90
  40.9 4.6 collective-permute-start.7
  47.4 14.0 %collective-permute-done.5 = bf16[400,128]{1,0:T(8,128)(2,1)S(1)} collective-permute-done((bf16[400,128]{1,0:T(8,128)(2,1)S(1)}, bf16[400,128]{1,0:T(8,128)(2,1)S(1)}, u32[]{:S(2)}, u32[]{:S(2)}) %collective-permute-start.5) | collective-permute-done | bytes 102432 | tf_op jit(solution)/shard_map/gather_one/to_heads/ppermute | solution.py:217
  64.2 2.0 collective-permute-start.10
  66.2 11.9 %collective-permute-done.9.rest_6_ = bf16[128,1600]{1,0:T(8,128)(2,1)S(1)} collective-permute-done((bf16[128,1600]{1,0:T(8,128)(2,1)S(1)}, bf16[128,1600]{1,0:T(8,128)(2,1)S(1)}, u32[]{:S(2)}, u32[]{:S(2)}) %collective-permute-start.9) | collective-permute-done | bytes 409632 | tf_op jit(solution)/shard_map/gather_one/ppermute | solution.py:90
  80.3 2.2 copy.56
  85.0 2.3 collective-permute-start.13
  88.4 8.4 %collective-permute-done.12.rest_4_ = bf16[64,1600]{1,0:T(8,128)(2,1)S(1)} collective-permute-done((bf16[64,1600]{1,0:T(8,128)(2,1)S(1)}, bf16[64,1600]{1,0:T(8,128)(2,1)S(1)}, u32[]{:S(2)}, u32[]{:S(2)}) %collective-permute-start.12) | collective-permute-done | bytes 204832 | tf_op jit(solution)/shard_map/gather_one/ppermute | solution.py:90
  96.8 4.6 collective-permute-done.13.rest_5_
  102.1 15.0 %attend.1 = (bf16[1024,1600]{1,0:T(8,128)(2,1)}, bf16[1600,768]{1,0:T(8,128)(2,1)}, bf16[1024,768]{1,0:T(8,128)(2,1)}, f32[1024,256]{1,0:T(8,128)}, bf16[8,128,256]{2,1,0:T(8,128)(2,1)}, /*index=5*/f32[1024,4]{1,0:T(8,128)}) custom-call(s32[8]{0:T(128)} %get-tuple-element.250.member_ref, s32[1]{0:T(128)} %bitcast.1.place_ref, s32[8]{0:T(128)} %pair_of_ref.1, ...), custom_call_target="tpu_custom_call" | custom-call | flops 1000 | bytes 180000000 | tf_op jit(solution)/shard_map/attend/pallas_call | solution.py:246
  118.5 5.0 all-to-all-start
  127.0 14.4 %collective-permute-done.15 = bf16[400,800]{1,0:T(8,128)(2,1)S(1)} collective-permute-done((bf16[400,800]{1,0:T(8,128)(2,1)S(1)}, bf16[400,800]{1,0:T(8,128)(2,1)S(1)}, u32[]{:S(2)}, u32[]{:S(2)}) %collective-permute-start.15) | collective-permute-done | bytes 640032 | tf_op jit(solution)/shard_map/unit_parts/ppermute | solution.py:60
  142.7 3.0 all-to-all-done.back_ref
  145.7 7.4 %out.1 = (f32[128,1600]{1,0:T(8,128)}, bf16[128,1600]{1,0:T(8,128)(2,1)}, f32[128,1600]{1,0:T(8,128)}, f32[128,1]{1,0:T(8,128)}, bf16[128,1600]{1,0:T(8,128)(2,1)}) custom-call(bf16[8,128,256]{2,1,0:T(8,128)(2,1)} %all-to-all-done.back_ref, bf16[128,1600]{1,0:T(8,128)(2,1)} %bitcast.99, f32[1,1600]{1,0:T(1,128)} %broadcast_in_dim.59.bias_ref, ...), custom_call_target="tpu_custom_call" | custom-call | flops 1000 | bytes 90000000 | tf_op jit(solution)/shard_map/out/pallas_call | solution.py:246
  153.0 2.0 collective-permute-start.18
  155.6 13.7 %collective-permute-done.21.rest_8_ = bf16[128,1600]{1,0:T(8,128)(2,1)S(1)} collective-permute-done((bf16[128,1600]{1,0:T(8,128)(2,1)}, bf16[128,1600]{1,0:T(8,128)(2,1)S(1)}, u32[]{:S(2)}, u32[]{:S(2)}) %collective-permute-start.21) | collective-permute-done | bytes 409632 | tf_op jit(solution)/shard_map/gather_two/ppermute | solution.py:90
  169.3 4.7 collective-permute-start.22
  174.1 6.2 %collective-permute-done.18.rest_1_ = bf16[128,1600]{1,0:T(8,128)(2,1)S(1)} collective-permute-done((bf16[128,1600]{1,0:T(8,128)(2,1)}, bf16[128,1600]{1,0:T(8,128)(2,1)S(1)}, u32[]{:S(2)}, u32[]{:S(2)}) %collective-permute-start.18) | collective-permute-done | bytes 409632 | tf_op jit(solution)/shard_map/gather_two/ppermute | solution.py:90
  180.3 8.5 %collective-permute-done.22.rest_7_ = bf16[128,1600]{1,0:T(8,128)(2,1)S(1)} collective-permute-done((bf16[128,1600]{1,0:T(8,128)(2,1)S(1)}, bf16[128,1600]{1,0:T(8,128)(2,1)S(1)}, u32[]{:S(2)}, u32[]{:S(2)}) %collective-permute-start.22) | collective-permute-done | bytes 409632 | tf_op jit(solution)/shard_map/gather_two/ppermute | solution.py:90
  188.8 8.2 %collective-permute-start.23 = (bf16[128,1600]{1,0:T(8,128)(2,1)S(1)}, bf16[128,1600]{1,0:T(8,128)(2,1)S(1)}, u32[]{:S(2)}, u32[]{:S(2)}) collective-permute-start(bf16[128,1600]{1,0:T(8,128)(2,1)S(1)} %collective-permute-done.22.rest_7_), channel_id=1, source_target_pairs={{0,2},{2,4},{4,6},{6,7},{7,5},{5,3},{3,1},{1,0},{8,10},{10,12},{12... | collective-permute-start | bytes 1228808 | tf_op jit(solution)/shard_map/gather_two/ppermute | solution.py:90
  197.0 4.4 collective-permute-done.19.rest_2_
  201.4 5.9 %collective-permute-done.23.rest_6_ = bf16[128,1600]{1,0:T(8,128)(2,1)S(1)} collective-permute-done((bf16[128,1600]{1,0:T(8,128)(2,1)S(1)}, bf16[128,1600]{1,0:T(8,128)(2,1)S(1)}, u32[]{:S(2)}, u32[]{:S(2)}) %collective-permute-start.23) | collective-permute-done | bytes 409632 | tf_op jit(solution)/shard_map/gather_two/ppermute | solution.py:90
  208.1 2.2 collective-permute-start.24
  211.7 2.3 collective-permute-start.25
  216.6 8.8 %hidden_grad.1 = (bf16[1600,800]{1,0:T(8,128)(2,1)}, f32[1024,800]{1,0:T(8,128)}) custom-call(s32[1]{0:T(128)} %bitcast.1.place_ref, bf16[1024,1600]{1,0:T(8,128)(2,1)} %all-gather.4.cloned.1.call-done.cot_ref.rest_2_, bf16[2,400,800]{2,1,0:T(8,128)(2,1)} %copy-done.5, bf16[2,400,800]{2,1,0:T(8,128)(2,1)} %collective-permute-done.17.peer_ref), custom_call_target="tpu_custom_call" | custom-call | flops 1000 | bytes 27000000 | tf_op jit(solution)/shard_map/hidden_grad/pallas_call | solution.py:246
  225.4 18.6 %hidden.1 = (bf16[1024,1600]{1,0:T(8,128)(2,1)}, bf16[1024,800]{1,0:T(8,128)(2,1)}, bf16[1024,800]{1,0:T(8,128)(2,1)}, bf16[8,128,1600]{2,1,0:T(8,128)(2,1)}, bf...) custom-call(s32[8]{0:T(128)} %get-tuple-element.250.member_ref, s32[8]{0:T(128)} %fusion.23.offset_ref, s32[1]{0:T(128)} %bitcast.1.place_ref, ...), custom_call_target="tpu_custom_call" | custom-call | flops 1000 | bytes 240000000 | tf_op jit(solution)/shard_map/hidden/pallas_call | solution.py:246
  245.1 2.1 collective-permute-start.27
  247.4 8.1 %branch.1 = bf16[1024,1600]{1,0:T(8,128)(2,1)} custom-call(bf16[1024,800]{1,0:T(8,128)(2,1)} %get-tuple-element.109.value_ref.rest_3_, bf16[1600,800]{1,0:T(8,128)(2,1)} %get-tuple-element.110.w_ref), custom_call_target="tpu_custom_call" | custom-call | flops 1000 | bytes 24000000 | tf_op jit(solution)/shard_map/sum_two/branch/pallas_call | solution.py:246
  256.8 2.1 collective-permute-start.29
  258.9 14.7 %collective-permute-done.29 = bf16[128,1600]{1,0:T(8,128)(2,1)S(1)} collective-permute-done((bf16[128,1600]{1,0:T(8,128)(2,1)S(1)}, bf16[128,1600]{1,0:T(8,128)(2,1)S(1)}, u32[]{:S(2)}, u32[]{:S(2)}) %collective-permute-start.29) | collective-permute-done | bytes 409632 | tf_op jit(solution)/shard_map/sum_two/ppermute | solution.py:90
  273.6 2.3 collective-permute-done.28
  277.3 6.6 %collective-permute-start.31 = (bf16[128,1600]{1,0:T(8,128)(2,1)S(1)}, bf16[128,1600]{1,0:T(8,128)(2,1)S(1)}, u32[]{:S(2)}, u32[]{:S(2)}) collective-permute-start(bf16[128,1600]{1,0:T(8,128)(2,1)S(1)} %get-tuple-element.112), channel_id=1, source_target_pairs={{0,1},{2,0},{4,2},{6,4},{7,6},{5,7},{3,5},{1,3},{8,9},{10,8},{12,1... | collective-permute-start | bytes 1228808 | tf_op jit(solution)/shard_map/sum_two/ppermute | solution.py:90
  283.9 11.2 %unit_other.1 = bf16[2,2,400,800]{3,2,1,0:T(8,128)(2,1)} custom-call(s32[1]{0:T(128)} %bitcast.22.core_ref, bf16[1024,1600]{1,0:T(8,128)(2,1)} %get-tuple-element.114.rest_0_, bf16[1024,800]{1,0:T(8,128)(2,1)} %get-tuple-element.115.rest_1_, bf16[1024,1600]{1,0:T(8,128)(2,1)} %all-gather.4.cloned.1.call-done.cot_ref.rest_2_, ...), custom_call_target="tpu_custom_call" | custom-call | flops 1000 | bytes 24000000 | tf_op jit(solution)/shard_map/sum_two/unit_sum/unit_other/pallas_call | solution.py:246
  295.0 10.1 %collective-permute-done.31 = bf16[128,1600]{1,0:T(8,128)(2,1)S(1)} collective-permute-done((bf16[128,1600]{1,0:T(8,128)(2,1)S(1)}, bf16[128,1600]{1,0:T(8,128)(2,1)S(1)}, u32[]{:S(2)}, u32[]{:S(2)}) %collective-permute-start.31) | collective-permute-done | bytes 409632 | tf_op jit(solution)/shard_map/sum_two/ppermute | solution.py:90
  306.6 3.7 collective-permute-start.33
  310.7 8.7 %collective-permute-done.33 = bf16[128,1600]{1,0:T(8,128)(2,1)S(1)} collective-permute-done((bf16[128,1600]{1,0:T(8,128)(2,1)S(1)}, bf16[128,1600]{1,0:T(8,128)(2,1)S(1)}, u32[]{:S(2)}, u32[]{:S(2)}) %collective-permute-start.33) | collective-permute-done | bytes 409632 | tf_op jit(solution)/shard_map/sum_two/ppermute | solution.py:90
  319.5 4.0 collective-permute-done.32
  323.4 2.1 fusion.18.sum_ref
  325.5 10.9 %out_back.1 = (f32[128,1600]{1,0:T(8,128)}, bf16[128,1600]{1,0:T(8,128)(2,1)}, bf16[8,128,256]{2,1,0:T(8,128)(2,1)}, f32[4,1600]{1,0:T(4,128)}, f32[8,200,800]{2,1,0:T(8,128)}, /*index=5*/bf16[8,200,800]{2,1,0:T(8,128)(2,1)}) custom-call(s32[1]{0:T(128)} %bitcast.22.core_ref, f32[128,1600]{1,0:T(8,128)} %fusion.18.sum_ref, bf16[128,1600]{1,0:T(8,128)(2,1)} %bitcast.101, ...), custom_call_target="tpu_custom_call" | custom-call | flops 1000 | bytes 135000000 | tf_op jit(solution)/shard_map/out_back/pallas_call | solution.py:246
  336.9 4.2 all-to-all-start.1
  341.2 4.2 collective-permute-done.34
  345.4 5.6 %add_convert_fusion = bf16[8,200,800]{2,1,0:T(8,128)(2,1)} fusion(f32[8,200,800]{2,1,0:T(8,128)} %get-tuple-element.122, bf16[8,200,800]{2,1,0:T(8,128)(2,1)} %collective-permute-done.34), kind=kLoop, calls=%fused_computation.1 | loop fusion | flops 3840000 | bytes 10240000 | tf_op jit(solution)/shard_map/out_sum/convert_element_type | solution.py:782
  351.0 13.2 %unit_mine.1 = (f32[2,400,800]{2,1,0:T(8,128)}, bf16[2,400,800]{2,1,0:T(8,128)(2,1)}) custom-call(s32[1]{0:T(128)} %bitcast.22.core_ref, s32[1]{0:T(128)} %bitcast.28.row_ref, bf16[2,2,400,800]{3,2,1,0:T(8,128)(2,1)} %collective-permute-done.35.got_ref, bf16[1024,1600]{1,0:T(8,128)(2,1)} %get-tuple-element.114.rest_0_, ...), custom_call_target="tpu_custom_call" | custom-call | flops 1000 | bytes 30000000 | tf_op jit(solution)/shard_map/out_sum/unit_sum/unit_mine/pallas_call | solution.py:246
  370.8 20.4 %attend_back.1 = (bf16[1024,768]{1,0:T(8,128)(2,1)}, f32[1,768]{1,0:T(1,128)}, bf16[128,1600]{1,0:T(8,128)(2,1)}) custom-call(s32[16]{0:T(128)} %pad_add_fusion.who_ref, s32[2]{0:T(128)} %pad_add_fusion.1.far_ref, bf16[1024,768]{1,0:T(8,128)(2,1)} %get-tuple-element.128.qkv_ref, bf16[1600,768]{1,0:T(8,128)(2,1)} %get-tuple-element.129.w_ref, ...), custom_call_target="tpu_custom_call" | custom-call | flops 1000 | bytes 240000000 | tf_op jit(solution)/shard_map/attend_back/pallas_call | solution.py:246
  391.2 6.1 %qkv_other.1 = bf16[1,2,400,768]{3,2,1,0:T(8,128)(2,1)} custom-call(s32[1]{0:T(128)} %bitcast.22.core_ref, bf16[1024,1600]{1,0:T(8,128)(2,1)} %get-tuple-element.135.x_ref.rest_0_, bf16[1024,768]{1,0:T(8,128)(2,1)} %get-tuple-element.134.grad_ref.rest_1_), custom_call_target="tpu_custom_call" | custom-call | flops 1000 | bytes 15000000 | tf_op jit(solution)/shard_map/sum_one/qkv_sum/qkv_other/pallas_call | solution.py:246
  402.2 8.4 %project_back.1 = (bf16[8,128,1600]{2,1,0:T(8,128)(2,1)}, f32[2,1600]{1,0:T(2,128)}) custom-call(s32[16]{0:T(128)} %gather_fusion, bf16[1024,768]{1,0:T(8,128)(2,1)} %get-tuple-element.134.grad_ref.rest_1_, bf16[1600,768]{1,0:T(8,128)(2,1)} %get-tuple-element.129.w_ref, bf16[1024,1600]{1,0:T(8,128)(2,1)} %get-tuple-element.135.x_ref.rest_0_), custom_call_target="tpu_custom_call" | custom-call | flops 1000 | bytes 18000000 | tf_op jit(solution)/shard_map/project_back/pallas_call | solution.py:246
  410.5 2.7 collective-permute-done.38
  413.2 2.2 convert_add_fusion.2
  418.0 7.2 %qkv_mine.1 = (f32[1,400,768]{2,1,0:T(8,128)}, bf16[1,400,768]{2,1,0:T(8,128)(2,1)}) custom-call(s32[1]{0:T(128)} %bitcast.22.core_ref, s32[1]{0:T(128)} %bitcast.28.row_ref, bf16[1,2,400,768]{3,2,1,0:T(8,128)(2,1)} %copy-done.10, bf16[1024,1600]{1,0:T(8,128)(2,1)} %get-tuple-element.135.x_ref.rest_0_, bf16[1024,768]{1,0:T(8,128)(2,1)} %get-tuple-element.134.grad_ref.rest_1_), custom_call_target="tpu_custom_call" | custom-call | flops 1000 | bytes 18000000 | tf_op jit(solution)/shard_map/sum_one/qkv_sum/qkv_mine/pallas_call | solution.py:246
  425.2 5.2 %collective-permute-done.41 = bf16[128,1600]{1,0:T(8,128)(2,1)S(1)} collective-permute-done((bf16[128,1600]{1,0:T(8,128)(2,1)}, bf16[128,1600]{1,0:T(8,128)(2,1)S(1)}, u32[]{:S(2)}, u32[]{:S(2)}) %collective-permute-start.41) | collective-permute-done | bytes 409632 | tf_op jit(solution)/shard_map/sum_one/ppermute | solution.py:90
  431.7 2.2 convert_add_fusion.1
  440.9 14.6 %collective-permute-done.48 = f32[19200]{0:T(1024)S(1)} collective-permute-done((f32[19200]{0:T(1024)S(1)}, f32[19200]{0:T(1024)S(1)}, u32[]{:S(2)}, u32[]{:S(2)}) %collective-permute-start.48) | collective-permute-done | bytes 76832 | tf_op jit(solution)/shard_map/sum_one/sum_vectors/ppermute | solution.py:60
  456.5 2.3 convert_add_fusion
  459.9 2.0 fusion.8
  463.6 2.6 collective-permute-start.54
  466.9 6.0 %collective-permute-start.56 = (bf16[400,128]{1,0:T(8,128)(2,1)S(1)}, bf16[400,128]{1,0:T(8,128)(2,1)S(1)}, u32[]{:S(2)}, u32[]{:S(2)}) collective-permute-start(bf16[400,128]{1,0:T(8,128)(2,1)S(1)} %slice.261), channel_id=1, source_target_pairs={{4,2},{5,4},{0,3},{6,5},{2,0},{3,7},{1,6},{12,10},{13,12},{8,11},{... | collective-permute-start | bytes 307208 | tf_op jit(solution)/shard_map/sum_one/from_heads/ppermute | solution.py:217
  475.0 5.0 collective-permute-done.50
  484.8 4.6 collective-permute-done.44
  492.7 3.0 fusion.2
  500.1 2.2 fusion.17.sum_ref
  502.3 2.9 input_grad.1
  (271 shorter events, 78.5 us)
Async XLA Ops:
  7.2 138.5 %all-gather.6.cloned.1.call-start = ((), (), s32[]{:S(2)}) async-start(), calls=%async_computation.6 | async-start | bytes 6758400 | tf_op jit(solution)/shard_map/gather_one/all_gather | solution.py:629
  11.0 19.4 %collective-permute-start.2 = (bf16[128,1600]{1,0:T(8,128)(2,1)S(1)}, bf16[128,1600]{1,0:T(8,128)(2,1)S(1)}, u32[]{:S(2)}, u32[]{:S(2)}) collective-permute-start(bf16[128,1600]{1,0:T(8,128)(2,1)S(1)} %get-tuple-element.236.rest_0_), channel_id=1, source_target_pairs={{0,2},{2,4},{4,6},{6,7},{7,5},{5,3},{3,1},{1,0},{8,10},{10,12},{12... | collective-permute-start | bytes 1228808 | tf_op jit(solution)/shard_map/gather_one/ppermute | solution.py:90
  14.0 16.4 %collective-permute-start.3 = (bf16[128,1600]{1,0:T(8,128)(2,1)S(1)}, bf16[128,1600]{1,0:T(8,128)(2,1)S(1)}, u32[]{:S(2)}, u32[]{:S(2)}) collective-permute-start(bf16[128,1600]{1,0:T(8,128)(2,1)S(1)} %get-tuple-element.236.rest_0_), channel_id=1, source_target_pairs={{0,1},{2,0},{4,2},{6,4},{7,6},{5,7},{3,5},{1,3},{8,9},{10,8},{12,1... | collective-permute-start | bytes 1228808 | tf_op jit(solution)/shard_map/gather_one/ppermute | solution.py:90
  15.7 14.7 %collective-permute-start = (bf16[400,256]{1,0:T(8,128)(2,1)S(1)}, bf16[400,256]{1,0:T(8,128)(2,1)S(1)}, u32[]{:S(2)}, u32[]{:S(2)}) collective-permute-start(bf16[400,256]{1,0:T(8,128)(2,1)S(1)} %get-tuple-element.234), channel_id=1, source_target_pairs={{2,5},{4,3},{1,4},{5,0},{3,1},{6,2},{7,6},{10,13},{12,11},{9,12},{... | collective-permute-start | bytes 614408 | tf_op jit(solution)/shard_map/gather_one/to_heads/ppermute | solution.py:217
  17.0 13.4 %collective-permute-start.1 = (bf16[400,256]{1,0:T(8,128)(2,1)S(1)}, bf16[400,256]{1,0:T(8,128)(2,1)S(1)}, u32[]{:S(2)}, u32[]{:S(2)}) collective-permute-start(bf16[400,256]{1,0:T(8,128)(2,1)S(1)} %get-tuple-element.233), channel_id=1, source_target_pairs={{6,3},{1,2},{5,5},{7,4},{2,0},{0,1},{14,11},{9,10},{13,13},{15,12}... | collective-permute-start | bytes 614408 | tf_op jit(solution)/shard_map/gather_one/to_heads/ppermute | solution.py:217
  31.4 185.2 %all-gather.4.cloned.1.call-start = ((), (), s32[]{:S(2)}) async-start(), calls=%async_computation.4 | async-start | bytes 3833856 | tf_op jit(solution)/shard_map/all_gather | solution.py:675
  32.3 15.1 %collective-permute-start.4 = (bf16[400,256]{1,0:T(8,128)(2,1)S(1)}, bf16[400,256]{1,0:T(8,128)(2,1)S(1)}, u32[]{:S(2)}, u32[]{:S(2)}) collective-permute-start(bf16[400,256]{1,0:T(8,128)(2,1)S(1)} %slice.192), channel_id=1, source_target_pairs={{5,1},{0,0},{1,3},{3,2},{4,4},{7,5},{2,6},{13,9},{8,8},{9,11},{11,... | collective-permute-start | bytes 614408 | tf_op jit(solution)/shard_map/gather_one/to_heads/ppermute | solution.py:217
  33.1 28.4 %collective-permute-start.6 = (bf16[128,1600]{1,0:T(8,128)(2,1)S(1)}, bf16[128,1600]{1,0:T(8,128)(2,1)S(1)}, u32[]{:S(2)}, u32[]{:S(2)}) collective-permute-start(bf16[128,1600]{1,0:T(8,128)(2,1)S(1)} %collective-permute-done.2.rest_8_), channel_id=1, source_target_pairs={{0,2},{2,4},{4,6},{6,7},{7,5},{5,3},{3,1},{1,0},{8,10},{10,12},{12... | collective-permute-start | bytes 1228808 | tf_op jit(solution)/shard_map/gather_one/ppermute | solution.py:90
  40.9 20.6 %collective-permute-start.7 = (bf16[128,1600]{1,0:T(8,128)(2,1)S(1)}, bf16[128,1600]{1,0:T(8,128)(2,1)S(1)}, u32[]{:S(2)}, u32[]{:S(2)}) collective-permute-start(bf16[128,1600]{1,0:T(8,128)(2,1)S(1)} %collective-permute-done.3.rest_1_), channel_id=1, source_target_pairs={{0,1},{2,0},{4,2},{6,4},{7,6},{5,7},{3,5},{1,3},{8,9},{10,8},{12,1... | collective-permute-start | bytes 1228808 | tf_op jit(solution)/shard_map/gather_one/ppermute | solution.py:90
  45.5 15.9 %collective-permute-start.5 = (bf16[400,128]{1,0:T(8,128)(2,1)S(1)}, bf16[400,128]{1,0:T(8,128)(2,1)S(1)}, u32[]{:S(2)}, u32[]{:S(2)}) collective-permute-start(bf16[400,128]{1,0:T(8,128)(2,1)S(1)} %slice.193), channel_id=1, source_target_pairs={{2,4},{4,5},{3,0},{5,6},{0,2},{7,3},{6,1},{10,12},{12,13},{11,8},{... | collective-permute-start | bytes 307208 | tf_op jit(solution)/shard_map/gather_one/to_heads/ppermute | solution.py:217
  62.5 17.6 %collective-permute-start.8 = (bf16[400,768]{1,0:T(8,128)(2,1)S(1)}, bf16[400,768]{1,0:T(8,128)(2,1)S(1)}, u32[]{:S(2)}, u32[]{:S(2)}) collective-permute-start(bf16[400,768]{1,0:T(8,128)(2,1)S(1)} %fusion.10), channel_id=1, source_target_pairs={{0,16},{8,24},{16,0},{24,8},{1,17},{9,25},{17,1},{25,9},{2,18},{10... | collective-permute-start | bytes 1843208 | tf_op jit(solution)/shard_map/gather_one/qkv_parts/ppermute | solution.py:60
  64.2 13.9 %collective-permute-start.9 = (bf16[128,1600]{1,0:T(8,128)(2,1)S(1)}, bf16[128,1600]{1,0:T(8,128)(2,1)S(1)}, u32[]{:S(2)}, u32[]{:S(2)}) collective-permute-start(bf16[128,1600]{1,0:T(8,128)(2,1)S(1)} %collective-permute-done.6.rest_7_), channel_id=1, source_target_pairs={{0,2},{2,4},{4,6},{6,7},{7,5},{5,3},{3,1},{1,0},{8,10},{10,12},{12... | collective-permute-start | bytes 1228808 | tf_op jit(solution)/shard_map/gather_one/ppermute | solution.py:90
  64.2 15.9 %collective-permute-start.10 = (bf16[128,1600]{1,0:T(8,128)(2,1)S(1)}, bf16[128,1600]{1,0:T(8,128)(2,1)S(1)}, u32[]{:S(2)}, u32[]{:S(2)}) collective-permute-start(bf16[128,1600]{1,0:T(8,128)(2,1)S(1)} %collective-permute-done.7.rest_2_), channel_id=1, source_target_pairs={{0,1},{2,0},{4,2},{6,4},{7,6},{5,7},{3,5},{1,3},{8,9},{10,8},{12,1... | collective-permute-start | bytes 1228808 | tf_op jit(solution)/shard_map/gather_one/ppermute | solution.py:90
  80.2 3.0 collective-permute-start.11
  83.2 33.9 %collective-permute-start.14 = (bf16[400,800]{1,0:T(8,128)(2,1)}, bf16[400,800]{1,0:T(8,128)(2,1)}, u32[]{:S(2)}, u32[]{:S(2)}) collective-permute-start(bf16[400,800]{1,0:T(8,128)(2,1)} %bitcast.107), channel_id=1, source_target_pairs={{0,16},{8,24},{16,0},{24,8},{1,17},{9,25},{17,1},{25,9},{2,18},{10... | collective-permute-start | bytes 1920008 | tf_op jit(solution)/shard_map/unit_parts/ppermute | solution.py:60
  84.9 11.9 %collective-permute-start.12 = (bf16[64,1600]{1,0:T(8,128)(2,1)S(1)}, bf16[64,1600]{1,0:T(8,128)(2,1)S(1)}, u32[]{:S(2)}, u32[]{:S(2)}) collective-permute-start(bf16[64,1600]{1,0:T(8,128)(2,1)S(1)} %slice.249), channel_id=1, source_target_pairs={{0,2},{2,4},{4,6},{6,7},{7,5},{5,3},{3,1},{1,0},{8,10},{10,12},{12... | collective-permute-start | bytes 614408 | tf_op jit(solution)/shard_map/gather_one/ppermute | solution.py:90
  85.0 16.4 %collective-permute-start.13 = (bf16[64,1600]{1,0:T(8,128)(2,1)S(1)}, bf16[64,1600]{1,0:T(8,128)(2,1)S(1)}, u32[]{:S(2)}, u32[]{:S(2)}) collective-permute-start(bf16[64,1600]{1,0:T(8,128)(2,1)S(1)} %slice.250), channel_id=1, source_target_pairs={{0,1},{2,0},{4,2},{6,4},{7,6},{5,7},{3,5},{1,3},{8,9},{10,8},{12,1... | collective-permute-start | bytes 614408 | tf_op jit(solution)/shard_map/gather_one/ppermute | solution.py:90
  118.5 36.5 %copy-start.5 = (bf16[2,400,800]{2,1,0:T(8,128)(2,1)}, bf16[2,400,800]{2,1,0:T(8,128)(2,1)S(1)}, u32[]{:S(2)}) copy-start(bf16[2,400,800]{2,1,0:T(8,128)(2,1)S(1)} %pad_maximum_fusion.pair_ref) | copy-start | bytes 3840004
  118.5 27.1 %all-to-all-start = ((bf16[8,128,256]{2,1,0:T(8,128)(2,1)}), bf16[8,128,256]{2,1,0:T(8,128)(2,1)}, u32[]{:S(2)}, u32[]{:S(2)}) async-start(bf16[8,128,256]{2,1,0:T(8,128)(2,1)} %get-tuple-element.95), calls=%async_computation | async-start | bytes 1048576 | tf_op jit(solution)/shard_map/all_to_all | solution.py:677
  123.6 310.4 %reduce-scatter.5.cloned.1.call-start = ((), (), s32[]{:S(2)}) async-start(), calls=%async_computation.5 | async-start | bytes 3833856 | tf_op jit(solution)/shard_map/reduce_scatter | solution.py:759
  123.6 17.7 %collective-permute-start.15 = (bf16[400,800]{1,0:T(8,128)(2,1)S(1)}, bf16[400,800]{1,0:T(8,128)(2,1)S(1)}, u32[]{:S(2)}, u32[]{:S(2)}) collective-permute-start(bf16[400,800]{1,0:T(8,128)(2,1)S(1)} %copy-done.18), channel_id=1, source_target_pairs={{0,16},{8,24},{16,0},{24,8},{1,17},{9,25},{17,1},{25,9},{2,18},{10... | collective-permute-start | bytes 1920008 | tf_op jit(solution)/shard_map/unit_parts/ppermute | solution.py:60
  153.0 16.3 %collective-permute-start.21 = (bf16[128,1600]{1,0:T(8,128)(2,1)}, bf16[128,1600]{1,0:T(8,128)(2,1)S(1)}, u32[]{:S(2)}, u32[]{:S(2)}) collective-permute-start(bf16[128,1600]{1,0:T(8,128)(2,1)} %get-tuple-element.105.rest_0_), channel_id=1, source_target_pairs={{0,2},{2,4},{4,6},{6,7},{7,5},{5,3},{3,1},{1,0},{8,10},{10,12},{12... | collective-permute-start | bytes 1228808 | tf_op jit(solution)/shard_map/gather_two/ppermute | solution.py:90
  153.0 27.3 %collective-permute-start.18 = (bf16[128,1600]{1,0:T(8,128)(2,1)}, bf16[128,1600]{1,0:T(8,128)(2,1)S(1)}, u32[]{:S(2)}, u32[]{:S(2)}) collective-permute-start(bf16[128,1600]{1,0:T(8,128)(2,1)} %get-tuple-element.105.rest_0_), channel_id=1, source_target_pairs={{0,1},{2,0},{4,2},{6,4},{7,6},{5,7},{3,5},{1,3},{8,9},{10,8},{12,1... | collective-permute-start | bytes 1228808 | tf_op jit(solution)/shard_map/gather_two/ppermute | solution.py:90
  155.1 61.6 %collective-permute-start.17 = (bf16[2,400,800]{2,1,0:T(8,128)(2,1)S(1)}, bf16[2,400,800]{2,1,0:T(8,128)(2,1)}, u32[]{:S(2)}, u32[]{:S(2)}) collective-permute-start(bf16[2,400,800]{2,1,0:T(8,128)(2,1)S(1)} %pad_maximum_fusion.pair_ref), channel_id=1, source_target_pairs={{0,8},{8,0},{16,24},{24,16},{1,9},{9,1},{17,25},{25,17},{2,10},{10... | collective-permute-start | bytes 3840008 | tf_op jit(solution)/shard_map/unit_parts/ppermute | solution.py:60
  155.1 70.4 %collective-permute-start.16 = (bf16[2,400,800]{2,1,0:T(8,128)(2,1)S(1)}, bf16[2,400,800]{2,1,0:T(8,128)(2,1)}, u32[]{:S(2)}, u32[]{:S(2)}) collective-permute-start(bf16[2,400,800]{2,1,0:T(8,128)(2,1)S(1)} %pad_maximum_fusion.1.pair_ref), channel_id=1, source_target_pairs={{0,8},{8,0},{16,24},{24,16},{1,9},{9,1},{17,25},{25,17},{2,10},{10... | collective-permute-start | bytes 3840008 | tf_op jit(solution)/shard_map/unit_parts/ppermute | solution.py:60
  169.3 19.4 %collective-permute-start.22 = (bf16[128,1600]{1,0:T(8,128)(2,1)S(1)}, bf16[128,1600]{1,0:T(8,128)(2,1)S(1)}, u32[]{:S(2)}, u32[]{:S(2)}) collective-permute-start(bf16[128,1600]{1,0:T(8,128)(2,1)S(1)} %collective-permute-done.21.rest_8_), channel_id=1, source_target_pairs={{0,2},{2,4},{4,6},{6,7},{7,5},{5,3},{3,1},{1,0},{8,10},{10,12},{12... | collective-permute-start | bytes 1228808 | tf_op jit(solution)/shard_map/gather_two/ppermute | solution.py:90
  180.3 21.1 %collective-permute-start.19 = (bf16[128,1600]{1,0:T(8,128)(2,1)S(1)}, bf16[128,1600]{1,0:T(8,128)(2,1)S(1)}, u32[]{:S(2)}, u32[]{:S(2)}) collective-permute-start(bf16[128,1600]{1,0:T(8,128)(2,1)S(1)} %collective-permute-done.18.rest_1_), channel_id=1, source_target_pairs={{0,1},{2,0},{4,2},{6,4},{7,6},{5,7},{3,5},{1,3},{8,9},{10,8},{12,1... | collective-permute-start | bytes 1228808 | tf_op jit(solution)/shard_map/gather_two/ppermute | solution.py:90
  188.8 18.6 %collective-permute-start.23 = (bf16[128,1600]{1,0:T(8,128)(2,1)S(1)}, bf16[128,1600]{1,0:T(8,128)(2,1)S(1)}, u32[]{:S(2)}, u32[]{:S(2)}) collective-permute-start(bf16[128,1600]{1,0:T(8,128)(2,1)S(1)} %collective-permute-done.22.rest_7_), channel_id=1, source_target_pairs={{0,2},{2,4},{4,6},{6,7},{7,5},{5,3},{3,1},{1,0},{8,10},{10,12},{12... | collective-permute-start | bytes 1228808 | tf_op jit(solution)/shard_map/gather_two/ppermute | solution.py:90
  201.4 8.9 %collective-permute-start.20 = (bf16[128,1600]{1,0:T(8,128)(2,1)S(1)}, bf16[128,1600]{1,0:T(8,128)(2,1)S(1)}, u32[]{:S(2)}, u32[]{:S(2)}) collective-permute-start(bf16[128,1600]{1,0:T(8,128)(2,1)S(1)} %collective-permute-done.19.rest_2_), channel_id=1, source_target_pairs={{0,1},{2,0},{4,2},{6,4},{7,6},{5,7},{3,5},{1,3},{8,9},{10,8},{12,1... | collective-permute-start | bytes 1228808 | tf_op jit(solution)/shard_map/gather_two/ppermute | solution.py:90
  208.1 17.4 %collective-permute-start.24 = (bf16[64,1600]{1,0:T(8,128)(2,1)}, bf16[64,1600]{1,0:T(8,128)(2,1)}, u32[]{:S(2)}, u32[]{:S(2)}) collective-permute-start(bf16[64,1600]{1,0:T(8,128)(2,1)} %slice.251), channel_id=1, source_target_pairs={{0,2},{2,4},{4,6},{6,7},{7,5},{5,3},{3,1},{1,0},{8,10},{10,12},{12... | collective-permute-start | bytes 614408 | tf_op jit(solution)/shard_map/gather_two/ppermute | solution.py:90
  211.7 13.7 %collective-permute-start.25 = (bf16[64,1600]{1,0:T(8,128)(2,1)}, bf16[64,1600]{1,0:T(8,128)(2,1)}, u32[]{:S(2)}, u32[]{:S(2)}) collective-permute-start(bf16[64,1600]{1,0:T(8,128)(2,1)} %slice.252), channel_id=1, source_target_pairs={{0,1},{2,0},{4,2},{6,4},{7,6},{5,7},{3,5},{1,3},{8,9},{10,8},{12,1... | collective-permute-start | bytes 614408 | tf_op jit(solution)/shard_map/gather_two/ppermute | solution.py:90
  245.1 10.4 %collective-permute-start.27 = (bf16[64,1600]{1,0:T(8,128)(2,1)S(1)}, bf16[64,1600]{1,0:T(8,128)(2,1)S(1)}, u32[]{:S(2)}, u32[]{:S(2)}) collective-permute-start(bf16[64,1600]{1,0:T(8,128)(2,1)S(1)} %get-tuple-element.239), channel_id=1, source_target_pairs={{0,1},{2,0},{4,2},{6,4},{7,6},{5,7},{3,5},{1,3},{8,9},{10,8},{12,1... | collective-permute-start | bytes 614408 | tf_op jit(solution)/shard_map/sum_two/ppermute | solution.py:90
  247.2 8.3 %collective-permute-start.26 = (bf16[64,1600]{1,0:T(8,128)(2,1)S(1)}, bf16[64,1600]{1,0:T(8,128)(2,1)S(1)}, u32[]{:S(2)}, u32[]{:S(2)}) collective-permute-start(bf16[64,1600]{1,0:T(8,128)(2,1)S(1)} %get-tuple-element.240), channel_id=1, source_target_pairs={{0,2},{2,4},{4,6},{6,7},{7,5},{5,3},{3,1},{1,0},{8,10},{10,12},{12... | collective-permute-start | bytes 614408 | tf_op jit(solution)/shard_map/sum_two/ppermute | solution.py:90
  256.8 16.8 %collective-permute-start.29 = (bf16[128,1600]{1,0:T(8,128)(2,1)S(1)}, bf16[128,1600]{1,0:T(8,128)(2,1)S(1)}, u32[]{:S(2)}, u32[]{:S(2)}) collective-permute-start(bf16[128,1600]{1,0:T(8,128)(2,1)S(1)} %get-tuple-element.228), channel_id=1, source_target_pairs={{0,1},{2,0},{4,2},{6,4},{7,6},{5,7},{3,5},{1,3},{8,9},{10,8},{12,1... | collective-permute-start | bytes 1228808 | tf_op jit(solution)/shard_map/sum_two/ppermute | solution.py:90
  258.8 17.1 %collective-permute-start.28 = (bf16[128,1600]{1,0:T(8,128)(2,1)S(1)}, bf16[128,1600]{1,0:T(8,128)(2,1)S(1)}, u32[]{:S(2)}, u32[]{:S(2)}) collective-permute-start(bf16[128,1600]{1,0:T(8,128)(2,1)S(1)} %get-tuple-element.229), channel_id=1, source_target_pairs={{0,2},{2,4},{4,6},{6,7},{7,5},{5,3},{3,1},{1,0},{8,10},{10,12},{12... | collective-permute-start | bytes 1228808 | tf_op jit(solution)/shard_map/sum_two/ppermute | solution.py:90
  277.3 27.9 %collective-permute-start.31 = (bf16[128,1600]{1,0:T(8,128)(2,1)S(1)}, bf16[128,1600]{1,0:T(8,128)(2,1)S(1)}, u32[]{:S(2)}, u32[]{:S(2)}) collective-permute-start(bf16[128,1600]{1,0:T(8,128)(2,1)S(1)} %get-tuple-element.112), channel_id=1, source_target_pairs={{0,1},{2,0},{4,2},{6,4},{7,6},{5,7},{3,5},{1,3},{8,9},{10,8},{12,1... | collective-permute-start | bytes 1228808 | tf_op jit(solution)/shard_map/sum_two/ppermute | solution.py:90
  283.9 21.3 %collective-permute-start.30 = (bf16[128,1600]{1,0:T(8,128)(2,1)S(1)}, bf16[128,1600]{1,0:T(8,128)(2,1)S(1)}, u32[]{:S(2)}, u32[]{:S(2)}) collective-permute-start(bf16[128,1600]{1,0:T(8,128)(2,1)S(1)} %get-tuple-element.111), channel_id=1, source_target_pairs={{0,2},{2,4},{4,6},{6,7},{7,5},{5,3},{3,1},{1,0},{8,10},{10,12},{12... | collective-permute-start | bytes 1228808 | tf_op jit(solution)/shard_map/sum_two/ppermute | solution.py:90
  306.6 12.9 %collective-permute-start.33 = (bf16[128,1600]{1,0:T(8,128)(2,1)S(1)}, bf16[128,1600]{1,0:T(8,128)(2,1)S(1)}, u32[]{:S(2)}, u32[]{:S(2)}) collective-permute-start(bf16[128,1600]{1,0:T(8,128)(2,1)S(1)} %get-tuple-element.117), channel_id=1, source_target_pairs={{0,1},{2,0},{4,2},{6,4},{7,6},{5,7},{3,5},{1,3},{8,9},{10,8},{12,1... | collective-permute-start | bytes 1228808 | tf_op jit(solution)/shard_map/sum_two/ppermute | solution.py:90
  310.3 13.1 %collective-permute-start.32 = (bf16[128,1600]{1,0:T(8,128)(2,1)S(1)}, bf16[128,1600]{1,0:T(8,128)(2,1)S(1)}, u32[]{:S(2)}, u32[]{:S(2)}) collective-permute-start(bf16[128,1600]{1,0:T(8,128)(2,1)S(1)} %get-tuple-element.116), channel_id=1, source_target_pairs={{0,2},{2,4},{4,6},{6,7},{7,5},{5,3},{3,1},{1,0},{8,10},{10,12},{12... | collective-permute-start | bytes 1228808 | tf_op jit(solution)/shard_map/sum_two/ppermute | solution.py:90
  336.4 9.0 %collective-permute-start.34 = (bf16[8,200,800]{2,1,0:T(8,128)(2,1)}, bf16[8,200,800]{2,1,0:T(8,128)(2,1)}, u32[]{:S(2)}, u32[]{:S(2)}) collective-permute-start(bf16[8,200,800]{2,1,0:T(8,128)(2,1)} %get-tuple-element.123), channel_id=1, source_target_pairs={{0,8},{8,0},{16,24},{24,16},{1,9},{9,1},{17,25},{25,17},{2,10},{10... | collective-permute-start | bytes 7680008 | tf_op jit(solution)/shard_map/out_sum/ppermute | solution.py:60
  336.4 14.6 %collective-permute-start.35 = (bf16[2,2,400,800]{3,2,1,0:T(8,128)(2,1)S(1)}, bf16[2,2,400,800]{3,2,1,0:T(8,128)(2,1)}, u32[]{:S(2)}, u32[]{:S(2)}) collective-permute-start(bf16[2,2,400,800]{3,2,1,0:T(8,128)(2,1)S(1)} %copy-done.8), channel_id=1, source_target_pairs={{0,8},{8,0},{16,24},{24,16},{1,9},{9,1},{17,25},{25,17},{2,10},{10... | collective-permute-start | bytes 7680008 | tf_op jit(solution)/shard_map/sum_two/unit_sum/ppermute | solution.py:60
  336.9 27.3 %all-to-all-start.1 = ((bf16[8,128,256]{2,1,0:T(8,128)(2,1)}), bf16[8,128,256]{2,1,0:T(8,128)(2,1)}, u32[]{:S(2)}, u32[]{:S(2)}) async-start(bf16[8,128,256]{2,1,0:T(8,128)(2,1)} %get-tuple-element.121), calls=%async_computation.2 | async-start | bytes 1048576 | tf_op jit(solution)/shard_map/all_to_all | solution.py:779
  341.1 140.4 %reduce-scatter.7.cloned.1.call-start = ((), (), s32[]{:S(2)}) async-start(), calls=%async_computation.7 | async-start | bytes 3225600
  364.2 38.0 %collective-permute-start.36 = (bf16[2,400,800]{2,1,0:T(8,128)(2,1)}, bf16[2,400,800]{2,1,0:T(8,128)(2,1)S(1)}, u32[]{:S(2)}, u32[]{:S(2)}) collective-permute-start(bf16[2,400,800]{2,1,0:T(8,128)(2,1)} %get-tuple-element.126), channel_id=1, source_target_pairs={{0,16},{8,24},{16,0},{24,8},{1,17},{9,25},{17,1},{25,9},{2,18},{10... | collective-permute-start | bytes 3840008 | tf_op jit(solution)/shard_map/out_sum/unit_sum/ppermute | solution.py:60
  397.2 18.2 %collective-permute-start.39 = (bf16[1,2,400,768]{3,2,1,0:T(8,128)(2,1)}, bf16[1,2,400,768]{3,2,1,0:T(8,128)(2,1)S(1)}, u32[]{:S(2)}, u32[]{:S(2)}) collective-permute-start(bf16[1,2,400,768]{3,2,1,0:T(8,128)(2,1)} %qkv_other.1), channel_id=1, source_target_pairs={{0,8},{8,0},{16,24},{24,16},{1,9},{9,1},{17,25},{25,17},{2,10},{10... | collective-permute-start | bytes 3686408 | tf_op jit(solution)/shard_map/sum_one/qkv_sum/ppermute | solution.py:60
  398.9 14.3 %collective-permute-start.38 = (bf16[64,1600]{1,0:T(8,128)(2,1)}, bf16[64,1600]{1,0:T(8,128)(2,1)S(1)}, u32[]{:S(2)}, u32[]{:S(2)}) collective-permute-start(bf16[64,1600]{1,0:T(8,128)(2,1)} %get-tuple-element.237), channel_id=1, source_target_pairs={{0,1},{2,0},{4,2},{6,4},{7,6},{5,7},{3,5},{1,3},{8,9},{10,8},{12,1... | collective-permute-start | bytes 614408 | tf_op jit(solution)/shard_map/sum_one/ppermute | solution.py:90
  398.9 14.3 %collective-permute-start.37 = (bf16[64,1600]{1,0:T(8,128)(2,1)S(1)}, bf16[64,1600]{1,0:T(8,128)(2,1)S(1)}, u32[]{:S(2)}, u32[]{:S(2)}) collective-permute-start(bf16[64,1600]{1,0:T(8,128)(2,1)S(1)} %get-tuple-element.238), channel_id=1, source_target_pairs={{0,2},{2,4},{4,6},{6,7},{7,5},{5,3},{3,1},{1,0},{8,10},{10,12},{12... | collective-permute-start | bytes 614408 | tf_op jit(solution)/shard_map/sum_one/ppermute | solution.py:90
  415.4 15.0 %collective-permute-start.41 = (bf16[128,1600]{1,0:T(8,128)(2,1)}, bf16[128,1600]{1,0:T(8,128)(2,1)S(1)}, u32[]{:S(2)}, u32[]{:S(2)}) collective-permute-start(bf16[128,1600]{1,0:T(8,128)(2,1)} %get-tuple-element.139), channel_id=1, source_target_pairs={{0,1},{2,0},{4,2},{6,4},{7,6},{5,7},{3,5},{1,3},{8,9},{10,8},{12,1... | collective-permute-start | bytes 1228808 | tf_op jit(solution)/shard_map/sum_one/ppermute | solution.py:90
  415.4 16.3 %collective-permute-start.40 = (bf16[128,1600]{1,0:T(8,128)(2,1)}, bf16[128,1600]{1,0:T(8,128)(2,1)}, u32[]{:S(2)}, u32[]{:S(2)}) collective-permute-start(bf16[128,1600]{1,0:T(8,128)(2,1)} %get-tuple-element.138), channel_id=1, source_target_pairs={{0,2},{2,4},{4,6},{6,7},{7,5},{5,3},{3,1},{1,0},{8,10},{10,12},{12... | collective-permute-start | bytes 1228808 | tf_op jit(solution)/shard_map/sum_one/ppermute | solution.py:90
  435.1 21.4 %collective-permute-start.43 = (bf16[128,1600]{1,0:T(8,128)(2,1)}, bf16[128,1600]{1,0:T(8,128)(2,1)S(1)}, u32[]{:S(2)}, u32[]{:S(2)}) collective-permute-start(bf16[128,1600]{1,0:T(8,128)(2,1)} %get-tuple-element.143), channel_id=1, source_target_pairs={{0,1},{2,0},{4,2},{6,4},{7,6},{5,7},{3,5},{1,3},{8,9},{10,8},{12,1... | collective-permute-start | bytes 1228808 | tf_op jit(solution)/shard_map/sum_one/ppermute | solution.py:90
  436.2 20.3 %collective-permute-start.42 = (bf16[128,1600]{1,0:T(8,128)(2,1)S(1)}, bf16[128,1600]{1,0:T(8,128)(2,1)}, u32[]{:S(2)}, u32[]{:S(2)}) collective-permute-start(bf16[128,1600]{1,0:T(8,128)(2,1)S(1)} %get-tuple-element.142), channel_id=1, source_target_pairs={{0,2},{2,4},{4,6},{6,7},{7,5},{5,3},{3,1},{1,0},{8,10},{10,12},{12... | collective-permute-start | bytes 1228808 | tf_op jit(solution)/shard_map/sum_one/ppermute | solution.py:90
  437.3 1.3 collective-permute-start.47
  437.3 22.5 %collective-permute-start.52 = (bf16[1,400,768]{2,1,0:T(8,128)(2,1)}, bf16[1,400,768]{2,1,0:T(8,128)(2,1)}, u32[]{:S(2)}, u32[]{:S(2)}) collective-permute-start(bf16[1,400,768]{2,1,0:T(8,128)(2,1)} %get-tuple-element.141), channel_id=1, source_target_pairs={{0,16},{8,24},{16,0},{24,8},{1,17},{9,25},{17,1},{25,9},{2,18},{10... | collective-permute-start | bytes 1843208 | tf_op jit(solution)/shard_map/sum_one/qkv_sum/ppermute | solution.py:60
  438.6 16.9 %collective-permute-start.48 = (f32[19200]{0:T(1024)S(1)}, f32[19200]{0:T(1024)S(1)}, u32[]{:S(2)}, u32[]{:S(2)}) collective-permute-start(f32[19200]{0:T(1024)S(1)} %add.196), channel_id=1, source_target_pairs={{0,16},{8,24},{16,0},{24,8},{1,17},{9,25},{17,1},{25,9},{2,18},{10... | collective-permute-start | bytes 230408 | tf_op jit(solution)/shard_map/sum_one/sum_vectors/ppermute | solution.py:60
  458.8 14.2 %collective-permute-start.49 = (f32[19200]{0:T(1024)S(1)}, f32[19200]{0:T(1024)S(1)}, u32[]{:S(2)}, u32[]{:S(2)}) collective-permute-start(f32[19200]{0:T(1024)S(1)} %add.197), channel_id=1, source_target_pairs={{0,1},{1,0},{2,3},{3,2},{4,5},{5,4},{6,7},{7,6},{8,9},{9,8},{10,11... | collective-permute-start | bytes 230408 | tf_op jit(solution)/shard_map/sum_one/sum_vectors/ppermute | solution.py:60
  462.0 19.3 %collective-permute-start.53 = (bf16[400,256]{1,0:T(8,128)(2,1)S(1)}, bf16[400,256]{1,0:T(8,128)(2,1)S(1)}, u32[]{:S(2)}, u32[]{:S(2)}) collective-permute-start(bf16[400,256]{1,0:T(8,128)(2,1)S(1)} %get-tuple-element.232), channel_id=1, source_target_pairs={{5,2},{3,4},{4,1},{0,5},{1,3},{2,6},{6,7},{13,10},{11,12},{12,9},{... | collective-permute-start | bytes 614408 | tf_op jit(solution)/shard_map/sum_one/from_heads/ppermute | solution.py:217
  463.6 17.8 %collective-permute-start.54 = (bf16[400,256]{1,0:T(8,128)(2,1)S(1)}, bf16[400,256]{1,0:T(8,128)(2,1)S(1)}, u32[]{:S(2)}, u32[]{:S(2)}) collective-permute-start(bf16[400,256]{1,0:T(8,128)(2,1)S(1)} %get-tuple-element.231), channel_id=1, source_target_pairs={{3,6},{2,1},{5,5},{4,7},{0,2},{1,0},{11,14},{10,9},{13,13},{12,15}... | collective-permute-start | bytes 614408 | tf_op jit(solution)/shard_map/sum_one/from_heads/ppermute | solution.py:217
  466.2 15.2 %collective-permute-start.55 = (bf16[400,256]{1,0:T(8,128)(2,1)S(1)}, bf16[400,256]{1,0:T(8,128)(2,1)S(1)}, u32[]{:S(2)}, u32[]{:S(2)}) collective-permute-start(bf16[400,256]{1,0:T(8,128)(2,1)S(1)} %get-tuple-element.230), channel_id=1, source_target_pairs={{1,5},{0,0},{3,1},{2,3},{4,4},{5,7},{6,2},{9,13},{8,8},{11,9},{10,... | collective-permute-start | bytes 614408 | tf_op jit(solution)/shard_map/sum_one/from_heads/ppermute | solution.py:217
  466.9 14.6 %collective-permute-start.56 = (bf16[400,128]{1,0:T(8,128)(2,1)S(1)}, bf16[400,128]{1,0:T(8,128)(2,1)S(1)}, u32[]{:S(2)}, u32[]{:S(2)}) collective-permute-start(bf16[400,128]{1,0:T(8,128)(2,1)S(1)} %slice.261), channel_id=1, source_target_pairs={{4,2},{5,4},{0,3},{6,5},{2,0},{3,7},{1,6},{12,10},{13,12},{8,11},{... | collective-permute-start | bytes 307208 | tf_op jit(solution)/shard_map/sum_one/from_heads/ppermute | solution.py:217
  473.1 7.0 %collective-permute-start.50 = (f32[19200]{0:T(1024)S(1)}, f32[19200]{0:T(1024)S(1)}, u32[]{:S(2)}, u32[]{:S(2)}) collective-permute-start(f32[19200]{0:T(1024)S(1)} %add.198), channel_id=1, source_target_pairs={{0,2},{1,3},{2,0},{3,1},{4,6},{5,7},{6,4},{7,5},{8,10},{9,11},{10,... | collective-permute-start | bytes 230408 | tf_op jit(solution)/shard_map/sum_one/sum_vectors/ppermute | solution.py:60
  480.1 15.6 %collective-permute-start.51 = (f32[19200]{0:T(1024)S(1)}, f32[19200]{0:T(1024)S(1)}, u32[]{:S(2)}, u32[]{:S(2)}) collective-permute-start(f32[19200]{0:T(1024)S(1)} %add.199), channel_id=1, source_target_pairs={{0,4},{1,5},{2,6},{3,7},{4,0},{5,1},{6,2},{7,3},{8,12},{9,13},{10,... | collective-permute-start | bytes 230408 | tf_op jit(solution)/shard_map/sum_one/sum_vectors/ppermute | solution.py:60
  483.5 5.9 %collective-permute-start.44 = (bf16[200,400]{1,0:T(8,128)(2,1)S(1)}, bf16[200,400]{1,0:T(8,128)(2,1)S(1)}, u32[]{:S(2)}, u32[]{:S(2)}) collective-permute-start(bf16[200,400]{1,0:T(8,128)(2,1)S(1)} %broadcast_select_fusion), channel_id=1, source_target_pairs={{0,16},{8,24},{16,0},{24,8},{1,17},{9,25},{17,1},{25,9},{2,18},{10... | collective-permute-start | bytes 480008 | tf_op jit(solution)/shard_map/sum_one/out_sum/ppermute | solution.py:60
  490.6 9.4 %collective-permute-start.46 = (bf16[128,1600]{1,0:T(8,128)(2,1)S(1)}, bf16[128,1600]{1,0:T(8,128)(2,1)S(1)}, u32[]{:S(2)}, u32[]{:S(2)}) collective-permute-start(bf16[128,1600]{1,0:T(8,128)(2,1)S(1)} %copy-done.19), channel_id=1, source_target_pairs={{0,1},{2,0},{4,2},{6,4},{7,6},{5,7},{3,5},{1,3},{8,9},{10,8},{12,1... | collective-permute-start | bytes 1228808 | tf_op jit(solution)/shard_map/sum_one/ppermute | solution.py:90
  491.4 8.7 %collective-permute-start.45 = (bf16[128,1600]{1,0:T(8,128)(2,1)S(1)}, bf16[128,1600]{1,0:T(8,128)(2,1)S(1)}, u32[]{:S(2)}, u32[]{:S(2)}) collective-permute-start(bf16[128,1600]{1,0:T(8,128)(2,1)S(1)} %get-tuple-element.145), channel_id=1, source_target_pairs={{0,2},{2,4},{4,6},{6,7},{7,5},{5,3},{3,1},{1,0},{8,10},{10,12},{12... | collective-permute-start | bytes 1228808 | tf_op jit(solution)/shard_map/sum_one/ppermute | solution.py:90
  (46 other events, 610.9 us)
Sparse Core Ops, SparseCore 0:
  31.6 89.4 all-gather.5
  123.2 80.9 all-gather.3
  255.6 94.0 reduce-scatter.4
  369.7 90.9 reduce-scatter.6

commit v4 on v3

--- a/solution.py
+++ b/solution.py
@@ -792,7 +792,6 @@
         grad_part, send_units = lax.optimization_barrier((grad_part, send_units))
         with jax.named_scope("unit_sum"):
             got_units = swap(send_units, "seq", 2)
-        grad_part, half_sum = lax.optimization_barrier((grad_part, half_sum))
         out_sum = lax.psum_scatter(half_sum, "ctx", scatter_dimension=0)
 
     far_pair = pair_of[member[count // 2]]
@@ -847,24 +846,27 @@
         return (held["core"],)
 
     def ride_row(hold):
+        with jax.named_scope("sum_vectors"):
+            held["flat"] = sum_over(hold(flat), "seq")
         with jax.named_scope("qkv_sum"):
             held["qkv"], send = call(
                 mine_kernel,
                 [((1, width // 4, 3 * group), FULL), ((1, width // 4, 3 * group), LOW)],
                 [held["core"], one_tokens, qkv_grad],
-                [hold(core_at), row_at],
+                [hold(core_at, held["flat"]), row_at],
                 "qkv_mine",
                 0,
             )
             held["row"] = swap(send, "seq", 2)
-        with jax.named_scope("sum_vectors"):
-            held["flat"] = sum_over(hold(flat), "seq")
         return (send, block_output)
 
     def ride_out(hold):
         with jax.named_scope("out_sum"):
             keep, send = ordered(row, out_sum[:, :quarter], out_sum[:, quarter:])
-            held["out_sum"] = keep.astype(FULL) + swap(send, "seq", 2).astype(FULL)
+            some = send.shape[0] // 2
+            first = swap(send[:some], "seq", 2)
+            second = swap(after(send[some:], first), "seq", 2)
+            held["out_sum"] = keep.astype(FULL) + jnp.concatenate([first, second]).astype(FULL)
         return (held["out_sum"],)
 
     def ride_heads(hold):

time: 520 us -> 518 us (level)
  waiting for transfers between devices: 184 us -> 175 us
  starting transfers between devices: 104 us -> 112 us
    ppermute x17 -> x18, waiting for transfers between devices: 44.8 us -> 31.1 us  [swap(): return lax.ppermute(values, axis, [(i, i ^ bit) for i in range(count)])]
    ppermute x17 -> x18, starting transfers between devices: 10.8 us -> 13.6 us  [swap(): return lax.ppermute(values, axis, [(i, i ^ bit) for i in range(count)])]
  transfers between devices with their start and end apart: 63 -> 64, of which waited for: 29 -> 28; matrix products, arithmetic and copies ran while one was open for 11% -> 11% of each run, Pallas kernels for 23% -> 23%
where the time goes in v4:
time: 518 us; the launch traced here: 513 us
  waiting for transfers between devices  175 us (34%)
  Pallas kernels  138 us (27%)
  starting transfers between devices  112 us (22%)
  other arithmetic  34.4 us (7%)
  local copies, waits for them, and re-layouts  29.2 us (6%)
  between operations  17.8 us (3%)
  matrix products  6.79 us (1%)
    pallas_call x13, Pallas kernels, call(): pl.pallas_call(kernel, in_specs=spec, out_specs=[pl.BlockSpec(memory_spac...  138 us
    ppermute x32, waiting for transfers between devices, shift(): lax.ppermute(values, 'ctx', [(order[i], order[(i + offset) % count]) for...  120 us
    ppermute x32, starting transfers between devices, shift(): lax.ppermute(values, 'ctx', [(order[i], order[(i + offset) % count]) for...  63.6 us
    ppermute x18, waiting for transfers between devices, swap(): return lax.ppermute(values, axis, [(i, i ^ bit) for i in range(count)])  31.1 us
    ppermute x8, starting transfers between devices, move(): lax.ppermute(values, 'ctx', pairs)  25.2 us
    ppermute x8, waiting for transfers between devices, move(): lax.ppermute(values, 'ctx', pairs)  20.4 us
    ppermute x18, starting transfers between devices, swap(): return lax.ppermute(values, axis, [(i, i ^ bit) for i in range(count)])  13.6 us
  transfers between devices with their start and end apart: 64, of which 28 were waited for; matrix products, arithmetic and copies ran while one was open for 11% of the time, Pallas kernels for 23%

profile of v4, /device:TPU:0, one launch (start us, length us, event | category | flops | bytes accessed | tf_op | source)
XLA Modules:
  0.0 512.7 jit_solution(14330270703033116331)
XLA Ops:
  9.0 2.0 fusion.14
  11.0 3.0 collective-permute-start.2
  17.0 7.0 %collective-permute-start.1 = (bf16[400,256]{1,0:T(8,128)(2,1)S(1)}, bf16[400,256]{1,0:T(8,128)(2,1)S(1)}, u32[]{:S(2)}, u32[]{:S(2)}) collective-permute-start(bf16[400,256]{1,0:T(8,128)(2,1)S(1)} %get-tuple-element.231), channel_id=1, source_target_pairs={{6,3},{1,2},{5,5},{7,4},{2,0},{0,1},{14,11},{9,10},{13,13},{15,12}... | collective-permute-start | bytes 614408 | tf_op jit(solution)/shard_map/gather_one/to_heads/ppermute | solution.py:217
  24.1 6.4 %collective-permute-done = bf16[400,256]{1,0:T(8,128)(2,1)S(1)} collective-permute-done((bf16[400,256]{1,0:T(8,128)(2,1)S(1)}, bf16[400,256]{1,0:T(8,128)(2,1)S(1)}, u32[]{:S(2)}, u32[]{:S(2)}) %collective-permute-start) | collective-permute-done | bytes 204832 | tf_op jit(solution)/shard_map/gather_one/to_heads/ppermute | solution.py:217
  33.1 7.8 %collective-permute-start.6 = (bf16[128,1600]{1,0:T(8,128)(2,1)S(1)}, bf16[128,1600]{1,0:T(8,128)(2,1)S(1)}, u32[]{:S(2)}, u32[]{:S(2)}) collective-permute-start(bf16[128,1600]{1,0:T(8,128)(2,1)S(1)} %collective-permute-done.2.rest_8_), channel_id=1, source_target_pairs={{0,2},{2,4},{4,6},{6,7},{7,5},{5,3},{3,1},{1,0},{8,10},{10,12},{12... | collective-permute-start | bytes 1228808 | tf_op jit(solution)/shard_map/gather_one/ppermute | solution.py:90
  40.9 4.6 collective-permute-start.7
  47.4 14.0 %collective-permute-done.5 = bf16[400,128]{1,0:T(8,128)(2,1)S(1)} collective-permute-done((bf16[400,128]{1,0:T(8,128)(2,1)S(1)}, bf16[400,128]{1,0:T(8,128)(2,1)S(1)}, u32[]{:S(2)}, u32[]{:S(2)}) %collective-permute-start.5) | collective-permute-done | bytes 102432 | tf_op jit(solution)/shard_map/gather_one/to_heads/ppermute | solution.py:217
  64.2 2.0 collective-permute-start.10
  66.2 11.9 %collective-permute-done.9.rest_6_ = bf16[128,1600]{1,0:T(8,128)(2,1)S(1)} collective-permute-done((bf16[128,1600]{1,0:T(8,128)(2,1)S(1)}, bf16[128,1600]{1,0:T(8,128)(2,1)S(1)}, u32[]{:S(2)}, u32[]{:S(2)}) %collective-permute-start.9) | collective-permute-done | bytes 409632 | tf_op jit(solution)/shard_map/gather_one/ppermute | solution.py:90
  80.3 2.3 copy.56
  85.0 2.3 collective-permute-start.13
  88.4 8.4 %collective-permute-done.12.rest_4_ = bf16[64,1600]{1,0:T(8,128)(2,1)S(1)} collective-permute-done((bf16[64,1600]{1,0:T(8,128)(2,1)S(1)}, bf16[64,1600]{1,0:T(8,128)(2,1)S(1)}, u32[]{:S(2)}, u32[]{:S(2)}) %collective-permute-start.12) | collective-permute-done | bytes 204832 | tf_op jit(solution)/shard_map/gather_one/ppermute | solution.py:90
  96.8 4.6 collective-permute-done.13.rest_5_
  102.1 15.0 %attend.1 = (bf16[1024,1600]{1,0:T(8,128)(2,1)}, bf16[1600,768]{1,0:T(8,128)(2,1)}, bf16[1024,768]{1,0:T(8,128)(2,1)}, f32[1024,256]{1,0:T(8,128)}, bf16[8,128,256]{2,1,0:T(8,128)(2,1)}, /*index=5*/f32[1024,4]{1,0:T(8,128)}) custom-call(s32[8]{0:T(128)} %get-tuple-element.250.member_ref, s32[1]{0:T(128)} %bitcast.1.place_ref, s32[8]{0:T(128)} %pair_of_ref.1, ...), custom_call_target="tpu_custom_call" | custom-call | flops 1000 | bytes 180000000 | tf_op jit(solution)/shard_map/attend/pallas_call | solution.py:246
  118.5 5.0 all-to-all-start
  127.0 14.4 %collective-permute-done.15 = bf16[400,800]{1,0:T(8,128)(2,1)S(1)} collective-permute-done((bf16[400,800]{1,0:T(8,128)(2,1)S(1)}, bf16[400,800]{1,0:T(8,128)(2,1)S(1)}, u32[]{:S(2)}, u32[]{:S(2)}) %collective-permute-start.15) | collective-permute-done | bytes 640032 | tf_op jit(solution)/shard_map/unit_parts/ppermute | solution.py:60
  142.7 3.0 all-to-all-done.back_ref
  145.7 7.4 %out.1 = (f32[128,1600]{1,0:T(8,128)}, bf16[128,1600]{1,0:T(8,128)(2,1)}, f32[128,1600]{1,0:T(8,128)}, f32[128,1]{1,0:T(8,128)}, bf16[128,1600]{1,0:T(8,128)(2,1)}) custom-call(bf16[8,128,256]{2,1,0:T(8,128)(2,1)} %all-to-all-done.back_ref, bf16[128,1600]{1,0:T(8,128)(2,1)} %bitcast.99, f32[1,1600]{1,0:T(1,128)} %broadcast_in_dim.59.bias_ref, ...), custom_call_target="tpu_custom_call" | custom-call | flops 1000 | bytes 90000000 | tf_op jit(solution)/shard_map/out/pallas_call | solution.py:246
  153.1 2.0 collective-permute-start.18
  155.6 13.7 %collective-permute-done.21.rest_8_ = bf16[128,1600]{1,0:T(8,128)(2,1)S(1)} collective-permute-done((bf16[128,1600]{1,0:T(8,128)(2,1)}, bf16[128,1600]{1,0:T(8,128)(2,1)S(1)}, u32[]{:S(2)}, u32[]{:S(2)}) %collective-permute-start.21) | collective-permute-done | bytes 409632 | tf_op jit(solution)/shard_map/gather_two/ppermute | solution.py:90
  169.3 4.7 collective-permute-start.22
  174.0 6.2 %collective-permute-done.18.rest_1_ = bf16[128,1600]{1,0:T(8,128)(2,1)S(1)} collective-permute-done((bf16[128,1600]{1,0:T(8,128)(2,1)}, bf16[128,1600]{1,0:T(8,128)(2,1)S(1)}, u32[]{:S(2)}, u32[]{:S(2)}) %collective-permute-start.18) | collective-permute-done | bytes 409632 | tf_op jit(solution)/shard_map/gather_two/ppermute | solution.py:90
  180.3 8.5 %collective-permute-done.22.rest_7_ = bf16[128,1600]{1,0:T(8,128)(2,1)S(1)} collective-permute-done((bf16[128,1600]{1,0:T(8,128)(2,1)S(1)}, bf16[128,1600]{1,0:T(8,128)(2,1)S(1)}, u32[]{:S(2)}, u32[]{:S(2)}) %collective-permute-start.22) | collective-permute-done | bytes 409632 | tf_op jit(solution)/shard_map/gather_two/ppermute | solution.py:90
  188.8 8.4 %collective-permute-start.23 = (bf16[128,1600]{1,0:T(8,128)(2,1)S(1)}, bf16[128,1600]{1,0:T(8,128)(2,1)S(1)}, u32[]{:S(2)}, u32[]{:S(2)}) collective-permute-start(bf16[128,1600]{1,0:T(8,128)(2,1)S(1)} %collective-permute-done.22.rest_7_), channel_id=1, source_target_pairs={{0,2},{2,4},{4,6},{6,7},{7,5},{5,3},{3,1},{1,0},{8,10},{10,12},{12... | collective-permute-start | bytes 1228808 | tf_op jit(solution)/shard_map/gather_two/ppermute | solution.py:90
  197.2 4.2 collective-permute-done.19.rest_2_
  201.5 6.0 %collective-permute-done.23.rest_6_ = bf16[128,1600]{1,0:T(8,128)(2,1)S(1)} collective-permute-done((bf16[128,1600]{1,0:T(8,128)(2,1)S(1)}, bf16[128,1600]{1,0:T(8,128)(2,1)S(1)}, u32[]{:S(2)}, u32[]{:S(2)}) %collective-permute-start.23) | collective-permute-done | bytes 409632 | tf_op jit(solution)/shard_map/gather_two/ppermute | solution.py:90
  208.2 2.1 collective-permute-start.24
  211.8 2.6 collective-permute-start.25
  216.9 8.8 %hidden_grad.1 = (bf16[1600,800]{1,0:T(8,128)(2,1)}, f32[1024,800]{1,0:T(8,128)}) custom-call(s32[1]{0:T(128)} %bitcast.1.place_ref, bf16[1024,1600]{1,0:T(8,128)(2,1)} %all-gather.4.cloned.1.call-done.cot_ref.rest_2_, bf16[2,400,800]{2,1,0:T(8,128)(2,1)} %copy-done.5, bf16[2,400,800]{2,1,0:T(8,128)(2,1)} %collective-permute-done.17.peer_ref), custom_call_target="tpu_custom_call" | custom-call | flops 1000 | bytes 27000000 | tf_op jit(solution)/shard_map/hidden_grad/pallas_call | solution.py:246
  225.7 18.6 %hidden.1 = (bf16[1024,1600]{1,0:T(8,128)(2,1)}, bf16[1024,800]{1,0:T(8,128)(2,1)}, bf16[1024,800]{1,0:T(8,128)(2,1)}, bf16[8,128,1600]{2,1,0:T(8,128)(2,1)}, bf...) custom-call(s32[8]{0:T(128)} %get-tuple-element.250.member_ref, s32[8]{0:T(128)} %fusion.23.offset_ref, s32[1]{0:T(128)} %bitcast.1.place_ref, ...), custom_call_target="tpu_custom_call" | custom-call | flops 1000 | bytes 240000000 | tf_op jit(solution)/shard_map/hidden/pallas_call | solution.py:246
  245.4 2.1 collective-permute-start.27
  247.6 8.1 %branch.1 = bf16[1024,1600]{1,0:T(8,128)(2,1)} custom-call(bf16[1024,800]{1,0:T(8,128)(2,1)} %get-tuple-element.108.value_ref.rest_3_, bf16[1600,800]{1,0:T(8,128)(2,1)} %get-tuple-element.109.w_ref), custom_call_target="tpu_custom_call" | custom-call | flops 1000 | bytes 24000000 | tf_op jit(solution)/shard_map/sum_two/branch/pallas_call | solution.py:246
  257.0 2.1 collective-permute-start.29
  259.1 16.2 %collective-permute-done.29 = bf16[128,1600]{1,0:T(8,128)(2,1)S(1)} collective-permute-done((bf16[128,1600]{1,0:T(8,128)(2,1)S(1)}, bf16[128,1600]{1,0:T(8,128)(2,1)S(1)}, u32[]{:S(2)}, u32[]{:S(2)}) %collective-permute-start.29) | collective-permute-done | bytes 409632 | tf_op jit(solution)/shard_map/sum_two/ppermute | solution.py:90
  277.4 7.3 %collective-permute-start.31 = (bf16[128,1600]{1,0:T(8,128)(2,1)S(1)}, bf16[128,1600]{1,0:T(8,128)(2,1)S(1)}, u32[]{:S(2)}, u32[]{:S(2)}) collective-permute-start(bf16[128,1600]{1,0:T(8,128)(2,1)S(1)} %get-tuple-element.111), channel_id=1, source_target_pairs={{0,1},{2,0},{4,2},{6,4},{7,6},{5,7},{3,5},{1,3},{8,9},{10,8},{12,1... | collective-permute-start | bytes 1228808 | tf_op jit(solution)/shard_map/sum_two/ppermute | solution.py:90
  284.7 11.2 %unit_other.1 = bf16[2,2,400,800]{3,2,1,0:T(8,128)(2,1)} custom-call(s32[1]{0:T(128)} %bitcast.22.core_ref, bf16[1024,1600]{1,0:T(8,128)(2,1)} %get-tuple-element.113.rest_0_, bf16[1024,800]{1,0:T(8,128)(2,1)} %get-tuple-element.114.rest_1_, bf16[1024,1600]{1,0:T(8,128)(2,1)} %all-gather.4.cloned.1.call-done.cot_ref.rest_2_, ...), custom_call_target="tpu_custom_call" | custom-call | flops 1000 | bytes 24000000 | tf_op jit(solution)/shard_map/sum_two/unit_sum/unit_other/pallas_call | solution.py:246
  295.9 9.4 %collective-permute-done.31 = bf16[128,1600]{1,0:T(8,128)(2,1)S(1)} collective-permute-done((bf16[128,1600]{1,0:T(8,128)(2,1)S(1)}, bf16[128,1600]{1,0:T(8,128)(2,1)S(1)}, u32[]{:S(2)}, u32[]{:S(2)}) %collective-permute-start.31) | collective-permute-done | bytes 409632 | tf_op jit(solution)/shard_map/sum_two/ppermute | solution.py:90
  306.7 3.7 collective-permute-start.33
  310.8 8.9 %collective-permute-done.33 = bf16[128,1600]{1,0:T(8,128)(2,1)S(1)} collective-permute-done((bf16[128,1600]{1,0:T(8,128)(2,1)S(1)}, bf16[128,1600]{1,0:T(8,128)(2,1)S(1)}, u32[]{:S(2)}, u32[]{:S(2)}) %collective-permute-start.33) | collective-permute-done | bytes 409632 | tf_op jit(solution)/shard_map/sum_two/ppermute | solution.py:90
  319.8 3.7 collective-permute-done.32
  323.5 2.1 fusion.18.sum_ref
  325.6 10.9 %out_back.1 = (f32[128,1600]{1,0:T(8,128)}, bf16[128,1600]{1,0:T(8,128)(2,1)}, bf16[8,128,256]{2,1,0:T(8,128)(2,1)}, f32[4,1600]{1,0:T(4,128)}, f32[8,200,800]{2,1,0:T(8,128)}, /*index=5*/bf16[8,200,800]{2,1,0:T(8,128)(2,1)}) custom-call(s32[1]{0:T(128)} %bitcast.22.core_ref, f32[128,1600]{1,0:T(8,128)} %fusion.18.sum_ref, bf16[128,1600]{1,0:T(8,128)(2,1)} %bitcast.101, ...), custom_call_target="tpu_custom_call" | custom-call | flops 1000 | bytes 135000000 | tf_op jit(solution)/shard_map/out_back/pallas_call | solution.py:246
  337.0 4.1 all-to-all-start.1
  341.2 4.2 collective-permute-done.34
  345.5 5.6 %add_convert_fusion = bf16[8,200,800]{2,1,0:T(8,128)(2,1)} fusion(f32[8,200,800]{2,1,0:T(8,128)} %get-tuple-element.121, bf16[8,200,800]{2,1,0:T(8,128)(2,1)} %collective-permute-done.34), kind=kLoop, calls=%fused_computation.1 | loop fusion | flops 3840000 | bytes 10240000 | tf_op jit(solution)/shard_map/out_sum/convert_element_type | solution.py:782
  351.1 13.2 %unit_mine.1 = (f32[2,400,800]{2,1,0:T(8,128)}, bf16[2,400,800]{2,1,0:T(8,128)(2,1)}) custom-call(s32[1]{0:T(128)} %bitcast.22.core_ref, s32[1]{0:T(128)} %bitcast.28.row_ref, bf16[2,2,400,800]{3,2,1,0:T(8,128)(2,1)} %collective-permute-done.35.got_ref, bf16[1024,1600]{1,0:T(8,128)(2,1)} %get-tuple-element.113.rest_0_, ...), custom_call_target="tpu_custom_call" | custom-call | flops 1000 | bytes 30000000 | tf_op jit(solution)/shard_map/out_sum/unit_sum/unit_mine/pallas_call | solution.py:246
  372.7 20.4 %attend_back.1 = (bf16[1024,768]{1,0:T(8,128)(2,1)}, f32[1,768]{1,0:T(1,128)}, bf16[128,1600]{1,0:T(8,128)(2,1)}) custom-call(s32[16]{0:T(128)} %pad_add_fusion.who_ref, s32[2]{0:T(128)} %pad_add_fusion.1.far_ref, bf16[1024,768]{1,0:T(8,128)(2,1)} %get-tuple-element.127.qkv_ref, bf16[1600,768]{1,0:T(8,128)(2,1)} %get-tuple-element.128.w_ref, ...), custom_call_target="tpu_custom_call" | custom-call | flops 1000 | bytes 240000000 | tf_op jit(solution)/shard_map/attend_back/pallas_call | solution.py:246
  393.1 6.1 %qkv_other.1 = bf16[1,2,400,768]{3,2,1,0:T(8,128)(2,1)} custom-call(s32[1]{0:T(128)} %bitcast.22.core_ref, bf16[1024,1600]{1,0:T(8,128)(2,1)} %get-tuple-element.133.x_ref.rest_0_, bf16[1024,768]{1,0:T(8,128)(2,1)} %get-tuple-element.132.grad_ref.rest_1_), custom_call_target="tpu_custom_call" | custom-call | flops 1000 | bytes 15000000 | tf_op jit(solution)/shard_map/sum_one/qkv_sum/qkv_other/pallas_call | solution.py:246
  400.3 2.0 collective-permute-start.37
  402.5 8.4 %project_back.1 = (bf16[8,128,1600]{2,1,0:T(8,128)(2,1)}, f32[2,1600]{1,0:T(2,128)}) custom-call(s32[16]{0:T(128)} %gather_fusion, bf16[1024,768]{1,0:T(8,128)(2,1)} %get-tuple-element.132.grad_ref.rest_1_, bf16[1600,768]{1,0:T(8,128)(2,1)} %get-tuple-element.128.w_ref, bf16[1024,1600]{1,0:T(8,128)(2,1)} %get-tuple-element.133.x_ref.rest_0_), custom_call_target="tpu_custom_call" | custom-call | flops 1000 | bytes 18000000 | tf_op jit(solution)/shard_map/project_back/pallas_call | solution.py:246
  410.8 2.2 convert_add_fusion.2
  418.6 3.2 collective-permute-done.43
  421.8 7.2 %qkv_mine.1 = (f32[1,400,768]{2,1,0:T(8,128)}, bf16[1,400,768]{2,1,0:T(8,128)(2,1)}) custom-call(s32[1]{0:T(128)} %bitcast.22.core_ref, s32[1]{0:T(128)} %bitcast.28.row_ref, bf16[1,2,400,768]{3,2,1,0:T(8,128)(2,1)} %copy-done.10, bf16[1024,1600]{1,0:T(8,128)(2,1)} %get-tuple-element.133.x_ref.rest_0_, bf16[1024,768]{1,0:T(8,128)(2,1)} %get-tuple-element.132.grad_ref.rest_1_), custom_call_target="tpu_custom_call" | custom-call | flops 1000 | bytes 18000000 | tf_op jit(solution)/shard_map/sum_one/qkv_sum/qkv_mine/pallas_call | solution.py:246
  429.0 2.3 convert_add_fusion.1
  438.1 14.1 %collective-permute-done.45 = bf16[128,1600]{1,0:T(8,128)(2,1)S(1)} collective-permute-done((bf16[128,1600]{1,0:T(8,128)(2,1)}, bf16[128,1600]{1,0:T(8,128)(2,1)S(1)}, u32[]{:S(2)}, u32[]{:S(2)}) %collective-permute-start.45) | collective-permute-done | bytes 409632 | tf_op jit(solution)/shard_map/sum_one/ppermute | solution.py:90
  452.2 2.3 convert_add_fusion
  456.6 5.1 collective-permute-start.54
  464.3 6.6 %collective-permute-start.57 = (bf16[400,128]{1,0:T(8,128)(2,1)S(1)}, bf16[400,128]{1,0:T(8,128)(2,1)S(1)}, u32[]{:S(2)}, u32[]{:S(2)}) collective-permute-start(bf16[400,128]{1,0:T(8,128)(2,1)S(1)} %slice.271), channel_id=1, source_target_pairs={{4,2},{5,4},{0,3},{6,5},{2,0},{3,7},{1,6},{12,10},{13,12},{8,11},{... | collective-permute-start | bytes 307208 | tf_op jit(solution)/shard_map/sum_one/from_heads/ppermute | solution.py:217
  473.1 2.5 collective-permute-done.51
  480.8 2.4 collective-permute-done.46
  485.5 2.4 collective-permute-done.47
  491.2 3.0 fusion.2
  498.8 2.1 fusion.17.sum_ref
  501.0 2.8 input_grad.1
  (272 shorter events, 80.1 us)
Async XLA Ops:
  7.2 138.5 %all-gather.6.cloned.1.call-start = ((), (), s32[]{:S(2)}) async-start(), calls=%async_computation.6 | async-start | bytes 6758400 | tf_op jit(solution)/shard_map/gather_one/all_gather | solution.py:629
  11.0 19.4 %collective-permute-start.2 = (bf16[128,1600]{1,0:T(8,128)(2,1)S(1)}, bf16[128,1600]{1,0:T(8,128)(2,1)S(1)}, u32[]{:S(2)}, u32[]{:S(2)}) collective-permute-start(bf16[128,1600]{1,0:T(8,128)(2,1)S(1)} %get-tuple-element.234.rest_0_), channel_id=1, source_target_pairs={{0,2},{2,4},{4,6},{6,7},{7,5},{5,3},{3,1},{1,0},{8,10},{10,12},{12... | collective-permute-start | bytes 1228808 | tf_op jit(solution)/shard_map/gather_one/ppermute | solution.py:90
  14.0 16.4 %collective-permute-start.3 = (bf16[128,1600]{1,0:T(8,128)(2,1)S(1)}, bf16[128,1600]{1,0:T(8,128)(2,1)S(1)}, u32[]{:S(2)}, u32[]{:S(2)}) collective-permute-start(bf16[128,1600]{1,0:T(8,128)(2,1)S(1)} %get-tuple-element.234.rest_0_), channel_id=1, source_target_pairs={{0,1},{2,0},{4,2},{6,4},{7,6},{5,7},{3,5},{1,3},{8,9},{10,8},{12,1... | collective-permute-start | bytes 1228808 | tf_op jit(solution)/shard_map/gather_one/ppermute | solution.py:90
  15.7 14.7 %collective-permute-start = (bf16[400,256]{1,0:T(8,128)(2,1)S(1)}, bf16[400,256]{1,0:T(8,128)(2,1)S(1)}, u32[]{:S(2)}, u32[]{:S(2)}) collective-permute-start(bf16[400,256]{1,0:T(8,128)(2,1)S(1)} %get-tuple-element.232), channel_id=1, source_target_pairs={{2,5},{4,3},{1,4},{5,0},{3,1},{6,2},{7,6},{10,13},{12,11},{9,12},{... | collective-permute-start | bytes 614408 | tf_op jit(solution)/shard_map/gather_one/to_heads/ppermute | solution.py:217
  17.0 13.4 %collective-permute-start.1 = (bf16[400,256]{1,0:T(8,128)(2,1)S(1)}, bf16[400,256]{1,0:T(8,128)(2,1)S(1)}, u32[]{:S(2)}, u32[]{:S(2)}) collective-permute-start(bf16[400,256]{1,0:T(8,128)(2,1)S(1)} %get-tuple-element.231), channel_id=1, source_target_pairs={{6,3},{1,2},{5,5},{7,4},{2,0},{0,1},{14,11},{9,10},{13,13},{15,12}... | collective-permute-start | bytes 614408 | tf_op jit(solution)/shard_map/gather_one/to_heads/ppermute | solution.py:217
  31.4 185.5 %all-gather.4.cloned.1.call-start = ((), (), s32[]{:S(2)}) async-start(), calls=%async_computation.4 | async-start | bytes 3833856 | tf_op jit(solution)/shard_map/all_gather | solution.py:675
  32.3 15.1 %collective-permute-start.4 = (bf16[400,256]{1,0:T(8,128)(2,1)S(1)}, bf16[400,256]{1,0:T(8,128)(2,1)S(1)}, u32[]{:S(2)}, u32[]{:S(2)}) collective-permute-start(bf16[400,256]{1,0:T(8,128)(2,1)S(1)} %slice.198), channel_id=1, source_target_pairs={{5,1},{0,0},{1,3},{3,2},{4,4},{7,5},{2,6},{13,9},{8,8},{9,11},{11,... | collective-permute-start | bytes 614408 | tf_op jit(solution)/shard_map/gather_one/to_heads/ppermute | solution.py:217
  33.1 28.4 %collective-permute-start.6 = (bf16[128,1600]{1,0:T(8,128)(2,1)S(1)}, bf16[128,1600]{1,0:T(8,128)(2,1)S(1)}, u32[]{:S(2)}, u32[]{:S(2)}) collective-permute-start(bf16[128,1600]{1,0:T(8,128)(2,1)S(1)} %collective-permute-done.2.rest_8_), channel_id=1, source_target_pairs={{0,2},{2,4},{4,6},{6,7},{7,5},{5,3},{3,1},{1,0},{8,10},{10,12},{12... | collective-permute-start | bytes 1228808 | tf_op jit(solution)/shard_map/gather_one/ppermute | solution.py:90
  40.9 20.6 %collective-permute-start.7 = (bf16[128,1600]{1,0:T(8,128)(2,1)S(1)}, bf16[128,1600]{1,0:T(8,128)(2,1)S(1)}, u32[]{:S(2)}, u32[]{:S(2)}) collective-permute-start(bf16[128,1600]{1,0:T(8,128)(2,1)S(1)} %collective-permute-done.3.rest_1_), channel_id=1, source_target_pairs={{0,1},{2,0},{4,2},{6,4},{7,6},{5,7},{3,5},{1,3},{8,9},{10,8},{12,1... | collective-permute-start | bytes 1228808 | tf_op jit(solution)/shard_map/gather_one/ppermute | solution.py:90
  45.5 15.9 %collective-permute-start.5 = (bf16[400,128]{1,0:T(8,128)(2,1)S(1)}, bf16[400,128]{1,0:T(8,128)(2,1)S(1)}, u32[]{:S(2)}, u32[]{:S(2)}) collective-permute-start(bf16[400,128]{1,0:T(8,128)(2,1)S(1)} %slice.199), channel_id=1, source_target_pairs={{2,4},{4,5},{3,0},{5,6},{0,2},{7,3},{6,1},{10,12},{12,13},{11,8},{... | collective-permute-start | bytes 307208 | tf_op jit(solution)/shard_map/gather_one/to_heads/ppermute | solution.py:217
  62.5 17.6 %collective-permute-start.8 = (bf16[400,768]{1,0:T(8,128)(2,1)S(1)}, bf16[400,768]{1,0:T(8,128)(2,1)S(1)}, u32[]{:S(2)}, u32[]{:S(2)}) collective-permute-start(bf16[400,768]{1,0:T(8,128)(2,1)S(1)} %fusion.10), channel_id=1, source_target_pairs={{0,16},{8,24},{16,0},{24,8},{1,17},{9,25},{17,1},{25,9},{2,18},{10... | collective-permute-start | bytes 1843208 | tf_op jit(solution)/shard_map/gather_one/qkv_parts/ppermute | solution.py:60
  64.2 13.9 %collective-permute-start.9 = (bf16[128,1600]{1,0:T(8,128)(2,1)S(1)}, bf16[128,1600]{1,0:T(8,128)(2,1)S(1)}, u32[]{:S(2)}, u32[]{:S(2)}) collective-permute-start(bf16[128,1600]{1,0:T(8,128)(2,1)S(1)} %collective-permute-done.6.rest_7_), channel_id=1, source_target_pairs={{0,2},{2,4},{4,6},{6,7},{7,5},{5,3},{3,1},{1,0},{8,10},{10,12},{12... | collective-permute-start | bytes 1228808 | tf_op jit(solution)/shard_map/gather_one/ppermute | solution.py:90
  64.2 15.9 %collective-permute-start.10 = (bf16[128,1600]{1,0:T(8,128)(2,1)S(1)}, bf16[128,1600]{1,0:T(8,128)(2,1)S(1)}, u32[]{:S(2)}, u32[]{:S(2)}) collective-permute-start(bf16[128,1600]{1,0:T(8,128)(2,1)S(1)} %collective-permute-done.7.rest_2_), channel_id=1, source_target_pairs={{0,1},{2,0},{4,2},{6,4},{7,6},{5,7},{3,5},{1,3},{8,9},{10,8},{12,1... | collective-permute-start | bytes 1228808 | tf_op jit(solution)/shard_map/gather_one/ppermute | solution.py:90
  80.2 3.0 collective-permute-start.11
  83.2 33.9 %collective-permute-start.14 = (bf16[400,800]{1,0:T(8,128)(2,1)}, bf16[400,800]{1,0:T(8,128)(2,1)}, u32[]{:S(2)}, u32[]{:S(2)}) collective-permute-start(bf16[400,800]{1,0:T(8,128)(2,1)} %bitcast.107), channel_id=1, source_target_pairs={{0,16},{8,24},{16,0},{24,8},{1,17},{9,25},{17,1},{25,9},{2,18},{10... | collective-permute-start | bytes 1920008 | tf_op jit(solution)/shard_map/unit_parts/ppermute | solution.py:60
  84.9 11.9 %collective-permute-start.12 = (bf16[64,1600]{1,0:T(8,128)(2,1)S(1)}, bf16[64,1600]{1,0:T(8,128)(2,1)S(1)}, u32[]{:S(2)}, u32[]{:S(2)}) collective-permute-start(bf16[64,1600]{1,0:T(8,128)(2,1)S(1)} %slice.257), channel_id=1, source_target_pairs={{0,2},{2,4},{4,6},{6,7},{7,5},{5,3},{3,1},{1,0},{8,10},{10,12},{12... | collective-permute-start | bytes 614408 | tf_op jit(solution)/shard_map/gather_one/ppermute | solution.py:90
  85.0 16.4 %collective-permute-start.13 = (bf16[64,1600]{1,0:T(8,128)(2,1)S(1)}, bf16[64,1600]{1,0:T(8,128)(2,1)S(1)}, u32[]{:S(2)}, u32[]{:S(2)}) collective-permute-start(bf16[64,1600]{1,0:T(8,128)(2,1)S(1)} %slice.258), channel_id=1, source_target_pairs={{0,1},{2,0},{4,2},{6,4},{7,6},{5,7},{3,5},{1,3},{8,9},{10,8},{12,1... | collective-permute-start | bytes 614408 | tf_op jit(solution)/shard_map/gather_one/ppermute | solution.py:90
  118.5 27.1 %all-to-all-start = ((bf16[8,128,256]{2,1,0:T(8,128)(2,1)}), bf16[8,128,256]{2,1,0:T(8,128)(2,1)}, u32[]{:S(2)}, u32[]{:S(2)}) async-start(bf16[8,128,256]{2,1,0:T(8,128)(2,1)} %get-tuple-element.94), calls=%async_computation | async-start | bytes 1048576 | tf_op jit(solution)/shard_map/all_to_all | solution.py:677
  123.6 307.8 %reduce-scatter.5.cloned.1.call-start = ((), (), s32[]{:S(2)}) async-start(), calls=%async_computation.5 | async-start | bytes 3833856 | tf_op jit(solution)/shard_map/reduce_scatter | solution.py:759
  123.6 17.7 %collective-permute-start.15 = (bf16[400,800]{1,0:T(8,128)(2,1)S(1)}, bf16[400,800]{1,0:T(8,128)(2,1)S(1)}, u32[]{:S(2)}, u32[]{:S(2)}) collective-permute-start(bf16[400,800]{1,0:T(8,128)(2,1)S(1)} %copy-done.18), channel_id=1, source_target_pairs={{0,16},{8,24},{16,0},{24,8},{1,17},{9,25},{17,1},{25,9},{2,18},{10... | collective-permute-start | bytes 1920008 | tf_op jit(solution)/shard_map/unit_parts/ppermute | solution.py:60
  153.1 16.2 %collective-permute-start.21 = (bf16[128,1600]{1,0:T(8,128)(2,1)}, bf16[128,1600]{1,0:T(8,128)(2,1)S(1)}, u32[]{:S(2)}, u32[]{:S(2)}) collective-permute-start(bf16[128,1600]{1,0:T(8,128)(2,1)} %get-tuple-element.104.rest_0_), channel_id=1, source_target_pairs={{0,2},{2,4},{4,6},{6,7},{7,5},{5,3},{3,1},{1,0},{8,10},{10,12},{12... | collective-permute-start | bytes 1228808 | tf_op jit(solution)/shard_map/gather_two/ppermute | solution.py:90
  153.1 27.2 %collective-permute-start.18 = (bf16[128,1600]{1,0:T(8,128)(2,1)}, bf16[128,1600]{1,0:T(8,128)(2,1)S(1)}, u32[]{:S(2)}, u32[]{:S(2)}) collective-permute-start(bf16[128,1600]{1,0:T(8,128)(2,1)} %get-tuple-element.104.rest_0_), channel_id=1, source_target_pairs={{0,1},{2,0},{4,2},{6,4},{7,6},{5,7},{3,5},{1,3},{8,9},{10,8},{12,1... | collective-permute-start | bytes 1228808 | tf_op jit(solution)/shard_map/gather_two/ppermute | solution.py:90
  155.1 61.8 %collective-permute-start.17 = (bf16[2,400,800]{2,1,0:T(8,128)(2,1)S(1)}, bf16[2,400,800]{2,1,0:T(8,128)(2,1)}, u32[]{:S(2)}, u32[]{:S(2)}) collective-permute-start(bf16[2,400,800]{2,1,0:T(8,128)(2,1)S(1)} %pad_maximum_fusion.pair_ref), channel_id=1, source_target_pairs={{0,8},{8,0},{16,24},{24,16},{1,9},{9,1},{17,25},{25,17},{2,10},{10... | collective-permute-start | bytes 3840008 | tf_op jit(solution)/shard_map/unit_parts/ppermute | solution.py:60
  155.1 70.6 %collective-permute-start.16 = (bf16[2,400,800]{2,1,0:T(8,128)(2,1)S(1)}, bf16[2,400,800]{2,1,0:T(8,128)(2,1)}, u32[]{:S(2)}, u32[]{:S(2)}) collective-permute-start(bf16[2,400,800]{2,1,0:T(8,128)(2,1)S(1)} %pad_maximum_fusion.1.pair_ref), channel_id=1, source_target_pairs={{0,8},{8,0},{16,24},{24,16},{1,9},{9,1},{17,25},{25,17},{2,10},{10... | collective-permute-start | bytes 3840008 | tf_op jit(solution)/shard_map/unit_parts/ppermute | solution.py:60
  169.3 19.5 %collective-permute-start.22 = (bf16[128,1600]{1,0:T(8,128)(2,1)S(1)}, bf16[128,1600]{1,0:T(8,128)(2,1)S(1)}, u32[]{:S(2)}, u32[]{:S(2)}) collective-permute-start(bf16[128,1600]{1,0:T(8,128)(2,1)S(1)} %collective-permute-done.21.rest_8_), channel_id=1, source_target_pairs={{0,2},{2,4},{4,6},{6,7},{7,5},{5,3},{3,1},{1,0},{8,10},{10,12},{12... | collective-permute-start | bytes 1228808 | tf_op jit(solution)/shard_map/gather_two/ppermute | solution.py:90
  180.3 21.1 %collective-permute-start.19 = (bf16[128,1600]{1,0:T(8,128)(2,1)S(1)}, bf16[128,1600]{1,0:T(8,128)(2,1)S(1)}, u32[]{:S(2)}, u32[]{:S(2)}) collective-permute-start(bf16[128,1600]{1,0:T(8,128)(2,1)S(1)} %collective-permute-done.18.rest_1_), channel_id=1, source_target_pairs={{0,1},{2,0},{4,2},{6,4},{7,6},{5,7},{3,5},{1,3},{8,9},{10,8},{12,1... | collective-permute-start | bytes 1228808 | tf_op jit(solution)/shard_map/gather_two/ppermute | solution.py:90
  188.8 18.7 %collective-permute-start.23 = (bf16[128,1600]{1,0:T(8,128)(2,1)S(1)}, bf16[128,1600]{1,0:T(8,128)(2,1)S(1)}, u32[]{:S(2)}, u32[]{:S(2)}) collective-permute-start(bf16[128,1600]{1,0:T(8,128)(2,1)S(1)} %collective-permute-done.22.rest_7_), channel_id=1, source_target_pairs={{0,2},{2,4},{4,6},{6,7},{7,5},{5,3},{3,1},{1,0},{8,10},{10,12},{12... | collective-permute-start | bytes 1228808 | tf_op jit(solution)/shard_map/gather_two/ppermute | solution.py:90
  201.4 8.9 %collective-permute-start.20 = (bf16[128,1600]{1,0:T(8,128)(2,1)S(1)}, bf16[128,1600]{1,0:T(8,128)(2,1)S(1)}, u32[]{:S(2)}, u32[]{:S(2)}) collective-permute-start(bf16[128,1600]{1,0:T(8,128)(2,1)S(1)} %collective-permute-done.19.rest_2_), channel_id=1, source_target_pairs={{0,1},{2,0},{4,2},{6,4},{7,6},{5,7},{3,5},{1,3},{8,9},{10,8},{12,1... | collective-permute-start | bytes 1228808 | tf_op jit(solution)/shard_map/gather_two/ppermute | solution.py:90
  208.2 17.5 %collective-permute-start.24 = (bf16[64,1600]{1,0:T(8,128)(2,1)}, bf16[64,1600]{1,0:T(8,128)(2,1)}, u32[]{:S(2)}, u32[]{:S(2)}) collective-permute-start(bf16[64,1600]{1,0:T(8,128)(2,1)} %slice.259), channel_id=1, source_target_pairs={{0,2},{2,4},{4,6},{6,7},{7,5},{5,3},{3,1},{1,0},{8,10},{10,12},{12... | collective-permute-start | bytes 614408 | tf_op jit(solution)/shard_map/gather_two/ppermute | solution.py:90
  211.8 13.9 %collective-permute-start.25 = (bf16[64,1600]{1,0:T(8,128)(2,1)}, bf16[64,1600]{1,0:T(8,128)(2,1)}, u32[]{:S(2)}, u32[]{:S(2)}) collective-permute-start(bf16[64,1600]{1,0:T(8,128)(2,1)} %slice.260), channel_id=1, source_target_pairs={{0,1},{2,0},{4,2},{6,4},{7,6},{5,7},{3,5},{1,3},{8,9},{10,8},{12,1... | collective-permute-start | bytes 614408 | tf_op jit(solution)/shard_map/gather_two/ppermute | solution.py:90
  245.4 10.3 %collective-permute-start.27 = (bf16[64,1600]{1,0:T(8,128)(2,1)S(1)}, bf16[64,1600]{1,0:T(8,128)(2,1)S(1)}, u32[]{:S(2)}, u32[]{:S(2)}) collective-permute-start(bf16[64,1600]{1,0:T(8,128)(2,1)S(1)} %get-tuple-element.237), channel_id=1, source_target_pairs={{0,1},{2,0},{4,2},{6,4},{7,6},{5,7},{3,5},{1,3},{8,9},{10,8},{12,1... | collective-permute-start | bytes 614408 | tf_op jit(solution)/shard_map/sum_two/ppermute | solution.py:90
  247.5 8.3 %collective-permute-start.26 = (bf16[64,1600]{1,0:T(8,128)(2,1)S(1)}, bf16[64,1600]{1,0:T(8,128)(2,1)S(1)}, u32[]{:S(2)}, u32[]{:S(2)}) collective-permute-start(bf16[64,1600]{1,0:T(8,128)(2,1)S(1)} %get-tuple-element.238), channel_id=1, source_target_pairs={{0,2},{2,4},{4,6},{6,7},{7,5},{5,3},{3,1},{1,0},{8,10},{10,12},{12... | collective-permute-start | bytes 614408 | tf_op jit(solution)/shard_map/sum_two/ppermute | solution.py:90
  257.0 18.3 %collective-permute-start.29 = (bf16[128,1600]{1,0:T(8,128)(2,1)S(1)}, bf16[128,1600]{1,0:T(8,128)(2,1)S(1)}, u32[]{:S(2)}, u32[]{:S(2)}) collective-permute-start(bf16[128,1600]{1,0:T(8,128)(2,1)S(1)} %get-tuple-element.226), channel_id=1, source_target_pairs={{0,1},{2,0},{4,2},{6,4},{7,6},{5,7},{3,5},{1,3},{8,9},{10,8},{12,1... | collective-permute-start | bytes 1228808 | tf_op jit(solution)/shard_map/sum_two/ppermute | solution.py:90
  259.1 16.9 %collective-permute-start.28 = (bf16[128,1600]{1,0:T(8,128)(2,1)S(1)}, bf16[128,1600]{1,0:T(8,128)(2,1)S(1)}, u32[]{:S(2)}, u32[]{:S(2)}) collective-permute-start(bf16[128,1600]{1,0:T(8,128)(2,1)S(1)} %get-tuple-element.227), channel_id=1, source_target_pairs={{0,2},{2,4},{4,6},{6,7},{7,5},{5,3},{3,1},{1,0},{8,10},{10,12},{12... | collective-permute-start | bytes 1228808 | tf_op jit(solution)/shard_map/sum_two/ppermute | solution.py:90
  277.4 27.9 %collective-permute-start.31 = (bf16[128,1600]{1,0:T(8,128)(2,1)S(1)}, bf16[128,1600]{1,0:T(8,128)(2,1)S(1)}, u32[]{:S(2)}, u32[]{:S(2)}) collective-permute-start(bf16[128,1600]{1,0:T(8,128)(2,1)S(1)} %get-tuple-element.111), channel_id=1, source_target_pairs={{0,1},{2,0},{4,2},{6,4},{7,6},{5,7},{3,5},{1,3},{8,9},{10,8},{12,1... | collective-permute-start | bytes 1228808 | tf_op jit(solution)/shard_map/sum_two/ppermute | solution.py:90
  284.7 20.6 %collective-permute-start.30 = (bf16[128,1600]{1,0:T(8,128)(2,1)S(1)}, bf16[128,1600]{1,0:T(8,128)(2,1)S(1)}, u32[]{:S(2)}, u32[]{:S(2)}) collective-permute-start(bf16[128,1600]{1,0:T(8,128)(2,1)S(1)} %get-tuple-element.110), channel_id=1, source_target_pairs={{0,2},{2,4},{4,6},{6,7},{7,5},{5,3},{3,1},{1,0},{8,10},{10,12},{12... | collective-permute-start | bytes 1228808 | tf_op jit(solution)/shard_map/sum_two/ppermute | solution.py:90
  306.7 13.0 %collective-permute-start.33 = (bf16[128,1600]{1,0:T(8,128)(2,1)S(1)}, bf16[128,1600]{1,0:T(8,128)(2,1)S(1)}, u32[]{:S(2)}, u32[]{:S(2)}) collective-permute-start(bf16[128,1600]{1,0:T(8,128)(2,1)S(1)} %get-tuple-element.116), channel_id=1, source_target_pairs={{0,1},{2,0},{4,2},{6,4},{7,6},{5,7},{3,5},{1,3},{8,9},{10,8},{12,1... | collective-permute-start | bytes 1228808 | tf_op jit(solution)/shard_map/sum_two/ppermute | solution.py:90
  310.4 13.1 %collective-permute-start.32 = (bf16[128,1600]{1,0:T(8,128)(2,1)S(1)}, bf16[128,1600]{1,0:T(8,128)(2,1)S(1)}, u32[]{:S(2)}, u32[]{:S(2)}) collective-permute-start(bf16[128,1600]{1,0:T(8,128)(2,1)S(1)} %get-tuple-element.115), channel_id=1, source_target_pairs={{0,2},{2,4},{4,6},{6,7},{7,5},{5,3},{3,1},{1,0},{8,10},{10,12},{12... | collective-permute-start | bytes 1228808 | tf_op jit(solution)/shard_map/sum_two/ppermute | solution.py:90
  336.5 9.0 %collective-permute-start.34 = (bf16[8,200,800]{2,1,0:T(8,128)(2,1)}, bf16[8,200,800]{2,1,0:T(8,128)(2,1)}, u32[]{:S(2)}, u32[]{:S(2)}) collective-permute-start(bf16[8,200,800]{2,1,0:T(8,128)(2,1)} %get-tuple-element.122), channel_id=1, source_target_pairs={{0,8},{8,0},{16,24},{24,16},{1,9},{9,1},{17,25},{25,17},{2,10},{10... | collective-permute-start | bytes 7680008 | tf_op jit(solution)/shard_map/out_sum/ppermute | solution.py:60
  336.5 14.6 %collective-permute-start.35 = (bf16[2,2,400,800]{3,2,1,0:T(8,128)(2,1)S(1)}, bf16[2,2,400,800]{3,2,1,0:T(8,128)(2,1)}, u32[]{:S(2)}, u32[]{:S(2)}) collective-permute-start(bf16[2,2,400,800]{3,2,1,0:T(8,128)(2,1)S(1)} %copy-done.8), channel_id=1, source_target_pairs={{0,8},{8,0},{16,24},{24,16},{1,9},{9,1},{17,25},{25,17},{2,10},{10... | collective-permute-start | bytes 7680008 | tf_op jit(solution)/shard_map/sum_two/unit_sum/ppermute | solution.py:60
  337.0 27.3 %all-to-all-start.1 = ((bf16[8,128,256]{2,1,0:T(8,128)(2,1)}), bf16[8,128,256]{2,1,0:T(8,128)(2,1)}, u32[]{:S(2)}, u32[]{:S(2)}) async-start(bf16[8,128,256]{2,1,0:T(8,128)(2,1)} %get-tuple-element.120), calls=%async_computation.2 | async-start | bytes 1048576 | tf_op jit(solution)/shard_map/all_to_all | solution.py:779
  341.2 135.6 %reduce-scatter.7.cloned.1.call-start = ((), (), s32[]{:S(2)}) async-start(), calls=%async_computation.7 | async-start | bytes 3225600
  364.3 38.1 %collective-permute-start.36 = (bf16[2,400,800]{2,1,0:T(8,128)(2,1)}, bf16[2,400,800]{2,1,0:T(8,128)(2,1)S(1)}, u32[]{:S(2)}, u32[]{:S(2)}) collective-permute-start(bf16[2,400,800]{2,1,0:T(8,128)(2,1)} %get-tuple-element.125), channel_id=1, source_target_pairs={{0,16},{8,24},{16,0},{24,8},{1,17},{9,25},{17,1},{25,9},{2,18},{10... | collective-permute-start | bytes 3840008 | tf_op jit(solution)/shard_map/out_sum/unit_sum/ppermute | solution.py:60
  399.1 13.9 %collective-permute-start.39 = (bf16[1,2,400,768]{3,2,1,0:T(8,128)(2,1)}, bf16[1,2,400,768]{3,2,1,0:T(8,128)(2,1)S(1)}, u32[]{:S(2)}, u32[]{:S(2)}) collective-permute-start(bf16[1,2,400,768]{3,2,1,0:T(8,128)(2,1)} %qkv_other.1), channel_id=1, source_target_pairs={{0,8},{8,0},{16,24},{24,16},{1,9},{9,1},{17,25},{25,17},{2,10},{10... | collective-permute-start | bytes 3686408 | tf_op jit(solution)/shard_map/sum_one/qkv_sum/ppermute | solution.py:60
  400.3 10.5 %collective-permute-start.38 = (bf16[64,1600]{1,0:T(8,128)(2,1)}, bf16[64,1600]{1,0:T(8,128)(2,1)S(1)}, u32[]{:S(2)}, u32[]{:S(2)}) collective-permute-start(bf16[64,1600]{1,0:T(8,128)(2,1)} %get-tuple-element.235), channel_id=1, source_target_pairs={{0,1},{2,0},{4,2},{6,4},{7,6},{5,7},{3,5},{1,3},{8,9},{10,8},{12,1... | collective-permute-start | bytes 614408 | tf_op jit(solution)/shard_map/sum_one/ppermute | solution.py:90
  400.3 10.5 %collective-permute-start.37 = (bf16[64,1600]{1,0:T(8,128)(2,1)S(1)}, bf16[64,1600]{1,0:T(8,128)(2,1)S(1)}, u32[]{:S(2)}, u32[]{:S(2)}) collective-permute-start(bf16[64,1600]{1,0:T(8,128)(2,1)S(1)} %get-tuple-element.236), channel_id=1, source_target_pairs={{0,2},{2,4},{4,6},{6,7},{7,5},{5,3},{3,1},{1,0},{8,10},{10,12},{12... | collective-permute-start | bytes 614408 | tf_op jit(solution)/shard_map/sum_one/ppermute | solution.py:90
  413.0 16.0 %collective-permute-start.41 = (bf16[128,1600]{1,0:T(8,128)(2,1)}, bf16[128,1600]{1,0:T(8,128)(2,1)S(1)}, u32[]{:S(2)}, u32[]{:S(2)}) collective-permute-start(bf16[128,1600]{1,0:T(8,128)(2,1)} %get-tuple-element.137), channel_id=1, source_target_pairs={{0,1},{2,0},{4,2},{6,4},{7,6},{5,7},{3,5},{1,3},{8,9},{10,8},{12,1... | collective-permute-start | bytes 1228808 | tf_op jit(solution)/shard_map/sum_one/ppermute | solution.py:90
  413.1 16.0 %collective-permute-start.40 = (bf16[128,1600]{1,0:T(8,128)(2,1)}, bf16[128,1600]{1,0:T(8,128)(2,1)}, u32[]{:S(2)}, u32[]{:S(2)}) collective-permute-start(bf16[128,1600]{1,0:T(8,128)(2,1)} %get-tuple-element.136), channel_id=1, source_target_pairs={{0,2},{2,4},{4,6},{6,7},{7,5},{5,3},{3,1},{1,0},{8,10},{10,12},{12... | collective-permute-start | bytes 1228808 | tf_op jit(solution)/shard_map/sum_one/ppermute | solution.py:90
  416.0 1.3 collective-permute-start.42
  417.3 4.5 collective-permute-start.43
  432.5 19.7 %collective-permute-start.45 = (bf16[128,1600]{1,0:T(8,128)(2,1)}, bf16[128,1600]{1,0:T(8,128)(2,1)S(1)}, u32[]{:S(2)}, u32[]{:S(2)}) collective-permute-start(bf16[128,1600]{1,0:T(8,128)(2,1)} %get-tuple-element.146), channel_id=1, source_target_pairs={{0,1},{2,0},{4,2},{6,4},{7,6},{5,7},{3,5},{1,3},{8,9},{10,8},{12,1... | collective-permute-start | bytes 1228808 | tf_op jit(solution)/shard_map/sum_one/ppermute | solution.py:90
  432.6 19.6 %collective-permute-start.44 = (bf16[128,1600]{1,0:T(8,128)(2,1)S(1)}, bf16[128,1600]{1,0:T(8,128)(2,1)}, u32[]{:S(2)}, u32[]{:S(2)}) collective-permute-start(bf16[128,1600]{1,0:T(8,128)(2,1)S(1)} %get-tuple-element.145), channel_id=1, source_target_pairs={{0,2},{2,4},{4,6},{6,7},{7,5},{5,3},{3,1},{1,0},{8,10},{10,12},{12... | collective-permute-start | bytes 1228808 | tf_op jit(solution)/shard_map/sum_one/ppermute | solution.py:90
  434.6 19.9 %collective-permute-start.53 = (bf16[1,400,768]{2,1,0:T(8,128)(2,1)}, bf16[1,400,768]{2,1,0:T(8,128)(2,1)}, u32[]{:S(2)}, u32[]{:S(2)}) collective-permute-start(bf16[1,400,768]{2,1,0:T(8,128)(2,1)} %get-tuple-element.144), channel_id=1, source_target_pairs={{0,16},{8,24},{16,0},{24,8},{1,17},{9,25},{17,1},{25,9},{2,18},{10... | collective-permute-start | bytes 1843208 | tf_op jit(solution)/shard_map/sum_one/qkv_sum/ppermute | solution.py:60
  454.4 16.7 %collective-permute-start.50 = (f32[19200]{0:T(1024)S(1)}, f32[19200]{0:T(1024)S(1)}, u32[]{:S(2)}, u32[]{:S(2)}) collective-permute-start(f32[19200]{0:T(1024)S(1)} %add.192), channel_id=1, source_target_pairs={{0,1},{1,0},{2,3},{3,2},{4,5},{5,4},{6,7},{7,6},{8,9},{9,8},{10,11... | collective-permute-start | bytes 230408 | tf_op jit(solution)/shard_map/sum_one/sum_vectors/ppermute | solution.py:60
  456.6 20.1 %collective-permute-start.54 = (bf16[400,256]{1,0:T(8,128)(2,1)S(1)}, bf16[400,256]{1,0:T(8,128)(2,1)S(1)}, u32[]{:S(2)}, u32[]{:S(2)}) collective-permute-start(bf16[400,256]{1,0:T(8,128)(2,1)S(1)} %get-tuple-element.230), channel_id=1, source_target_pairs={{5,2},{3,4},{4,1},{0,5},{1,3},{2,6},{6,7},{13,10},{11,12},{12,9},{... | collective-permute-start | bytes 614408 | tf_op jit(solution)/shard_map/sum_one/from_heads/ppermute | solution.py:217
  461.7 15.0 %collective-permute-start.55 = (bf16[400,256]{1,0:T(8,128)(2,1)S(1)}, bf16[400,256]{1,0:T(8,128)(2,1)S(1)}, u32[]{:S(2)}, u32[]{:S(2)}) collective-permute-start(bf16[400,256]{1,0:T(8,128)(2,1)S(1)} %get-tuple-element.229), channel_id=1, source_target_pairs={{3,6},{2,1},{5,5},{4,7},{0,2},{1,0},{11,14},{10,9},{13,13},{12,15}... | collective-permute-start | bytes 614408 | tf_op jit(solution)/shard_map/sum_one/from_heads/ppermute | solution.py:217
  463.6 13.1 %collective-permute-start.56 = (bf16[400,256]{1,0:T(8,128)(2,1)S(1)}, bf16[400,256]{1,0:T(8,128)(2,1)S(1)}, u32[]{:S(2)}, u32[]{:S(2)}) collective-permute-start(bf16[400,256]{1,0:T(8,128)(2,1)S(1)} %get-tuple-element.228), channel_id=1, source_target_pairs={{1,5},{0,0},{3,1},{2,3},{4,4},{5,7},{6,2},{9,13},{8,8},{11,9},{10,... | collective-permute-start | bytes 614408 | tf_op jit(solution)/shard_map/sum_one/from_heads/ppermute | solution.py:217
  464.3 15.8 %collective-permute-start.57 = (bf16[400,128]{1,0:T(8,128)(2,1)S(1)}, bf16[400,128]{1,0:T(8,128)(2,1)S(1)}, u32[]{:S(2)}, u32[]{:S(2)}) collective-permute-start(bf16[400,128]{1,0:T(8,128)(2,1)S(1)} %slice.271), channel_id=1, source_target_pairs={{4,2},{5,4},{0,3},{6,5},{2,0},{3,7},{1,6},{12,10},{13,12},{8,11},{... | collective-permute-start | bytes 307208 | tf_op jit(solution)/shard_map/sum_one/from_heads/ppermute | solution.py:217
  471.2 4.5 collective-permute-start.51
  475.6 18.5 %collective-permute-start.52 = (f32[19200]{0:T(1024)S(1)}, f32[19200]{0:T(1024)S(1)}, u32[]{:S(2)}, u32[]{:S(2)}) collective-permute-start(f32[19200]{0:T(1024)S(1)} %add.199), channel_id=1, source_target_pairs={{0,4},{1,5},{2,6},{3,7},{4,0},{5,1},{6,2},{7,3},{8,12},{9,13},{10,... | collective-permute-start | bytes 230408 | tf_op jit(solution)/shard_map/sum_one/sum_vectors/ppermute | solution.py:60
  478.3 4.9 collective-permute-start.46
  483.2 4.7 collective-permute-start.47
  489.1 8.2 %collective-permute-start.49 = (bf16[128,1600]{1,0:T(8,128)(2,1)S(1)}, bf16[128,1600]{1,0:T(8,128)(2,1)S(1)}, u32[]{:S(2)}, u32[]{:S(2)}) collective-permute-start(bf16[128,1600]{1,0:T(8,128)(2,1)S(1)} %copy-done.19), channel_id=1, source_target_pairs={{0,1},{2,0},{4,2},{6,4},{7,6},{5,7},{3,5},{1,3},{8,9},{10,8},{12,1... | collective-permute-start | bytes 1228808 | tf_op jit(solution)/shard_map/sum_one/ppermute | solution.py:90
  489.7 9.1 %collective-permute-start.48 = (bf16[128,1600]{1,0:T(8,128)(2,1)S(1)}, bf16[128,1600]{1,0:T(8,128)(2,1)S(1)}, u32[]{:S(2)}, u32[]{:S(2)}) collective-permute-start(bf16[128,1600]{1,0:T(8,128)(2,1)S(1)} %get-tuple-element.148), channel_id=1, source_target_pairs={{0,2},{2,4},{4,6},{6,7},{7,5},{5,3},{3,1},{1,0},{8,10},{10,12},{12... | collective-permute-start | bytes 1228808 | tf_op jit(solution)/shard_map/sum_one/ppermute | solution.py:90
  (46 other events, 610.1 us)
Sparse Core Ops, SparseCore 0:
  31.6 89.4 all-gather.5
  123.2 80.8 all-gather.3
  255.9 93.6 reduce-scatter.4
  366.2 93.2 reduce-scatter.6

commit v5 on v4

--- a/solution.py
+++ b/solution.py
@@ -621,12 +621,12 @@
     def ride_first(hold):
         with jax.named_scope("to_heads"):
             held["first"] = take_rounds(sent_heads, moves[:first])
+        held["out"] = lax.all_gather(jnp.transpose(out_weight), ("seq", "ctx"), axis=0)
         return held["first"]
 
     def ride_second(hold):
         with jax.named_scope("to_heads"):
             held["second"] = take_rounds(hold(sent_heads), moves[first:])
-        held["out"] = lax.all_gather(jnp.transpose(hold(out_weight)), ("seq", "ctx"), axis=0)
         return held["second"]
 
     def ride_row_parts(hold):

time: 518 us -> 508 us (0.981)
  waiting for transfers between devices: 175 us -> 168 us
    ppermute x32, waiting for transfers between devices: 120 us -> 98.8 us  [shift(): lax.ppermute(values, 'ctx', [(order[i], order[(i + offset) % count]) for...]
    ppermute x8, waiting for transfers between devices: 20.4 us -> 26.8 us  [move(): lax.ppermute(values, 'ctx', pairs)]
    unnamed x105 -> x104, local copies, waits for them, and re-layouts: 9.77 us -> 11.5 us
  transfers between devices with their start and end apart: 64 -> 64, of which waited for: 28 -> 30; matrix products, arithmetic and copies ran while one was open for 11% -> 12% of each run, Pallas kernels for 23% -> 23%
where the time goes in v5:
time: 508 us; the launch traced here: 503 us
  waiting for transfers between devices  168 us (33%)
  Pallas kernels  138 us (27%)
  starting transfers between devices  108 us (21%)
  other arithmetic  34.3 us (7%)
  local copies, waits for them, and re-layouts  30 us (6%)
  between operations  17.7 us (3%)
  matrix products  6.78 us (1%)
    pallas_call x13, Pallas kernels, call(): pl.pallas_call(kernel, in_specs=spec, out_specs=[pl.BlockSpec(memory_spac...  138 us
    ppermute x32, waiting for transfers between devices, shift(): lax.ppermute(values, 'ctx', [(order[i], order[(i + offset) % count]) for...  98.8 us
    ppermute x32, starting transfers between devices, shift(): lax.ppermute(values, 'ctx', [(order[i], order[(i + offset) % count]) for...  61.5 us
    ppermute x18, waiting for transfers between devices, swap(): return lax.ppermute(values, axis, [(i, i ^ bit) for i in range(count)])  35 us
    ppermute x8, waiting for transfers between devices, move(): lax.ppermute(values, 'ctx', pairs)  26.8 us
    ppermute x8, starting transfers between devices, move(): lax.ppermute(values, 'ctx', pairs)  25.1 us
    unnamed x104, local copies, waits for them, and re-layouts  11.5 us
    ppermute x18, starting transfers between devices, swap(): return lax.ppermute(values, axis, [(i, i ^ bit) for i in range(count)])  10.6 us
  transfers between devices with their start and end apart: 64, of which 30 were waited for; matrix products, arithmetic and copies ran while one was open for 12% of the time, Pallas kernels for 23%

profile of v5, /device:TPU:0, one launch (start us, length us, event | category | flops | bytes accessed | tf_op | source)
XLA Modules:
  0.0 502.5 jit_solution(14268065371325154948)
XLA Ops:
  10.8 2.0 fusion.14
  12.8 3.0 collective-permute-start.2
  18.8 7.0 %collective-permute-start.1 = (bf16[400,256]{1,0:T(8,128)(2,1)S(1)}, bf16[400,256]{1,0:T(8,128)(2,1)S(1)}, u32[]{:S(2)}, u32[]{:S(2)}) collective-permute-start(bf16[400,256]{1,0:T(8,128)(2,1)S(1)} %get-tuple-element.229), channel_id=1, source_target_pairs={{6,3},{1,2},{5,5},{7,4},{2,0},{0,1},{14,11},{9,10},{13,13},{15,12}... | collective-permute-start | bytes 614408 | tf_op jit(solution)/shard_map/gather_one/to_heads/ppermute | solution.py:217
  26.6 9.1 %collective-permute-done = bf16[400,256]{1,0:T(8,128)(2,1)S(1)} collective-permute-done((bf16[400,256]{1,0:T(8,128)(2,1)S(1)}, bf16[400,256]{1,0:T(8,128)(2,1)S(1)}, u32[]{:S(2)}, u32[]{:S(2)}) %collective-permute-start) | collective-permute-done | bytes 204832 | tf_op jit(solution)/shard_map/gather_one/to_heads/ppermute | solution.py:217
  36.5 8.4 %collective-permute-start.6 = (bf16[128,1600]{1,0:T(8,128)(2,1)S(1)}, bf16[128,1600]{1,0:T(8,128)(2,1)S(1)}, u32[]{:S(2)}, u32[]{:S(2)}) collective-permute-start(bf16[128,1600]{1,0:T(8,128)(2,1)S(1)} %collective-permute-done.2.rest_8_), channel_id=1, source_target_pairs={{0,2},{2,4},{4,6},{6,7},{7,5},{5,3},{3,1},{1,0},{8,10},{10,12},{12... | collective-permute-start | bytes 1228808 | tf_op jit(solution)/shard_map/gather_one/ppermute | solution.py:90
  44.9 4.9 collective-permute-start.7
  51.8 17.7 %collective-permute-done.5 = bf16[400,128]{1,0:T(8,128)(2,1)S(1)} collective-permute-done((bf16[400,128]{1,0:T(8,128)(2,1)S(1)}, bf16[400,128]{1,0:T(8,128)(2,1)S(1)}, u32[]{:S(2)}, u32[]{:S(2)}) %collective-permute-start.5) | collective-permute-done | bytes 102432 | tf_op jit(solution)/shard_map/gather_one/to_heads/ppermute | solution.py:217
  72.1 2.0 collective-permute-start.10
  74.2 18.9 %collective-permute-done.9.rest_6_ = bf16[128,1600]{1,0:T(8,128)(2,1)S(1)} collective-permute-done((bf16[128,1600]{1,0:T(8,128)(2,1)S(1)}, bf16[128,1600]{1,0:T(8,128)(2,1)S(1)}, u32[]{:S(2)}, u32[]{:S(2)}) %collective-permute-start.9) | collective-permute-done | bytes 409632 | tf_op jit(solution)/shard_map/gather_one/ppermute | solution.py:90
  93.1 4.0 collective-permute-done.8
  97.3 2.3 copy.56
  102.2 2.3 collective-permute-start.13
  105.6 3.6 collective-permute-done.12.rest_4_
  110.2 15.0 %attend.1 = (bf16[1024,1600]{1,0:T(8,128)(2,1)}, bf16[1600,768]{1,0:T(8,128)(2,1)}, bf16[1024,768]{1,0:T(8,128)(2,1)}, f32[1024,256]{1,0:T(8,128)}, bf16[8,128,256]{2,1,0:T(8,128)(2,1)}, /*index=5*/f32[1024,4]{1,0:T(8,128)}) custom-call(s32[8]{0:T(128)} %get-tuple-element.248.member_ref, s32[1]{0:T(128)} %bitcast.1.place_ref, s32[8]{0:T(128)} %pair_of_ref.1, ...), custom_call_target="tpu_custom_call" | custom-call | flops 1000 | bytes 180000000 | tf_op jit(solution)/shard_map/attend/pallas_call | solution.py:246
  126.6 6.2 %all-to-all-start = ((bf16[8,128,256]{2,1,0:T(8,128)(2,1)}), bf16[8,128,256]{2,1,0:T(8,128)(2,1)}, u32[]{:S(2)}, u32[]{:S(2)}) async-start(bf16[8,128,256]{2,1,0:T(8,128)(2,1)} %get-tuple-element.93), calls=%async_computation | async-start | bytes 1048576 | tf_op jit(solution)/shard_map/all_to_all | solution.py:677
  135.1 14.2 %collective-permute-done.15 = bf16[400,800]{1,0:T(8,128)(2,1)S(1)} collective-permute-done((bf16[400,800]{1,0:T(8,128)(2,1)S(1)}, bf16[400,800]{1,0:T(8,128)(2,1)S(1)}, u32[]{:S(2)}, u32[]{:S(2)}) %collective-permute-start.15) | collective-permute-done | bytes 640032 | tf_op jit(solution)/shard_map/unit_parts/ppermute | solution.py:60
  150.6 7.0 %all-to-all-done.back_ref = bf16[8,128,256]{2,1,0:T(8,128)(2,1)} async-done(((bf16[8,128,256]{2,1,0:T(8,128)(2,1)}), bf16[8,128,256]{2,1,0:T(8,128)(2,1)}, u32[]{:S(2)}, u32[]{:S(2)}) %all-to-all-start) | async-done | bytes 524320 | tf_op jit(solution)/shard_map/all_to_all | solution.py:677
  157.7 7.3 %out.1 = (f32[128,1600]{1,0:T(8,128)}, bf16[128,1600]{1,0:T(8,128)(2,1)}, f32[128,1600]{1,0:T(8,128)}, f32[128,1]{1,0:T(8,128)}, bf16[128,1600]{1,0:T(8,128)(2,1)}) custom-call(bf16[8,128,256]{2,1,0:T(8,128)(2,1)} %all-to-all-done.back_ref, bf16[128,1600]{1,0:T(8,128)(2,1)} %bitcast.99, f32[1,1600]{1,0:T(1,128)} %broadcast_in_dim.59.bias_ref, ...), custom_call_target="tpu_custom_call" | custom-call | flops 1000 | bytes 90000000 | tf_op jit(solution)/shard_map/out/pallas_call | solution.py:246
  165.0 2.1 collective-permute-start.18
  167.6 10.0 %collective-permute-done.21.rest_8_ = bf16[128,1600]{1,0:T(8,128)(2,1)S(1)} collective-permute-done((bf16[128,1600]{1,0:T(8,128)(2,1)}, bf16[128,1600]{1,0:T(8,128)(2,1)S(1)}, u32[]{:S(2)}, u32[]{:S(2)}) %collective-permute-start.21) | collective-permute-done | bytes 409632 | tf_op jit(solution)/shard_map/gather_two/ppermute | solution.py:90
  177.7 3.5 collective-permute-start.22
  183.5 8.4 %collective-permute-done.22.rest_7_ = bf16[128,1600]{1,0:T(8,128)(2,1)S(1)} collective-permute-done((bf16[128,1600]{1,0:T(8,128)(2,1)S(1)}, bf16[128,1600]{1,0:T(8,128)(2,1)S(1)}, u32[]{:S(2)}, u32[]{:S(2)}) %collective-permute-start.22) | collective-permute-done | bytes 409632 | tf_op jit(solution)/shard_map/gather_two/ppermute | solution.py:90
  191.9 2.1 collective-permute-start.20
  194.0 7.5 %collective-permute-done.23.rest_6_ = bf16[128,1600]{1,0:T(8,128)(2,1)S(1)} collective-permute-done((bf16[128,1600]{1,0:T(8,128)(2,1)S(1)}, bf16[128,1600]{1,0:T(8,128)(2,1)S(1)}, u32[]{:S(2)}, u32[]{:S(2)}) %collective-permute-start.23) | collective-permute-done | bytes 409632 | tf_op jit(solution)/shard_map/gather_two/ppermute | solution.py:90
  204.0 2.1 collective-permute-start.25
  208.7 8.8 %hidden_grad.1 = (bf16[1600,800]{1,0:T(8,128)(2,1)}, f32[1024,800]{1,0:T(8,128)}) custom-call(s32[1]{0:T(128)} %bitcast.1.place_ref, bf16[1024,1600]{1,0:T(8,128)(2,1)} %all-gather.4.cloned.1.call-done.cot_ref.rest_2_, bf16[2,400,800]{2,1,0:T(8,128)(2,1)} %copy-done.5, bf16[2,400,800]{2,1,0:T(8,128)(2,1)} %collective-permute-done.17.peer_ref), custom_call_target="tpu_custom_call" | custom-call | flops 1000 | bytes 27000000 | tf_op jit(solution)/shard_map/hidden_grad/pallas_call | solution.py:246
  217.5 18.6 %hidden.1 = (bf16[1024,1600]{1,0:T(8,128)(2,1)}, bf16[1024,800]{1,0:T(8,128)(2,1)}, bf16[1024,800]{1,0:T(8,128)(2,1)}, bf16[8,128,1600]{2,1,0:T(8,128)(2,1)}, bf...) custom-call(s32[8]{0:T(128)} %get-tuple-element.248.member_ref, s32[8]{0:T(128)} %fusion.23.offset_ref, s32[1]{0:T(128)} %bitcast.1.place_ref, ...), custom_call_target="tpu_custom_call" | custom-call | flops 1000 | bytes 240000000 | tf_op jit(solution)/shard_map/hidden/pallas_call | solution.py:246
  237.2 2.0 collective-permute-start.27
  239.4 8.1 %branch.1 = bf16[1024,1600]{1,0:T(8,128)(2,1)} custom-call(bf16[1024,800]{1,0:T(8,128)(2,1)} %get-tuple-element.106.value_ref.rest_3_, bf16[1600,800]{1,0:T(8,128)(2,1)} %get-tuple-element.107.w_ref), custom_call_target="tpu_custom_call" | custom-call | flops 1000 | bytes 24000000 | tf_op jit(solution)/shard_map/sum_two/branch/pallas_call | solution.py:246
  250.9 12.3 %collective-permute-done.29 = bf16[128,1600]{1,0:T(8,128)(2,1)S(1)} collective-permute-done((bf16[128,1600]{1,0:T(8,128)(2,1)S(1)}, bf16[128,1600]{1,0:T(8,128)(2,1)S(1)}, u32[]{:S(2)}, u32[]{:S(2)}) %collective-permute-start.29) | collective-permute-done | bytes 409632 | tf_op jit(solution)/shard_map/sum_two/ppermute | solution.py:90
  263.2 2.3 collective-permute-done.28
  266.9 11.8 %collective-permute-start.31 = (bf16[128,1600]{1,0:T(8,128)(2,1)S(1)}, bf16[128,1600]{1,0:T(8,128)(2,1)S(1)}, u32[]{:S(2)}, u32[]{:S(2)}) collective-permute-start(bf16[128,1600]{1,0:T(8,128)(2,1)S(1)} %get-tuple-element.109), channel_id=1, source_target_pairs={{0,1},{2,0},{4,2},{6,4},{7,6},{5,7},{3,5},{1,3},{8,9},{10,8},{12,1... | collective-permute-start | bytes 1228808 | tf_op jit(solution)/shard_map/sum_two/ppermute | solution.py:90
  278.7 11.1 %unit_other.1 = bf16[2,2,400,800]{3,2,1,0:T(8,128)(2,1)} custom-call(s32[1]{0:T(128)} %bitcast.22.core_ref, bf16[1024,1600]{1,0:T(8,128)(2,1)} %get-tuple-element.111.rest_0_, bf16[1024,800]{1,0:T(8,128)(2,1)} %get-tuple-element.112.rest_1_, bf16[1024,1600]{1,0:T(8,128)(2,1)} %all-gather.4.cloned.1.call-done.cot_ref.rest_2_, ...), custom_call_target="tpu_custom_call" | custom-call | flops 1000 | bytes 24000000 | tf_op jit(solution)/shard_map/sum_two/unit_sum/unit_other/pallas_call | solution.py:246
  289.8 4.7 collective-permute-done.31
  297.0 4.2 collective-permute-start.33
  301.6 9.8 %collective-permute-done.33 = bf16[128,1600]{1,0:T(8,128)(2,1)S(1)} collective-permute-done((bf16[128,1600]{1,0:T(8,128)(2,1)S(1)}, bf16[128,1600]{1,0:T(8,128)(2,1)S(1)}, u32[]{:S(2)}, u32[]{:S(2)}) %collective-permute-start.33) | collective-permute-done | bytes 409632 | tf_op jit(solution)/shard_map/sum_two/ppermute | solution.py:90
  311.4 2.8 collective-permute-done.32
  314.3 2.1 fusion.18.sum_ref
  316.4 10.9 %out_back.1 = (f32[128,1600]{1,0:T(8,128)}, bf16[128,1600]{1,0:T(8,128)(2,1)}, bf16[8,128,256]{2,1,0:T(8,128)(2,1)}, f32[4,1600]{1,0:T(4,128)}, f32[8,200,800]{2,1,0:T(8,128)}, /*index=5*/bf16[8,200,800]{2,1,0:T(8,128)(2,1)}) custom-call(s32[1]{0:T(128)} %bitcast.22.core_ref, f32[128,1600]{1,0:T(8,128)} %fusion.18.sum_ref, bf16[128,1600]{1,0:T(8,128)(2,1)} %bitcast.101, ...), custom_call_target="tpu_custom_call" | custom-call | flops 1000 | bytes 135000000 | tf_op jit(solution)/shard_map/out_back/pallas_call | solution.py:246
  327.8 4.2 all-to-all-start.1
  332.0 4.2 collective-permute-done.34
  336.2 5.7 %add_convert_fusion = bf16[8,200,800]{2,1,0:T(8,128)(2,1)} fusion(f32[8,200,800]{2,1,0:T(8,128)} %get-tuple-element.119, bf16[8,200,800]{2,1,0:T(8,128)(2,1)} %collective-permute-done.34), kind=kLoop, calls=%fused_computation.1 | loop fusion | flops 3840000 | bytes 10240000 | tf_op jit(solution)/shard_map/out_sum/convert_element_type | solution.py:782
  341.9 13.2 %unit_mine.1 = (f32[2,400,800]{2,1,0:T(8,128)}, bf16[2,400,800]{2,1,0:T(8,128)(2,1)}) custom-call(s32[1]{0:T(128)} %bitcast.22.core_ref, s32[1]{0:T(128)} %bitcast.28.row_ref, bf16[2,2,400,800]{3,2,1,0:T(8,128)(2,1)} %collective-permute-done.35.got_ref, bf16[1024,1600]{1,0:T(8,128)(2,1)} %get-tuple-element.111.rest_0_, ...), custom_call_target="tpu_custom_call" | custom-call | flops 1000 | bytes 30000000 | tf_op jit(solution)/shard_map/out_sum/unit_sum/unit_mine/pallas_call | solution.py:246
  361.9 20.4 %attend_back.1 = (bf16[1024,768]{1,0:T(8,128)(2,1)}, f32[1,768]{1,0:T(1,128)}, bf16[128,1600]{1,0:T(8,128)(2,1)}) custom-call(s32[16]{0:T(128)} %pad_add_fusion.who_ref, s32[2]{0:T(128)} %pad_add_fusion.1.far_ref, bf16[1024,768]{1,0:T(8,128)(2,1)} %get-tuple-element.125.qkv_ref, bf16[1600,768]{1,0:T(8,128)(2,1)} %get-tuple-element.126.w_ref, ...), custom_call_target="tpu_custom_call" | custom-call | flops 1000 | bytes 240000000 | tf_op jit(solution)/shard_map/attend_back/pallas_call | solution.py:246
  382.2 6.1 %qkv_other.1 = bf16[1,2,400,768]{3,2,1,0:T(8,128)(2,1)} custom-call(s32[1]{0:T(128)} %bitcast.22.core_ref, bf16[1024,1600]{1,0:T(8,128)(2,1)} %get-tuple-element.131.x_ref.rest_0_, bf16[1024,768]{1,0:T(8,128)(2,1)} %get-tuple-element.130.grad_ref.rest_1_), custom_call_target="tpu_custom_call" | custom-call | flops 1000 | bytes 15000000 | tf_op jit(solution)/shard_map/sum_one/qkv_sum/qkv_other/pallas_call | solution.py:246
  389.7 2.0 collective-permute-start.37
  391.9 8.4 %project_back.1 = (bf16[8,128,1600]{2,1,0:T(8,128)(2,1)}, f32[2,1600]{1,0:T(2,128)}) custom-call(s32[16]{0:T(128)} %gather_fusion, bf16[1024,768]{1,0:T(8,128)(2,1)} %get-tuple-element.130.grad_ref.rest_1_, bf16[1600,768]{1,0:T(8,128)(2,1)} %get-tuple-element.126.w_ref, bf16[1024,1600]{1,0:T(8,128)(2,1)} %get-tuple-element.131.x_ref.rest_0_), custom_call_target="tpu_custom_call" | custom-call | flops 1000 | bytes 18000000 | tf_op jit(solution)/shard_map/project_back/pallas_call | solution.py:246
  401.2 2.2 convert_add_fusion.2
  403.5 2.0 collective-permute-start.40
  409.3 2.9 collective-permute-done.43
  412.2 7.4 %qkv_mine.1 = (f32[1,400,768]{2,1,0:T(8,128)}, bf16[1,400,768]{2,1,0:T(8,128)(2,1)}) custom-call(s32[1]{0:T(128)} %bitcast.22.core_ref, s32[1]{0:T(128)} %bitcast.28.row_ref, bf16[1,2,400,768]{3,2,1,0:T(8,128)(2,1)} %copy-done.10, bf16[1024,1600]{1,0:T(8,128)(2,1)} %get-tuple-element.131.x_ref.rest_0_, bf16[1024,768]{1,0:T(8,128)(2,1)} %get-tuple-element.130.grad_ref.rest_1_), custom_call_target="tpu_custom_call" | custom-call | flops 1000 | bytes 18000000 | tf_op jit(solution)/shard_map/sum_one/qkv_sum/qkv_mine/pallas_call | solution.py:246
  420.2 2.2 convert_add_fusion.1
  423.6 2.0 collective-permute-start.44
  428.7 14.1 %collective-permute-done.45 = bf16[128,1600]{1,0:T(8,128)(2,1)S(1)} collective-permute-done((bf16[128,1600]{1,0:T(8,128)(2,1)}, bf16[128,1600]{1,0:T(8,128)(2,1)S(1)}, u32[]{:S(2)}, u32[]{:S(2)}) %collective-permute-start.45) | collective-permute-done | bytes 409632 | tf_op jit(solution)/shard_map/sum_one/ppermute | solution.py:90
  442.9 2.3 convert_add_fusion
  445.2 2.0 fusion.8
  447.3 5.0 collective-permute-start.54
  454.9 6.6 %collective-permute-start.57 = (bf16[400,128]{1,0:T(8,128)(2,1)S(1)}, bf16[400,128]{1,0:T(8,128)(2,1)S(1)}, u32[]{:S(2)}, u32[]{:S(2)}) collective-permute-start(bf16[400,128]{1,0:T(8,128)(2,1)S(1)} %slice.271), channel_id=1, source_target_pairs={{4,2},{5,4},{0,3},{6,5},{2,0},{3,7},{1,6},{12,10},{13,12},{8,11},{... | collective-permute-start | bytes 307208 | tf_op jit(solution)/shard_map/sum_one/from_heads/ppermute | solution.py:217
  463.7 2.5 collective-permute-done.51
  471.2 2.6 collective-permute-done.46
  475.9 2.6 collective-permute-done.47
  481.8 3.0 fusion.2
  488.6 2.2 fusion.17.sum_ref
  490.8 2.8 input_grad.1
  (270 shorter events, 75.9 us)
Async XLA Ops:
  7.2 150.5 %all-gather.6.cloned.1.call-start = ((), (), s32[]{:S(2)}) async-start(), calls=%async_computation.6 | async-start | bytes 6758400 | tf_op jit(solution)/shard_map/gather_one/all_gather | solution.py:624
  9.0 199.7 %all-gather.4.cloned.1.call-start = ((), (), s32[]{:S(2)}) async-start(), calls=%async_computation.4 | async-start | bytes 3833856 | tf_op jit(solution)/shard_map/all_gather | solution.py:675
  12.8 22.9 %collective-permute-start.2 = (bf16[128,1600]{1,0:T(8,128)(2,1)S(1)}, bf16[128,1600]{1,0:T(8,128)(2,1)S(1)}, u32[]{:S(2)}, u32[]{:S(2)}) collective-permute-start(bf16[128,1600]{1,0:T(8,128)(2,1)S(1)} %get-tuple-element.232.rest_0_), channel_id=1, source_target_pairs={{0,2},{2,4},{4,6},{6,7},{7,5},{5,3},{3,1},{1,0},{8,10},{10,12},{12... | collective-permute-start | bytes 1228808 | tf_op jit(solution)/shard_map/gather_one/ppermute | solution.py:90
  15.8 19.9 %collective-permute-start.3 = (bf16[128,1600]{1,0:T(8,128)(2,1)S(1)}, bf16[128,1600]{1,0:T(8,128)(2,1)S(1)}, u32[]{:S(2)}, u32[]{:S(2)}) collective-permute-start(bf16[128,1600]{1,0:T(8,128)(2,1)S(1)} %get-tuple-element.232.rest_0_), channel_id=1, source_target_pairs={{0,1},{2,0},{4,2},{6,4},{7,6},{5,7},{3,5},{1,3},{8,9},{10,8},{12,1... | collective-permute-start | bytes 1228808 | tf_op jit(solution)/shard_map/gather_one/ppermute | solution.py:90
  17.5 18.2 %collective-permute-start = (bf16[400,256]{1,0:T(8,128)(2,1)S(1)}, bf16[400,256]{1,0:T(8,128)(2,1)S(1)}, u32[]{:S(2)}, u32[]{:S(2)}) collective-permute-start(bf16[400,256]{1,0:T(8,128)(2,1)S(1)} %get-tuple-element.230), channel_id=1, source_target_pairs={{2,5},{4,3},{1,4},{5,0},{3,1},{6,2},{7,6},{10,13},{12,11},{9,12},{... | collective-permute-start | bytes 614408 | tf_op jit(solution)/shard_map/gather_one/to_heads/ppermute | solution.py:217
  18.8 16.9 %collective-permute-start.1 = (bf16[400,256]{1,0:T(8,128)(2,1)S(1)}, bf16[400,256]{1,0:T(8,128)(2,1)S(1)}, u32[]{:S(2)}, u32[]{:S(2)}) collective-permute-start(bf16[400,256]{1,0:T(8,128)(2,1)S(1)} %get-tuple-element.229), channel_id=1, source_target_pairs={{6,3},{1,2},{5,5},{7,4},{2,0},{0,1},{14,11},{9,10},{13,13},{15,12}... | collective-permute-start | bytes 614408 | tf_op jit(solution)/shard_map/gather_one/to_heads/ppermute | solution.py:217
  35.8 16.0 %collective-permute-start.4 = (bf16[400,256]{1,0:T(8,128)(2,1)S(1)}, bf16[400,256]{1,0:T(8,128)(2,1)S(1)}, u32[]{:S(2)}, u32[]{:S(2)}) collective-permute-start(bf16[400,256]{1,0:T(8,128)(2,1)S(1)} %slice.198), channel_id=1, source_target_pairs={{5,1},{0,0},{1,3},{3,2},{4,4},{7,5},{2,6},{13,9},{8,8},{9,11},{11,... | collective-permute-start | bytes 614408 | tf_op jit(solution)/shard_map/gather_one/to_heads/ppermute | solution.py:217
  36.5 33.0 %collective-permute-start.6 = (bf16[128,1600]{1,0:T(8,128)(2,1)S(1)}, bf16[128,1600]{1,0:T(8,128)(2,1)S(1)}, u32[]{:S(2)}, u32[]{:S(2)}) collective-permute-start(bf16[128,1600]{1,0:T(8,128)(2,1)S(1)} %collective-permute-done.2.rest_8_), channel_id=1, source_target_pairs={{0,2},{2,4},{4,6},{6,7},{7,5},{5,3},{3,1},{1,0},{8,10},{10,12},{12... | collective-permute-start | bytes 1228808 | tf_op jit(solution)/shard_map/gather_one/ppermute | solution.py:90
  44.9 24.7 %collective-permute-start.7 = (bf16[128,1600]{1,0:T(8,128)(2,1)S(1)}, bf16[128,1600]{1,0:T(8,128)(2,1)S(1)}, u32[]{:S(2)}, u32[]{:S(2)}) collective-permute-start(bf16[128,1600]{1,0:T(8,128)(2,1)S(1)} %collective-permute-done.3.rest_1_), channel_id=1, source_target_pairs={{0,1},{2,0},{4,2},{6,4},{7,6},{5,7},{3,5},{1,3},{8,9},{10,8},{12,1... | collective-permute-start | bytes 1228808 | tf_op jit(solution)/shard_map/gather_one/ppermute | solution.py:90
  49.8 19.7 %collective-permute-start.5 = (bf16[400,128]{1,0:T(8,128)(2,1)S(1)}, bf16[400,128]{1,0:T(8,128)(2,1)S(1)}, u32[]{:S(2)}, u32[]{:S(2)}) collective-permute-start(bf16[400,128]{1,0:T(8,128)(2,1)S(1)} %slice.199), channel_id=1, source_target_pairs={{2,4},{4,5},{3,0},{5,6},{0,2},{7,3},{6,1},{10,12},{12,13},{11,8},{... | collective-permute-start | bytes 307208 | tf_op jit(solution)/shard_map/gather_one/to_heads/ppermute | solution.py:217
  70.6 26.5 %collective-permute-start.8 = (bf16[400,768]{1,0:T(8,128)(2,1)S(1)}, bf16[400,768]{1,0:T(8,128)(2,1)S(1)}, u32[]{:S(2)}, u32[]{:S(2)}) collective-permute-start(bf16[400,768]{1,0:T(8,128)(2,1)S(1)} %fusion.10), channel_id=1, source_target_pairs={{0,16},{8,24},{16,0},{24,8},{1,17},{9,25},{17,1},{25,9},{2,18},{10... | collective-permute-start | bytes 1843208 | tf_op jit(solution)/shard_map/gather_one/qkv_parts/ppermute | solution.py:60
  72.1 21.0 %collective-permute-start.9 = (bf16[128,1600]{1,0:T(8,128)(2,1)S(1)}, bf16[128,1600]{1,0:T(8,128)(2,1)S(1)}, u32[]{:S(2)}, u32[]{:S(2)}) collective-permute-start(bf16[128,1600]{1,0:T(8,128)(2,1)S(1)} %collective-permute-done.6.rest_7_), channel_id=1, source_target_pairs={{0,2},{2,4},{4,6},{6,7},{7,5},{5,3},{3,1},{1,0},{8,10},{10,12},{12... | collective-permute-start | bytes 1228808 | tf_op jit(solution)/shard_map/gather_one/ppermute | solution.py:90
  72.1 21.0 %collective-permute-start.10 = (bf16[128,1600]{1,0:T(8,128)(2,1)S(1)}, bf16[128,1600]{1,0:T(8,128)(2,1)S(1)}, u32[]{:S(2)}, u32[]{:S(2)}) collective-permute-start(bf16[128,1600]{1,0:T(8,128)(2,1)S(1)} %collective-permute-done.7.rest_2_), channel_id=1, source_target_pairs={{0,1},{2,0},{4,2},{6,4},{7,6},{5,7},{3,5},{1,3},{8,9},{10,8},{12,1... | collective-permute-start | bytes 1228808 | tf_op jit(solution)/shard_map/gather_one/ppermute | solution.py:90
  97.2 3.0 collective-permute-start.11
  100.2 25.1 %collective-permute-start.14 = (bf16[400,800]{1,0:T(8,128)(2,1)}, bf16[400,800]{1,0:T(8,128)(2,1)}, u32[]{:S(2)}, u32[]{:S(2)}) collective-permute-start(bf16[400,800]{1,0:T(8,128)(2,1)} %bitcast.107), channel_id=1, source_target_pairs={{0,16},{8,24},{16,0},{24,8},{1,17},{9,25},{17,1},{25,9},{2,18},{10... | collective-permute-start | bytes 1920008 | tf_op jit(solution)/shard_map/unit_parts/ppermute | solution.py:60
  102.1 7.1 %collective-permute-start.12 = (bf16[64,1600]{1,0:T(8,128)(2,1)S(1)}, bf16[64,1600]{1,0:T(8,128)(2,1)S(1)}, u32[]{:S(2)}, u32[]{:S(2)}) collective-permute-start(bf16[64,1600]{1,0:T(8,128)(2,1)S(1)} %slice.257), channel_id=1, source_target_pairs={{0,2},{2,4},{4,6},{6,7},{7,5},{5,3},{3,1},{1,0},{8,10},{10,12},{12... | collective-permute-start | bytes 614408 | tf_op jit(solution)/shard_map/gather_one/ppermute | solution.py:90
  102.2 7.3 %collective-permute-start.13 = (bf16[64,1600]{1,0:T(8,128)(2,1)S(1)}, bf16[64,1600]{1,0:T(8,128)(2,1)S(1)}, u32[]{:S(2)}, u32[]{:S(2)}) collective-permute-start(bf16[64,1600]{1,0:T(8,128)(2,1)S(1)} %slice.258), channel_id=1, source_target_pairs={{0,1},{2,0},{4,2},{6,4},{7,6},{5,7},{3,5},{1,3},{8,9},{10,8},{12,1... | collective-permute-start | bytes 614408 | tf_op jit(solution)/shard_map/gather_one/ppermute | solution.py:90
  126.6 31.0 %all-to-all-start = ((bf16[8,128,256]{2,1,0:T(8,128)(2,1)}), bf16[8,128,256]{2,1,0:T(8,128)(2,1)}, u32[]{:S(2)}, u32[]{:S(2)}) async-start(bf16[8,128,256]{2,1,0:T(8,128)(2,1)} %get-tuple-element.93), calls=%async_computation | async-start | bytes 1048576 | tf_op jit(solution)/shard_map/all_to_all | solution.py:677
  132.8 289.6 %reduce-scatter.5.cloned.1.call-start = ((), (), s32[]{:S(2)}) async-start(), calls=%async_computation.5 | async-start | bytes 3833856 | tf_op jit(solution)/shard_map/reduce_scatter | solution.py:759
  132.9 16.4 %collective-permute-start.15 = (bf16[400,800]{1,0:T(8,128)(2,1)S(1)}, bf16[400,800]{1,0:T(8,128)(2,1)S(1)}, u32[]{:S(2)}, u32[]{:S(2)}) collective-permute-start(bf16[400,800]{1,0:T(8,128)(2,1)S(1)} %copy-done.18), channel_id=1, source_target_pairs={{0,16},{8,24},{16,0},{24,8},{1,17},{9,25},{17,1},{25,9},{2,18},{10... | collective-permute-start | bytes 1920008 | tf_op jit(solution)/shard_map/unit_parts/ppermute | solution.py:60
  165.0 12.7 %collective-permute-start.21 = (bf16[128,1600]{1,0:T(8,128)(2,1)}, bf16[128,1600]{1,0:T(8,128)(2,1)S(1)}, u32[]{:S(2)}, u32[]{:S(2)}) collective-permute-start(bf16[128,1600]{1,0:T(8,128)(2,1)} %get-tuple-element.102.rest_0_), channel_id=1, source_target_pairs={{0,2},{2,4},{4,6},{6,7},{7,5},{5,3},{3,1},{1,0},{8,10},{10,12},{12... | collective-permute-start | bytes 1228808 | tf_op jit(solution)/shard_map/gather_two/ppermute | solution.py:90
  165.0 16.6 %collective-permute-start.18 = (bf16[128,1600]{1,0:T(8,128)(2,1)}, bf16[128,1600]{1,0:T(8,128)(2,1)S(1)}, u32[]{:S(2)}, u32[]{:S(2)}) collective-permute-start(bf16[128,1600]{1,0:T(8,128)(2,1)} %get-tuple-element.102.rest_0_), channel_id=1, source_target_pairs={{0,1},{2,0},{4,2},{6,4},{7,6},{5,7},{3,5},{1,3},{8,9},{10,8},{12,1... | collective-permute-start | bytes 1228808 | tf_op jit(solution)/shard_map/gather_two/ppermute | solution.py:90
  167.1 41.6 %collective-permute-start.17 = (bf16[2,400,800]{2,1,0:T(8,128)(2,1)S(1)}, bf16[2,400,800]{2,1,0:T(8,128)(2,1)}, u32[]{:S(2)}, u32[]{:S(2)}) collective-permute-start(bf16[2,400,800]{2,1,0:T(8,128)(2,1)S(1)} %pad_maximum_fusion.pair_ref), channel_id=1, source_target_pairs={{0,8},{8,0},{16,24},{24,16},{1,9},{9,1},{17,25},{25,17},{2,10},{10... | collective-permute-start | bytes 3840008 | tf_op jit(solution)/shard_map/unit_parts/ppermute | solution.py:60
  167.1 50.4 %collective-permute-start.16 = (bf16[2,400,800]{2,1,0:T(8,128)(2,1)S(1)}, bf16[2,400,800]{2,1,0:T(8,128)(2,1)}, u32[]{:S(2)}, u32[]{:S(2)}) collective-permute-start(bf16[2,400,800]{2,1,0:T(8,128)(2,1)S(1)} %pad_maximum_fusion.1.pair_ref), channel_id=1, source_target_pairs={{0,8},{8,0},{16,24},{24,16},{1,9},{9,1},{17,25},{25,17},{2,10},{10... | collective-permute-start | bytes 3840008 | tf_op jit(solution)/shard_map/unit_parts/ppermute | solution.py:60
  177.7 14.2 %collective-permute-start.22 = (bf16[128,1600]{1,0:T(8,128)(2,1)S(1)}, bf16[128,1600]{1,0:T(8,128)(2,1)S(1)}, u32[]{:S(2)}, u32[]{:S(2)}) collective-permute-start(bf16[128,1600]{1,0:T(8,128)(2,1)S(1)} %collective-permute-done.21.rest_8_), channel_id=1, source_target_pairs={{0,2},{2,4},{4,6},{6,7},{7,5},{5,3},{3,1},{1,0},{8,10},{10,12},{12... | collective-permute-start | bytes 1228808 | tf_op jit(solution)/shard_map/gather_two/ppermute | solution.py:90
  181.6 10.3 %collective-permute-start.19 = (bf16[128,1600]{1,0:T(8,128)(2,1)S(1)}, bf16[128,1600]{1,0:T(8,128)(2,1)S(1)}, u32[]{:S(2)}, u32[]{:S(2)}) collective-permute-start(bf16[128,1600]{1,0:T(8,128)(2,1)S(1)} %collective-permute-done.18.rest_1_), channel_id=1, source_target_pairs={{0,1},{2,0},{4,2},{6,4},{7,6},{5,7},{3,5},{1,3},{8,9},{10,8},{12,1... | collective-permute-start | bytes 1228808 | tf_op jit(solution)/shard_map/gather_two/ppermute | solution.py:90
  191.9 9.6 %collective-permute-start.23 = (bf16[128,1600]{1,0:T(8,128)(2,1)S(1)}, bf16[128,1600]{1,0:T(8,128)(2,1)S(1)}, u32[]{:S(2)}, u32[]{:S(2)}) collective-permute-start(bf16[128,1600]{1,0:T(8,128)(2,1)S(1)} %collective-permute-done.22.rest_7_), channel_id=1, source_target_pairs={{0,2},{2,4},{4,6},{6,7},{7,5},{5,3},{3,1},{1,0},{8,10},{10,12},{12... | collective-permute-start | bytes 1228808 | tf_op jit(solution)/shard_map/gather_two/ppermute | solution.py:90
  191.9 10.6 %collective-permute-start.20 = (bf16[128,1600]{1,0:T(8,128)(2,1)S(1)}, bf16[128,1600]{1,0:T(8,128)(2,1)S(1)}, u32[]{:S(2)}, u32[]{:S(2)}) collective-permute-start(bf16[128,1600]{1,0:T(8,128)(2,1)S(1)} %collective-permute-done.19.rest_2_), channel_id=1, source_target_pairs={{0,1},{2,0},{4,2},{6,4},{7,6},{5,7},{3,5},{1,3},{8,9},{10,8},{12,1... | collective-permute-start | bytes 1228808 | tf_op jit(solution)/shard_map/gather_two/ppermute | solution.py:90
  202.3 15.2 %collective-permute-start.24 = (bf16[64,1600]{1,0:T(8,128)(2,1)}, bf16[64,1600]{1,0:T(8,128)(2,1)}, u32[]{:S(2)}, u32[]{:S(2)}) collective-permute-start(bf16[64,1600]{1,0:T(8,128)(2,1)} %slice.259), channel_id=1, source_target_pairs={{0,2},{2,4},{4,6},{6,7},{7,5},{5,3},{3,1},{1,0},{8,10},{10,12},{12... | collective-permute-start | bytes 614408 | tf_op jit(solution)/shard_map/gather_two/ppermute | solution.py:90
  204.0 13.5 %collective-permute-start.25 = (bf16[64,1600]{1,0:T(8,128)(2,1)}, bf16[64,1600]{1,0:T(8,128)(2,1)}, u32[]{:S(2)}, u32[]{:S(2)}) collective-permute-start(bf16[64,1600]{1,0:T(8,128)(2,1)} %slice.260), channel_id=1, source_target_pairs={{0,1},{2,0},{4,2},{6,4},{7,6},{5,7},{3,5},{1,3},{8,9},{10,8},{12,1... | collective-permute-start | bytes 614408 | tf_op jit(solution)/shard_map/gather_two/ppermute | solution.py:90
  237.2 10.3 %collective-permute-start.27 = (bf16[64,1600]{1,0:T(8,128)(2,1)S(1)}, bf16[64,1600]{1,0:T(8,128)(2,1)S(1)}, u32[]{:S(2)}, u32[]{:S(2)}) collective-permute-start(bf16[64,1600]{1,0:T(8,128)(2,1)S(1)} %get-tuple-element.235), channel_id=1, source_target_pairs={{0,1},{2,0},{4,2},{6,4},{7,6},{5,7},{3,5},{1,3},{8,9},{10,8},{12,1... | collective-permute-start | bytes 614408 | tf_op jit(solution)/shard_map/sum_two/ppermute | solution.py:90
  239.2 8.4 %collective-permute-start.26 = (bf16[64,1600]{1,0:T(8,128)(2,1)S(1)}, bf16[64,1600]{1,0:T(8,128)(2,1)S(1)}, u32[]{:S(2)}, u32[]{:S(2)}) collective-permute-start(bf16[64,1600]{1,0:T(8,128)(2,1)S(1)} %get-tuple-element.236), channel_id=1, source_target_pairs={{0,2},{2,4},{4,6},{6,7},{7,5},{5,3},{3,1},{1,0},{8,10},{10,12},{12... | collective-permute-start | bytes 614408 | tf_op jit(solution)/shard_map/sum_two/ppermute | solution.py:90
  248.8 14.4 %collective-permute-start.29 = (bf16[128,1600]{1,0:T(8,128)(2,1)S(1)}, bf16[128,1600]{1,0:T(8,128)(2,1)S(1)}, u32[]{:S(2)}, u32[]{:S(2)}) collective-permute-start(bf16[128,1600]{1,0:T(8,128)(2,1)S(1)} %get-tuple-element.224), channel_id=1, source_target_pairs={{0,1},{2,0},{4,2},{6,4},{7,6},{5,7},{3,5},{1,3},{8,9},{10,8},{12,1... | collective-permute-start | bytes 1228808 | tf_op jit(solution)/shard_map/sum_two/ppermute | solution.py:90
  250.8 14.7 %collective-permute-start.28 = (bf16[128,1600]{1,0:T(8,128)(2,1)S(1)}, bf16[128,1600]{1,0:T(8,128)(2,1)S(1)}, u32[]{:S(2)}, u32[]{:S(2)}) collective-permute-start(bf16[128,1600]{1,0:T(8,128)(2,1)S(1)} %get-tuple-element.225), channel_id=1, source_target_pairs={{0,2},{2,4},{4,6},{6,7},{7,5},{5,3},{3,1},{1,0},{8,10},{10,12},{12... | collective-permute-start | bytes 1228808 | tf_op jit(solution)/shard_map/sum_two/ppermute | solution.py:90
  266.9 27.6 %collective-permute-start.31 = (bf16[128,1600]{1,0:T(8,128)(2,1)S(1)}, bf16[128,1600]{1,0:T(8,128)(2,1)S(1)}, u32[]{:S(2)}, u32[]{:S(2)}) collective-permute-start(bf16[128,1600]{1,0:T(8,128)(2,1)S(1)} %get-tuple-element.109), channel_id=1, source_target_pairs={{0,1},{2,0},{4,2},{6,4},{7,6},{5,7},{3,5},{1,3},{8,9},{10,8},{12,1... | collective-permute-start | bytes 1228808 | tf_op jit(solution)/shard_map/sum_two/ppermute | solution.py:90
  278.7 16.9 %collective-permute-start.30 = (bf16[128,1600]{1,0:T(8,128)(2,1)S(1)}, bf16[128,1600]{1,0:T(8,128)(2,1)S(1)}, u32[]{:S(2)}, u32[]{:S(2)}) collective-permute-start(bf16[128,1600]{1,0:T(8,128)(2,1)S(1)} %get-tuple-element.108), channel_id=1, source_target_pairs={{0,2},{2,4},{4,6},{6,7},{7,5},{5,3},{3,1},{1,0},{8,10},{10,12},{12... | collective-permute-start | bytes 1228808 | tf_op jit(solution)/shard_map/sum_two/ppermute | solution.py:90
  297.0 14.4 %collective-permute-start.33 = (bf16[128,1600]{1,0:T(8,128)(2,1)S(1)}, bf16[128,1600]{1,0:T(8,128)(2,1)S(1)}, u32[]{:S(2)}, u32[]{:S(2)}) collective-permute-start(bf16[128,1600]{1,0:T(8,128)(2,1)S(1)} %get-tuple-element.114), channel_id=1, source_target_pairs={{0,1},{2,0},{4,2},{6,4},{7,6},{5,7},{3,5},{1,3},{8,9},{10,8},{12,1... | collective-permute-start | bytes 1228808 | tf_op jit(solution)/shard_map/sum_two/ppermute | solution.py:90
  301.2 13.1 %collective-permute-start.32 = (bf16[128,1600]{1,0:T(8,128)(2,1)S(1)}, bf16[128,1600]{1,0:T(8,128)(2,1)S(1)}, u32[]{:S(2)}, u32[]{:S(2)}) collective-permute-start(bf16[128,1600]{1,0:T(8,128)(2,1)S(1)} %get-tuple-element.113), channel_id=1, source_target_pairs={{0,2},{2,4},{4,6},{6,7},{7,5},{5,3},{3,1},{1,0},{8,10},{10,12},{12... | collective-permute-start | bytes 1228808 | tf_op jit(solution)/shard_map/sum_two/ppermute | solution.py:90
  327.2 9.0 %collective-permute-start.34 = (bf16[8,200,800]{2,1,0:T(8,128)(2,1)}, bf16[8,200,800]{2,1,0:T(8,128)(2,1)}, u32[]{:S(2)}, u32[]{:S(2)}) collective-permute-start(bf16[8,200,800]{2,1,0:T(8,128)(2,1)} %get-tuple-element.120), channel_id=1, source_target_pairs={{0,8},{8,0},{16,24},{24,16},{1,9},{9,1},{17,25},{25,17},{2,10},{10... | collective-permute-start | bytes 7680008 | tf_op jit(solution)/shard_map/out_sum/ppermute | solution.py:60
  327.3 14.6 %collective-permute-start.35 = (bf16[2,2,400,800]{3,2,1,0:T(8,128)(2,1)S(1)}, bf16[2,2,400,800]{3,2,1,0:T(8,128)(2,1)}, u32[]{:S(2)}, u32[]{:S(2)}) collective-permute-start(bf16[2,2,400,800]{3,2,1,0:T(8,128)(2,1)S(1)} %copy-done.8), channel_id=1, source_target_pairs={{0,8},{8,0},{16,24},{24,16},{1,9},{9,1},{17,25},{25,17},{2,10},{10... | collective-permute-start | bytes 7680008 | tf_op jit(solution)/shard_map/sum_two/unit_sum/ppermute | solution.py:60
  327.8 27.3 %all-to-all-start.1 = ((bf16[8,128,256]{2,1,0:T(8,128)(2,1)}), bf16[8,128,256]{2,1,0:T(8,128)(2,1)}, u32[]{:S(2)}, u32[]{:S(2)}) async-start(bf16[8,128,256]{2,1,0:T(8,128)(2,1)} %get-tuple-element.118), calls=%async_computation.2 | async-start | bytes 1048576 | tf_op jit(solution)/shard_map/all_to_all | solution.py:779
  331.9 135.6 %reduce-scatter.7.cloned.1.call-start = ((), (), s32[]{:S(2)}) async-start(), calls=%async_computation.7 | async-start | bytes 3225600
  355.1 36.8 %collective-permute-start.36 = (bf16[2,400,800]{2,1,0:T(8,128)(2,1)}, bf16[2,400,800]{2,1,0:T(8,128)(2,1)S(1)}, u32[]{:S(2)}, u32[]{:S(2)}) collective-permute-start(bf16[2,400,800]{2,1,0:T(8,128)(2,1)} %get-tuple-element.123), channel_id=1, source_target_pairs={{0,16},{8,24},{16,0},{24,8},{1,17},{9,25},{17,1},{25,9},{2,18},{10... | collective-permute-start | bytes 3840008 | tf_op jit(solution)/shard_map/out_sum/unit_sum/ppermute | solution.py:60
  388.4 15.0 %collective-permute-start.39 = (bf16[1,2,400,768]{3,2,1,0:T(8,128)(2,1)}, bf16[1,2,400,768]{3,2,1,0:T(8,128)(2,1)S(1)}, u32[]{:S(2)}, u32[]{:S(2)}) collective-permute-start(bf16[1,2,400,768]{3,2,1,0:T(8,128)(2,1)} %qkv_other.1), channel_id=1, source_target_pairs={{0,8},{8,0},{16,24},{24,16},{1,9},{9,1},{17,25},{25,17},{2,10},{10... | collective-permute-start | bytes 3686408 | tf_op jit(solution)/shard_map/sum_one/qkv_sum/ppermute | solution.py:60
  389.7 11.5 %collective-permute-start.38 = (bf16[64,1600]{1,0:T(8,128)(2,1)}, bf16[64,1600]{1,0:T(8,128)(2,1)S(1)}, u32[]{:S(2)}, u32[]{:S(2)}) collective-permute-start(bf16[64,1600]{1,0:T(8,128)(2,1)} %get-tuple-element.233), channel_id=1, source_target_pairs={{0,1},{2,0},{4,2},{6,4},{7,6},{5,7},{3,5},{1,3},{8,9},{10,8},{12,1... | collective-permute-start | bytes 614408 | tf_op jit(solution)/shard_map/sum_one/ppermute | solution.py:90
  389.7 11.5 %collective-permute-start.37 = (bf16[64,1600]{1,0:T(8,128)(2,1)S(1)}, bf16[64,1600]{1,0:T(8,128)(2,1)S(1)}, u32[]{:S(2)}, u32[]{:S(2)}) collective-permute-start(bf16[64,1600]{1,0:T(8,128)(2,1)S(1)} %get-tuple-element.234), channel_id=1, source_target_pairs={{0,2},{2,4},{4,6},{6,7},{7,5},{5,3},{3,1},{1,0},{8,10},{10,12},{12... | collective-permute-start | bytes 614408 | tf_op jit(solution)/shard_map/sum_one/ppermute | solution.py:90
  403.4 16.2 %collective-permute-start.41 = (bf16[128,1600]{1,0:T(8,128)(2,1)}, bf16[128,1600]{1,0:T(8,128)(2,1)S(1)}, u32[]{:S(2)}, u32[]{:S(2)}) collective-permute-start(bf16[128,1600]{1,0:T(8,128)(2,1)} %get-tuple-element.135), channel_id=1, source_target_pairs={{0,1},{2,0},{4,2},{6,4},{7,6},{5,7},{3,5},{1,3},{8,9},{10,8},{12,1... | collective-permute-start | bytes 1228808 | tf_op jit(solution)/shard_map/sum_one/ppermute | solution.py:90
  403.5 16.8 %collective-permute-start.40 = (bf16[128,1600]{1,0:T(8,128)(2,1)}, bf16[128,1600]{1,0:T(8,128)(2,1)}, u32[]{:S(2)}, u32[]{:S(2)}) collective-permute-start(bf16[128,1600]{1,0:T(8,128)(2,1)} %get-tuple-element.134), channel_id=1, source_target_pairs={{0,2},{2,4},{4,6},{6,7},{7,5},{5,3},{3,1},{1,0},{8,10},{10,12},{12... | collective-permute-start | bytes 1228808 | tf_op jit(solution)/shard_map/sum_one/ppermute | solution.py:90
  406.4 1.3 collective-permute-start.42
  407.7 4.5 collective-permute-start.43
  423.6 19.3 %collective-permute-start.45 = (bf16[128,1600]{1,0:T(8,128)(2,1)}, bf16[128,1600]{1,0:T(8,128)(2,1)S(1)}, u32[]{:S(2)}, u32[]{:S(2)}) collective-permute-start(bf16[128,1600]{1,0:T(8,128)(2,1)} %get-tuple-element.144), channel_id=1, source_target_pairs={{0,1},{2,0},{4,2},{6,4},{7,6},{5,7},{3,5},{1,3},{8,9},{10,8},{12,1... | collective-permute-start | bytes 1228808 | tf_op jit(solution)/shard_map/sum_one/ppermute | solution.py:90
  423.6 19.3 %collective-permute-start.44 = (bf16[128,1600]{1,0:T(8,128)(2,1)S(1)}, bf16[128,1600]{1,0:T(8,128)(2,1)}, u32[]{:S(2)}, u32[]{:S(2)}) collective-permute-start(bf16[128,1600]{1,0:T(8,128)(2,1)S(1)} %get-tuple-element.143), channel_id=1, source_target_pairs={{0,2},{2,4},{4,6},{6,7},{7,5},{5,3},{3,1},{1,0},{8,10},{10,12},{12... | collective-permute-start | bytes 1228808 | tf_op jit(solution)/shard_map/sum_one/ppermute | solution.py:90
  425.6 19.5 %collective-permute-start.53 = (bf16[1,400,768]{2,1,0:T(8,128)(2,1)}, bf16[1,400,768]{2,1,0:T(8,128)(2,1)}, u32[]{:S(2)}, u32[]{:S(2)}) collective-permute-start(bf16[1,400,768]{2,1,0:T(8,128)(2,1)} %get-tuple-element.142), channel_id=1, source_target_pairs={{0,16},{8,24},{16,0},{24,8},{1,17},{9,25},{17,1},{25,9},{2,18},{10... | collective-permute-start | bytes 1843208 | tf_op jit(solution)/shard_map/sum_one/qkv_sum/ppermute | solution.py:60
  445.1 16.6 %collective-permute-start.50 = (f32[19200]{0:T(1024)S(1)}, f32[19200]{0:T(1024)S(1)}, u32[]{:S(2)}, u32[]{:S(2)}) collective-permute-start(f32[19200]{0:T(1024)S(1)} %add.192), channel_id=1, source_target_pairs={{0,1},{1,0},{2,3},{3,2},{4,5},{5,4},{6,7},{7,6},{8,9},{9,8},{10,11... | collective-permute-start | bytes 230408 | tf_op jit(solution)/shard_map/sum_one/sum_vectors/ppermute | solution.py:60
  447.3 20.2 %collective-permute-start.54 = (bf16[400,256]{1,0:T(8,128)(2,1)S(1)}, bf16[400,256]{1,0:T(8,128)(2,1)S(1)}, u32[]{:S(2)}, u32[]{:S(2)}) collective-permute-start(bf16[400,256]{1,0:T(8,128)(2,1)S(1)} %get-tuple-element.228), channel_id=1, source_target_pairs={{5,2},{3,4},{4,1},{0,5},{1,3},{2,6},{6,7},{13,10},{11,12},{12,9},{... | collective-permute-start | bytes 614408 | tf_op jit(solution)/shard_map/sum_one/from_heads/ppermute | solution.py:217
  452.3 15.2 %collective-permute-start.55 = (bf16[400,256]{1,0:T(8,128)(2,1)S(1)}, bf16[400,256]{1,0:T(8,128)(2,1)S(1)}, u32[]{:S(2)}, u32[]{:S(2)}) collective-permute-start(bf16[400,256]{1,0:T(8,128)(2,1)S(1)} %get-tuple-element.227), channel_id=1, source_target_pairs={{3,6},{2,1},{5,5},{4,7},{0,2},{1,0},{11,14},{10,9},{13,13},{12,15}... | collective-permute-start | bytes 614408 | tf_op jit(solution)/shard_map/sum_one/from_heads/ppermute | solution.py:217
  454.2 13.3 %collective-permute-start.56 = (bf16[400,256]{1,0:T(8,128)(2,1)S(1)}, bf16[400,256]{1,0:T(8,128)(2,1)S(1)}, u32[]{:S(2)}, u32[]{:S(2)}) collective-permute-start(bf16[400,256]{1,0:T(8,128)(2,1)S(1)} %get-tuple-element.226), channel_id=1, source_target_pairs={{1,5},{0,0},{3,1},{2,3},{4,4},{5,7},{6,2},{9,13},{8,8},{11,9},{10,... | collective-permute-start | bytes 614408 | tf_op jit(solution)/shard_map/sum_one/from_heads/ppermute | solution.py:217
  454.9 15.6 %collective-permute-start.57 = (bf16[400,128]{1,0:T(8,128)(2,1)S(1)}, bf16[400,128]{1,0:T(8,128)(2,1)S(1)}, u32[]{:S(2)}, u32[]{:S(2)}) collective-permute-start(bf16[400,128]{1,0:T(8,128)(2,1)S(1)} %slice.271), channel_id=1, source_target_pairs={{4,2},{5,4},{0,3},{6,5},{2,0},{3,7},{1,6},{12,10},{13,12},{8,11},{... | collective-permute-start | bytes 307208 | tf_op jit(solution)/shard_map/sum_one/from_heads/ppermute | solution.py:217
  461.7 4.5 collective-permute-start.51
  466.2 18.6 %collective-permute-start.52 = (f32[19200]{0:T(1024)S(1)}, f32[19200]{0:T(1024)S(1)}, u32[]{:S(2)}, u32[]{:S(2)}) collective-permute-start(f32[19200]{0:T(1024)S(1)} %add.199), channel_id=1, source_target_pairs={{0,4},{1,5},{2,6},{3,7},{4,0},{5,1},{6,2},{7,3},{8,12},{9,13},{10,... | collective-permute-start | bytes 230408 | tf_op jit(solution)/shard_map/sum_one/sum_vectors/ppermute | solution.py:60
  469.1 4.8 collective-permute-start.46
  473.8 4.7 collective-permute-start.47
  479.7 8.2 %collective-permute-start.49 = (bf16[128,1600]{1,0:T(8,128)(2,1)S(1)}, bf16[128,1600]{1,0:T(8,128)(2,1)S(1)}, u32[]{:S(2)}, u32[]{:S(2)}) collective-permute-start(bf16[128,1600]{1,0:T(8,128)(2,1)S(1)} %copy-done.19), channel_id=1, source_target_pairs={{0,1},{2,0},{4,2},{6,4},{7,6},{5,7},{3,5},{1,3},{8,9},{10,8},{12,1... | collective-permute-start | bytes 1228808 | tf_op jit(solution)/shard_map/sum_one/ppermute | solution.py:90
  480.5 8.1 %collective-permute-start.48 = (bf16[128,1600]{1,0:T(8,128)(2,1)S(1)}, bf16[128,1600]{1,0:T(8,128)(2,1)S(1)}, u32[]{:S(2)}, u32[]{:S(2)}) collective-permute-start(bf16[128,1600]{1,0:T(8,128)(2,1)S(1)} %get-tuple-element.146), channel_id=1, source_target_pairs={{0,2},{2,4},{4,6},{6,7},{7,5},{5,3},{3,1},{1,0},{8,10},{10,12},{12... | collective-permute-start | bytes 1228808 | tf_op jit(solution)/shard_map/sum_one/ppermute | solution.py:90
  (45 other events, 580.3 us)
Sparse Core Ops, SparseCore 0:
  11.5 91.3 all-gather.5
  105.1 74.5 all-gather.3
  247.7 90.6 reduce-scatter.4
  355.4 94.7 reduce-scatter.6

commit v6 on v5

--- a/solution.py
+++ b/solution.py
@@ -704,7 +704,7 @@
         2 * tokens * width * units,
     )
     with jax.named_scope("gather_two"):
-        two_gathered = ring_gather(normed_two)
+        two_gathered = ring_gather(normed_two, [lambda hold: (), lambda hold: (), lambda hold: (hidden_grad,)])
     bias_units = lax.dynamic_slice_in_dim(fc_bias, ctx * units, units)[None]
     if fused:
         two_tokens, hidden, hidden_pre_grad, two_parts, two_far, units_grad = call(

time: 508 us -> 508 us (level)
  starting transfers between devices: 108 us -> 101 us
  waiting for transfers between devices: 168 us -> 175 us
    ppermute x32, starting transfers between devices: 61.5 us -> 46.9 us  [shift(): lax.ppermute(values, 'ctx', [(order[i], order[(i + offset) % count]) for...]
    ppermute x18, starting transfers between devices: 10.6 us -> 20.4 us  [swap(): return lax.ppermute(values, axis, [(i, i ^ bit) for i in range(count)])]
    all_to_all x1, waiting for transfers between devices: 0.01 us -> 5.2 us  [body(): grad_part = lax.all_to_all(attn_grad, 'ctx', 0, 0, tiled=True)]
    unnamed x104 -> x102, local copies, waits for them, and re-layouts: 11.5 us -> 11.5 us
  transfers between devices with their start and end apart: 64 -> 64, of which waited for: 30 -> 32; matrix products, arithmetic and copies ran while one was open for 12% -> 12% of each run, Pallas kernels for 23% -> 23%
where the time goes in v6:
time: 508 us; the launch traced here: 502 us
  waiting for transfers between devices  175 us (34%)
  Pallas kernels  138 us (27%)
  starting transfers between devices  101 us (20%)
  other arithmetic  34.3 us (7%)
  local copies, waits for them, and re-layouts  29.4 us (6%)
  between operations  17.7 us (3%)
  matrix products  6.79 us (1%)
    pallas_call x13, Pallas kernels, call(): pl.pallas_call(kernel, in_specs=spec, out_specs=[pl.BlockSpec(memory_spac...  138 us
    ppermute x32, waiting for transfers between devices, shift(): lax.ppermute(values, 'ctx', [(order[i], order[(i + offset) % count]) for...  97.6 us
    ppermute x32, starting transfers between devices, shift(): lax.ppermute(values, 'ctx', [(order[i], order[(i + offset) % count]) for...  46.9 us
    ppermute x18, waiting for transfers between devices, swap(): return lax.ppermute(values, axis, [(i, i ^ bit) for i in range(count)])  37.8 us
    ppermute x8, waiting for transfers between devices, move(): lax.ppermute(values, 'ctx', pairs)  26.8 us
    ppermute x8, starting transfers between devices, move(): lax.ppermute(values, 'ctx', pairs)  22.2 us
    ppermute x18, starting transfers between devices, swap(): return lax.ppermute(values, axis, [(i, i ^ bit) for i in range(count)])  20.4 us
    unnamed x102, local copies, waits for them, and re-layouts  11.5 us
  transfers between devices with their start and end apart: 64, of which 32 were waited for; matrix products, arithmetic and copies ran while one was open for 12% of the time, Pallas kernels for 23%

profile of v6, /device:TPU:0, one launch (start us, length us, event | category | flops | bytes accessed | tf_op | source)
XLA Modules:
  0.0 501.8 jit_solution(8887139526713474816)
XLA Ops:
  12.8 3.0 collective-permute-start.2
  18.8 7.0 %collective-permute-start.1 = (bf16[400,256]{1,0:T(8,128)(2,1)S(1)}, bf16[400,256]{1,0:T(8,128)(2,1)S(1)}, u32[]{:S(2)}, u32[]{:S(2)}) collective-permute-start(bf16[400,256]{1,0:T(8,128)(2,1)S(1)} %get-tuple-element.233), channel_id=1, source_target_pairs={{6,3},{1,2},{5,5},{7,4},{2,0},{0,1},{14,11},{9,10},{13,13},{15,12}... | collective-permute-start | bytes 614408 | tf_op jit(solution)/shard_map/gather_one/to_heads/ppermute | solution.py:217
  26.6 9.1 %collective-permute-done = bf16[400,256]{1,0:T(8,128)(2,1)S(1)} collective-permute-done((bf16[400,256]{1,0:T(8,128)(2,1)S(1)}, bf16[400,256]{1,0:T(8,128)(2,1)S(1)}, u32[]{:S(2)}, u32[]{:S(2)}) %collective-permute-start) | collective-permute-done | bytes 204832 | tf_op jit(solution)/shard_map/gather_one/to_heads/ppermute | solution.py:217
  36.5 8.4 %collective-permute-start.6 = (bf16[128,1600]{1,0:T(8,128)(2,1)S(1)}, bf16[128,1600]{1,0:T(8,128)(2,1)S(1)}, u32[]{:S(2)}, u32[]{:S(2)}) collective-permute-start(bf16[128,1600]{1,0:T(8,128)(2,1)S(1)} %collective-permute-done.2.rest_8_), channel_id=1, source_target_pairs={{0,2},{2,4},{4,6},{6,7},{7,5},{5,3},{3,1},{1,0},{8,10},{10,12},{12... | collective-permute-start | bytes 1228808 | tf_op jit(solution)/shard_map/gather_one/ppermute | solution.py:90
  44.9 4.9 collective-permute-start.7
  51.8 17.7 %collective-permute-done.5 = bf16[400,128]{1,0:T(8,128)(2,1)S(1)} collective-permute-done((bf16[400,128]{1,0:T(8,128)(2,1)S(1)}, bf16[400,128]{1,0:T(8,128)(2,1)S(1)}, u32[]{:S(2)}, u32[]{:S(2)}) %collective-permute-start.5) | collective-permute-done | bytes 102432 | tf_op jit(solution)/shard_map/gather_one/to_heads/ppermute | solution.py:217
  72.1 2.0 collective-permute-start.10
  74.1 18.9 %collective-permute-done.9.rest_6_ = bf16[128,1600]{1,0:T(8,128)(2,1)S(1)} collective-permute-done((bf16[128,1600]{1,0:T(8,128)(2,1)S(1)}, bf16[128,1600]{1,0:T(8,128)(2,1)S(1)}, u32[]{:S(2)}, u32[]{:S(2)}) %collective-permute-start.9) | collective-permute-done | bytes 409632 | tf_op jit(solution)/shard_map/gather_one/ppermute | solution.py:90
  93.1 4.0 collective-permute-done.8
  97.3 2.3 copy.56
  102.2 2.3 collective-permute-start.13
  105.6 3.6 collective-permute-done.12.rest_4_
  110.2 15.0 %attend.1 = (bf16[1024,1600]{1,0:T(8,128)(2,1)}, bf16[1600,768]{1,0:T(8,128)(2,1)}, bf16[1024,768]{1,0:T(8,128)(2,1)}, f32[1024,256]{1,0:T(8,128)}, bf16[8,128,256]{2,1,0:T(8,128)(2,1)}, /*index=5*/f32[1024,4]{1,0:T(8,128)}) custom-call(s32[8]{0:T(128)} %get-tuple-element.252.member_ref, s32[1]{0:T(128)} %bitcast.1.place_ref, s32[8]{0:T(128)} %pair_of_ref.1, ...), custom_call_target="tpu_custom_call" | custom-call | flops 1000 | bytes 180000000 | tf_op jit(solution)/shard_map/attend/pallas_call | solution.py:246
  126.6 6.3 %all-to-all-start = ((bf16[8,128,256]{2,1,0:T(8,128)(2,1)}), bf16[8,128,256]{2,1,0:T(8,128)(2,1)}, u32[]{:S(2)}, u32[]{:S(2)}) async-start(bf16[8,128,256]{2,1,0:T(8,128)(2,1)} %get-tuple-element.95), calls=%async_computation | async-start | bytes 1048576 | tf_op jit(solution)/shard_map/all_to_all | solution.py:677
  133.4 16.0 %collective-permute-done.15 = bf16[400,800]{1,0:T(8,128)(2,1)S(1)} collective-permute-done((bf16[400,800]{1,0:T(8,128)(2,1)S(1)}, bf16[400,800]{1,0:T(8,128)(2,1)S(1)}, u32[]{:S(2)}, u32[]{:S(2)}) %collective-permute-start.15) | collective-permute-done | bytes 640032 | tf_op jit(solution)/shard_map/unit_parts/ppermute | solution.py:60
  150.7 7.1 %all-to-all-done.back_ref = bf16[8,128,256]{2,1,0:T(8,128)(2,1)} async-done(((bf16[8,128,256]{2,1,0:T(8,128)(2,1)}), bf16[8,128,256]{2,1,0:T(8,128)(2,1)}, u32[]{:S(2)}, u32[]{:S(2)}) %all-to-all-start) | async-done | bytes 524320 | tf_op jit(solution)/shard_map/all_to_all | solution.py:677
  159.7 7.4 %out.1 = (f32[128,1600]{1,0:T(8,128)}, bf16[128,1600]{1,0:T(8,128)(2,1)}, f32[128,1600]{1,0:T(8,128)}, f32[128,1]{1,0:T(8,128)}, bf16[128,1600]{1,0:T(8,128)(2,1)}) custom-call(bf16[8,128,256]{2,1,0:T(8,128)(2,1)} %all-to-all-done.back_ref, bf16[128,1600]{1,0:T(8,128)(2,1)} %bitcast.99, f32[1,1600]{1,0:T(1,128)} %broadcast_in_dim.59.bias_ref, ...), custom_call_target="tpu_custom_call" | custom-call | flops 1000 | bytes 90000000 | tf_op jit(solution)/shard_map/out/pallas_call | solution.py:246
  169.3 13.6 %collective-permute-done.18.rest_1_ = bf16[128,1600]{1,0:T(8,128)(2,1)S(1)} collective-permute-done((bf16[128,1600]{1,0:T(8,128)(2,1)}, bf16[128,1600]{1,0:T(8,128)(2,1)S(1)}, u32[]{:S(2)}, u32[]{:S(2)}) %collective-permute-start.18) | collective-permute-done | bytes 409632 | tf_op jit(solution)/shard_map/gather_two/ppermute | solution.py:90
  182.9 2.0 collective-permute-start.22
  184.9 9.8 %collective-permute-done.19.rest_2_ = bf16[128,1600]{1,0:T(8,128)(2,1)} collective-permute-done((bf16[128,1600]{1,0:T(8,128)(2,1)S(1)}, bf16[128,1600]{1,0:T(8,128)(2,1)}, u32[]{:S(2)}, u32[]{:S(2)}) %collective-permute-start.19) | collective-permute-done | bytes 409632 | tf_op jit(solution)/shard_map/gather_two/ppermute | solution.py:90
  195.0 2.1 collective-permute-start.23
  197.1 8.8 %hidden_grad.1 = (bf16[1600,800]{1,0:T(8,128)(2,1)}, f32[1024,800]{1,0:T(8,128)}) custom-call(s32[1]{0:T(128)} %bitcast.1.place_ref, bf16[1024,1600]{1,0:T(8,128)(2,1)} %all-gather.4.cloned.1.call-done.cot_ref.rest_2_, bf16[2,400,800]{2,1,0:T(8,128)(2,1)} %copy-done.5, bf16[2,400,800]{2,1,0:T(8,128)(2,1)} %collective-permute-done.17.peer_ref), custom_call_target="tpu_custom_call" | custom-call | flops 1000 | bytes 27000000 | tf_op jit(solution)/shard_map/hidden_grad/pallas_call | solution.py:246
  215.6 18.6 %hidden.1 = (bf16[1024,1600]{1,0:T(8,128)(2,1)}, bf16[1024,800]{1,0:T(8,128)(2,1)}, bf16[1024,800]{1,0:T(8,128)(2,1)}, bf16[8,128,1600]{2,1,0:T(8,128)(2,1)}, bf...) custom-call(s32[8]{0:T(128)} %get-tuple-element.252.member_ref, s32[8]{0:T(128)} %fusion.23.offset_ref, s32[1]{0:T(128)} %bitcast.1.place_ref, ...), custom_call_target="tpu_custom_call" | custom-call | flops 1000 | bytes 240000000 | tf_op jit(solution)/shard_map/hidden/pallas_call | solution.py:246
  237.5 8.1 %branch.1 = bf16[1024,1600]{1,0:T(8,128)(2,1)} custom-call(bf16[1024,800]{1,0:T(8,128)(2,1)} %get-tuple-element.110.value_ref.rest_3_, bf16[1600,800]{1,0:T(8,128)(2,1)} %get-tuple-element.111.w_ref), custom_call_target="tpu_custom_call" | custom-call | flops 1000 | bytes 24000000 | tf_op jit(solution)/shard_map/sum_two/branch/pallas_call | solution.py:246
  249.0 12.4 %collective-permute-done.29 = bf16[128,1600]{1,0:T(8,128)(2,1)S(1)} collective-permute-done((bf16[128,1600]{1,0:T(8,128)(2,1)S(1)}, bf16[128,1600]{1,0:T(8,128)(2,1)S(1)}, u32[]{:S(2)}, u32[]{:S(2)}) %collective-permute-start.29) | collective-permute-done | bytes 409632 | tf_op jit(solution)/shard_map/sum_two/ppermute | solution.py:90
  264.1 2.5 collective-permute-start.30
  266.6 11.1 %unit_other.1 = bf16[2,2,400,800]{3,2,1,0:T(8,128)(2,1)} custom-call(s32[1]{0:T(128)} %bitcast.22.core_ref, bf16[1024,1600]{1,0:T(8,128)(2,1)} %get-tuple-element.115.rest_0_, bf16[1024,800]{1,0:T(8,128)(2,1)} %get-tuple-element.116.rest_1_, bf16[1024,1600]{1,0:T(8,128)(2,1)} %all-gather.4.cloned.1.call-done.cot_ref.rest_2_, ...), custom_call_target="tpu_custom_call" | custom-call | flops 1000 | bytes 24000000 | tf_op jit(solution)/shard_map/sum_two/unit_sum/unit_other/pallas_call | solution.py:246
  277.8 11.4 %collective-permute-done.31 = bf16[128,1600]{1,0:T(8,128)(2,1)S(1)} collective-permute-done((bf16[128,1600]{1,0:T(8,128)(2,1)S(1)}, bf16[128,1600]{1,0:T(8,128)(2,1)S(1)}, u32[]{:S(2)}, u32[]{:S(2)}) %collective-permute-start.31) | collective-permute-done | bytes 409632 | tf_op jit(solution)/shard_map/sum_two/ppermute | solution.py:90
  290.8 2.2 collective-permute-start.32
  293.0 8.0 %collective-permute-done.33 = bf16[128,1600]{1,0:T(8,128)(2,1)S(1)} collective-permute-done((bf16[128,1600]{1,0:T(8,128)(2,1)S(1)}, bf16[128,1600]{1,0:T(8,128)(2,1)S(1)}, u32[]{:S(2)}, u32[]{:S(2)}) %collective-permute-start.33) | collective-permute-done | bytes 409632 | tf_op jit(solution)/shard_map/sum_two/ppermute | solution.py:90
  302.4 2.1 fusion.18.sum_ref
  304.5 11.0 %out_back.1 = (f32[128,1600]{1,0:T(8,128)}, bf16[128,1600]{1,0:T(8,128)(2,1)}, bf16[8,128,256]{2,1,0:T(8,128)(2,1)}, f32[4,1600]{1,0:T(4,128)}, f32[8,200,800]{2,1,0:T(8,128)}, /*index=5*/bf16[8,200,800]{2,1,0:T(8,128)(2,1)}) custom-call(s32[1]{0:T(128)} %bitcast.22.core_ref, f32[128,1600]{1,0:T(8,128)} %fusion.18.sum_ref, bf16[128,1600]{1,0:T(8,128)(2,1)} %bitcast.101, ...), custom_call_target="tpu_custom_call" | custom-call | flops 1000 | bytes 135000000 | tf_op jit(solution)/shard_map/out_back/pallas_call | solution.py:246
  316.0 5.0 %all-to-all-start.1 = ((bf16[8,128,256]{2,1,0:T(8,128)(2,1)}), bf16[8,128,256]{2,1,0:T(8,128)(2,1)}, u32[]{:S(2)}, u32[]{:S(2)}) async-start(bf16[8,128,256]{2,1,0:T(8,128)(2,1)} %get-tuple-element.122), calls=%async_computation.2 | async-start | bytes 1048576 | tf_op jit(solution)/shard_map/all_to_all | solution.py:779
  321.1 3.3 collective-permute-done.34
  324.5 5.7 %add_convert_fusion = bf16[8,200,800]{2,1,0:T(8,128)(2,1)} fusion(f32[8,200,800]{2,1,0:T(8,128)} %get-tuple-element.123, bf16[8,200,800]{2,1,0:T(8,128)(2,1)} %collective-permute-done.34), kind=kLoop, calls=%fused_computation.1 | loop fusion | flops 3840000 | bytes 10240000 | tf_op jit(solution)/shard_map/out_sum/convert_element_type | solution.py:782
  330.1 13.2 %unit_mine.1 = (f32[2,400,800]{2,1,0:T(8,128)}, bf16[2,400,800]{2,1,0:T(8,128)(2,1)}) custom-call(s32[1]{0:T(128)} %bitcast.22.core_ref, s32[1]{0:T(128)} %bitcast.28.row_ref, bf16[2,2,400,800]{3,2,1,0:T(8,128)(2,1)} %collective-permute-done.35.got_ref, bf16[1024,1600]{1,0:T(8,128)(2,1)} %get-tuple-element.115.rest_0_, ...), custom_call_target="tpu_custom_call" | custom-call | flops 1000 | bytes 30000000 | tf_op jit(solution)/shard_map/out_sum/unit_sum/unit_mine/pallas_call | solution.py:246
  343.3 5.2 %all-to-all-done.1.come_ref = bf16[8,128,256]{2,1,0:T(8,128)(2,1)} async-done(((bf16[8,128,256]{2,1,0:T(8,128)(2,1)}), bf16[8,128,256]{2,1,0:T(8,128)(2,1)}, u32[]{:S(2)}, u32[]{:S(2)}) %all-to-all-start.1) | async-done | bytes 524320 | tf_op jit(solution)/shard_map/all_to_all | solution.py:779
  355.3 20.4 %attend_back.1 = (bf16[1024,768]{1,0:T(8,128)(2,1)}, f32[1,768]{1,0:T(1,128)}, bf16[128,1600]{1,0:T(8,128)(2,1)}) custom-call(s32[16]{0:T(128)} %pad_add_fusion.who_ref, s32[2]{0:T(128)} %pad_add_fusion.1.far_ref, bf16[1024,768]{1,0:T(8,128)(2,1)} %get-tuple-element.129.qkv_ref, bf16[1600,768]{1,0:T(8,128)(2,1)} %get-tuple-element.130.w_ref, ...), custom_call_target="tpu_custom_call" | custom-call | flops 1000 | bytes 240000000 | tf_op jit(solution)/shard_map/attend_back/pallas_call | solution.py:246
  375.6 6.1 %qkv_other.1 = bf16[1,2,400,768]{3,2,1,0:T(8,128)(2,1)} custom-call(s32[1]{0:T(128)} %bitcast.22.core_ref, bf16[1024,1600]{1,0:T(8,128)(2,1)} %get-tuple-element.135.x_ref.rest_0_, bf16[1024,768]{1,0:T(8,128)(2,1)} %get-tuple-element.134.grad_ref.rest_1_), custom_call_target="tpu_custom_call" | custom-call | flops 1000 | bytes 15000000 | tf_op jit(solution)/shard_map/sum_one/qkv_sum/qkv_other/pallas_call | solution.py:246
  384.6 8.4 %project_back.1 = (bf16[8,128,1600]{2,1,0:T(8,128)(2,1)}, f32[2,1600]{1,0:T(2,128)}) custom-call(s32[16]{0:T(128)} %gather_fusion, bf16[1024,768]{1,0:T(8,128)(2,1)} %get-tuple-element.134.grad_ref.rest_1_, bf16[1600,768]{1,0:T(8,128)(2,1)} %get-tuple-element.130.w_ref, bf16[1024,1600]{1,0:T(8,128)(2,1)} %get-tuple-element.135.x_ref.rest_0_), custom_call_target="tpu_custom_call" | custom-call | flops 1000 | bytes 18000000 | tf_op jit(solution)/shard_map/project_back/pallas_call | solution.py:246
  393.0 4.3 collective-permute-done.38
  397.3 2.1 convert_add_fusion.2
  399.5 2.0 collective-permute-start.40
  405.6 2.7 collective-permute-done.43
  408.3 7.2 %qkv_mine.1 = (f32[1,400,768]{2,1,0:T(8,128)}, bf16[1,400,768]{2,1,0:T(8,128)(2,1)}) custom-call(s32[1]{0:T(128)} %bitcast.22.core_ref, s32[1]{0:T(128)} %bitcast.28.row_ref, bf16[1,2,400,768]{3,2,1,0:T(8,128)(2,1)} %copy-done.10, bf16[1024,1600]{1,0:T(8,128)(2,1)} %get-tuple-element.135.x_ref.rest_0_, bf16[1024,768]{1,0:T(8,128)(2,1)} %get-tuple-element.134.grad_ref.rest_1_), custom_call_target="tpu_custom_call" | custom-call | flops 1000 | bytes 18000000 | tf_op jit(solution)/shard_map/sum_one/qkv_sum/qkv_mine/pallas_call | solution.py:246
  415.5 2.3 collective-permute-done.40
  417.9 2.2 convert_add_fusion.1
  421.3 2.0 collective-permute-start.44
  423.3 3.3 collective-permute-start.53
  428.9 6.0 %collective-permute-done.45 = bf16[128,1600]{1,0:T(8,128)(2,1)S(1)} collective-permute-done((bf16[128,1600]{1,0:T(8,128)(2,1)}, bf16[128,1600]{1,0:T(8,128)(2,1)S(1)}, u32[]{:S(2)}, u32[]{:S(2)}) %collective-permute-start.45) | collective-permute-done | bytes 409632 | tf_op jit(solution)/shard_map/sum_one/ppermute | solution.py:90
  434.9 2.2 convert_add_fusion
  437.4 2.6 collective-permute-done.53
  440.0 2.0 fusion.8
  442.1 2.1 collective-permute-start.54
  444.3 2.2 collective-permute-start.55
  447.2 6.3 %collective-permute-start.57 = (bf16[400,128]{1,0:T(8,128)(2,1)S(1)}, bf16[400,128]{1,0:T(8,128)(2,1)S(1)}, u32[]{:S(2)}, u32[]{:S(2)}) collective-permute-start(bf16[400,128]{1,0:T(8,128)(2,1)S(1)} %slice.269), channel_id=1, source_target_pairs={{4,2},{5,4},{0,3},{6,5},{2,0},{3,7},{1,6},{12,10},{13,12},{8,11},{... | collective-permute-start | bytes 307208 | tf_op jit(solution)/shard_map/sum_one/from_heads/ppermute | solution.py:217
  455.7 3.3 collective-permute-done.51
  461.9 8.4 %collective-permute-start.46 = (bf16[100,400]{1,0:T(8,128)(2,1)S(1)}, bf16[100,400]{1,0:T(8,128)(2,1)S(1)}, u32[]{:S(2)}, u32[]{:S(2)}) collective-permute-start(bf16[100,400]{1,0:T(8,128)(2,1)S(1)} %get-tuple-element.241), channel_id=1, source_target_pairs={{0,16},{8,24},{16,0},{24,8},{1,17},{9,25},{17,1},{25,9},{2,18},{10... | collective-permute-start | bytes 240008 | tf_op jit(solution)/shard_map/sum_one/out_sum/ppermute | solution.py:60
  471.0 2.0 collective-permute-done.46
  473.0 2.1 collective-permute-start.47
  475.7 2.0 collective-permute-done.47
  481.0 3.0 fusion.2
  487.9 2.2 fusion.17.sum_ref
  490.0 2.8 input_grad.1
  (268 shorter events, 80.7 us)
Async XLA Ops:
  7.2 152.5 %all-gather.6.cloned.1.call-start = ((), (), s32[]{:S(2)}) async-start(), calls=%async_computation.6 | async-start | bytes 6758400 | tf_op jit(solution)/shard_map/gather_one/all_gather | solution.py:624
  9.0 188.1 %all-gather.4.cloned.1.call-start = ((), (), s32[]{:S(2)}) async-start(), calls=%async_computation.4 | async-start | bytes 3833856 | tf_op jit(solution)/shard_map/all_gather | solution.py:675
  12.8 22.9 %collective-permute-start.2 = (bf16[128,1600]{1,0:T(8,128)(2,1)S(1)}, bf16[128,1600]{1,0:T(8,128)(2,1)S(1)}, u32[]{:S(2)}, u32[]{:S(2)}) collective-permute-start(bf16[128,1600]{1,0:T(8,128)(2,1)S(1)} %get-tuple-element.236.rest_0_), channel_id=1, source_target_pairs={{0,2},{2,4},{4,6},{6,7},{7,5},{5,3},{3,1},{1,0},{8,10},{10,12},{12... | collective-permute-start | bytes 1228808 | tf_op jit(solution)/shard_map/gather_one/ppermute | solution.py:90
  15.8 19.9 %collective-permute-start.3 = (bf16[128,1600]{1,0:T(8,128)(2,1)S(1)}, bf16[128,1600]{1,0:T(8,128)(2,1)S(1)}, u32[]{:S(2)}, u32[]{:S(2)}) collective-permute-start(bf16[128,1600]{1,0:T(8,128)(2,1)S(1)} %get-tuple-element.236.rest_0_), channel_id=1, source_target_pairs={{0,1},{2,0},{4,2},{6,4},{7,6},{5,7},{3,5},{1,3},{8,9},{10,8},{12,1... | collective-permute-start | bytes 1228808 | tf_op jit(solution)/shard_map/gather_one/ppermute | solution.py:90
  17.5 18.2 %collective-permute-start = (bf16[400,256]{1,0:T(8,128)(2,1)S(1)}, bf16[400,256]{1,0:T(8,128)(2,1)S(1)}, u32[]{:S(2)}, u32[]{:S(2)}) collective-permute-start(bf16[400,256]{1,0:T(8,128)(2,1)S(1)} %get-tuple-element.234), channel_id=1, source_target_pairs={{2,5},{4,3},{1,4},{5,0},{3,1},{6,2},{7,6},{10,13},{12,11},{9,12},{... | collective-permute-start | bytes 614408 | tf_op jit(solution)/shard_map/gather_one/to_heads/ppermute | solution.py:217
  18.8 16.9 %collective-permute-start.1 = (bf16[400,256]{1,0:T(8,128)(2,1)S(1)}, bf16[400,256]{1,0:T(8,128)(2,1)S(1)}, u32[]{:S(2)}, u32[]{:S(2)}) collective-permute-start(bf16[400,256]{1,0:T(8,128)(2,1)S(1)} %get-tuple-element.233), channel_id=1, source_target_pairs={{6,3},{1,2},{5,5},{7,4},{2,0},{0,1},{14,11},{9,10},{13,13},{15,12}... | collective-permute-start | bytes 614408 | tf_op jit(solution)/shard_map/gather_one/to_heads/ppermute | solution.py:217
  35.7 16.0 %collective-permute-start.4 = (bf16[400,256]{1,0:T(8,128)(2,1)S(1)}, bf16[400,256]{1,0:T(8,128)(2,1)S(1)}, u32[]{:S(2)}, u32[]{:S(2)}) collective-permute-start(bf16[400,256]{1,0:T(8,128)(2,1)S(1)} %slice.198), channel_id=1, source_target_pairs={{5,1},{0,0},{1,3},{3,2},{4,4},{7,5},{2,6},{13,9},{8,8},{9,11},{11,... | collective-permute-start | bytes 614408 | tf_op jit(solution)/shard_map/gather_one/to_heads/ppermute | solution.py:217
  36.5 33.0 %collective-permute-start.6 = (bf16[128,1600]{1,0:T(8,128)(2,1)S(1)}, bf16[128,1600]{1,0:T(8,128)(2,1)S(1)}, u32[]{:S(2)}, u32[]{:S(2)}) collective-permute-start(bf16[128,1600]{1,0:T(8,128)(2,1)S(1)} %collective-permute-done.2.rest_8_), channel_id=1, source_target_pairs={{0,2},{2,4},{4,6},{6,7},{7,5},{5,3},{3,1},{1,0},{8,10},{10,12},{12... | collective-permute-start | bytes 1228808 | tf_op jit(solution)/shard_map/gather_one/ppermute | solution.py:90
  44.9 24.7 %collective-permute-start.7 = (bf16[128,1600]{1,0:T(8,128)(2,1)S(1)}, bf16[128,1600]{1,0:T(8,128)(2,1)S(1)}, u32[]{:S(2)}, u32[]{:S(2)}) collective-permute-start(bf16[128,1600]{1,0:T(8,128)(2,1)S(1)} %collective-permute-done.3.rest_1_), channel_id=1, source_target_pairs={{0,1},{2,0},{4,2},{6,4},{7,6},{5,7},{3,5},{1,3},{8,9},{10,8},{12,1... | collective-permute-start | bytes 1228808 | tf_op jit(solution)/shard_map/gather_one/ppermute | solution.py:90
  49.8 19.7 %collective-permute-start.5 = (bf16[400,128]{1,0:T(8,128)(2,1)S(1)}, bf16[400,128]{1,0:T(8,128)(2,1)S(1)}, u32[]{:S(2)}, u32[]{:S(2)}) collective-permute-start(bf16[400,128]{1,0:T(8,128)(2,1)S(1)} %slice.199), channel_id=1, source_target_pairs={{2,4},{4,5},{3,0},{5,6},{0,2},{7,3},{6,1},{10,12},{12,13},{11,8},{... | collective-permute-start | bytes 307208 | tf_op jit(solution)/shard_map/gather_one/to_heads/ppermute | solution.py:217
  70.6 26.5 %collective-permute-start.8 = (bf16[400,768]{1,0:T(8,128)(2,1)S(1)}, bf16[400,768]{1,0:T(8,128)(2,1)S(1)}, u32[]{:S(2)}, u32[]{:S(2)}) collective-permute-start(bf16[400,768]{1,0:T(8,128)(2,1)S(1)} %fusion.10), channel_id=1, source_target_pairs={{0,16},{8,24},{16,0},{24,8},{1,17},{9,25},{17,1},{25,9},{2,18},{10... | collective-permute-start | bytes 1843208 | tf_op jit(solution)/shard_map/gather_one/qkv_parts/ppermute | solution.py:60
  72.1 21.0 %collective-permute-start.9 = (bf16[128,1600]{1,0:T(8,128)(2,1)S(1)}, bf16[128,1600]{1,0:T(8,128)(2,1)S(1)}, u32[]{:S(2)}, u32[]{:S(2)}) collective-permute-start(bf16[128,1600]{1,0:T(8,128)(2,1)S(1)} %collective-permute-done.6.rest_7_), channel_id=1, source_target_pairs={{0,2},{2,4},{4,6},{6,7},{7,5},{5,3},{3,1},{1,0},{8,10},{10,12},{12... | collective-permute-start | bytes 1228808 | tf_op jit(solution)/shard_map/gather_one/ppermute | solution.py:90
  72.1 21.0 %collective-permute-start.10 = (bf16[128,1600]{1,0:T(8,128)(2,1)S(1)}, bf16[128,1600]{1,0:T(8,128)(2,1)S(1)}, u32[]{:S(2)}, u32[]{:S(2)}) collective-permute-start(bf16[128,1600]{1,0:T(8,128)(2,1)S(1)} %collective-permute-done.7.rest_2_), channel_id=1, source_target_pairs={{0,1},{2,0},{4,2},{6,4},{7,6},{5,7},{3,5},{1,3},{8,9},{10,8},{12,1... | collective-permute-start | bytes 1228808 | tf_op jit(solution)/shard_map/gather_one/ppermute | solution.py:90
  97.2 3.0 collective-permute-start.11
  100.2 25.0 %collective-permute-start.14 = (bf16[400,800]{1,0:T(8,128)(2,1)}, bf16[400,800]{1,0:T(8,128)(2,1)}, u32[]{:S(2)}, u32[]{:S(2)}) collective-permute-start(bf16[400,800]{1,0:T(8,128)(2,1)} %bitcast.107), channel_id=1, source_target_pairs={{0,16},{8,24},{16,0},{24,8},{1,17},{9,25},{17,1},{25,9},{2,18},{10... | collective-permute-start | bytes 1920008 | tf_op jit(solution)/shard_map/unit_parts/ppermute | solution.py:60
  102.1 7.1 %collective-permute-start.12 = (bf16[64,1600]{1,0:T(8,128)(2,1)S(1)}, bf16[64,1600]{1,0:T(8,128)(2,1)S(1)}, u32[]{:S(2)}, u32[]{:S(2)}) collective-permute-start(bf16[64,1600]{1,0:T(8,128)(2,1)S(1)} %slice.257), channel_id=1, source_target_pairs={{0,2},{2,4},{4,6},{6,7},{7,5},{5,3},{3,1},{1,0},{8,10},{10,12},{12... | collective-permute-start | bytes 614408 | tf_op jit(solution)/shard_map/gather_one/ppermute | solution.py:90
  102.2 7.3 %collective-permute-start.13 = (bf16[64,1600]{1,0:T(8,128)(2,1)S(1)}, bf16[64,1600]{1,0:T(8,128)(2,1)S(1)}, u32[]{:S(2)}, u32[]{:S(2)}) collective-permute-start(bf16[64,1600]{1,0:T(8,128)(2,1)S(1)} %slice.258), channel_id=1, source_target_pairs={{0,1},{2,0},{4,2},{6,4},{7,6},{5,7},{3,5},{1,3},{8,9},{10,8},{12,1... | collective-permute-start | bytes 614408 | tf_op jit(solution)/shard_map/gather_one/ppermute | solution.py:90
  126.6 31.2 %all-to-all-start = ((bf16[8,128,256]{2,1,0:T(8,128)(2,1)}), bf16[8,128,256]{2,1,0:T(8,128)(2,1)}, u32[]{:S(2)}, u32[]{:S(2)}) async-start(bf16[8,128,256]{2,1,0:T(8,128)(2,1)} %get-tuple-element.95), calls=%async_computation | async-start | bytes 1048576 | tf_op jit(solution)/shard_map/all_to_all | solution.py:677
  133.0 287.1 %reduce-scatter.5.cloned.1.call-start = ((), (), s32[]{:S(2)}) async-start(), calls=%async_computation.5 | async-start | bytes 3833856 | tf_op jit(solution)/shard_map/reduce_scatter | solution.py:759
  133.0 16.4 %collective-permute-start.15 = (bf16[400,800]{1,0:T(8,128)(2,1)S(1)}, bf16[400,800]{1,0:T(8,128)(2,1)S(1)}, u32[]{:S(2)}, u32[]{:S(2)}) collective-permute-start(bf16[400,800]{1,0:T(8,128)(2,1)S(1)} %copy-done.17), channel_id=1, source_target_pairs={{0,16},{8,24},{16,0},{24,8},{1,17},{9,25},{17,1},{25,9},{2,18},{10... | collective-permute-start | bytes 1920008 | tf_op jit(solution)/shard_map/unit_parts/ppermute | solution.py:60
  157.8 39.2 %collective-permute-start.17 = (bf16[2,400,800]{2,1,0:T(8,128)(2,1)S(1)}, bf16[2,400,800]{2,1,0:T(8,128)(2,1)}, u32[]{:S(2)}, u32[]{:S(2)}) collective-permute-start(bf16[2,400,800]{2,1,0:T(8,128)(2,1)S(1)} %pad_maximum_fusion.pair_ref), channel_id=1, source_target_pairs={{0,8},{8,0},{16,24},{24,16},{1,9},{9,1},{17,25},{25,17},{2,10},{10... | collective-permute-start | bytes 3840008 | tf_op jit(solution)/shard_map/unit_parts/ppermute | solution.py:60
  167.1 15.8 %collective-permute-start.18 = (bf16[128,1600]{1,0:T(8,128)(2,1)}, bf16[128,1600]{1,0:T(8,128)(2,1)S(1)}, u32[]{:S(2)}, u32[]{:S(2)}) collective-permute-start(bf16[128,1600]{1,0:T(8,128)(2,1)} %get-tuple-element.104.rest_0_), channel_id=1, source_target_pairs={{0,1},{2,0},{4,2},{6,4},{7,6},{5,7},{3,5},{1,3},{8,9},{10,8},{12,1... | collective-permute-start | bytes 1228808 | tf_op jit(solution)/shard_map/gather_two/ppermute | solution.py:90
  169.1 13.8 %collective-permute-start.21 = (bf16[128,1600]{1,0:T(8,128)(2,1)}, bf16[128,1600]{1,0:T(8,128)(2,1)S(1)}, u32[]{:S(2)}, u32[]{:S(2)}) collective-permute-start(bf16[128,1600]{1,0:T(8,128)(2,1)} %get-tuple-element.104.rest_0_), channel_id=1, source_target_pairs={{0,2},{2,4},{4,6},{6,7},{7,5},{5,3},{3,1},{1,0},{8,10},{10,12},{12... | collective-permute-start | bytes 1228808 | tf_op jit(solution)/shard_map/gather_two/ppermute | solution.py:90
  169.1 43.1 %collective-permute-start.16 = (bf16[2,400,800]{2,1,0:T(8,128)(2,1)S(1)}, bf16[2,400,800]{2,1,0:T(8,128)(2,1)}, u32[]{:S(2)}, u32[]{:S(2)}) collective-permute-start(bf16[2,400,800]{2,1,0:T(8,128)(2,1)S(1)} %pad_maximum_fusion.1.pair_ref), channel_id=1, source_target_pairs={{0,8},{8,0},{16,24},{24,16},{1,9},{9,1},{17,25},{25,17},{2,10},{10... | collective-permute-start | bytes 3840008 | tf_op jit(solution)/shard_map/unit_parts/ppermute | solution.py:60
  182.9 11.8 %collective-permute-start.19 = (bf16[128,1600]{1,0:T(8,128)(2,1)S(1)}, bf16[128,1600]{1,0:T(8,128)(2,1)}, u32[]{:S(2)}, u32[]{:S(2)}) collective-permute-start(bf16[128,1600]{1,0:T(8,128)(2,1)S(1)} %collective-permute-done.18.rest_1_), channel_id=1, source_target_pairs={{0,1},{2,0},{4,2},{6,4},{7,6},{5,7},{3,5},{1,3},{8,9},{10,8},{12,1... | collective-permute-start | bytes 1228808 | tf_op jit(solution)/shard_map/gather_two/ppermute | solution.py:90
  182.9 12.1 %collective-permute-start.22 = (bf16[128,1600]{1,0:T(8,128)(2,1)S(1)}, bf16[128,1600]{1,0:T(8,128)(2,1)}, u32[]{:S(2)}, u32[]{:S(2)}) collective-permute-start(bf16[128,1600]{1,0:T(8,128)(2,1)S(1)} %collective-permute-done.21.rest_8_), channel_id=1, source_target_pairs={{0,2},{2,4},{4,6},{6,7},{7,5},{5,3},{3,1},{1,0},{8,10},{10,12},{12... | collective-permute-start | bytes 1228808 | tf_op jit(solution)/shard_map/gather_two/ppermute | solution.py:90
  194.7 11.2 %collective-permute-start.20 = (bf16[128,1600]{1,0:T(8,128)(2,1)}, bf16[128,1600]{1,0:T(8,128)(2,1)S(1)}, u32[]{:S(2)}, u32[]{:S(2)}) collective-permute-start(bf16[128,1600]{1,0:T(8,128)(2,1)} %collective-permute-done.19.rest_2_), channel_id=1, source_target_pairs={{0,1},{2,0},{4,2},{6,4},{7,6},{5,7},{3,5},{1,3},{8,9},{10,8},{12,1... | collective-permute-start | bytes 1228808 | tf_op jit(solution)/shard_map/gather_two/ppermute | solution.py:90
  195.0 11.6 %collective-permute-start.23 = (bf16[128,1600]{1,0:T(8,128)(2,1)}, bf16[128,1600]{1,0:T(8,128)(2,1)}, u32[]{:S(2)}, u32[]{:S(2)}) collective-permute-start(bf16[128,1600]{1,0:T(8,128)(2,1)} %collective-permute-done.22.rest_7_), channel_id=1, source_target_pairs={{0,2},{2,4},{4,6},{6,7},{7,5},{5,3},{3,1},{1,0},{8,10},{10,12},{12... | collective-permute-start | bytes 1228808 | tf_op jit(solution)/shard_map/gather_two/ppermute | solution.py:90
  207.5 5.9 %collective-permute-start.24 = (bf16[64,1600]{1,0:T(8,128)(2,1)S(1)}, bf16[64,1600]{1,0:T(8,128)(2,1)S(1)}, u32[]{:S(2)}, u32[]{:S(2)}) collective-permute-start(bf16[64,1600]{1,0:T(8,128)(2,1)S(1)} %slice.205), channel_id=1, source_target_pairs={{0,2},{2,4},{4,6},{6,7},{7,5},{5,3},{3,1},{1,0},{8,10},{10,12},{12... | collective-permute-start | bytes 614408 | tf_op jit(solution)/shard_map/gather_two/ppermute | solution.py:90
  209.0 5.9 %collective-permute-start.25 = (bf16[64,1600]{1,0:T(8,128)(2,1)S(1)}, bf16[64,1600]{1,0:T(8,128)(2,1)S(1)}, u32[]{:S(2)}, u32[]{:S(2)}) collective-permute-start(bf16[64,1600]{1,0:T(8,128)(2,1)S(1)} %slice.206), channel_id=1, source_target_pairs={{0,1},{2,0},{4,2},{6,4},{7,6},{5,7},{3,5},{1,3},{8,9},{10,8},{12,1... | collective-permute-start | bytes 614408 | tf_op jit(solution)/shard_map/gather_two/ppermute | solution.py:90
  235.3 10.3 %collective-permute-start.27 = (bf16[64,1600]{1,0:T(8,128)(2,1)S(1)}, bf16[64,1600]{1,0:T(8,128)(2,1)S(1)}, u32[]{:S(2)}, u32[]{:S(2)}) collective-permute-start(bf16[64,1600]{1,0:T(8,128)(2,1)S(1)} %get-tuple-element.239), channel_id=1, source_target_pairs={{0,1},{2,0},{4,2},{6,4},{7,6},{5,7},{3,5},{1,3},{8,9},{10,8},{12,1... | collective-permute-start | bytes 614408 | tf_op jit(solution)/shard_map/sum_two/ppermute | solution.py:90
  235.9 9.7 %collective-permute-start.26 = (bf16[64,1600]{1,0:T(8,128)(2,1)S(1)}, bf16[64,1600]{1,0:T(8,128)(2,1)S(1)}, u32[]{:S(2)}, u32[]{:S(2)}) collective-permute-start(bf16[64,1600]{1,0:T(8,128)(2,1)S(1)} %get-tuple-element.240), channel_id=1, source_target_pairs={{0,2},{2,4},{4,6},{6,7},{7,5},{5,3},{3,1},{1,0},{8,10},{10,12},{12... | collective-permute-start | bytes 614408 | tf_op jit(solution)/shard_map/sum_two/ppermute | solution.py:90
  246.9 14.5 %collective-permute-start.29 = (bf16[128,1600]{1,0:T(8,128)(2,1)S(1)}, bf16[128,1600]{1,0:T(8,128)(2,1)S(1)}, u32[]{:S(2)}, u32[]{:S(2)}) collective-permute-start(bf16[128,1600]{1,0:T(8,128)(2,1)S(1)} %get-tuple-element.228), channel_id=1, source_target_pairs={{0,1},{2,0},{4,2},{6,4},{7,6},{5,7},{3,5},{1,3},{8,9},{10,8},{12,1... | collective-permute-start | bytes 1228808 | tf_op jit(solution)/shard_map/sum_two/ppermute | solution.py:90
  247.6 15.0 %collective-permute-start.28 = (bf16[128,1600]{1,0:T(8,128)(2,1)S(1)}, bf16[128,1600]{1,0:T(8,128)(2,1)S(1)}, u32[]{:S(2)}, u32[]{:S(2)}) collective-permute-start(bf16[128,1600]{1,0:T(8,128)(2,1)S(1)} %get-tuple-element.229), channel_id=1, source_target_pairs={{0,2},{2,4},{4,6},{6,7},{7,5},{5,3},{3,1},{1,0},{8,10},{10,12},{12... | collective-permute-start | bytes 1228808 | tf_op jit(solution)/shard_map/sum_two/ppermute | solution.py:90
  264.0 25.1 %collective-permute-start.31 = (bf16[128,1600]{1,0:T(8,128)(2,1)S(1)}, bf16[128,1600]{1,0:T(8,128)(2,1)S(1)}, u32[]{:S(2)}, u32[]{:S(2)}) collective-permute-start(bf16[128,1600]{1,0:T(8,128)(2,1)S(1)} %get-tuple-element.113), channel_id=1, source_target_pairs={{0,1},{2,0},{4,2},{6,4},{7,6},{5,7},{3,5},{1,3},{8,9},{10,8},{12,1... | collective-permute-start | bytes 1228808 | tf_op jit(solution)/shard_map/sum_two/ppermute | solution.py:90
  264.1 25.1 %collective-permute-start.30 = (bf16[128,1600]{1,0:T(8,128)(2,1)S(1)}, bf16[128,1600]{1,0:T(8,128)(2,1)S(1)}, u32[]{:S(2)}, u32[]{:S(2)}) collective-permute-start(bf16[128,1600]{1,0:T(8,128)(2,1)S(1)} %get-tuple-element.112), channel_id=1, source_target_pairs={{0,2},{2,4},{4,6},{6,7},{7,5},{5,3},{3,1},{1,0},{8,10},{10,12},{12... | collective-permute-start | bytes 1228808 | tf_op jit(solution)/shard_map/sum_two/ppermute | solution.py:90
  290.6 10.4 %collective-permute-start.33 = (bf16[128,1600]{1,0:T(8,128)(2,1)S(1)}, bf16[128,1600]{1,0:T(8,128)(2,1)S(1)}, u32[]{:S(2)}, u32[]{:S(2)}) collective-permute-start(bf16[128,1600]{1,0:T(8,128)(2,1)S(1)} %get-tuple-element.118), channel_id=1, source_target_pairs={{0,1},{2,0},{4,2},{6,4},{7,6},{5,7},{3,5},{1,3},{8,9},{10,8},{12,1... | collective-permute-start | bytes 1228808 | tf_op jit(solution)/shard_map/sum_two/ppermute | solution.py:90
  290.8 11.6 %collective-permute-start.32 = (bf16[128,1600]{1,0:T(8,128)(2,1)S(1)}, bf16[128,1600]{1,0:T(8,128)(2,1)S(1)}, u32[]{:S(2)}, u32[]{:S(2)}) collective-permute-start(bf16[128,1600]{1,0:T(8,128)(2,1)S(1)} %get-tuple-element.117), channel_id=1, source_target_pairs={{0,2},{2,4},{4,6},{6,7},{7,5},{5,3},{3,1},{1,0},{8,10},{10,12},{12... | collective-permute-start | bytes 1228808 | tf_op jit(solution)/shard_map/sum_two/ppermute | solution.py:90
  315.5 9.0 %collective-permute-start.34 = (bf16[8,200,800]{2,1,0:T(8,128)(2,1)}, bf16[8,200,800]{2,1,0:T(8,128)(2,1)}, u32[]{:S(2)}, u32[]{:S(2)}) collective-permute-start(bf16[8,200,800]{2,1,0:T(8,128)(2,1)} %get-tuple-element.124), channel_id=1, source_target_pairs={{0,8},{8,0},{16,24},{24,16},{1,9},{9,1},{17,25},{25,17},{2,10},{10... | collective-permute-start | bytes 7680008 | tf_op jit(solution)/shard_map/out_sum/ppermute | solution.py:60
  315.5 14.6 %collective-permute-start.35 = (bf16[2,2,400,800]{3,2,1,0:T(8,128)(2,1)S(1)}, bf16[2,2,400,800]{3,2,1,0:T(8,128)(2,1)}, u32[]{:S(2)}, u32[]{:S(2)}) collective-permute-start(bf16[2,2,400,800]{3,2,1,0:T(8,128)(2,1)S(1)} %copy-done.8), channel_id=1, source_target_pairs={{0,8},{8,0},{16,24},{24,16},{1,9},{9,1},{17,25},{25,17},{2,10},{10... | collective-permute-start | bytes 7680008 | tf_op jit(solution)/shard_map/sum_two/unit_sum/ppermute | solution.py:60
  316.0 32.5 %all-to-all-start.1 = ((bf16[8,128,256]{2,1,0:T(8,128)(2,1)}), bf16[8,128,256]{2,1,0:T(8,128)(2,1)}, u32[]{:S(2)}, u32[]{:S(2)}) async-start(bf16[8,128,256]{2,1,0:T(8,128)(2,1)} %get-tuple-element.122), calls=%async_computation.2 | async-start | bytes 1048576 | tf_op jit(solution)/shard_map/all_to_all | solution.py:779
  321.1 139.3 %reduce-scatter.7.cloned.1.call-start = ((), (), s32[]{:S(2)}) async-start(), calls=%async_computation.7 | async-start | bytes 3225600
  348.5 36.0 %collective-permute-start.36 = (bf16[2,400,800]{2,1,0:T(8,128)(2,1)}, bf16[2,400,800]{2,1,0:T(8,128)(2,1)S(1)}, u32[]{:S(2)}, u32[]{:S(2)}) collective-permute-start(bf16[2,400,800]{2,1,0:T(8,128)(2,1)} %get-tuple-element.127), channel_id=1, source_target_pairs={{0,16},{8,24},{16,0},{24,8},{1,17},{9,25},{17,1},{25,9},{2,18},{10... | collective-permute-start | bytes 3840008 | tf_op jit(solution)/shard_map/out_sum/unit_sum/ppermute | solution.py:60
  381.7 17.7 %collective-permute-start.39 = (bf16[1,2,400,768]{3,2,1,0:T(8,128)(2,1)}, bf16[1,2,400,768]{3,2,1,0:T(8,128)(2,1)S(1)}, u32[]{:S(2)}, u32[]{:S(2)}) collective-permute-start(bf16[1,2,400,768]{3,2,1,0:T(8,128)(2,1)} %qkv_other.1), channel_id=1, source_target_pairs={{0,8},{8,0},{16,24},{24,16},{1,9},{9,1},{17,25},{25,17},{2,10},{10... | collective-permute-start | bytes 3686408 | tf_op jit(solution)/shard_map/sum_one/qkv_sum/ppermute | solution.py:60
  382.4 14.8 %collective-permute-start.38 = (bf16[64,1600]{1,0:T(8,128)(2,1)}, bf16[64,1600]{1,0:T(8,128)(2,1)S(1)}, u32[]{:S(2)}, u32[]{:S(2)}) collective-permute-start(bf16[64,1600]{1,0:T(8,128)(2,1)} %get-tuple-element.237), channel_id=1, source_target_pairs={{0,1},{2,0},{4,2},{6,4},{7,6},{5,7},{3,5},{1,3},{8,9},{10,8},{12,1... | collective-permute-start | bytes 614408 | tf_op jit(solution)/shard_map/sum_one/ppermute | solution.py:90
  383.8 13.4 %collective-permute-start.37 = (bf16[64,1600]{1,0:T(8,128)(2,1)S(1)}, bf16[64,1600]{1,0:T(8,128)(2,1)S(1)}, u32[]{:S(2)}, u32[]{:S(2)}) collective-permute-start(bf16[64,1600]{1,0:T(8,128)(2,1)S(1)} %get-tuple-element.238), channel_id=1, source_target_pairs={{0,2},{2,4},{4,6},{6,7},{7,5},{5,3},{3,1},{1,0},{8,10},{10,12},{12... | collective-permute-start | bytes 614408 | tf_op jit(solution)/shard_map/sum_one/ppermute | solution.py:90
  399.4 16.1 %collective-permute-start.41 = (bf16[128,1600]{1,0:T(8,128)(2,1)}, bf16[128,1600]{1,0:T(8,128)(2,1)S(1)}, u32[]{:S(2)}, u32[]{:S(2)}) collective-permute-start(bf16[128,1600]{1,0:T(8,128)(2,1)} %get-tuple-element.139), channel_id=1, source_target_pairs={{0,1},{2,0},{4,2},{6,4},{7,6},{5,7},{3,5},{1,3},{8,9},{10,8},{12,1... | collective-permute-start | bytes 1228808 | tf_op jit(solution)/shard_map/sum_one/ppermute | solution.py:90
  399.5 18.4 %collective-permute-start.40 = (bf16[128,1600]{1,0:T(8,128)(2,1)}, bf16[128,1600]{1,0:T(8,128)(2,1)}, u32[]{:S(2)}, u32[]{:S(2)}) collective-permute-start(bf16[128,1600]{1,0:T(8,128)(2,1)} %get-tuple-element.138), channel_id=1, source_target_pairs={{0,2},{2,4},{4,6},{6,7},{7,5},{5,3},{3,1},{1,0},{8,10},{10,12},{12... | collective-permute-start | bytes 1228808 | tf_op jit(solution)/shard_map/sum_one/ppermute | solution.py:90
  402.4 1.3 collective-permute-start.42
  403.7 4.6 collective-permute-start.43
  421.2 13.7 %collective-permute-start.45 = (bf16[128,1600]{1,0:T(8,128)(2,1)}, bf16[128,1600]{1,0:T(8,128)(2,1)S(1)}, u32[]{:S(2)}, u32[]{:S(2)}) collective-permute-start(bf16[128,1600]{1,0:T(8,128)(2,1)} %get-tuple-element.148), channel_id=1, source_target_pairs={{0,1},{2,0},{4,2},{6,4},{7,6},{5,7},{3,5},{1,3},{8,9},{10,8},{12,1... | collective-permute-start | bytes 1228808 | tf_op jit(solution)/shard_map/sum_one/ppermute | solution.py:90
  421.3 13.6 %collective-permute-start.44 = (bf16[128,1600]{1,0:T(8,128)(2,1)S(1)}, bf16[128,1600]{1,0:T(8,128)(2,1)}, u32[]{:S(2)}, u32[]{:S(2)}) collective-permute-start(bf16[128,1600]{1,0:T(8,128)(2,1)S(1)} %get-tuple-element.147), channel_id=1, source_target_pairs={{0,2},{2,4},{4,6},{6,7},{7,5},{5,3},{3,1},{1,0},{8,10},{10,12},{12... | collective-permute-start | bytes 1228808 | tf_op jit(solution)/shard_map/sum_one/ppermute | solution.py:90
  423.3 16.7 %collective-permute-start.53 = (bf16[1,400,768]{2,1,0:T(8,128)(2,1)}, bf16[1,400,768]{2,1,0:T(8,128)(2,1)}, u32[]{:S(2)}, u32[]{:S(2)}) collective-permute-start(bf16[1,400,768]{2,1,0:T(8,128)(2,1)} %get-tuple-element.146), channel_id=1, source_target_pairs={{0,16},{8,24},{16,0},{24,8},{1,17},{9,25},{17,1},{25,9},{2,18},{10... | collective-permute-start | bytes 1843208 | tf_op jit(solution)/shard_map/sum_one/qkv_sum/ppermute | solution.py:60
  437.1 16.6 %collective-permute-start.50 = (f32[19200]{0:T(1024)S(1)}, f32[19200]{0:T(1024)S(1)}, u32[]{:S(2)}, u32[]{:S(2)}) collective-permute-start(f32[19200]{0:T(1024)S(1)} %add.192), channel_id=1, source_target_pairs={{0,1},{1,0},{2,3},{3,2},{4,5},{5,4},{6,7},{7,6},{8,9},{9,8},{10,11... | collective-permute-start | bytes 230408 | tf_op jit(solution)/shard_map/sum_one/sum_vectors/ppermute | solution.py:60
  442.1 18.2 %collective-permute-start.54 = (bf16[400,256]{1,0:T(8,128)(2,1)S(1)}, bf16[400,256]{1,0:T(8,128)(2,1)S(1)}, u32[]{:S(2)}, u32[]{:S(2)}) collective-permute-start(bf16[400,256]{1,0:T(8,128)(2,1)S(1)} %get-tuple-element.232), channel_id=1, source_target_pairs={{5,2},{3,4},{4,1},{0,5},{1,3},{2,6},{6,7},{13,10},{11,12},{12,9},{... | collective-permute-start | bytes 614408 | tf_op jit(solution)/shard_map/sum_one/from_heads/ppermute | solution.py:217
  444.3 16.0 %collective-permute-start.55 = (bf16[400,256]{1,0:T(8,128)(2,1)S(1)}, bf16[400,256]{1,0:T(8,128)(2,1)S(1)}, u32[]{:S(2)}, u32[]{:S(2)}) collective-permute-start(bf16[400,256]{1,0:T(8,128)(2,1)S(1)} %get-tuple-element.231), channel_id=1, source_target_pairs={{3,6},{2,1},{5,5},{4,7},{0,2},{1,0},{11,14},{10,9},{13,13},{12,15}... | collective-permute-start | bytes 614408 | tf_op jit(solution)/shard_map/sum_one/from_heads/ppermute | solution.py:217
  446.5 13.8 %collective-permute-start.56 = (bf16[400,256]{1,0:T(8,128)(2,1)S(1)}, bf16[400,256]{1,0:T(8,128)(2,1)S(1)}, u32[]{:S(2)}, u32[]{:S(2)}) collective-permute-start(bf16[400,256]{1,0:T(8,128)(2,1)S(1)} %get-tuple-element.230), channel_id=1, source_target_pairs={{1,5},{0,0},{3,1},{2,3},{4,4},{5,7},{6,2},{9,13},{8,8},{11,9},{10,... | collective-permute-start | bytes 614408 | tf_op jit(solution)/shard_map/sum_one/from_heads/ppermute | solution.py:217
  447.2 23.1 %collective-permute-start.57 = (bf16[400,128]{1,0:T(8,128)(2,1)S(1)}, bf16[400,128]{1,0:T(8,128)(2,1)S(1)}, u32[]{:S(2)}, u32[]{:S(2)}) collective-permute-start(bf16[400,128]{1,0:T(8,128)(2,1)S(1)} %slice.269), channel_id=1, source_target_pairs={{4,2},{5,4},{0,3},{6,5},{2,0},{3,7},{1,6},{12,10},{13,12},{8,11},{... | collective-permute-start | bytes 307208 | tf_op jit(solution)/shard_map/sum_one/from_heads/ppermute | solution.py:217
  453.7 5.2 %collective-permute-start.51 = (f32[19200]{0:T(1024)S(1)}, f32[19200]{0:T(1024)S(1)}, u32[]{:S(2)}, u32[]{:S(2)}) collective-permute-start(f32[19200]{0:T(1024)S(1)} %add.198), channel_id=1, source_target_pairs={{0,2},{1,3},{2,0},{3,1},{4,6},{5,7},{6,4},{7,5},{8,10},{9,11},{10,... | collective-permute-start | bytes 230408 | tf_op jit(solution)/shard_map/sum_one/sum_vectors/ppermute | solution.py:60
  459.0 25.0 %collective-permute-start.52 = (f32[19200]{0:T(1024)S(1)}, f32[19200]{0:T(1024)S(1)}, u32[]{:S(2)}, u32[]{:S(2)}) collective-permute-start(f32[19200]{0:T(1024)S(1)} %add.199), channel_id=1, source_target_pairs={{0,4},{1,5},{2,6},{3,7},{4,0},{5,1},{6,2},{7,3},{8,12},{9,13},{10,... | collective-permute-start | bytes 230408 | tf_op jit(solution)/shard_map/sum_one/sum_vectors/ppermute | solution.py:60
  461.9 11.1 %collective-permute-start.46 = (bf16[100,400]{1,0:T(8,128)(2,1)S(1)}, bf16[100,400]{1,0:T(8,128)(2,1)S(1)}, u32[]{:S(2)}, u32[]{:S(2)}) collective-permute-start(bf16[100,400]{1,0:T(8,128)(2,1)S(1)} %get-tuple-element.241), channel_id=1, source_target_pairs={{0,16},{8,24},{16,0},{24,8},{1,17},{9,25},{17,1},{25,9},{2,18},{10... | collective-permute-start | bytes 240008 | tf_op jit(solution)/shard_map/sum_one/out_sum/ppermute | solution.py:60
  473.0 4.7 collective-permute-start.47
  478.9 8.2 %collective-permute-start.49 = (bf16[128,1600]{1,0:T(8,128)(2,1)S(1)}, bf16[128,1600]{1,0:T(8,128)(2,1)S(1)}, u32[]{:S(2)}, u32[]{:S(2)}) collective-permute-start(bf16[128,1600]{1,0:T(8,128)(2,1)S(1)} %copy-done.18), channel_id=1, source_target_pairs={{0,1},{2,0},{4,2},{6,4},{7,6},{5,7},{3,5},{1,3},{8,9},{10,8},{12,1... | collective-permute-start | bytes 1228808 | tf_op jit(solution)/shard_map/sum_one/ppermute | solution.py:90
  479.7 8.1 %collective-permute-start.48 = (bf16[128,1600]{1,0:T(8,128)(2,1)S(1)}, bf16[128,1600]{1,0:T(8,128)(2,1)S(1)}, u32[]{:S(2)}, u32[]{:S(2)}) collective-permute-start(bf16[128,1600]{1,0:T(8,128)(2,1)S(1)} %get-tuple-element.150), channel_id=1, source_target_pairs={{0,2},{2,4},{4,6},{6,7},{7,5},{5,3},{3,1},{1,0},{8,10},{10,12},{12... | collective-permute-start | bytes 1228808 | tf_op jit(solution)/shard_map/sum_one/ppermute | solution.py:90
  (44 other events, 658.2 us)
Sparse Core Ops, SparseCore 0:
  11.5 91.2 all-gather.5
  105.0 72.5 all-gather.3
  245.7 103.8 reduce-scatter.4
  353.3 95.2 reduce-scatter.6
